TPU v7x, 32 devices: a whole 2x2x4 slice. The times are simulated.
32 devices in a mesh: section: 2 (over core), seq: 16 (over z, y, x).
Axes of the slice: x: 2, y: 2, z: 4, core: 2. Of those that a mesh axis runs over, the one named last changes fastest.
Arguments:
- hidden_in: bfloat16 [2, 2048, 2048], P(None, 'seq'), may hold values from -6 to 6
- cotangent: float32 [2, 2048, 2048], P(None, 'seq'), may hold values from -6 to 6
- norm_gain: bfloat16 [2, 2048], P('section', 'seq'), may hold values from 0.5 to 1.5
- in_weight: bfloat16 [2, 2048, 8192], P('section', 'seq'), may hold values from -0.125 to 0.125
- conv_weight: bfloat16 [2, 4, 4096], P('section', None, 'seq'), may hold values from -3 to 3
- conv_bias: bfloat16 [2, 4096], P('section', 'seq'), may hold values from -3 to 3
- xproj_weight: bfloat16 [2, 4096, 160], P('section', 'seq'), may hold values from -0.09375 to 0.09375
- dt_weight: bfloat16 [2, 128, 4096], P('section', None, 'seq'), may hold values from -0.5 to 0.5
- dt_bias: bfloat16 [2, 4096], P('section', 'seq'), may hold values from -12 to -2
- skip_gain: bfloat16 [2, 4096], P('section', 'seq'), may hold values from 0.5 to 1.5
- out_weight: bfloat16 [2, 4096, 2048], P('section', 'seq'), may hold values from -0.25 to 0.25
Outputs:
- layer_outputs: float32 [2, 2, 2048, 2048], P('section', None, 'seq')
- input_grads: float32 [2, 2, 2048, 2048], P('section', None, 'seq')
- norm_gain_grad: float32 [2, 2048], P('section', 'seq')
- in_weight_grad: float32 [2, 2048, 8192], P('section', 'seq')
- conv_weight_grad: float32 [2, 4, 4096], P('section', None, 'seq')
- conv_bias_grad: float32 [2, 4096], P('section', 'seq')
- xproj_weight_grad: float32 [2, 4096, 160], P('section', 'seq')
- dt_weight_grad: float32 [2, 128, 4096], P('section', None, 'seq')
- dt_bias_grad: float32 [2, 4096], P('section', 'seq')
- skip_gain_grad: float32 [2, 4096], P('section', 'seq')
- out_weight_grad: float32 [2, 4096, 2048], P('section', 'seq')
All inputs are finite; a program needn't handle non-finite values.
Results may differ from a plain program's by a relative error of at most 0.018.
Values may be sent and summed in bfloat16 or wider, within the bound.
A program may use at most 384 MiB of HBM per device.

v0:
```python
import jax
import jax.numpy as jnp
from jax import lax
from jax.sharding import PartitionSpec as P

E = 4096
N = 16
R = 128
KC = 4


block_len = 16
norm_eps = 1e-05


def from_behind(x, axis, by):
    count = lax.axis_size(axis)
    pairs = [(i, i + by) for i in range(count) if 0 <= i + by < count]
    return lax.ppermute(x, axis, pairs)


def entering(x, axis, combine, identity, reverse):
    count, index = (lax.axis_size(axis), lax.axis_index(axis))
    everything = jax.tree.map(lambda part: lax.all_gather(part, axis), x)
    start = jax.tree.map(
        lambda part, zero: jnp.broadcast_to(jnp.asarray(zero, part.dtype), part.shape), x, identity
    )

    def hop(k, before):
        at = count - 1 - k if reverse else k
        reached = at > index if reverse else at < index
        new = combine(before, jax.tree.map(lambda part: part[at], everything))
        return jax.tree.map(lambda a, b: jnp.where(reached, a, b), new, before)

    return lax.fori_loop(0, count, hop, start)


def forward_dot(operand, factor):
    return jnp.dot(operand, factor, preferred_element_type=jnp.float32)


def cross_dot(operand, factor):
    return lax.dot_general(
        operand, factor, (((0,), (0,)), ((), ())), preferred_element_type=jnp.float32
    )


def back_dot(operand, factor):
    return lax.dot_general(
        operand, factor, (((1,), (1,)), ((), ())), preferred_element_type=jnp.float32
    )


def rms_norm(stream, norm_gain):
    inverse_rms = lax.rsqrt(jnp.mean(stream * stream, axis=-1, keepdims=True) + norm_eps)
    return stream * inverse_rms * norm_gain[None, :]


def causal_conv(extended, conv_taps, conv_shift):
    length = extended.shape[0] - conv_taps.shape[0] + 1
    summed = jnp.broadcast_to(conv_shift[None, :], (length, conv_shift.shape[0]))
    for offset in range(conv_taps.shape[0]):
        summed = summed + conv_taps[offset][None, :] * extended[offset : offset + length]
    return jax.nn.silu(summed)


def step_rates(delta_dot, delta_bias, key_vec):
    write_gate = jax.nn.sigmoid(delta_dot + delta_bias[None, :])
    return write_gate / (1.0 + write_gate * jnp.sum(key_vec * key_vec, axis=-1, keepdims=True))


def run_block(memory, strengths, key_blk, inner_blk, query_blk):
    outputs = []
    for position in range(strengths.shape[0]):
        square = key_blk[position] * key_blk[position]
        fading = 1.0 - square[:, None] * strengths[position][None, :]
        memory = (
            fading * memory
            + key_blk[position][:, None] * (strengths[position] * inner_blk[position])[None, :]
        )
        outputs.append(jnp.sum(memory * query_blk[position][:, None], axis=0))
    return (memory, jnp.stack(outputs))


def blocks_of(values):
    return values.reshape((values.shape[0] // block_len, block_len) + values.shape[1:])


def local_totals(strengths, key_vec, inner_act):

    def local_advance(running, pieces):
        product, memory = running
        rate_blk, key_blk, inner_blk = pieces
        for position in range(block_len):
            square = key_blk[position] * key_blk[position]
            fading = 1.0 - square[:, None] * rate_blk[position][None, :]
            product = product * fading
            memory = (
                fading * memory
                + key_blk[position][:, None] * (rate_blk[position] * inner_blk[position])[None, :]
            )
        return ((product, memory), None)

    extent = (key_vec.shape[1], strengths.shape[1])
    opening = (jnp.ones(extent, jnp.float32), jnp.zeros(extent, jnp.float32))
    return lax.scan(
        local_advance, opening, (blocks_of(strengths), blocks_of(key_vec), blocks_of(inner_act))
    )[0]


def start_totals(strengths, key_vec, query_vec, d_recur):

    def start_advance(running, pieces):
        product, pulled = running
        rate_blk, key_blk, query_blk, grad_blk = pieces
        for position in range(block_len):
            square = key_blk[position] * key_blk[position]
            product = product * (1.0 - square[:, None] * rate_blk[position][None, :])
            pulled = pulled + product * (query_blk[position][:, None] * grad_blk[position][None, :])
        return ((product, pulled), None)

    extent = (key_vec.shape[1], strengths.shape[1])
    opening = (jnp.ones(extent, jnp.float32), jnp.zeros(extent, jnp.float32))
    return lax.scan(
        start_advance,
        opening,
        (blocks_of(strengths), blocks_of(key_vec), blocks_of(query_vec), blocks_of(d_recur)),
    )[0]


def run_all(opening, strengths, key_vec, inner_act, query_vec):

    def run_advance(memory, pieces):
        closing, outputs = run_block(memory, pieces[0], pieces[1], pieces[2], pieces[3])
        return (closing, (memory, outputs))

    results = lax.scan(
        run_advance,
        opening,
        (blocks_of(strengths), blocks_of(key_vec), blocks_of(inner_act), blocks_of(query_vec)),
    )[1]
    return (results[0], results[1].reshape(strengths.shape))


def back_blocks(end_grad, borders, strengths, key_vec, inner_act, query_vec, d_recur):

    def retreat(running, pieces):
        border, rate_blk, key_blk, inner_blk, query_blk, grad_blk = pieces
        primal, pullback = jax.vjp(run_block, border, rate_blk, key_blk, inner_blk, query_blk)
        returned = pullback((running, grad_blk))
        return (returned[0], (returned[1], returned[2], returned[3], returned[4], primal[1]))

    results = lax.scan(
        retreat,
        end_grad,
        (
            borders,
            blocks_of(strengths),
            blocks_of(key_vec),
            blocks_of(inner_act),
            blocks_of(query_vec),
            blocks_of(d_recur),
        ),
        reverse=True,
    )[1]
    rows_total = strengths.shape[0]
    return tuple((piece.reshape((rows_total,) + piece.shape[2:]) for piece in results))


def chain_forward(earlier, later):
    return (earlier[0] * later[0], later[0] * earlier[1] + later[1])


def chain_backward(earlier, later):
    return (later[0] * earlier[0], later[1] + later[0] * earlier[1])


def project(stream, weights):
    normed = rms_norm(stream, weights[0].astype(jnp.float32)).astype(jnp.bfloat16)
    projected = forward_dot(normed, weights[1]).astype(jnp.bfloat16)
    return (normed, projected[:, :E], projected[:, E:].astype(jnp.float32))


def mixer_inputs(inner_bf, edge_rows, weights):
    extended = jnp.concatenate([edge_rows, inner_bf], axis=0).astype(jnp.float32)
    inner_act = causal_conv(
        extended, weights[2].astype(jnp.float32), weights[3].astype(jnp.float32)
    )
    inner_low = inner_act.astype(jnp.bfloat16)
    xproj_out = forward_dot(inner_low, weights[4]).astype(jnp.bfloat16)
    delta_low = xproj_out[:, :R]
    key_vec = xproj_out[:, R : R + N].astype(jnp.float32)
    query_vec = xproj_out[:, R + N :].astype(jnp.float32)
    delta_dot = forward_dot(delta_low, weights[5])
    strengths = step_rates(delta_dot, weights[6].astype(jnp.float32), key_vec)
    return (extended, inner_act, inner_low, delta_low, key_vec, query_vec, delta_dot, strengths)


def layer_forward(stream, weights):
    normed, inner_bf, gate_in = project(stream, weights)
    edge_rows = from_behind(inner_bf[inner_bf.shape[0] - KC + 1 :], "seq", 1)
    extended, inner_act, inner_low, delta_low, key_vec, query_vec, delta_dot, strengths = (
        mixer_inputs(inner_bf, edge_rows, weights)
    )
    product, memory = local_totals(strengths, key_vec, inner_act)
    opening = entering(
        (product, memory),
        "seq",
        chain_forward,
        (jnp.ones_like(product), jnp.zeros_like(memory)),
        False,
    )[1]
    borders, recur_out = run_all(opening, strengths, key_vec, inner_act, query_vec)
    recur_out = recur_out + weights[7].astype(jnp.float32)[None, :] * inner_act
    gated_bf = (recur_out * jax.nn.silu(gate_in)).astype(jnp.bfloat16)
    return (stream + forward_dot(gated_bf, weights[8]), edge_rows, borders)


def layer_backward(stream, edge_rows, borders, grad_out, weights):
    normed, inner_bf, gate_in = project(stream, weights)
    extended, inner_act, inner_low, delta_low, key_vec, query_vec, delta_dot, strengths = (
        mixer_inputs(inner_bf, edge_rows, weights)
    )
    skip_f = weights[7].astype(jnp.float32)
    grad_low = grad_out.astype(jnp.bfloat16)
    d_gated = lax.optimization_barrier(back_dot(grad_low, weights[8]).astype(jnp.bfloat16)).astype(
        jnp.float32
    )
    d_recur = d_gated * jax.nn.silu(gate_in)
    product, pulled = start_totals(strengths, key_vec, query_vec, d_recur)
    end_grad = entering(
        (product, pulled),
        "seq",
        chain_backward,
        (jnp.ones_like(product), jnp.zeros_like(pulled)),
        True,
    )[1]
    d_strength, d_key_rec, d_inner_rec, d_query, recur_part = back_blocks(
        end_grad, borders, strengths, key_vec, inner_act, query_vec, d_recur
    )
    recur_out = recur_part + skip_f[None, :] * inner_act
    gated_bf = (recur_out * jax.nn.silu(gate_in)).astype(jnp.bfloat16)
    d_out_weight = cross_dot(gated_bf, grad_low)
    d_gate_in = jax.vjp(jax.nn.silu, gate_in)[1](d_gated * recur_out)[0]
    d_skip = jnp.sum(d_recur * inner_act, axis=0)
    rate_pull = jax.vjp(step_rates, delta_dot, weights[6].astype(jnp.float32), key_vec)[1]
    d_delta_dot, d_dt_bias, d_key_rate = rate_pull(d_strength)
    d_delta_low = d_delta_dot.astype(jnp.bfloat16)
    d_dt_weight = cross_dot(delta_low, d_delta_low)
    d_xproj = jnp.concatenate(
        [back_dot(d_delta_low, weights[5]), d_key_rec + d_key_rate, d_query], axis=1
    ).astype(jnp.bfloat16)
    d_xproj_weight = cross_dot(inner_low, d_xproj)
    d_inner_act = back_dot(d_xproj, weights[4]) + skip_f[None, :] * d_recur + d_inner_rec
    conv_pull = jax.vjp(
        causal_conv, extended, weights[2].astype(jnp.float32), weights[3].astype(jnp.float32)
    )[1]
    d_extended, d_conv_weight, d_conv_bias = conv_pull(d_inner_act)
    spill = from_behind(d_extended[: KC - 1], "seq", -1)
    d_inner = d_extended[KC - 1 :] + jnp.pad(spill, ((d_inner_act.shape[0] - KC + 1, 0), (0, 0)))
    d_projected = jnp.concatenate([d_inner, d_gate_in], axis=1).astype(jnp.bfloat16)
    d_in_weight = cross_dot(normed, d_projected)
    d_normed = back_dot(d_projected, weights[1])
    norm_pull = jax.vjp(rms_norm, stream, weights[0].astype(jnp.float32))[1]
    d_stream, d_norm_gain = norm_pull(d_normed)
    gradients = (
        d_norm_gain,
        d_in_weight,
        d_conv_weight,
        d_conv_bias,
        d_xproj_weight,
        d_dt_weight,
        d_dt_bias,
        d_skip,
        d_out_weight,
    )
    return (grad_out + d_stream, gradients)


def place_into(store, micro_slot, active, values):
    current = lax.dynamic_index_in_dim(store, micro_slot, 0, keepdims=False)
    return lax.dynamic_update_index_in_dim(store, jnp.where(active, values, current), micro_slot, 0)


def on_device(
    hidden_in,
    cotangent,
    norm_gain,
    in_weight,
    conv_weight,
    conv_bias,
    xproj_weight,
    dt_weight,
    dt_bias,
    skip_gain,
    out_weight,
):
    section_index = lax.axis_index("section")
    gathered = (
        lax.all_gather(norm_gain, "seq", axis=1, tiled=True),
        lax.all_gather(in_weight, "seq", axis=1, tiled=True),
        lax.all_gather(conv_weight, "seq", axis=2, tiled=True),
        lax.all_gather(conv_bias, "seq", axis=1, tiled=True),
        lax.all_gather(xproj_weight, "seq", axis=1, tiled=True),
        lax.all_gather(dt_weight, "seq", axis=2, tiled=True),
        lax.all_gather(dt_bias, "seq", axis=1, tiled=True),
        lax.all_gather(skip_gain, "seq", axis=1, tiled=True),
        lax.all_gather(out_weight, "seq", axis=1, tiled=True),
    )
    weights = tuple((piece[0] for piece in gathered))
    micro_count, token_rows, model_width = hidden_in.shape
    inner_width = weights[3].shape[0]
    kept_stream = jnp.zeros((micro_count, token_rows, model_width), jnp.float32)
    kept_edges = jnp.zeros((micro_count, KC - 1, inner_width), jnp.bfloat16)
    kept_borders = jnp.zeros((micro_count, token_rows // block_len, N, inner_width), jnp.float32)
    produced = jnp.zeros((micro_count, token_rows, model_width), jnp.float32)
    arriving = jnp.zeros((token_rows, model_width), jnp.bfloat16)
    for moment in range(micro_count + 1):
        micro_index = moment - section_index
        active = (micro_index >= 0) & (micro_index < micro_count)
        micro_slot = jnp.clip(micro_index, 0, micro_count - 1)
        own_input = lax.dynamic_index_in_dim(hidden_in, micro_slot, 0, keepdims=False).astype(
            jnp.float32
        )
        stream = jnp.where(section_index == 0, own_input, arriving.astype(jnp.float32))
        result, edge_rows, borders = layer_forward(stream, weights)
        sent_rows = result.astype(jnp.bfloat16)
        shown = jnp.where(section_index == 0, sent_rows.astype(jnp.float32), result)
        kept_stream = place_into(kept_stream, micro_slot, active, stream)
        kept_edges = place_into(kept_edges, micro_slot, active, edge_rows)
        kept_borders = place_into(kept_borders, micro_slot, active, borders)
        produced = place_into(produced, micro_slot, active, shown)
        if moment < micro_count:
            arriving = from_behind(sent_rows, "section", 1)
    totals = tuple((jnp.zeros(piece.shape, jnp.float32) for piece in weights))
    input_grads = jnp.zeros((micro_count, token_rows, model_width), jnp.float32)
    returning = jnp.zeros((token_rows, model_width), jnp.bfloat16)
    for moment in range(micro_count + 1):
        micro_index = moment - (1 - section_index)
        active = (micro_index >= 0) & (micro_index < micro_count)
        micro_slot = jnp.clip(micro_index, 0, micro_count - 1)
        own_grad = lax.dynamic_index_in_dim(cotangent, micro_slot, 0, keepdims=False)
        grad_out = jnp.where(section_index == 1, own_grad, returning.astype(jnp.float32))
        stream = lax.dynamic_index_in_dim(kept_stream, micro_slot, 0, keepdims=False)
        edge_rows = lax.dynamic_index_in_dim(kept_edges, micro_slot, 0, keepdims=False)
        borders = lax.dynamic_index_in_dim(kept_borders, micro_slot, 0, keepdims=False)
        d_stream, gradients = layer_backward(stream, edge_rows, borders, grad_out, weights)
        masked = tuple((jnp.where(active, piece, 0.0) for piece in gradients))
        input_grads = place_into(input_grads, micro_slot, active, d_stream)
        totals = tuple((earlier_sum + addition for earlier_sum, addition in zip(totals, masked)))
        if moment < micro_count:
            returning = from_behind(d_stream.astype(jnp.bfloat16), "section", -1)
    totals = (
        lax.psum_scatter(totals[0][None], "seq", scatter_dimension=1, tiled=True),
        lax.psum_scatter(totals[1][None], "seq", scatter_dimension=1, tiled=True),
        lax.psum_scatter(totals[2][None], "seq", scatter_dimension=2, tiled=True),
        lax.psum_scatter(totals[3][None], "seq", scatter_dimension=1, tiled=True),
        lax.psum_scatter(totals[4][None], "seq", scatter_dimension=1, tiled=True),
        lax.psum_scatter(totals[5][None], "seq", scatter_dimension=2, tiled=True),
        lax.psum_scatter(totals[6][None], "seq", scatter_dimension=1, tiled=True),
        lax.psum_scatter(totals[7][None], "seq", scatter_dimension=1, tiled=True),
        lax.psum_scatter(totals[8][None], "seq", scatter_dimension=1, tiled=True),
    )
    return (
        produced[None],
        input_grads[None],
        totals[0],
        totals[1],
        totals[2],
        totals[3],
        totals[4],
        totals[5],
        totals[6],
        totals[7],
        totals[8],
    )


def solution(mesh):
    placed = (
        P(None, "seq", None),
        P(None, "seq", None),
        P("section", "seq"),
        P("section", "seq", None),
        P("section", None, "seq"),
        P("section", "seq"),
        P("section", "seq", None),
        P("section", None, "seq"),
        P("section", "seq"),
        P("section", "seq"),
        P("section", "seq", None),
    )
    return jax.shard_map(
        on_device,
        mesh=mesh,
        in_specs=placed,
        out_specs=(
            P("section", None, "seq", None),
            P("section", None, "seq", None),
            P("section", "seq"),
            P("section", "seq", None),
            P("section", None, "seq"),
            P("section", "seq"),
            P("section", "seq", None),
            P("section", None, "seq"),
            P("section", "seq"),
            P("section", "seq"),
            P("section", "seq", None),
        ),
        check_vma=False,
    )
```

profile of v0, /device:TPU:9, one launch (start us, length us, event | category | flops | bytes accessed | tf_op | source)
XLA Modules:
  0.0 6057.9 jit_solution(8395724052662417333)
XLA Ops:
  67.8 293.1 %all-gather.29.cloned.1.call-done = bf16[1,2048,8192]{2,1,0:T(8,128)(2,1)} async-done(((bf16[1,128,8192]{2,1,0:T(8,128)(2,1)}), bf16[1,2048,8192]{2,1,0:T(8,128)(2,1)}) %all-gather.29.cloned.1.call-update) | async-done | bytes 33554448 | tf_op jit(solution)/shard_map/all_gather | solution.py:301
  606.7 77.9 %all-gather.37.cloned.1.call-done = f32[256,4096]{1,0:T(8,128)} async-done(((f32[16,4096]{1,0:T(8,128)}), f32[256,4096]{1,0:T(8,128)}) %all-gather.37.cloned.1.call-update) | async-done | bytes 4194320 | tf_op jit(solution)/shard_map/all_gather | solution.py:24
  708.2 92.9 %while.282 = (s32[]{:T(128)}, f32[16,4096]{1,0:T(8,128)S(1)}, f32[8,16,4096]{2,1,0:T(8,128)}, f32[8,16,4096]{2,1,0:T(8,128)}, f32[8,16,16]{2,1,0:T(8,128)}, /*in...) while((s32[]{:T(128)}, f32[16,4096]{1,0:T(8,128)S(1)}, ...), condition=%wide.region_23.24_spmd, body=%wide.region_6.23_spmd.sunk | while | flops 9961745 | bytes 9447069 | solution.py:137
  807.6 68.8 %all-gather.35.cloned.1.call-done = bf16[1,4096,2048]{2,1,0:T(8,128)(2,1)} async-done(((bf16[1,256,2048]{2,1,0:T(8,128)(2,1)}), bf16[1,4096,2048]{2,1,0:T(8,128)(2,1)}) %all-gather.35.cloned.1.call-update) | async-done | bytes 16777232 | tf_op jit(solution)/shard_map/all_gather | solution.py:308
  923.7 50.6 while.290
  997.1 53.4 all-gather.43.cloned.1.call-done
  1050.4 77.5 %all-gather.41.cloned.1.call-done = f32[256,4096]{1,0:T(8,128)} async-done(((f32[16,4096]{1,0:T(8,128)}), f32[256,4096]{1,0:T(8,128)}) %all-gather.41.cloned.1.call-update) | async-done | bytes 4194320 | tf_op jit(solution)/shard_map/all_gather | solution.py:24
  1151.3 155.9 %while.283 = (s32[]{:T(128)}, f32[16,4096]{1,0:T(8,128)S(1)}, f32[8,16,4096]{2,1,0:T(8,128)}, f32[8,16,4096]{2,1,0:T(8,128)}, f32[8,16,16]{2,1,0:T(8,128)}, /*in...) while((s32[]{:T(128)}, f32[16,4096]{1,0:T(8,128)S(1)}, ...), condition=%wide.region_47.48_spmd, body=%wide.region_30.47_spmd.sunk | while | flops 9961745 | bytes 9447069 | solution.py:137
  1377.5 50.3 while.292
  1501.7 77.3 %all-gather.45.cloned.1.call-done = f32[256,4096]{1,0:T(8,128)} async-done(((f32[16,4096]{1,0:T(8,128)}), f32[256,4096]{1,0:T(8,128)}) %all-gather.45.cloned.1.call-update) | async-done | bytes 4194320 | tf_op jit(solution)/shard_map/all_gather | solution.py:24
  1602.5 84.1 %while.284 = (s32[]{:T(128)}, f32[16,4096]{1,0:T(8,128)S(1)}, f32[8,16,4096]{2,1,0:T(8,128)}, f32[8,16,4096]{2,1,0:T(8,128)}, f32[8,16,16]{2,1,0:T(8,128)S(1)}, ...) while((s32[]{:T(128)}, f32[16,4096]{1,0:T(8,128)S(1)}, ...), condition=%wide.region_71.72_spmd, body=%wide.region_54.71_spmd.sunk | while | flops 9961745 | bytes 9447069 | solution.py:137
  1759.6 354.6 %while.285 = (s32[]{:T(128)}, f32[16,4096]{1,0:T(8,128)S(1)}, f32[8,16,4096]{2,1,0:T(8,128)}, f32[8,16,16]{2,1,0:T(8,128)}, f32[8,16,4096]{2,1,0:T(8,128)}, /*in...) while((s32[]{:T(128)}, f32[16,4096]{1,0:T(8,128)S(1)}, ...), condition=%wide.region_175.176_spmd, body=%wide.region_78.175_spmd.sunk | while | flops 32914704 | bytes 18369260 | solution.py:153
  2281.3 72.9 %all-gather.53.cloned.1.call-done = f32[256,4096]{1,0:T(8,128)} async-done(((f32[16,4096]{1,0:T(8,128)}), f32[256,4096]{1,0:T(8,128)}) %all-gather.53.cloned.1.call-update) | async-done | bytes 4194320 | tf_op jit(solution)/shard_map/all_gather | solution.py:24
  2354.3 77.3 %all-gather.55.cloned.1.call-done = f32[256,4096]{1,0:T(8,128)} async-done(((f32[16,4096]{1,0:T(8,128)}), f32[256,4096]{1,0:T(8,128)}) %all-gather.55.cloned.1.call-update) | async-done | bytes 4194320 | tf_op jit(solution)/shard_map/all_gather | solution.py:24
  2457.3 356.2 %while.286 = (s32[]{:T(128)}, f32[16,4096]{1,0:T(8,128)S(1)}, f32[8,16,4096]{2,1,0:T(8,128)}, f32[8,16,16]{2,1,0:T(8,128)}, f32[8,16,4096]{2,1,0:T(8,128)}, /*in...) while((s32[]{:T(128)}, f32[16,4096]{1,0:T(8,128)S(1)}, ...), condition=%wide.region_281.282_spmd, body=%wide.region_184.281_spmd.sunk | while | flops 32914704 | bytes 18369260 | solution.py:153
  2895.9 59.5 while.298
  2961.0 70.3 %all-gather.57.cloned.1.call-done = f32[256,4096]{1,0:T(8,128)} async-done(((f32[16,4096]{1,0:T(8,128)}), f32[256,4096]{1,0:T(8,128)}) %all-gather.57.cloned.1.call-update) | async-done | bytes 4194320 | tf_op jit(solution)/shard_map/all_gather | solution.py:24
  3031.3 77.3 %all-gather.59.cloned.1.call-done = f32[256,4096]{1,0:T(8,128)} async-done(((f32[16,4096]{1,0:T(8,128)}), f32[256,4096]{1,0:T(8,128)}) %all-gather.59.cloned.1.call-update) | async-done | bytes 4194320 | tf_op jit(solution)/shard_map/all_gather | solution.py:24
  3134.3 361.3 %while.287 = (s32[]{:T(128)}, f32[16,4096]{1,0:T(8,128)S(1)}, f32[8,16,4096]{2,1,0:T(8,128)}, f32[8,16,16]{2,1,0:T(8,128)}, f32[8,16,4096]{2,1,0:T(8,128)}, /*in...) while((s32[]{:T(128)}, f32[16,4096]{1,0:T(8,128)S(1)}, ...), condition=%wide.region_387.388_spmd, body=%wide.region_290.387_spmd.sunk | while | flops 32914704 | bytes 18369260 | solution.py:153
  3681.0 66.4 %add_bitcast_fusion = f32[1,2048,8192]{2,1,0:T(8,128)} fusion(f32[2048,8192]{1,0:T(8,128)} %fusion.723, f32[2048,8192]{1,0:T(8,128)} %fusion.724, pred[]{:T(512)S(6)} %and.25, pred[]{:T(512)S(6)} %and.24, pred[]{:T(512)S(6)} %and.23, bf16[128,4096]{1,0:T(8,128)(2,1)S(1)} %copy-done.37, bf16[128,4096]{1,0:T(8,128)(2,1)} %fusion.693, ...), kind=kOutput, calls=%fused_computation.2280 | convolution fusion | flops 4383834112 | bytes 204481024 | tf_op jit(solution)/shard_map/dot_general | solution.py:43
  3823.2 78.9 %reduce-scatter.24.cloned.1.call-done = f32[1,128,256]{2,1,0:T(8,128)} async-done(((f32[1,128,4096]{2,1,0:T(8,128)}), f32[1,128,256]{2,1,0:T(8,128)}) %reduce-scatter.24.cloned.1.call-update) | async-done | bytes 131088 | tf_op jit(solution)/shard_map/reduce_scatter | solution.py:359
  3902.1 82.1 %reduce-scatter.22.cloned.1.call-done = f32[1,256,160]{1,2,0:T(8,128)} async-done(((f32[1,4096,160]{1,2,0:T(8,128)}), f32[1,256,160]{1,2,0:T(8,128)}) %reduce-scatter.22.cloned.1.call-update) | async-done | bytes 163856 | tf_op jit(solution)/shard_map/reduce_scatter | solution.py:358
  3984.2 700.5 %reduce-scatter.26.cloned.1.call-done = f32[1,256,2048]{2,1,0:T(8,128)} async-done(((f32[1,4096,2048]{2,1,0:T(8,128)}), f32[1,256,2048]{2,1,0:T(8,128)}) %reduce-scatter.26.cloned.1.call-update) | async-done | bytes 2097168 | tf_op jit(solution)/shard_map/reduce_scatter | solution.py:362
  4684.6 1366.3 %reduce-scatter.20.cloned.1.call-done = f32[1,128,8192]{2,1,0:T(8,128)} async-done(((f32[1,2048,8192]{2,1,0:T(8,128)}), f32[1,128,8192]{2,1,0:T(8,128)}) %reduce-scatter.20.cloned.1.call-update) | async-done | bytes 4194320 | tf_op jit(solution)/shard_map/reduce_scatter | solution.py:355
  (3853 shorter events, 3049.1 us)
Async XLA Ops:
  7.2 353.6 %all-gather.29.cloned.1.call-start = ((), (), s32[]{:S(2)}) async-start(), calls=%async_computation.9 | async-start | bytes 35651584 | tf_op jit(solution)/shard_map/all_gather | solution.py:301
  7.9 430.8 %all-gather.31.cloned.1.call-start = ((), (), s32[]{:S(2)}) async-start(), calls=%async_computation.10 | async-start | bytes 1392640 | tf_op jit(solution)/shard_map/all_gather | solution.py:304
  8.7 466.6 %all-gather.33.cloned.1.call-start = ((), (), s32[]{:S(2)}) async-start(), calls=%async_computation.11 | async-start | bytes 1114112 | tf_op jit(solution)/shard_map/all_gather | solution.py:305
  9.4 597.2 %all-gather.39.cloned.1.call-start = ((), (), s32[]{:S(2)}) async-start(), calls=%async_computation.18 | async-start | bytes 4456448 | tf_op jit(solution)/shard_map/all_gather | solution.py:24
  529.8 154.7 %all-gather.37.cloned.1.call-start = ((), (), s32[]{:S(2)}) async-start(), calls=%async_computation.17 | async-start | bytes 4456448 | tf_op jit(solution)/shard_map/all_gather | solution.py:24
  530.4 345.9 %all-gather.35.cloned.1.call-start = ((), (), s32[]{:S(2)}) async-start(), calls=%async_computation.12 | async-start | bytes 17825792 | tf_op jit(solution)/shard_map/all_gather | solution.py:308
  531.0 519.4 %all-gather.43.cloned.1.call-start = ((), (), s32[]{:S(2)}) async-start(), calls=%async_computation.20 | async-start | bytes 4456448 | tf_op jit(solution)/shard_map/all_gather | solution.py:24
  975.1 152.8 %all-gather.41.cloned.1.call-start = ((), (), s32[]{:S(2)}) async-start(), calls=%async_computation.19 | async-start | bytes 4456448 | tf_op jit(solution)/shard_map/all_gather | solution.py:24
  975.8 525.9 %all-gather.47.cloned.1.call-start = ((), (), s32[]{:S(2)}) async-start(), calls=%async_computation.22 | async-start | bytes 4456448 | tf_op jit(solution)/shard_map/all_gather | solution.py:24
  1431.5 264.6 %all-gather.49.cloned.1.call-start = ((), (), s32[]{:S(2)}) async-start(), calls=%async_computation.23 | async-start | bytes 4456448 | tf_op jit(solution)/shard_map/all_gather | solution.py:24
  1482.7 251.2 %all-gather.51.cloned.1.call-start = ((), (), s32[]{:S(2)}) async-start(), calls=%async_computation.24 | async-start | bytes 4456448 | tf_op jit(solution)/shard_map/all_gather | solution.py:24
  1491.9 862.3 %all-gather.53.cloned.1.call-start = ((), (), s32[]{:S(2)}) async-start(), calls=%async_computation.25 | async-start | bytes 4456448 | tf_op jit(solution)/shard_map/all_gather | solution.py:24
  2279.3 152.3 %all-gather.55.cloned.1.call-start = ((), (), s32[]{:S(2)}) async-start(), calls=%async_computation.26 | async-start | bytes 4456448 | tf_op jit(solution)/shard_map/all_gather | solution.py:24
  2279.9 751.4 %all-gather.57.cloned.1.call-start = ((), (), s32[]{:S(2)}) async-start(), calls=%async_computation.27 | async-start | bytes 4456448 | tf_op jit(solution)/shard_map/all_gather | solution.py:24
  2956.1 152.5 %all-gather.59.cloned.1.call-start = ((), (), s32[]{:S(2)}) async-start(), calls=%async_computation.28 | async-start | bytes 4456448 | tf_op jit(solution)/shard_map/all_gather | solution.py:24
  2956.7 799.2 %reduce-scatter.36.cloned.1.call-start = ((), (), s32[]{:S(2)}) async-start(), calls=%async_computation.33 | async-start | bytes 2228224
  2960.6 806.7 %reduce-scatter.32.cloned.1.call-start = ((), (), s32[]{:S(2)}) async-start(), calls=%async_computation.31 | async-start | bytes 2228224
  3521.1 247.7 %reduce-scatter.34.cloned.1.call-start = ((), (), s32[]{:S(2)}) async-start(), calls=%async_computation.32 | async-start | bytes 2228224
  3523.3 250.5 %reduce-scatter.28.cloned.1.call-start = ((), (), s32[]{:S(2)}) async-start(), calls=%async_computation.29 | async-start | bytes 1114112
  3546.6 275.0 %reduce-scatter.30.cloned.1.call-start = ((), (), s32[]{:S(2)}) async-start(), calls=%async_computation.30 | async-start | bytes 2228224
  3552.1 350.0 %reduce-scatter.24.cloned.1.call-start = ((), (), s32[]{:S(2)}) async-start(), calls=%async_computation.15 | async-start | bytes 2228224 | tf_op jit(solution)/shard_map/reduce_scatter | solution.py:359
  3556.3 427.9 %reduce-scatter.22.cloned.1.call-start = ((), (), s32[]{:S(2)}) async-start(), calls=%async_computation.14 | async-start | bytes 2785280 | tf_op jit(solution)/shard_map/reduce_scatter | solution.py:358
  3578.3 1106.3 %reduce-scatter.26.cloned.1.call-start = ((), (), s32[]{:S(2)}) async-start(), calls=%async_computation.16 | async-start | bytes 35651584 | tf_op jit(solution)/shard_map/reduce_scatter | solution.py:362
  3630.4 2420.6 %reduce-scatter.20.cloned.1.call-start = ((), (), s32[]{:S(2)}) async-start(), calls=%async_computation.13 | async-start | bytes 71303168 | tf_op jit(solution)/shard_map/reduce_scatter | solution.py:355
  (246 other events, 3768.6 us)
Sparse Core Ops, SparseCore 0:
  10.8 349.9 all-gather.28
  363.6 56.2 all-gather.30
  530.0 76.6 all-gather.38
  609.9 74.6 all-gather.36
  687.2 189.1 all-gather.34
  975.2 75.1 all-gather.42
  1053.2 74.6 all-gather.40
  1427.9 73.7 all-gather.46
  1504.3 74.6 all-gather.44
  1581.8 74.6 all-gather.48
  1659.2 74.7 all-gather.50
  2279.4 74.7 all-gather.52
  2356.9 74.6 all-gather.54
  2956.2 75.0 all-gather.56
  3033.9 74.6 all-gather.58
  3110.7 63.9 reduce-scatter.35
  3521.2 64.5 reduce-scatter.31
  3588.1 77.1 reduce-scatter.33
  3667.5 74.1 reduce-scatter.27
  3744.0 77.5 reduce-scatter.29
  3824.6 77.4 reduce-scatter.23
  3905.0 79.0 reduce-scatter.21
  3987.1 697.5 reduce-scatter.25
  4687.7 1363.1 reduce-scatter.19
  (1 shorter events, 52.6 us)
where the time goes:
time: 6090 us; the launch traced here: 6060 us
  waiting for transfers between devices  3370 us (55%)
  other arithmetic  1340 us (22%)
  local copies, waits for them, and re-layouts  686 us (11%)
  matrix products  455 us (7%)
  blocking collectives  141 us (2%)
    reduce_scatter x1, waiting for transfers between devices, on_device(): lax.psum_scatter(totals[1][None], 'seq', scatter_dimension=1, tiled=True)  1370 us
    reduce_scatter x1, waiting for transfers between devices, on_device(): lax.psum_scatter(totals[8][None], 'seq', scatter_dimension=1, tiled=True)  700 us
    all_gather x12, waiting for transfers between devices, entering(): everything = jax.tree.map(lambda part: lax.all_gather(part, axis), x)  678 us
    all_gather x1, waiting for transfers between devices, on_device(): lax.all_gather(in_weight, 'seq', axis=1, tiled=True)  293 us
    reduce_sum x192, other arithmetic, run_block(): fading = 1.0 - square[:, None] * strengths[position][None, :]  275 us
    mul x432, other arithmetic, run_block(): square = key_blk[position] * key_blk[position]  272 us
    dot_general x12, matrix products, cross_dot(): lax.dot_general(operand, factor, (((0,), (0,)), ((), ())), preferred_elem...  194 us
    mul x1152, other arithmetic, run_block(): strengths[position] * inner_blk[position]  155 us
  transfers between devices with their start and end apart: 35, of which 25 were waited for; matrix products, arithmetic and copies ran while one was open for 17% of the time, Pallas kernels for 0%

commit v1 on v0

v1 whole, which is shorter than its diff:
```python
import functools

import jax
import jax.numpy as jnp
from jax import lax
from jax.experimental import pallas as pl
from jax.experimental.pallas import tpu as pltpu
from jax.sharding import Mesh, PartitionSpec as P


N = 16
R = 128
KC = 4
BLOCK = 128
norm_eps = 1e-05
BF = jnp.bfloat16
F32 = jnp.float32
MESH = pl.DeviceIdType.MESH


def forward_dot(operand, factor):
    return jnp.dot(operand, factor, preferred_element_type=F32)


def cross_dot(operand, factor):
    return lax.dot_general(operand, factor, (((0,), (0,)), ((), ())), preferred_element_type=F32)


def back_dot(operand, factor):
    return lax.dot_general(operand, factor, (((1,), (1,)), ((), ())), preferred_element_type=F32)


def widths(channels):
    wide = min(channels, 128)
    return wide, channels // wide


def sum_rows(pieces):
    row = lax.broadcasted_iota(jnp.int32, pieces[0].shape, 0)
    shift = 1
    while len(pieces) > 1:
        keep = (row & shift) == 0
        pieces = [
            jnp.where(keep, a, b) + pltpu.roll(jnp.where(keep, b, a), shift, 0)
            for a, b in zip(pieces[0::2], pieces[1::2])
        ]
        shift *= 2
    return pieces[0]


def halves(v):
    return v[:8] + v[8:]


def lanes_of(p, wide):
    return slice(p * wide, (p + 1) * wide)


def recur_forward_kernel(rate_ref, act_ref, key_ref, query_ref, out_ref, before_ref, last_ref, memory_ref):
    wide, parts = widths(rate_ref.shape[1])

    @pl.when(pl.program_id(0) == 0)
    def _():
        memory_ref[...] = jnp.zeros_like(memory_ref)

    memory = [memory_ref[:, lanes_of(p, wide)] for p in range(parts)]
    for base in range(0, rate_ref.shape[0], 8):
        rates = rate_ref[base : base + 8, :]
        feeds = rates * act_ref[base : base + 8, :]
        sums = [[] for _ in range(parts)]
        for i in range(8):
            key = jnp.broadcast_to(key_ref[:, base + i : base + i + 1], (N, wide))
            query = jnp.broadcast_to(query_ref[:, base + i : base + i + 1], (N, wide))
            square = key * key
            for p in range(parts):
                lanes = lanes_of(p, wide)
                before_ref[base + i, :, lanes] = memory[p]
                memory[p] = (1.0 - rates[i : i + 1, lanes] * square) * memory[p] + key * feeds[i : i + 1, lanes]
                sums[p].append(halves(memory[p] * query))
        for p in range(parts):
            out_ref[base : base + 8, lanes_of(p, wide)] = sum_rows(sums[p])
    for p in range(parts):
        memory_ref[:, lanes_of(p, wide)] = memory[p]

    @pl.when(pl.program_id(0) == pl.num_programs(0) - 1)
    def _():
        last_ref[...] = memory_ref[...]


def recur_forward(rate, act, key_t, query_t):
    tokens, channels = rate.shape
    rows = pl.BlockSpec((BLOCK, channels), lambda i: (i, 0))
    cols = pl.BlockSpec((N, BLOCK), lambda i: (0, i))
    return pl.pallas_call(
        recur_forward_kernel,
        grid=(tokens // BLOCK,),
        in_specs=[rows, rows, cols, cols],
        out_specs=[
            rows,
            pl.BlockSpec((BLOCK, N, channels), lambda i: (i, 0, 0)),
            pl.BlockSpec((N, channels), lambda i: (0, 0)),
        ],
        out_shape=[
            jax.ShapeDtypeStruct((tokens, channels), F32),
            jax.ShapeDtypeStruct((tokens, N, channels), F32),
            jax.ShapeDtypeStruct((N, channels), F32),
        ],
        scratch_shapes=[pltpu.VMEM((N, channels), F32)],
        compiler_params=pltpu.CompilerParams(
            dimension_semantics=("arbitrary",), vmem_limit_bytes=40 * 2**20
        ),
        cost_estimate=pl.CostEstimate(
            flops=10 * tokens * N * channels, bytes_accessed=4 * tokens * channels * (N + 3), transcendentals=0
        ),
    )(rate, act, key_t, query_t)


def recur_backward_kernel(
    rate_ref, act_ref, grad_ref, key_ref, query_ref, before_ref, last_ref,
    d_rate_ref, d_act_ref, d_key_ref, d_query_ref, lam_ref, memory_ref, key_rows, query_rows,
):
    wide, parts = widths(rate_ref.shape[1])
    block = rate_ref.shape[0]

    @pl.when(pl.program_id(0) == 0)
    def _():
        lam_ref[...] = jnp.zeros_like(lam_ref)
        memory_ref[...] = last_ref[...]

    lam = [lam_ref[:, lanes_of(p, wide)] for p in range(parts)]
    memory = [memory_ref[:, lanes_of(p, wide)] for p in range(parts)]
    for base in reversed(range(0, block, 8)):
        rates = rate_ref[base : base + 8, :]
        acts = act_ref[base : base + 8, :]
        grads = grad_ref[base : base + 8, :]
        d_rates = [[None] * 8 for _ in range(parts)]
        d_acts = [[None] * 8 for _ in range(parts)]
        for i in reversed(range(8)):
            at = base + i
            key = jnp.broadcast_to(key_ref[:, at : at + 1], (N, wide))
            query = jnp.broadcast_to(query_ref[:, at : at + 1], (N, wide))
            square = key * key
            key_sum = query_sum = None
            for p in range(parts):
                lanes = lanes_of(p, wide)
                grad = grads[i : i + 1, lanes]
                before = before_ref[at, :, lanes]
                pulled = query * grad + lam[p]
                kept = key * before
                missing = acts[i : i + 1, lanes] - kept
                keyed = pulled * key
                scaled = pulled * rates[i : i + 1, lanes]
                d_acts[p][i] = halves(keyed)
                d_rates[p][i] = halves(keyed * missing)
                to_key = scaled * (missing - kept)
                to_query = memory[p] * grad
                key_sum = to_key if key_sum is None else key_sum + to_key
                query_sum = to_query if query_sum is None else query_sum + to_query
                lam[p] = pulled - scaled * square
                memory[p] = before
            key_rows[at * N : (at + 1) * N, :] = key_sum.astype(BF)
            query_rows[at * N : (at + 1) * N, :] = query_sum.astype(BF)
        for p in range(parts):
            lanes = lanes_of(p, wide)
            d_rate_ref[base : base + 8, lanes] = sum_rows(d_rates[p])
            d_act_ref[base : base + 8, lanes] = rates[:, lanes] * sum_rows(d_acts[p])
    for p in range(parts):
        lam_ref[:, lanes_of(p, wide)] = lam[p]
        memory_ref[:, lanes_of(p, wide)] = memory[p]

    ones = jnp.ones((wide, block), BF)
    token = lax.broadcasted_iota(jnp.int32, (block, N, block), 0)
    own = token == lax.broadcasted_iota(jnp.int32, (block, N, block), 2)
    for rows, result in ((key_rows, d_key_ref), (query_rows, d_query_ref)):
        sums = forward_dot(rows[...], ones).reshape(block, N, block)
        result[...] = jnp.sum(jnp.where(own, sums, 0.0), axis=0)


def recur_backward(rate, act, grad, key_t, query_t, before, last):
    tokens, channels = rate.shape
    count = tokens // BLOCK
    rows = pl.BlockSpec((BLOCK, channels), lambda i: (count - 1 - i, 0))
    cols = pl.BlockSpec((N, BLOCK), lambda i: (0, count - 1 - i))
    products = pltpu.VMEM((BLOCK * N, widths(channels)[0]), BF)
    return pl.pallas_call(
        recur_backward_kernel,
        grid=(count,),
        in_specs=[
            rows, rows, rows, cols, cols,
            pl.BlockSpec((BLOCK, N, channels), lambda i: (count - 1 - i, 0, 0)),
            pl.BlockSpec((N, channels), lambda i: (0, 0)),
        ],
        out_specs=[rows, rows, cols, cols],
        out_shape=[
            jax.ShapeDtypeStruct((tokens, channels), F32),
            jax.ShapeDtypeStruct((tokens, channels), F32),
            jax.ShapeDtypeStruct((N, tokens), F32),
            jax.ShapeDtypeStruct((N, tokens), F32),
        ],
        scratch_shapes=[pltpu.VMEM((N, channels), F32), pltpu.VMEM((N, channels), F32), products, products],
        compiler_params=pltpu.CompilerParams(
            dimension_semantics=("arbitrary",), vmem_limit_bytes=40 * 2**20
        ),
        cost_estimate=pl.CostEstimate(
            flops=30 * tokens * N * channels, bytes_accessed=4 * tokens * channels * (N + 5), transcendentals=0
        ),
    )(rate, act, grad, key_t, query_t, before, last)


def swap(value, axis):
    return lax.ppermute(value, axis, [(0, 1), (1, 0)])


def meet(z, count):
    barrier = pltpu.get_barrier_semaphore()

    def greet(where):
        pl.semaphore_signal(barrier, inc=1, device_id=where, device_id_type=MESH)

    greet({"y": 1 - lax.axis_index("y")})
    greet({"section": 1 - lax.axis_index("section")})
    pl.when(z > 0)(lambda: greet({"z": z - 1}))
    pl.when(z < count - 1)(lambda: greet({"z": z + 1}))
    inside = jnp.logical_and(z > 0, z < count - 1)
    pl.semaphore_wait(barrier, 2 + min(count - 1, 1) + inside.astype(jnp.int32))


def gather_kernel(
    count, shard_ref, out_ref, local_sem, right_send, right_recv, left_send, left_recv, y_send, y_recv, core_send, core_recv
):
    z, y, s = lax.axis_index("z"), lax.axis_index("y"), lax.axis_index("section")

    def at(z_of, y_of, s_of):
        return out_ref.at[(z_of * 2 + y_of) * 2 + s_of]

    def move(origin, y_of, send, recv, where, own=False):
        place = at(origin, y_of, s)
        return pltpu.make_async_remote_copy(
            src_ref=shard_ref if own else place,
            dst_ref=place,
            send_sem=send,
            recv_sem=recv,
            device_id=where,
            device_id_type=MESH,
        )

    def right(j, own=False):
        return move(z - j, y, right_send.at[j], right_recv.at[j], {"z": z + 1}, own)

    def left(j, own=False):
        return move(z + j, y, left_send.at[j], left_recv.at[j], {"z": z - 1}, own)

    def across(origin, own=False):
        return move(origin, y, y_send.at[origin], y_recv.at[origin], {"y": 1 - y}, own)

    def core(origin, y_of, own=False):
        k = origin * 2 + y_of
        return move(origin, y_of, core_send.at[k], core_recv.at[k], {"section": 1 - s}, own)

    def arrived(origin, y_of, s_of, recv):
        place = at(origin, y_of, s_of)
        pltpu.make_async_copy(place, place, recv).wait()

    meet(z, count)
    pl.when(z < count - 1)(lambda: right(0, True).start())
    pl.when(z > 0)(lambda: left(0, True).start())
    across(z, True).start()
    core(z, y, True).start()
    own = pltpu.make_async_copy(shard_ref, at(z, y, s), local_sem)
    own.start()

    def from_y(origin):
        arrived(origin, 1 - y, s, y_recv.at[origin])
        core(origin, 1 - y).start()

    for j in range(count - 1):

        @pl.when(z - 1 - j >= 0)
        def _(j=j):
            origin = z - 1 - j
            arrived(origin, y, s, right_recv.at[j])
            pl.when(z < count - 1)(lambda: right(j + 1).start())
            across(origin).start()
            core(origin, y).start()

        @pl.when(z + 1 + j <= count - 1)
        def _(j=j):
            origin = z + 1 + j
            arrived(origin, y, s, left_recv.at[j])
            pl.when(z > 0)(lambda: left(j + 1).start())
            across(origin).start()
            core(origin, y).start()

        if j == 0:
            from_y(z)
        else:
            pl.when(z - j >= 0)(lambda j=j: from_y(z - j))
            pl.when(z + j <= count - 1)(lambda j=j: from_y(z + j))

    last = count - 1
    if count > 1:
        pl.when(z - last >= 0)(lambda: from_y(z - last))
        pl.when(z + last <= count - 1)(lambda: from_y(z + last))
    else:
        from_y(z)

    own.wait()
    for k in range(count):
        for y_of in range(2):
            arrived(k, y_of, 1 - s, core_recv.at[k * 2 + y_of])
            core(k, y_of).wait_send()
        across(k).wait_send()
    for j in range(count - 1):
        pl.when((z - j >= 0) & (z < count - 1))(lambda j=j: right(j).wait_send())
        pl.when((z + j <= count - 1) & (z > 0))(lambda j=j: left(j).wait_send())


def gather_tokens(shard):
    count = lax.axis_size("z")
    rows, width = shard.shape
    dma = pltpu.SemaphoreType.DMA
    out = pl.pallas_call(
        functools.partial(gather_kernel, count),
        out_shape=jax.ShapeDtypeStruct((4 * count, rows, width), shard.dtype),
        in_specs=[pl.BlockSpec(memory_space=pl.ANY)],
        out_specs=pl.BlockSpec(memory_space=pl.ANY),
        scratch_shapes=[dma]
        + [dma((count,))] * 6
        + [dma((2 * count,))] * 2,
        compiler_params=pltpu.CompilerParams(collective_id=0, has_side_effects=True),
    )(shard)
    return out.reshape((-1, width))


def target_at(i, z, count):
    rights, lefts = count - 1 - z, z
    right_first = rights >= lefts
    fewer = jnp.minimum(rights, lefts)
    half = i // 2
    paired = i < 2 * fewer
    longer = jnp.logical_or(jnp.logical_not(paired), i % 2 == 0)
    index = jnp.where(paired, half, i - fewer)
    is_right = longer == right_first
    return jnp.where(i == count - 1, z, jnp.where(is_right, count - 1 - index, index))


def scatter_kernel(
    count, turned, a_ref, b_ref, out_ref, part, core_in, y_in, right_in, left_in,
    core_send, core_recv, y_send, y_recv, right_send, right_recv, left_send, left_recv,
):
    z, y, s = lax.axis_index("z"), lax.axis_index("y"), lax.axis_index("section")
    rows, width = out_ref.shape
    tile = min(width, 512)
    step = 32

    def core(slot):
        return pltpu.make_async_remote_copy(
            src_ref=part.at[slot, 1 - s], dst_ref=core_in.at[slot], send_sem=core_send.at[slot],
            recv_sem=core_recv.at[slot], device_id={"section": 1 - s}, device_id_type=MESH,
        )

    def across(k):
        return pltpu.make_async_remote_copy(
            src_ref=part.at[k * 2 + 1 - y, s], dst_ref=y_in.at[k], send_sem=y_send.at[k],
            recv_sem=y_recv.at[k], device_id={"y": 1 - y}, device_id_type=MESH,
        )

    def right(k):
        return pltpu.make_async_remote_copy(
            src_ref=part.at[k * 2 + y, s], dst_ref=right_in.at[k], send_sem=right_send.at[k],
            recv_sem=right_recv.at[k], device_id={"z": z + 1}, device_id_type=MESH,
        )

    def left(k):
        return pltpu.make_async_remote_copy(
            src_ref=part.at[k * 2 + y, s], dst_ref=left_in.at[k], send_sem=left_send.at[k],
            recv_sem=left_recv.at[k], device_id={"z": z - 1}, device_id_type=MESH,
        )

    def arrived(place, sem):
        pltpu.make_async_copy(place, place, sem).wait()

    def add_into(place, terms):
        @pl.loop(0, rows // step)
        def _(r):
            lines = pl.ds(pl.multiple_of(r * step, step), step)
            total = place[lines, :].astype(F32)
            for term in terms:
                total = total + term[lines, :].astype(F32)
            place[lines, :] = total.astype(place.dtype)

    meet(z, count)

    @pl.loop(0, count + 1)
    def _(i):
        @pl.when(i < count)
        def _():
            k = target_at(i, z, count)
            for turn in range(2):
                slot = k * 2 + (1 - y if turn == 0 else y)
                lines = pl.ds(pl.multiple_of(slot * 2 * rows, 2 * rows), 2 * rows)
                for c in range(0, width, tile):
                    if turned:
                        value = back_dot(a_ref[lines, :], b_ref[c : c + tile, :])
                    else:
                        value = forward_dot(a_ref[lines, :], b_ref[:, c : c + tile])
                    part[slot, :, :, c : c + tile] = value.astype(BF).reshape(2, rows, tile)
                core(slot).start()

        @pl.when(i > 0)
        def _():
            k = target_at(i - 1, z, count)
            slot = k * 2 + 1 - y
            arrived(core_in.at[slot], core_recv.at[slot])
            add_into(part.at[slot, s], [core_in.at[slot]])
            across(k).start()

    @pl.loop(0, count - 1)
    def _(i):
        k = target_at(i, z, count)
        slot = k * 2 + y
        arrived(core_in.at[slot], core_recv.at[slot])
        arrived(y_in.at[k], y_recv.at[k])
        add_into(part.at[slot, s], [core_in.at[slot], y_in.at[k]])

        @pl.when(k > z)
        def _():
            @pl.when(z > 0)
            def _():
                arrived(right_in.at[k], right_recv.at[k])
                add_into(part.at[slot, s], [right_in.at[k]])

            right(k).start()

        @pl.when(k < z)
        def _():
            @pl.when(z < count - 1)
            def _():
                arrived(left_in.at[k], left_recv.at[k])
                add_into(part.at[slot, s], [left_in.at[k]])

            left(k).start()

    slot = z * 2 + y
    arrived(core_in.at[slot], core_recv.at[slot])
    arrived(y_in.at[z], y_recv.at[z])

    @pl.loop(0, rows // step)
    def _(r):
        lines = pl.ds(pl.multiple_of(r * step, step), step)
        total = part[slot, s, lines, :].astype(F32)
        total = total + core_in[slot, lines, :].astype(F32)
        out_ref[lines, :] = total + y_in[z, lines, :].astype(F32)

    def add_out(place):
        @pl.loop(0, rows // step)
        def _(r):
            lines = pl.ds(pl.multiple_of(r * step, step), step)
            out_ref[lines, :] += place[z, lines, :].astype(F32)

    @pl.when(z > 0)
    def _():
        arrived(right_in.at[z], right_recv.at[z])
        add_out(right_in)

    @pl.when(z < count - 1)
    def _():
        arrived(left_in.at[z], left_recv.at[z])
        add_out(left_in)

    @pl.loop(0, count)
    def _(k):
        core(k * 2).wait_send()
        core(k * 2 + 1).wait_send()
        across(k).wait_send()
        pl.when(k > z)(lambda: right(k).wait_send())
        pl.when(k < z)(lambda: left(k).wait_send())


def scatter_columns(a, b, turned):
    count = lax.axis_size("z")
    tokens, width = a.shape[0], b.shape[0 if turned else 1]
    rows = tokens // (4 * count)
    dma = pltpu.SemaphoreType.DMA
    block = (rows, width)
    return pl.pallas_call(
        functools.partial(scatter_kernel, count, turned),
        out_shape=jax.ShapeDtypeStruct(block, F32),
        in_specs=[pl.BlockSpec(memory_space=pltpu.VMEM)] * 2,
        out_specs=pl.BlockSpec(memory_space=pltpu.VMEM),
        scratch_shapes=[
            pltpu.VMEM((2 * count, 2) + block, BF),
            pltpu.VMEM((2 * count,) + block, BF),
            pltpu.VMEM((count,) + block, BF),
            pltpu.VMEM((count,) + block, BF),
            pltpu.VMEM((count,) + block, BF),
            dma((2 * count,)), dma((2 * count,)),
        ]
        + [dma((count,))] * 6,
        compiler_params=pltpu.CompilerParams(
            collective_id=1 + turned, has_side_effects=True, vmem_limit_bytes=56 * 2**20
        ),
    )(a, b)


def scatter_dot(a, b, turned):
    tokens, width = a.shape[0], b.shape[0 if turned else 1]
    pieces = max(1, tokens * width // 2**22)
    size = width // pieces
    parts = [slice(i * size, (i + 1) * size) for i in range(pieces)]
    return jnp.concatenate([scatter_columns(a, b[at] if turned else b[:, at], turned) for at in parts], axis=1)


def total_kernel(
    count, x_ref, out_ref, part, core_in, y_out, y_in, z_out, z_in, done,
    core_send, core_recv, y_send, y_recv, z_send, z_recv, zb_send, zb_recv, yb_send, yb_recv, cb_send, cb_recv,
):
    z, y, s = lax.axis_index("z"), lax.axis_index("y"), lax.axis_index("section")
    lanes = part.shape[4]

    def span(k, y_of, s_of):
        at = ((k * 2 + y_of) * 2 + s_of) * lanes
        return slice(at, at + lanes)

    def remote(src, dst, send, recv, where):
        return pltpu.make_async_remote_copy(
            src_ref=src, dst_ref=dst, send_sem=send, recv_sem=recv, device_id=where, device_id_type=MESH
        )

    barrier = pltpu.get_barrier_semaphore()

    def greet(where):
        pl.semaphore_signal(barrier, inc=1, device_id=where, device_id_type=MESH)

    greet({"y": 1 - y})
    greet({"section": 1 - s})
    for hop in range(1, count):
        greet({"z": lax.rem(z + hop, count)})

    for k in range(count):
        for y_of in range(2):
            for s_of in range(2):
                part[s_of, y_of, k] = x_ref[:, span(k, y_of, s_of)]
    pl.semaphore_wait(barrier, count + 1)

    first = remote(part.at[1 - s], core_in, core_send, core_recv, {"section": 1 - s})
    first.start()
    first.wait_recv()
    for k in range(count):
        y_out[k] = (part[s, 1 - y, k] + core_in[1 - y, k]).astype(BF)
    second = remote(y_out, y_in, y_send, y_recv, {"y": 1 - y})
    second.start()
    for k in range(count):
        part[s, y, k] = part[s, y, k] + core_in[y, k]
    second.wait_recv()
    for k in range(count):
        total = part[s, y, k] + y_in[k].astype(F32)
        part[s, y, k] = total
        z_out[k] = total.astype(BF)

    def third(hop):
        to = lax.rem(z + hop, count)
        return remote(z_out.at[to], z_in.at[hop], z_send.at[hop], z_recv.at[hop], {"z": to})

    for hop in range(1, count):
        third(hop).start()
    total = part[s, y, z]
    for hop in range(1, count):
        third(hop).wait_recv()
        total = total + z_in[hop].astype(F32)
    done[s, y, z] = total.astype(BF)

    def fourth(hop):
        to = lax.rem(z + hop, count)
        return remote(done.at[s, y, z], done.at[s, y, z], zb_send.at[hop], zb_recv.at[hop], {"z": to})

    for hop in range(1, count):
        fourth(hop).start()
    for hop in range(1, count):
        fourth(hop).wait_recv()
    fifth = remote(done.at[s, y], done.at[s, y], yb_send, yb_recv, {"y": 1 - y})
    fifth.start()
    fifth.wait_recv()
    sixth = remote(done.at[s], done.at[s], cb_send, cb_recv, {"section": 1 - s})
    sixth.start()
    sixth.wait_recv()
    for k in range(count):
        for y_of in range(2):
            for s_of in range(2):
                out_ref[:, span(k, y_of, s_of)] = done[s_of, y_of, k]
    first.wait_send()
    second.wait_send()
    for hop in range(1, count):
        third(hop).wait_send()
        fourth(hop).wait_send()
    fifth.wait_send()
    sixth.wait_send()


def sum_columns(x):
    count = lax.axis_size("z")
    rows, tokens = x.shape
    lanes = tokens // (4 * count)
    dma = pltpu.SemaphoreType.DMA
    vmem = pltpu.VMEM
    return pl.pallas_call(
        functools.partial(total_kernel, count),
        out_shape=jax.ShapeDtypeStruct((rows, tokens), BF),
        in_specs=[pl.BlockSpec(memory_space=pltpu.VMEM)],
        out_specs=pl.BlockSpec(memory_space=pltpu.VMEM),
        scratch_shapes=[
            vmem((2, 2, count, rows, lanes), F32),
            vmem((2, count, rows, lanes), F32),
            vmem((count, rows, lanes), BF),
            vmem((count, rows, lanes), BF),
            vmem((count, rows, lanes), BF),
            vmem((count, rows, lanes), BF),
            vmem((2, 2, count, rows, lanes), BF),
            dma, dma, dma, dma, dma((count,)), dma((count,)), dma((count,)), dma((count,)), dma, dma, dma, dma,
        ],
        compiler_params=pltpu.CompilerParams(
            collective_id=3, has_side_effects=True, vmem_limit_bytes=56 * 2**20
        ),
    )(x)


def spread_kernel(count, shard_ref, out_ref, z_send, z_recv, pair_send, pair_recv):
    z, y, x, s = (lax.axis_index(name) for name in ("z", "y", "x", "section"))

    def remote(place, send, recv, where):
        return pltpu.make_async_remote_copy(
            src_ref=place, dst_ref=place, send_sem=send, recv_sem=recv, device_id=where, device_id_type=MESH
        )

    barrier = pltpu.get_barrier_semaphore()
    peers = [{"y": 1 - y}, {"x": 1 - x}, {"section": 1 - s}]
    peers += [{"z": lax.rem(z + hop, count)} for hop in range(1, count)]
    for where in peers:
        pl.semaphore_signal(barrier, inc=1, device_id=where, device_id_type=MESH)
    out_ref[s, x, y, z] = shard_ref[...]
    pl.semaphore_wait(barrier, len(peers))
    along = [
        remote(out_ref.at[s, x, y, z], z_send.at[hop], z_recv.at[hop], {"z": lax.rem(z + hop, count)})
        for hop in range(1, count)
    ]
    steps = [
        remote(out_ref.at[s, x, y], pair_send.at[0], pair_recv.at[0], {"y": 1 - y}),
        remote(out_ref.at[s, x], pair_send.at[1], pair_recv.at[1], {"x": 1 - x}),
        remote(out_ref.at[s], pair_send.at[2], pair_recv.at[2], {"section": 1 - s}),
    ]
    for copy in along:
        copy.start()
    for copy in along:
        copy.wait_recv()
    for copy in steps:
        copy.start()
        copy.wait_recv()
    for copy in along + steps:
        copy.wait_send()


def spread(shard):
    count, width = lax.axis_size("z"), shard.shape[0]
    block = (16, max(width, 128))
    padded = jnp.pad(shard[None, :], ((0, block[0] - 1), (0, block[1] - width)))
    dma = pltpu.SemaphoreType.DMA
    out = pl.pallas_call(
        functools.partial(spread_kernel, count),
        out_shape=jax.ShapeDtypeStruct((2, 2, 2, count) + block, shard.dtype),
        in_specs=[pl.BlockSpec(memory_space=pltpu.VMEM)],
        out_specs=pl.BlockSpec(memory_space=pltpu.VMEM),
        scratch_shapes=[dma((count,)), dma((count,)), dma((3,)), dma((3,))],
        compiler_params=pltpu.CompilerParams(collective_id=4, has_side_effects=True),
    )(padded)
    return jnp.transpose(out[:, :, :, :, 0, :width], (0, 3, 2, 1, 4)).reshape((2, -1))


def send(value, axes, pairs):
    return lax.ppermute(value, axes, pairs)


def at_home():
    return lax.axis_index("x") == lax.axis_index("section")


def to_home(value):
    return lax.ppermute(value, ("section", "x"), [(1, 0), (2, 3)])


def from_home(value):
    return lax.ppermute(value, ("section", "x"), [(0, 1), (3, 2)])


def own_tokens(pair):
    low = lax.axis_index("x") == 0
    keep = jnp.where(low, pair[0], pair[1])
    return jnp.where(at_home(), keep, from_home(jnp.where(low, pair[1], pair[0])))


def own_block(piece, layer):
    other = 1 - layer
    sent = lax.ppermute(piece, ("section", "x"), [(layer * 2 + other, other * 2 + other)])
    held = jnp.where(lax.axis_index("section") == layer, piece, sent)
    return jnp.where(at_home(), held, from_home(held))


def own_columns(rows, layer):
    count = 2 * lax.axis_size("z")
    depth = rows.shape[0]
    blocks = jnp.transpose(rows.reshape((depth, 2, count, 2, -1)), (3, 2, 0, 1, 4)).reshape((2, count, depth, -1))
    sent = lax.ppermute(blocks[1 - layer], "section", [(layer, 1 - layer)])
    mine = jnp.where(lax.axis_index("section") == layer, blocks[layer], sent)
    mine = lax.all_to_all(mine, ("z", "y"), split_axis=0, concat_axis=0, tiled=True)
    other = swap(mine, "x")
    low = lax.axis_index("x") == 0
    both = jnp.stack([jnp.where(low, mine, other), jnp.where(low, other, mine)], axis=1)
    return both.reshape((2 * count * depth, -1))


def home_rows(grad, layer):
    count = 2 * lax.axis_size("z")
    pieces = grad.reshape((count, 2, -1, grad.shape[1]))
    low = lax.axis_index("x") == 0
    give = jnp.where(low, pieces[:, 1], pieces[:, 0])
    total = jnp.where(low, pieces[:, 0], pieces[:, 1]).astype(F32) + swap(give, "x").astype(F32)
    mine = lax.all_to_all(total.astype(BF), ("z", "y"), split_axis=0, concat_axis=0, tiled=True)
    return mine, lax.ppermute(mine, "section", [(1 - layer, layer)])


def home_block(piece, layer):
    total = piece + to_home(piece.astype(BF)).astype(F32)
    other = 1 - layer
    sent = lax.ppermute(total.astype(BF), ("section", "x"), [(other * 2 + other, layer * 2 + other)])
    return total, sent


def home_tokens(rows, layer):
    got = to_home(rows)
    low = lax.axis_index("x") == 0
    both = jnp.stack([jnp.where(low, rows, got), jnp.where(low, got, rows)])
    other = 1 - layer
    sent = lax.ppermute(both, ("section", "x"), [(other * 2 + other, layer * 2 + other)])
    return jnp.where(at_home(), both, sent)


def silu_slope(v):
    gate = jax.nn.sigmoid(v)
    return gate, gate * (1.0 + v * (1.0 - gate))


def layer_forward(stream, weights, hidden):
    gain, in_weight, conv_weight, conv_bias, xproj_weight, dt_weight, dt_bias, skip, out_weight = weights
    channels = conv_bias.shape[0]
    inverse = lax.rsqrt(jnp.mean(stream * stream, axis=-1, keepdims=True) + norm_eps)
    normed = gather_tokens((stream * inverse * gain[None, :]).astype(BF))
    projected = forward_dot(normed, in_weight).astype(BF)
    inner = projected[:, :channels].astype(F32)
    gate_in = projected[:, channels:].astype(F32)
    tokens = inner.shape[0]
    extended = jnp.concatenate([jnp.zeros((KC - 1, channels), F32), inner], axis=0)
    conv = jnp.broadcast_to(conv_bias[None, :], (tokens, channels))
    for tap in range(KC):
        conv = conv + conv_weight[tap][None, :] * extended[tap : tap + tokens]
    act = jax.nn.silu(conv)
    xproj = sum_columns(back_dot(xproj_weight, act.astype(BF)))
    key_t, query_t = xproj[R : R + N].astype(F32), xproj[R + N :].astype(F32)
    key_norm = jnp.sum(key_t * key_t, axis=0)[:, None]
    write = jax.nn.sigmoid(cross_dot(xproj[:R], dt_weight) + dt_bias[None, :])
    rate = write / (1.0 + write * key_norm)
    recur, before, last = recur_forward(rate, act, key_t, query_t)
    recur = recur + skip[None, :] * act
    gated = (recur * jax.nn.silu(gate_in)).astype(BF)
    if hidden:
        partial = forward_dot(gated, out_weight).astype(BF)
        out = lax.psum_scatter(partial, ("z", "y", "section"), scatter_dimension=0, tiled=True).astype(F32)
    else:
        out = scatter_dot(gated, out_weight, False)
    saved = (stream, inverse, normed, extended, gate_in, conv, act, xproj, key_t, query_t, key_norm, write, rate, recur, gated, before, last)
    return stream + out, saved


def layer_backward(grad_out, grad_low, saved, weights):
    gain, in_weight, conv_weight, conv_bias, xproj_weight, dt_weight, dt_bias, skip, out_weight = weights
    stream, inverse, normed, extended, gate_in, conv, act, xproj, key_t, query_t, key_norm, write, rate, recur, gated, before, last = saved
    tokens = act.shape[0]
    d_out_weight = cross_dot(gated, grad_low)
    d_gated = back_dot(grad_low, out_weight).astype(BF).astype(F32)
    gate, slope = silu_slope(gate_in)
    d_recur = d_gated * (gate_in * gate)
    d_gate_in = d_gated * recur * slope
    d_skip = jnp.sum(d_recur * act, axis=0)
    d_rate, d_act_rec, d_key_t, d_query_t = recur_backward(rate, act, d_recur, key_t, query_t, before, last)
    share = 1.0 / (1.0 + write * key_norm)
    pulled = d_rate * share * share
    d_pre = pulled * write * (1.0 - write)
    d_key_rate = -2.0 * key_t * jnp.sum(pulled * write * write, axis=1)[None, :]
    d_dt_bias = jnp.sum(d_pre, axis=0)
    d_delta = d_pre.astype(BF)
    d_dt_weight = forward_dot(xproj[:R], d_delta)
    d_xproj = jnp.concatenate([back_dot(dt_weight, d_delta), d_key_t + d_key_rate, d_query_t], axis=0)
    d_xproj = sum_columns(d_xproj)
    d_xproj_weight = forward_dot(d_xproj, act.astype(BF))
    d_act = cross_dot(d_xproj, xproj_weight) + skip[None, :] * d_recur + d_act_rec
    d_conv = d_act * silu_slope(conv)[1]
    d_conv_weight = jnp.stack([jnp.sum(d_conv * extended[tap : tap + tokens], axis=0) for tap in range(KC)])
    d_conv_bias = jnp.sum(d_conv, axis=0)
    later = jnp.concatenate([d_conv, jnp.zeros((KC - 1, d_conv.shape[1]), F32)], axis=0)
    d_inner = sum(conv_weight[tap][None, :] * later[KC - 1 - tap : KC - 1 - tap + tokens] for tap in range(KC))
    d_projected = jnp.concatenate([d_inner, d_gate_in], axis=1).astype(BF)
    d_in_weight = cross_dot(normed, d_projected)
    d_normed = scatter_dot(d_projected, in_weight, True)
    scaled = gain[None, :] * d_normed
    mean = jnp.mean(stream * scaled, axis=-1, keepdims=True)
    d_stream = grad_out + inverse * scaled - stream * inverse**3 * mean
    small = jnp.concatenate(
        [d_conv_weight, d_conv_bias[None], d_dt_bias[None], d_skip[None], d_dt_weight, d_xproj_weight],
        axis=0,
    )
    return d_stream, (d_in_weight.astype(BF), small, d_out_weight)


def on_device(
    hidden_in, cotangent, norm_gain, in_weight, conv_weight, conv_bias, xproj_weight, dt_weight, dt_bias, skip_gain, out_weight
):
    small = jnp.concatenate(
        [conv_weight[0], conv_bias, dt_bias, skip_gain, dt_weight[0], jnp.swapaxes(xproj_weight[0], 0, 1)], axis=0
    )
    gains = spread(norm_gain[0]).astype(F32)
    weights = []
    for layer in range(2):
        part = own_block(small, layer)
        part_f = part.astype(F32)
        weights.append(
            (
                gains[layer],
                own_columns(in_weight[0], layer),
                part_f[:KC],
                part_f[KC],
                part[KC + 3 + R :],
                part[KC + 3 : KC + 3 + R],
                part_f[KC + 1],
                part_f[KC + 2],
                own_block(out_weight[0], layer),
            )
        )

    stream = own_tokens(hidden_in).astype(F32)
    grad = own_tokens(cotangent)
    first, saved_first = layer_forward(stream, weights[0], False)
    first = first.astype(BF)
    grad_low, _ = lax.optimization_barrier((grad.astype(BF), saved_first[2]))
    grad_low = lax.all_gather(grad_low, ("z", "y", "section"), axis=0, tiled=True)
    second, saved_second = layer_forward(first.astype(F32), weights[1], True)
    grad_second, grads_second = layer_backward(grad, grad_low, saved_second, weights[1])
    grad_low = grad_second.astype(BF)
    grad_first, grads_first = layer_backward(grad_low.astype(F32), gather_tokens(grad_low), saved_first, weights[0])

    upper = lax.axis_index("section") == 1

    def of_layer(pair):
        return jnp.where(upper, pair[1], pair[0])

    layer_outputs = of_layer((home_tokens(first, 0), home_tokens(second.astype(BF), 1))).astype(F32)
    input_grads = of_layer((home_tokens(grad_first.astype(BF), 0), home_tokens(grad_second.astype(BF), 1))).astype(F32)
    columns = [home_rows(grads[0], layer) for layer, grads in enumerate((grads_first, grads_second))]
    mine, sent = of_layer([c[0] for c in columns]), of_layer([c[1] for c in columns])
    both = jnp.stack([jnp.where(upper, sent, mine), jnp.where(upper, mine, sent)])
    both = both.reshape((2, mine.shape[0], mine.shape[1], 2, -1))
    d_in = jnp.transpose(both, (2, 3, 1, 0, 4)).reshape((mine.shape[1], -1)).astype(F32)
    d_gain = jnp.sum(d_in * in_weight[0].astype(F32), axis=1) / norm_gain[0].astype(F32)

    def block_of(which):
        pieces = [home_block(grads[which], layer) for layer, grads in enumerate((grads_first, grads_second))]
        held, sent = of_layer([p[0] for p in pieces]), of_layer([p[1] for p in pieces])
        return jnp.where(at_home(), held, sent.astype(F32))

    small, d_out = block_of(1), block_of(2)
    return (
        layer_outputs[None],
        input_grads[None],
        d_gain[None],
        d_in[None],
        small[None, :KC],
        small[None, KC],
        jnp.swapaxes(small[KC + 3 + R :], 0, 1)[None],
        small[None, KC + 3 : KC + 3 + R],
        small[None, KC + 1],
        small[None, KC + 2],
        d_out[None],
    )


def solution(mesh):
    sections, seq = mesh.devices.shape
    split = Mesh(mesh.devices.reshape((sections, seq // 4, 2, 2)), ("section", "z", "y", "x"))
    seq = ("z", "y", "x")
    placed = (
        P(None, seq, None),
        P(None, seq, None),
        P("section", seq),
        P("section", seq, None),
        P("section", None, seq),
        P("section", seq),
        P("section", seq, None),
        P("section", None, seq),
        P("section", seq),
        P("section", seq),
        P("section", seq, None),
    )
    return jax.shard_map(
        on_device,
        mesh=split,
        in_specs=placed,
        out_specs=(P("section", None, seq, None), P("section", None, seq, None)) + placed[2:],
        check_vma=False,
    )
```

time: 6090 us -> 1100 us (0.18)
  waiting for transfers between devices: 3370 us -> 121 us
  other arithmetic: 1340 us -> 108 us
  local copies, waits for them, and re-layouts: 686 us -> 49.3 us
  Pallas kernels: 0 us -> 601 us
  matrix products: 455 us -> 84.9 us
  blocking collectives: 141 us -> 0 us
  starting transfers between devices: 35.3 us -> 104 us
    reduce_scatter x4 -> x1, waiting for transfers between devices: 2230 us -> 0.01 us  [layer_forward(): lax.psum_scatter(partial, ('z', 'y', 'section'), scatter_dimension=0, til...]
    all_gather x16 -> x1, waiting for transfers between devices: 1070 us -> 0.01 us  [on_device(): lax.all_gather(grad_low, ('z', 'y', 'section'), axis=0, tiled=True)]
    pallas_call x0 -> x15, Pallas kernels: none -> 601 us  [the longest x3 193 us: scatter_columns(): pl.pallas_call(functools.partial(scatter_kernel, count, turned), out_shap...]
    mul x2068 -> x4, other arithmetic: 493 us -> 5.22 us  [the longest x2 5.21 us: layer_forward(): act = jax.nn.silu(conv)]
    slice x156 -> x9, local copies, waits for them, and re-layouts: 421 us -> 8.51 us  [the longest x2 5.85 us: own_columns(): sent = lax.ppermute(blocks[1 - layer], 'section', [(layer, 1 - layer)])]
    reduce_sum x448 -> x11, other arithmetic: 420 us -> 26.2 us  [the longest x2 8.59 us: layer_backward(): d_skip = jnp.sum(d_recur * act, axis=0)]
    dot_general x12 -> x8, matrix products: 194 us -> 46 us  [cross_dot(): lax.dot_general(operand, factor, (((0,), (0,)), ((), ())), preferred_elem...]
    dynamic_update_slice x108 -> x0, other arithmetic: 141 us -> none  [the longest x48 80 us: run_all(): lax.scan(run_advance, opening, (blocks_of(strengths), blocks_of(key_vec),...]
  transfers between devices with their start and end apart: 35 -> 40, of which waited for: 25 -> 10; matrix products, arithmetic and copies ran while one was open for 17% -> 15% of each run, Pallas kernels for 0% -> 50%
where the time goes in v1:
time: 1100 us; the launch traced here: 1080 us
  Pallas kernels  601 us (55%)
  waiting for transfers between devices  121 us (11%)
  other arithmetic  108 us (10%)
  starting transfers between devices  104 us (9%)
  matrix products  84.9 us (8%)
  local copies, waits for them, and re-layouts  49.3 us (4%)
  between operations  16 us (1%)
    pallas_call x3, Pallas kernels, scatter_columns(): pl.pallas_call(functools.partial(scatter_kernel, count, turned), out_shap...  193 us
    pallas_call x3, Pallas kernels, gather_tokens(): pl.pallas_call(functools.partial(gather_kernel, count), out_shape=jax.Sha...  167 us
    pallas_call x4, Pallas kernels, sum_columns(): pl.pallas_call(functools.partial(total_kernel, count), out_shape=jax.Shap...  125 us
    pallas_call x2, Pallas kernels, recur_backward(): pl.pallas_call(recur_backward_kernel, grid=(count,), in_specs=[rows, rows...  60.9 us
    ppermute x8, waiting for transfers between devices, to_home(): return lax.ppermute(value, ('section', 'x'), [(1, 0), (2, 3)])  51.3 us
    dot_general x8, matrix products, cross_dot(): lax.dot_general(operand, factor, (((0,), (0,)), ((), ())), preferred_elem...  46 us
    pallas_call x2, Pallas kernels, recur_forward(): pl.pallas_call(recur_forward_kernel, grid=(tokens // BLOCK,), in_specs=[r...  36.6 us
    ppermute x8, starting transfers between devices, to_home(): return lax.ppermute(value, ('section', 'x'), [(1, 0), (2, 3)])  34 us
  transfers between devices with their start and end apart: 40, of which 10 were waited for; matrix products, arithmetic and copies ran while one was open for 15% of the time, Pallas kernels for 50%

profile of v1, /device:TPU:9, one launch (start us, length us, event | category | flops | bytes accessed | tf_op | source)
XLA Modules:
  0.0 1084.0 jit_solution(9791610930602083187)
XLA Ops:
  14.3 17.8 %shard_map.194 = bf16[2,2,2,4,16,128]{5,4,3,2,1,0:T(8,128)(2,1)} custom-call(bf16[16,128]{1,0:T(8,128)(2,1)} %pad.8.shard_ref), custom_call_target="tpu_custom_call" | custom-call | tf_op jit(solution)/shard_map/pallas_call | solution.py:667
  40.2 52.4 %shard_map.195 = bf16[16,128,2048]{2,1,0:T(8,128)(2,1)} custom-call(bf16[128,2048]{1,0:T(8,128)(2,1)} %fusion.36.shard_ref), custom_call_target="tpu_custom_call" | custom-call | tf_op jit(solution)/shard_map/pallas_call | solution.py:322
  132.6 27.7 %all-to-all-done = bf16[8,128,512]{2,1,0:T(8,128)(2,1)S(1)} async-done(((bf16[8,128,512]{2,1,0:T(8,128)(2,1)}), bf16[8,128,512]{2,1,0:T(8,128)(2,1)S(1)}, u32[]{:S(2)}, u32[]{:S(2)}) %all-to-all-start) | async-done | bytes 1048608 | tf_op jit(solution)/shard_map/all_to_all | solution.py:713
  176.4 20.9 %collective-permute-done.8 = bf16[295,256]{1,0:T(8,128)(2,1)S(1)} collective-permute-done((bf16[295,256]{1,0:T(8,128)(2,1)S(1)}, bf16[295,256]{1,0:T(8,128)(2,1)S(1)}, u32[]{:S(2)}, u32[]{:S(2)}) %collective-permute-start.8) | collective-permute-done | bytes 151072 | tf_op jit(solution)/shard_map/ppermute | solution.py:691
  213.3 8.9 convolution_convert_fusion.4
  226.6 33.4 %shard_map.196 = bf16[160,2048]{1,0:T(8,128)(2,1)} custom-call(f32[160,2048]{1,0:T(8,128)} %fusion.64.x_ref), custom_call_target="tpu_custom_call" | custom-call | tf_op jit(solution)/shard_map/pallas_call | solution.py:606
  265.1 18.4 %shard_map.197 = (f32[2048,256]{1,0:T(8,128)S(1)}, f32[2048,16,256]{2,1,0:T(8,128)}, f32[16,256]{1,0:T(8,128)S(1)}) custom-call(f32[2048,256]{1,0:T(8,128)S(1)} %get-tuple-element.131.rate_ref, f32[2048,256]{1,0:T(8,128)S(1)} %get-tuple-element.69.act_ref, f32[16,2048]{1,0:T(8,128)S(1)} %get-tuple-element.103.key_ref, ...), custom_call_target="tpu_custom_call" | custom-call | flops 83886080 | bytes 39845888 | tf_op jit(solution)/shard_map/pallas_call | solution.py:94
  286.5 55.7 %shard_map.198 = f32[128,2048]{1,0:T(8,128)} custom-call(bf16[2048,256]{1,0:T(8,128)(2,1)} %multiply_convert_fusion.1.a_ref, bf16[256,2048]{1,0:T(8,128)(2,1)} %broadcast_select_fusion.8.b_ref), custom_call_target="tpu_custom_call" | custom-call | tf_op jit(solution)/shard_map/pallas_call | solution.py:486
  345.5 53.6 %shard_map.199 = bf16[16,128,2048]{2,1,0:T(8,128)(2,1)} custom-call(bf16[128,2048]{1,0:T(8,128)(2,1)} %fusion.44.shard_ref), custom_call_target="tpu_custom_call" | custom-call | tf_op jit(solution)/shard_map/pallas_call | solution.py:322
  414.1 27.8 %shard_map.200 = bf16[160,2048]{1,0:T(8,128)(2,1)} custom-call(f32[160,2048]{1,0:T(8,128)} %fusion.60.x_ref), custom_call_target="tpu_custom_call" | custom-call | tf_op jit(solution)/shard_map/pallas_call | solution.py:606
  447.0 18.2 %shard_map.201 = (f32[2048,256]{1,0:T(8,128)S(1)}, f32[2048,16,256]{2,1,0:T(8,128)}, f32[16,256]{1,0:T(8,128)S(1)}) custom-call(f32[2048,256]{1,0:T(8,128)S(1)} %get-tuple-element.133.rate_ref, f32[2048,256]{1,0:T(8,128)S(1)} %get-tuple-element.65.act_ref, f32[16,2048]{1,0:T(8,128)S(1)} %get-tuple-element.101.key_ref, ...), custom_call_target="tpu_custom_call" | custom-call | flops 83886080 | bytes 39845888 | tf_op jit(solution)/shard_map/pallas_call | solution.py:94
  474.5 30.5 %shard_map.202 = (f32[2048,256]{1,0:T(8,128)S(1)}, f32[2048,256]{1,0:T(8,128)S(1)}, f32[16,2048]{1,0:T(8,128)S(1)}, f32[16,2048]{1,0:T(8,128)S(1)}) custom-call(f32[2048,256]{1,0:T(8,128)S(1)} %copy-done.6, f32[2048,256]{1,0:T(8,128)S(1)} %copy-done.1, f32[2048,256]{1,0:T(8,128)S(1)} %get-tuple-element.135.grad_ref, ...), custom_call_target="tpu_custom_call" | custom-call | flops 251658240 | bytes 44040192 | tf_op jit(solution)/shard_map/pallas_call | solution.py:185
  509.3 27.0 %shard_map.203 = bf16[160,2048]{1,0:T(8,128)(2,1)} custom-call(f32[160,2048]{1,0:T(8,128)} %pad_maximum_fusion.4.x_ref), custom_call_target="tpu_custom_call" | custom-call | tf_op jit(solution)/shard_map/pallas_call | solution.py:606
  569.7 9.3 fusion.89
  593.5 80.6 %shard_map.204 = f32[128,2048]{1,0:T(8,128)} custom-call(bf16[2048,512]{1,0:T(8,128)(2,1)} %pad_maximum_fusion.2.a_ref, bf16[2048,512]{1,0:T(8,128)(2,1)} %bitcast.175), custom_call_target="tpu_custom_call" | custom-call | tf_op jit(solution)/shard_map/pallas_call | solution.py:486
  680.6 13.9 %collective-permute-done.26 = bf16[295,256]{1,0:T(8,128)(2,1)S(1)} collective-permute-done((bf16[295,256]{1,0:T(8,128)(2,1)S(1)}, bf16[295,256]{1,0:T(8,128)(2,1)S(1)}, u32[]{:S(2)}, u32[]{:S(2)}) %collective-permute-start.26) | collective-permute-done | bytes 151072 | tf_op jit(solution)/shard_map/ppermute | solution.py:687
  703.7 10.5 all-to-all-start.2
  717.4 61.2 %shard_map.205 = bf16[16,128,2048]{2,1,0:T(8,128)(2,1)} custom-call(bf16[128,2048]{1,0:T(8,128)(2,1)} %get-tuple-element.104.shard_ref), custom_call_target="tpu_custom_call" | custom-call | tf_op jit(solution)/shard_map/pallas_call | solution.py:322
  790.0 30.4 %shard_map.206 = (f32[2048,256]{1,0:T(8,128)S(1)}, f32[2048,256]{1,0:T(8,128)S(1)}, f32[16,2048]{1,0:T(8,128)S(1)}, f32[16,2048]{1,0:T(8,128)S(1)}) custom-call(f32[2048,256]{1,0:T(8,128)S(1)} %copy-done.4, f32[2048,256]{1,0:T(8,128)S(1)} %get-tuple-element.69.act_ref, f32[2048,256]{1,0:T(8,128)S(1)} %get-tuple-element.137.grad_ref, ...), custom_call_target="tpu_custom_call" | custom-call | flops 251658240 | bytes 44040192 | tf_op jit(solution)/shard_map/pallas_call | solution.py:185
  832.4 36.8 %shard_map.207 = bf16[160,2048]{1,0:T(8,128)(2,1)} custom-call(f32[160,2048]{1,0:T(8,128)} %pad_maximum_fusion.5.x_ref), custom_call_target="tpu_custom_call" | custom-call | tf_op jit(solution)/shard_map/pallas_call | solution.py:606
  878.5 8.6 convolution_convert_fusion.1
  892.1 57.1 %shard_map.208 = f32[128,2048]{1,0:T(8,128)} custom-call(bf16[2048,512]{1,0:T(8,128)(2,1)} %pad_maximum_fusion.3.a_ref, bf16[2048,512]{1,0:T(8,128)(2,1)} %bitcast.173), custom_call_target="tpu_custom_call" | custom-call | tf_op jit(solution)/shard_map/pallas_call | solution.py:486
  965.3 29.6 %collective-permute-done.20 = bf16[128,2048]{1,0:T(8,128)(2,1)S(1)} collective-permute-done((bf16[128,2048]{1,0:T(8,128)(2,1)S(1)}, bf16[128,2048]{1,0:T(8,128)(2,1)S(1)}, u32[]{:S(2)}, u32[]{:S(2)}) %collective-permute-start.20) | collective-permute-done | bytes 524320 | tf_op jit(solution)/shard_map/ppermute | solution.py:687
  1021.2 9.9 all-to-all-done.3
  (390 shorter events, 327.8 us)
Async XLA Ops:
  7.2 459.4 %all-gather.2.cloned.1.call-start = ((), (), s32[]{:S(2)}) async-start(), calls=%async_computation.6 | async-start | bytes 8912896 | tf_op jit(solution)/shard_map/all_gather | solution.py:852
  8.5 27.8 %collective-permute-start = (bf16[128,2048]{1,0:T(8,128)(2,1)S(1)}, bf16[128,2048]{1,0:T(8,128)(2,1)S(1)}, u32[]{:S(2)}, u32[]{:S(2)}) collective-permute-start(bf16[128,2048]{1,0:T(8,128)(2,1)S(1)} %select_bitcast_fusion.16), channel_id=1, source_target_pairs={{0,1},{17,16},{2,3},{19,18},{4,5},{21,20},{6,7},{23,22},{8,9},{25,... | collective-permute-start | bytes 1572872 | tf_op jit(solution)/shard_map/ppermute | solution.py:691
  12.5 80.2 %collective-permute-start.17 = (f32[128,2048]{1,0:T(8,128)}, f32[128,2048]{1,0:T(8,128)}, u32[]{:S(2)}, u32[]{:S(2)}) collective-permute-start(f32[128,2048]{1,0:T(8,128)} %select_bitcast_fusion.3), channel_id=1, source_target_pairs={{0,1},{17,16},{2,3},{19,18},{4,5},{21,20},{6,7},{23,22},{8,9},{25,... | collective-permute-start | bytes 3145736 | tf_op jit(solution)/shard_map/ppermute | solution.py:691
  112.4 48.0 %all-to-all-start = ((bf16[8,128,512]{2,1,0:T(8,128)(2,1)}), bf16[8,128,512]{2,1,0:T(8,128)(2,1)S(1)}, u32[]{:S(2)}, u32[]{:S(2)}) async-start(bf16[8,128,512]{2,1,0:T(8,128)(2,1)} %broadcast_select_fusion.9), calls=%async_computation | async-start | bytes 2097152 | tf_op jit(solution)/shard_map/all_to_all | solution.py:713
  122.7 46.2 %collective-permute-start.11 = (bf16[256,2048]{1,0:T(8,128)(2,1)}, bf16[256,2048]{1,0:T(8,128)(2,1)}, u32[]{:S(2)}, u32[]{:S(2)}) collective-permute-start(bf16[256,2048]{1,0:T(8,128)(2,1)} %bitcast.180), channel_id=1, source_target_pairs={{16,0},{18,2},{20,4},{22,6},{24,8},{26,10},{28,12},{30,14}} | collective-permute-start | bytes 3145736 | tf_op jit(solution)/shard_map/ppermute | solution.py:702
  124.9 43.9 %collective-permute-start.5 = (bf16[256,2048]{1,0:T(8,128)(2,1)}, bf16[256,2048]{1,0:T(8,128)(2,1)}, u32[]{:S(2)}, u32[]{:S(2)}) collective-permute-start(bf16[256,2048]{1,0:T(8,128)(2,1)} %bitcast.181), channel_id=1, source_target_pairs={{1,17},{3,19},{5,21},{7,23},{9,25},{11,27},{13,29},{15,31}} | collective-permute-start | bytes 3145736 | tf_op jit(solution)/shard_map/ppermute | solution.py:702
  130.2 44.0 %collective-permute-start.2 = (bf16[295,256]{1,0:T(8,128)(2,1)S(1)}, bf16[295,256]{1,0:T(8,128)(2,1)S(1)}, u32[]{:S(2)}, u32[]{:S(2)}) collective-permute-start(bf16[295,256]{1,0:T(8,128)(2,1)S(1)} %get-tuple-element.117), channel_id=1, source_target_pairs={{0,1},{17,16},{2,3},{19,18},{4,5},{21,20},{6,7},{23,22},{8,9},{25,... | collective-permute-start | bytes 453128 | tf_op jit(solution)/shard_map/ppermute | solution.py:691
  160.3 43.1 %all-to-all-start.1 = ((bf16[8,128,512]{2,1,0:T(8,128)(2,1)}), bf16[8,128,512]{2,1,0:T(8,128)(2,1)}, u32[]{:S(2)}, u32[]{:S(2)}) async-start(bf16[8,128,512]{2,1,0:T(8,128)(2,1)} %broadcast_select_fusion.5), calls=%async_computation.1 | async-start | bytes 2097152 | tf_op jit(solution)/shard_map/all_to_all | solution.py:713
  168.9 545.4 %reduce-scatter.2.cloned.1.call-start = ((), (), s32[]{:S(2)}) async-start(), calls=%async_computation.5 | async-start | bytes 8912896 | tf_op jit(solution)/shard_map/reduce_scatter | solution.py:775
  171.6 27.3 %collective-permute-start.6 = (bf16[256,2048]{1,0:T(8,128)(2,1)S(1)}, bf16[256,2048]{1,0:T(8,128)(2,1)S(1)}, u32[]{:S(2)}, u32[]{:S(2)}) collective-permute-start(bf16[256,2048]{1,0:T(8,128)(2,1)S(1)} %get-tuple-element.97), channel_id=1, source_target_pairs={{0,1},{17,16},{2,3},{19,18},{4,5},{21,20},{6,7},{23,22},{8,9},{25,... | collective-permute-start | bytes 3145736 | tf_op jit(solution)/shard_map/ppermute | solution.py:691
  174.2 37.5 %collective-permute-start.4 = (bf16[8,128,512]{2,1,0:T(8,128)(2,1)S(1)}, bf16[8,128,512]{2,1,0:T(8,128)(2,1)}, u32[]{:S(2)}, u32[]{:S(2)}) collective-permute-start(bf16[8,128,512]{2,1,0:T(8,128)(2,1)S(1)} %all-to-all-done), channel_id=1, source_target_pairs={{0,1},{1,0},{2,3},{3,2},{4,5},{5,4},{6,7},{7,6},{8,9},{9,8},{10,11... | collective-permute-start | bytes 3145736 | tf_op jit(solution)/shard_map/ppermute | solution.py:211
  197.4 269.2 %collective-permute-start.12 = (bf16[256,2048]{1,0:T(8,128)(2,1)}, bf16[256,2048]{1,0:T(8,128)(2,1)}, u32[]{:S(2)}, u32[]{:S(2)}) collective-permute-start(bf16[256,2048]{1,0:T(8,128)(2,1)} %get-tuple-element.96), channel_id=1, source_target_pairs={{0,1},{17,16},{2,3},{19,18},{4,5},{21,20},{6,7},{23,22},{8,9},{25,... | collective-permute-start | bytes 3145736 | tf_op jit(solution)/shard_map/ppermute | solution.py:691
  203.4 195.7 %collective-permute-start.10 = (bf16[8,128,512]{2,1,0:T(8,128)(2,1)}, bf16[8,128,512]{2,1,0:T(8,128)(2,1)}, u32[]{:S(2)}, u32[]{:S(2)}) collective-permute-start(bf16[8,128,512]{2,1,0:T(8,128)(2,1)} %all-to-all-done.1), channel_id=1, source_target_pairs={{0,1},{1,0},{2,3},{3,2},{4,5},{5,4},{6,7},{7,6},{8,9},{9,8},{10,11... | collective-permute-start | bytes 3145736 | tf_op jit(solution)/shard_map/ppermute | solution.py:211
  567.9 453.4 %collective-permute-start.16 = (bf16[2,128,2048]{2,1,0:T(8,128)(2,1)}, bf16[2,128,2048]{2,1,0:T(8,128)(2,1)}, u32[]{:S(2)}, u32[]{:S(2)}) collective-permute-start(bf16[2,128,2048]{2,1,0:T(8,128)(2,1)} %pad_maximum_fusion.7), channel_id=1, source_target_pairs={{17,1},{19,3},{21,5},{23,7},{25,9},{27,11},{29,13},{31,15}} | collective-permute-start | bytes 3145736 | tf_op jit(solution)/shard_map/ppermute | solution.py:742
  578.9 117.6 %collective-permute-start.30 = (bf16[256,2048]{1,0:T(8,128)(2,1)}, bf16[256,2048]{1,0:T(8,128)(2,1)}, u32[]{:S(2)}, u32[]{:S(2)}) collective-permute-start(bf16[256,2048]{1,0:T(8,128)(2,1)} %get-tuple-element.139), channel_id=1, source_target_pairs={{1,0},{16,17},{3,2},{18,19},{5,4},{20,21},{7,6},{22,23},{9,8},{24,... | collective-permute-start | bytes 3145736 | tf_op jit(solution)/shard_map/ppermute | solution.py:687
  695.2 257.0 %collective-permute-start.28 = (bf16[295,256]{1,0:T(8,128)(2,1)}, bf16[295,256]{1,0:T(8,128)(2,1)}, u32[]{:S(2)}, u32[]{:S(2)}) collective-permute-start(bf16[295,256]{1,0:T(8,128)(2,1)} %fusion.70), channel_id=1, source_target_pairs={{0,16},{2,18},{4,20},{6,22},{8,24},{10,26},{12,28},{14,30}} | collective-permute-start | bytes 453128 | tf_op jit(solution)/shard_map/ppermute | solution.py:733
  699.8 340.7 %collective-permute-start.32 = (bf16[256,2048]{1,0:T(8,128)(2,1)}, bf16[256,2048]{1,0:T(8,128)(2,1)}, u32[]{:S(2)}, u32[]{:S(2)}) collective-permute-start(bf16[256,2048]{1,0:T(8,128)(2,1)} %fusion.32), channel_id=1, source_target_pairs={{0,16},{2,18},{4,20},{6,22},{8,24},{10,26},{12,28},{14,30}} | collective-permute-start | bytes 3145736 | tf_op jit(solution)/shard_map/ppermute | solution.py:733
  703.7 301.7 %all-to-all-start.2 = ((bf16[8,128,512]{2,1,0:T(8,128)(2,1)}), bf16[8,128,512]{2,1,0:T(8,128)(2,1)}, u32[]{:S(2)}, u32[]{:S(2)}) async-start(bf16[8,128,512]{2,1,0:T(8,128)(2,1)} %fusion.27), calls=%async_computation.3 | async-start | bytes 2097152 | tf_op jit(solution)/shard_map/all_to_all | solution.py:726
  823.1 136.3 %collective-permute-start.18 = (bf16[128,2048]{1,0:T(8,128)(2,1)S(1)}, bf16[128,2048]{1,0:T(8,128)(2,1)}, u32[]{:S(2)}, u32[]{:S(2)}) collective-permute-start(bf16[128,2048]{1,0:T(8,128)(2,1)S(1)} %copy-done.31), channel_id=1, source_target_pairs={{1,0},{16,17},{3,2},{18,19},{5,4},{20,21},{7,6},{22,23},{9,8},{24,... | collective-permute-start | bytes 1572872 | tf_op jit(solution)/shard_map/ppermute | solution.py:687
  889.2 62.0 %collective-permute-start.27 = (bf16[295,256]{1,0:T(8,128)(2,1)S(1)}, bf16[295,256]{1,0:T(8,128)(2,1)S(1)}, u32[]{:S(2)}, u32[]{:S(2)}) collective-permute-start(bf16[295,256]{1,0:T(8,128)(2,1)S(1)} %convert_element_type.276), channel_id=1, source_target_pairs={{1,0},{16,17},{3,2},{18,19},{5,4},{20,21},{7,6},{22,23},{9,8},{24,... | collective-permute-start | bytes 453128 | tf_op jit(solution)/shard_map/ppermute | solution.py:687
  952.2 58.7 %collective-permute-start.31 = (bf16[256,2048]{1,0:T(8,128)(2,1)}, bf16[256,2048]{1,0:T(8,128)(2,1)}, u32[]{:S(2)}, u32[]{:S(2)}) collective-permute-start(bf16[256,2048]{1,0:T(8,128)(2,1)} %get-tuple-element.141), channel_id=1, source_target_pairs={{1,0},{16,17},{3,2},{18,19},{5,4},{20,21},{7,6},{22,23},{9,8},{24,... | collective-permute-start | bytes 3145736 | tf_op jit(solution)/shard_map/ppermute | solution.py:687
  955.8 44.8 %collective-permute-start.24 = (bf16[8,128,512]{2,1,0:T(8,128)(2,1)S(1)}, bf16[8,128,512]{2,1,0:T(8,128)(2,1)S(1)}, u32[]{:S(2)}, u32[]{:S(2)}) collective-permute-start(bf16[8,128,512]{2,1,0:T(8,128)(2,1)S(1)} %select_bitcast_fusion.1), channel_id=1, source_target_pairs={{0,1},{1,0},{2,3},{3,2},{4,5},{5,4},{6,7},{7,6},{8,9},{9,8},{10,11... | collective-permute-start | bytes 3145736 | tf_op jit(solution)/shard_map/ppermute | solution.py:211
  959.4 35.4 %collective-permute-start.20 = (bf16[128,2048]{1,0:T(8,128)(2,1)S(1)}, bf16[128,2048]{1,0:T(8,128)(2,1)S(1)}, u32[]{:S(2)}, u32[]{:S(2)}) collective-permute-start(bf16[128,2048]{1,0:T(8,128)(2,1)S(1)} %fusion.40), channel_id=1, source_target_pairs={{1,0},{16,17},{3,2},{18,19},{5,4},{20,21},{7,6},{22,23},{9,8},{24,... | collective-permute-start | bytes 1572872 | tf_op jit(solution)/shard_map/ppermute | solution.py:687
  1015.3 29.3 %collective-permute-start.23 = (bf16[8,128,512]{2,1,0:T(8,128)(2,1)}, bf16[8,128,512]{2,1,0:T(8,128)(2,1)}, u32[]{:S(2)}, u32[]{:S(2)}) collective-permute-start(bf16[8,128,512]{2,1,0:T(8,128)(2,1)} %all-to-all-done.2), channel_id=1, source_target_pairs={{0,16},{1,17},{2,18},{3,19},{4,20},{5,21},{6,22},{7,23},{8,24},{9,... | collective-permute-start | bytes 3145736 | tf_op jit(solution)/shard_map/ppermute | solution.py:727
  (114 other events, 2441.7 us)
Sparse Core Ops, SparseCore 0:
  96.1 98.9 all-gather.1
  553.3 125.8 reduce-scatter.1

commit v2 on v1

v2 whole, which is shorter than its diff:
```python
import functools

import jax
import jax.numpy as jnp
from jax import lax
from jax.experimental import pallas as pl
from jax.experimental.pallas import tpu as pltpu
from jax.sharding import Mesh, PartitionSpec as P


N = 16
R = 128
KC = 4
BLOCK = 128
norm_eps = 1e-05
BF = jnp.bfloat16
F32 = jnp.float32
MESH = pl.DeviceIdType.MESH


def forward_dot(operand, factor):
    return jnp.dot(operand, factor, preferred_element_type=F32)


def cross_dot(operand, factor):
    return lax.dot_general(operand, factor, (((0,), (0,)), ((), ())), preferred_element_type=F32)


def back_dot(operand, factor):
    return lax.dot_general(operand, factor, (((1,), (1,)), ((), ())), preferred_element_type=F32)


def widths(channels):
    wide = min(channels, 128)
    return wide, channels // wide


def sum_rows(pieces):
    row = lax.broadcasted_iota(jnp.int32, pieces[0].shape, 0)
    shift = 1
    while len(pieces) > 1:
        keep = (row & shift) == 0
        pieces = [
            jnp.where(keep, a, b) + pltpu.roll(jnp.where(keep, b, a), shift, 0)
            for a, b in zip(pieces[0::2], pieces[1::2])
        ]
        shift *= 2
    return pieces[0]


def halves(v):
    return v[:8] + v[8:]


def lanes_of(p, wide):
    return slice(p * wide, (p + 1) * wide)


def recur_forward_kernel(rate_ref, act_ref, key_ref, query_ref, out_ref, before_ref, last_ref, memory_ref):
    wide, parts = widths(rate_ref.shape[1])

    @pl.when(pl.program_id(0) == 0)
    def _():
        memory_ref[...] = jnp.zeros_like(memory_ref)

    memory = [memory_ref[:, lanes_of(p, wide)] for p in range(parts)]
    for base in range(0, rate_ref.shape[0], 8):
        rates = rate_ref[base : base + 8, :]
        feeds = rates * act_ref[base : base + 8, :]
        sums = [[] for _ in range(parts)]
        for i in range(8):
            key = jnp.broadcast_to(key_ref[:, base + i : base + i + 1], (N, wide))
            query = jnp.broadcast_to(query_ref[:, base + i : base + i + 1], (N, wide))
            square = key * key
            for p in range(parts):
                lanes = lanes_of(p, wide)
                before_ref[base + i, :, lanes] = memory[p]
                memory[p] = (1.0 - rates[i : i + 1, lanes] * square) * memory[p] + key * feeds[i : i + 1, lanes]
                sums[p].append(halves(memory[p] * query))
        for p in range(parts):
            out_ref[base : base + 8, lanes_of(p, wide)] = sum_rows(sums[p])
    for p in range(parts):
        memory_ref[:, lanes_of(p, wide)] = memory[p]

    @pl.when(pl.program_id(0) == pl.num_programs(0) - 1)
    def _():
        last_ref[...] = memory_ref[...]


def recur_forward(rate, act, key_t, query_t):
    tokens, channels = rate.shape
    rows = pl.BlockSpec((BLOCK, channels), lambda i: (i, 0))
    cols = pl.BlockSpec((N, BLOCK), lambda i: (0, i))
    return pl.pallas_call(
        recur_forward_kernel,
        grid=(tokens // BLOCK,),
        in_specs=[rows, rows, cols, cols],
        out_specs=[
            rows,
            pl.BlockSpec((BLOCK, N, channels), lambda i: (i, 0, 0)),
            pl.BlockSpec((N, channels), lambda i: (0, 0)),
        ],
        out_shape=[
            jax.ShapeDtypeStruct((tokens, channels), F32),
            jax.ShapeDtypeStruct((tokens, N, channels), F32),
            jax.ShapeDtypeStruct((N, channels), F32),
        ],
        scratch_shapes=[pltpu.VMEM((N, channels), F32)],
        compiler_params=pltpu.CompilerParams(
            dimension_semantics=("arbitrary",), vmem_limit_bytes=40 * 2**20
        ),
        cost_estimate=pl.CostEstimate(
            flops=10 * tokens * N * channels, bytes_accessed=4 * tokens * channels * (N + 3), transcendentals=0
        ),
    )(rate, act, key_t, query_t)


def recur_backward_kernel(
    rate_ref, act_ref, grad_ref, key_ref, query_ref, before_ref, last_ref,
    d_rate_ref, d_act_ref, d_key_ref, d_query_ref, lam_ref, memory_ref, key_rows, query_rows,
):
    wide, parts = widths(rate_ref.shape[1])
    block = rate_ref.shape[0]

    @pl.when(pl.program_id(0) == 0)
    def _():
        lam_ref[...] = jnp.zeros_like(lam_ref)
        memory_ref[...] = last_ref[...]

    lam = [lam_ref[:, lanes_of(p, wide)] for p in range(parts)]
    memory = [memory_ref[:, lanes_of(p, wide)] for p in range(parts)]
    for base in reversed(range(0, block, 8)):
        rates = rate_ref[base : base + 8, :]
        acts = act_ref[base : base + 8, :]
        grads = grad_ref[base : base + 8, :]
        d_rates = [[None] * 8 for _ in range(parts)]
        d_acts = [[None] * 8 for _ in range(parts)]
        for i in reversed(range(8)):
            at = base + i
            key = jnp.broadcast_to(key_ref[:, at : at + 1], (N, wide))
            query = jnp.broadcast_to(query_ref[:, at : at + 1], (N, wide))
            square = key * key
            key_sum = query_sum = None
            for p in range(parts):
                lanes = lanes_of(p, wide)
                grad = grads[i : i + 1, lanes]
                before = before_ref[at, :, lanes]
                pulled = query * grad + lam[p]
                kept = key * before
                missing = acts[i : i + 1, lanes] - kept
                keyed = pulled * key
                scaled = pulled * rates[i : i + 1, lanes]
                d_acts[p][i] = halves(keyed)
                d_rates[p][i] = halves(keyed * missing)
                to_key = scaled * (missing - kept)
                to_query = memory[p] * grad
                key_sum = to_key if key_sum is None else key_sum + to_key
                query_sum = to_query if query_sum is None else query_sum + to_query
                lam[p] = pulled - scaled * square
                memory[p] = before
            key_rows[at * N : (at + 1) * N, :] = key_sum.astype(BF)
            query_rows[at * N : (at + 1) * N, :] = query_sum.astype(BF)
        for p in range(parts):
            lanes = lanes_of(p, wide)
            d_rate_ref[base : base + 8, lanes] = sum_rows(d_rates[p])
            d_act_ref[base : base + 8, lanes] = rates[:, lanes] * sum_rows(d_acts[p])
    for p in range(parts):
        lam_ref[:, lanes_of(p, wide)] = lam[p]
        memory_ref[:, lanes_of(p, wide)] = memory[p]

    ones = jnp.ones((wide, block), BF)
    token = lax.broadcasted_iota(jnp.int32, (block, N, block), 0)
    own = token == lax.broadcasted_iota(jnp.int32, (block, N, block), 2)
    for rows, result in ((key_rows, d_key_ref), (query_rows, d_query_ref)):
        sums = forward_dot(rows[...], ones).reshape(block, N, block)
        result[...] = jnp.sum(jnp.where(own, sums, 0.0), axis=0)


def recur_backward(rate, act, grad, key_t, query_t, before, last):
    tokens, channels = rate.shape
    count = tokens // BLOCK
    rows = pl.BlockSpec((BLOCK, channels), lambda i: (count - 1 - i, 0))
    cols = pl.BlockSpec((N, BLOCK), lambda i: (0, count - 1 - i))
    products = pltpu.VMEM((BLOCK * N, widths(channels)[0]), BF)
    return pl.pallas_call(
        recur_backward_kernel,
        grid=(count,),
        in_specs=[
            rows, rows, rows, cols, cols,
            pl.BlockSpec((BLOCK, N, channels), lambda i: (count - 1 - i, 0, 0)),
            pl.BlockSpec((N, channels), lambda i: (0, 0)),
        ],
        out_specs=[rows, rows, cols, cols],
        out_shape=[
            jax.ShapeDtypeStruct((tokens, channels), F32),
            jax.ShapeDtypeStruct((tokens, channels), F32),
            jax.ShapeDtypeStruct((N, tokens), F32),
            jax.ShapeDtypeStruct((N, tokens), F32),
        ],
        scratch_shapes=[pltpu.VMEM((N, channels), F32), pltpu.VMEM((N, channels), F32), products, products],
        compiler_params=pltpu.CompilerParams(
            dimension_semantics=("arbitrary",), vmem_limit_bytes=40 * 2**20
        ),
        cost_estimate=pl.CostEstimate(
            flops=30 * tokens * N * channels, bytes_accessed=4 * tokens * channels * (N + 5), transcendentals=0
        ),
    )(rate, act, grad, key_t, query_t, before, last)


class Place:
    def __init__(self, bits):
        self.bits = bits
        self.n = len(bits)
        self.count = 2**self.n
        self.at = [lax.axis_index(name) for name in bits]
        self.s = lax.axis_index("section")

    def other(self, e):
        return sum(2**d * (c + e // 2**d % 2 * (1 - 2 * c)) for d, c in enumerate(self.at))

    def toward(self, e):
        return {self.bits[d]: 1 - self.at[d] for d in range(self.n) if e // 2**d % 2}

    def dims(self, p, m):
        return sum(2 ** ((p + t) % self.n) for t in range(self.n) if m // 2**t % 2)

    def positions(self, p, e):
        return sum(2**t * (e // 2 ** ((p + t) % self.n) % 2) for t in range(self.n))

    def meet(self, peers):
        barrier = pltpu.get_barrier_semaphore()
        for where in peers:
            pl.semaphore_signal(barrier, inc=1, device_id=where, device_id_type=MESH)
        pl.semaphore_wait(barrier, len(peers))


def spans_of(width, n):
    tiles = width // 128
    sizes = [(tiles // n + (p < tiles % n)) * 128 for p in range(n)]
    return [(sum(sizes[:p]), size) for p, size in enumerate(sizes)]


def remote(src, dst, send, recv, where):
    return pltpu.make_async_remote_copy(
        src_ref=src, dst_ref=dst, send_sem=send, recv_sem=recv, device_id=where, device_id_type=MESH
    )


def arrived(place, sem):
    pltpu.make_async_copy(place, place, sem).wait()


def lasting(us):
    return pl.CostEstimate(flops=0, bytes_accessed=int(us * 3.4e6), transcendentals=0)


def gather_kernel(bits, total, layer, *refs):
    here = Place(bits)
    n, s, count = here.n, here.s, here.count
    q, chip = lax.axis_index("q"), here.other(0)
    given, refs = refs[: total + (0 if layer is None else 2)], refs[total + (0 if layer is None else 2) :]
    made, refs = refs[: len(given)], refs[len(given) :]
    local_sem, send, recv, core_send, core_recv = refs[:5]
    spans = spans_of(given[0].shape[1], n)
    parts = [(k, p) for k in range(total) for p in range(n) if spans[p][1]]

    def block(k, e, p, s_of):
        return made[k].at[s_of, here.other(e), :, pl.ds(*spans[p])]

    def source(k, e, p):
        return block(k, e, p, s) if e else given[k].at[:, pl.ds(*spans[p])]

    def deliver(k, p, m):
        t = m.bit_length() - 1
        held = here.dims(p, m - 2**t)
        where = here.toward(2 ** ((p + t) % n))
        return remote(source(k, held, p), block(k, held, p, s), send.at[k, p, m], recv.at[k, p, m], where)

    def core(k, p, m):
        held = here.dims(p, m)
        sems = core_send.at[k, p, m], core_recv.at[k, p, m]
        return remote(source(k, held, p), block(k, held, p, s), *sems, {"section": 1 - s})

    if layer is None:
        here.meet([here.toward(2**d) for d in range(n)] + [{"section": 1 - s}])
    else:
        blocks, small = given[total:]
        rows, own_small = made[total:]
        piece_send, piece_recv, q_send, q_recv, small_send, small_recv = refs[5:]
        peers = [dict(here.toward(e), **extra) for e in range(count) for extra in ({}, {"section": 1 - s}) if e or extra]
        here.meet(peers + [{"q": 1 - q}, {"q": 1 - q, "section": 1 - s}])

        def piece(r, e):
            where = dict(here.toward(e), **({"section": 1 - s} if r else {}))
            src = blocks.at[1 - s if r else s, here.other(e)]
            return remote(src, rows.at[q, chip], piece_send.at[r, e], piece_recv.at[e], where)

        def pass_on(e):
            place = rows.at[q, here.other(e)]
            return remote(place, place, q_send.at[e], q_recv.at[e], {"q": 1 - q})

        def hand_small(k, where):
            return remote(small, own_small, small_send.at[k], small_recv, where)

        keep_piece = pltpu.make_async_copy(blocks.at[s, chip], rows.at[q, chip], piece_recv.at[0])
        keep_small = pltpu.make_async_copy(small, own_small, small_recv)
        at_layer = s == layer
        stays, leaves = jnp.logical_and(at_layer, q == s), jnp.logical_and(at_layer, q != s)

        @pl.when(at_layer)
        def _():
            keep_piece.start()
            for e in range(count):
                for r in range(2):
                    if e or r:
                        piece(r, e).start()

        @pl.when(stays)
        def _():
            keep_small.start()
            hand_small(0, {"q": 1 - q}).start()

        @pl.when(leaves)
        def _():
            hand_small(0, {"section": 1 - s}).start()
            hand_small(1, {"section": 1 - s, "q": 1 - q}).start()

    own = [pltpu.make_async_copy(given[k], made[k].at[s, chip], local_sem.at[k]) for k in range(total)]
    for k in range(total):
        for t in range(n):
            for p in range(n):
                if spans[p][1]:
                    deliver(k, p, 2**t).start()
        own[k].start()
    for k, p in parts:
        core(k, p, 0).start()
    for m in range(1, count):
        if layer is not None:
            for e in range(count * (m - 1) // (count - 1), count * m // (count - 1)):
                arrived(rows.at[q, here.other(e)], piece_recv.at[e])
                pass_on(e).start()
        for k, p in parts:
            arrived(block(k, here.dims(p, m), p, s), recv.at[k, p, m])
            for t in range(m.bit_length(), n):
                deliver(k, p, m + 2**t).start()
            core(k, p, m).start()
    for copy in own:
        copy.wait()
    for m in range(count):
        for k, p in parts:
            arrived(block(k, here.dims(p, m), p, 1 - s), core_recv.at[k, p, m])
    for m in range(count):
        for k, p in parts:
            core(k, p, m).wait_send()
            if m:
                deliver(k, p, m).wait_send()
    if layer is not None:
        arrived(own_small, small_recv)
        for e in range(count):
            arrived(rows.at[1 - q, here.other(e)], q_recv.at[e])
            pass_on(e).wait_send()

        @pl.when(at_layer)
        def _():
            for e in range(count):
                for r in range(2):
                    if e or r:
                        piece(r, e).wait_send()

        pl.when(stays)(lambda: hand_small(0, {"q": 1 - q}).wait_send())

        @pl.when(leaves)
        def _():
            hand_small(0, {"section": 1 - s}).wait_send()
            hand_small(1, {"section": 1 - s, "q": 1 - q}).wait_send()


def gather_call(bits, shards, layer=None, extras=(), us=35):
    rows, width = shards[0].shape
    n = len(bits)
    count = 2**n
    dma = pltpu.SemaphoreType.DMA
    sems = dma((len(shards), n, count))
    shapes = [jax.ShapeDtypeStruct((2, count, rows, width), shard.dtype) for shard in shards]
    scratch = [dma((len(shards),)), sems, sems, sems, sems]
    if layer is not None:
        shapes += [jax.ShapeDtypeStruct(extra.shape, extra.dtype) for extra in extras]
        scratch += [dma((2, count)), dma((count,)), dma((count,)), dma((count,)), dma((2,)), dma]
    out = pl.pallas_call(
        functools.partial(gather_kernel, bits, len(shards), layer),
        out_shape=shapes,
        in_specs=[pl.BlockSpec(memory_space=pl.ANY)] * len(shapes),
        out_specs=[pl.BlockSpec(memory_space=pl.ANY)] * len(shapes),
        scratch_shapes=scratch,
        compiler_params=pltpu.CompilerParams(
            collective_id=0 if layer is None else 5, has_side_effects=True
        ),
        cost_estimate=lasting(us),
    )(*shards, *extras)
    return [o.reshape((-1, width)) for o in out[: len(shards)]] + list(out[len(shards) :])


def gather_tokens(bits, shard):
    return gather_call(bits, [shard])[0]


def add_rows(place, terms, out=None):
    step = 32
    out = place if out is None else out

    @pl.loop(0, place.shape[0] // step)
    def _(r):
        lines = pl.ds(pl.multiple_of(r * step, step), step)
        total = place[lines, :].astype(F32)
        for term in terms:
            total = total + term[lines, :].astype(F32)
        out[lines, :] = total.astype(out.dtype)


def scatter_kernel(bits, turned, homing, a_ref, b_ref, *refs):
    if homing:
        grad, out_ref, home, other_home = refs[:4]
        q_in, ready, q_send, q_recv, home_send, home_recv, over_send, over_recv = refs[-8:]
        refs = refs[4:]
    else:
        out_ref, refs = refs[0], refs[1:]
    mine, give, core_in, landed, core_send, core_recv, send, recv = refs[:8]
    here = Place(bits)
    n, s, count = here.n, here.s, here.count
    rows, width = out_ref.shape
    tile = min(width, 512)
    spans = spans_of(width, n)
    parts = [p for p in range(n) if spans[p][1]]

    def core(chip):
        return remote(give.at[chip], core_in.at[chip], core_send.at[chip], core_recv.at[chip], {"section": 1 - s})

    def hand(p, m, t):
        e = here.dims(p, m) if isinstance(m, int) else sum(
            2 ** ((p + u) % n) * (m // 2**u % 2) for u in range(n)
        )
        cols = pl.ds(*spans[p])
        return remote(
            mine.at[here.other(e), :, cols], landed.at[m, :, cols], send.at[p, m], recv.at[p, m],
            here.toward(2 ** ((p + t) % n)),
        )

    def to_q(e):
        q, chip = lax.axis_index("q"), here.other(e)
        return remote(grad.at[1 - q, chip], q_in.at[chip], q_send.at[e], q_recv.at[e], {"q": 1 - q})

    def to_chip(e):
        return remote(ready.at[here.other(e)], home.at[here.other(0)], home_send.at[e], home_recv.at[e], here.toward(e))

    def to_core(e):
        chip = here.other(e)
        return remote(home.at[chip], other_home.at[chip], over_send.at[e], over_recv.at[e], {"section": 1 - s})

    def home_step(e):
        chip = here.other(e)
        arrived(q_in.at[chip], q_recv.at[e])
        place = ready.at[chip] if e else home.at[chip]
        add_rows(q_in.at[chip], [grad.at[lax.axis_index("q"), chip]], place)
        (to_chip(e) if e else to_core(0)).start()

    def home_end(e):
        if e:
            arrived(home.at[here.other(e)], home_recv.at[e])
            to_core(e).start()

    peers = [here.toward(2**d) for d in range(n)] + [{"section": 1 - s}]
    if homing:
        peers = [here.toward(e) for e in range(1, count)] + [{"section": 1 - s}, {"q": 1 - lax.axis_index("q")}]
    here.meet(peers)
    if homing:
        for e in range(count):
            to_q(e).start()

    @pl.loop(0, count + 1)
    def _(i):
        @pl.when(i < count)
        def _():
            chip = here.other(count - 1 - i)

            def lines(s_of):
                return pl.ds(pl.multiple_of((s_of * count + chip) * rows, rows), rows)

            left = jnp.concatenate([a_ref[lines(1 - s), :], a_ref[lines(s), :]], axis=0)
            for c in range(0, width, tile):
                if turned:
                    value = back_dot(left, b_ref[c : c + tile, :])
                else:
                    value = forward_dot(left, b_ref[:, c : c + tile])
                value = value.astype(BF)
                give[chip, :, c : c + tile] = value[:rows]
                mine[chip, :, c : c + tile] = value[rows:]
            core(chip).start()

        @pl.when(i > 0)
        def _():
            e = count - i
            chip = here.other(e)
            arrived(core_in.at[chip], core_recv.at[chip])
            add_rows(mine.at[chip], [core_in.at[chip]])
            for p in parts:
                pl.when(e // 2 ** ((p + n - 1) % n) % 2 == 1)(
                    lambda p=p: hand(p, here.positions(p, e), n - 1).start()
                )

    def waiting(p, m):
        cols = pl.ds(*spans[p])
        terms = [m + 2**t for t in range(m.bit_length(), n)]
        for term in terms:
            arrived(landed.at[term, :, cols], recv.at[p, term])
        return mine.at[here.other(here.dims(p, m)), :, cols], [landed.at[term, :, cols] for term in terms]

    steps = count // 2
    for m in range(steps - 1, 0, -1):
        if homing:
            home_step(steps - 1 - m)
        for p in parts:
            add_rows(*waiting(p, m))
            hand(p, m, m.bit_length() - 1).start()
    for p in parts:
        place, terms = waiting(p, 0)
        add_rows(place, terms, out_ref.at[:, pl.ds(*spans[p])])
    if homing:
        for e in range(steps - 1, count):
            home_step(e)
        for e in range(count):
            home_end(e)
        for e in range(count):
            arrived(other_home.at[here.other(e)], over_recv.at[e])
            to_core(e).wait_send()
            to_q(e).wait_send()
            if e:
                to_chip(e).wait_send()
    for chip in range(count):
        core(chip).wait_send()
    for m in range(1, count):
        for p in parts:
            hand(p, m, m.bit_length() - 1).wait_send()


def scatter_columns(bits, a, b, turned, grad=None):
    tokens, width = a.shape[0], b.shape[0 if turned else 1]
    n = len(bits)
    count = 2**n
    block = (tokens // (2 * count), width)
    dma = pltpu.SemaphoreType.DMA
    blocks = pltpu.VMEM((count,) + block, BF)
    shapes = [jax.ShapeDtypeStruct(block, F32)]
    scratch = [blocks] * 4 + [dma((count,))] * 2 + [dma((n, count))] * 2
    if grad is not None:
        shapes += [jax.ShapeDtypeStruct(grad.shape[1:], BF)] * 2
        scratch += [pltpu.VMEM(grad.shape[1:], BF)] * 2 + [dma((count,))] * 6
    return pl.pallas_call(
        functools.partial(scatter_kernel, bits, turned, grad is not None),
        out_shape=shapes,
        in_specs=[pl.BlockSpec(memory_space=pltpu.VMEM)] * (2 if grad is None else 3),
        out_specs=[pl.BlockSpec(memory_space=pltpu.VMEM)] * len(shapes),
        scratch_shapes=scratch,
        compiler_params=pltpu.CompilerParams(
            collective_id=(1 + turned) if grad is None else 6, has_side_effects=True, vmem_limit_bytes=56 * 2**20
        ),
        cost_estimate=lasting(40 if grad is None else 60),
    )(*((a, b) if grad is None else (a, b, grad)))


def scatter_dot(bits, a, b, turned, grad=None):
    tokens, width = a.shape[0], b.shape[0 if turned else 1]
    pieces = max(1, tokens * width // 2**22)
    size = width // pieces
    cuts = [slice(i * size, (i + 1) * size) for i in range(pieces)]
    done = [
        scatter_columns(bits, a, b[at] if turned else b[:, at], turned, grad if i == 0 else None)
        for i, at in enumerate(cuts)
    ]
    total = jnp.concatenate([d[0] for d in done], axis=1)
    return total if grad is None else (total, done[0][1], done[0][2])


def total_kernel(bits, x_ref, out_ref, part, core_in, ready, landed, done, pair_send, pair_recv, send, recv, back_send, back_recv):
    here = Place(bits)
    s, count = here.s, here.count
    lanes = part.shape[3]

    def span(s_of, chip):
        at = (s_of * count + chip) * lanes
        return slice(at, at + lanes)

    for s_of in range(2):
        for chip in range(count):
            part[s_of, chip] = x_ref[:, span(s_of, chip)]
    here.meet([here.toward(e) for e in range(1, count)] + [{"section": 1 - s}])
    first = remote(part.at[1 - s], core_in, pair_send.at[0], pair_recv.at[0], {"section": 1 - s})
    first.start()
    first.wait_recv()
    for chip in range(count):
        total = part[s, chip] + core_in[chip]
        part[s, chip] = total
        ready[chip] = total.astype(BF)

    def out(e):
        return remote(ready.at[here.other(e)], landed.at[e], send.at[e], recv.at[e], here.toward(e))

    def back(e):
        place = done.at[s, here.other(0)]
        return remote(place, place, back_send.at[e], back_recv.at[e], here.toward(e))

    others = range(1, count)
    for e in others:
        out(e).start()
    total = part[s, here.other(0)]
    for e in others:
        out(e).wait_recv()
        total = total + landed[e].astype(F32)
    done[s, here.other(0)] = total.astype(BF)
    for e in others:
        back(e).start()
    for e in others:
        place = done.at[s, here.other(e)]
        arrived(place, back_recv.at[e])
    last = remote(done.at[s], done.at[s], pair_send.at[1], pair_recv.at[1], {"section": 1 - s})
    last.start()
    last.wait_recv()
    for s_of in range(2):
        for chip in range(count):
            out_ref[:, span(s_of, chip)] = done[s_of, chip]
    first.wait_send()
    last.wait_send()
    for e in others:
        out(e).wait_send()
        back(e).wait_send()


def sum_columns(bits, x):
    rows, tokens = x.shape
    count = 2 ** len(bits)
    block = (rows, tokens // (2 * count))
    dma, vmem = pltpu.SemaphoreType.DMA, pltpu.VMEM
    return pl.pallas_call(
        functools.partial(total_kernel, bits),
        out_shape=jax.ShapeDtypeStruct((rows, tokens), BF),
        in_specs=[pl.BlockSpec(memory_space=pltpu.VMEM)],
        out_specs=pl.BlockSpec(memory_space=pltpu.VMEM),
        scratch_shapes=[
            vmem((2, count) + block, F32),
            vmem((count,) + block, F32),
            vmem((count,) + block, BF),
            vmem((count,) + block, BF),
            vmem((2, count) + block, BF),
        ]
        + [dma((2,))] * 2
        + [dma((count,))] * 4,
        compiler_params=pltpu.CompilerParams(
            collective_id=3, has_side_effects=True, vmem_limit_bytes=56 * 2**20
        ),
        cost_estimate=lasting(22),
    )(x)


def spread_kernel(bits, shard_ref, out_ref, send, recv, pair_send, pair_recv):
    here = Place(bits)
    s, q, chip = here.s, lax.axis_index("q"), here.other(0)
    others = range(1, here.count)
    here.meet([here.toward(e) for e in others] + [{"section": 1 - s}, {"q": 1 - q}])
    out_ref[s, q, chip] = shard_ref[...]
    own = out_ref.at[s, q, chip]
    copies = [remote(own, own, send.at[e], recv.at[e], here.toward(e)) for e in others]
    for copy in copies:
        copy.start()
    for e in others:
        arrived(out_ref.at[s, q, here.other(e)], recv.at[e])
    place = out_ref.at[s, q]
    first = remote(place, place, pair_send.at[0], pair_recv.at[0], {"q": 1 - q})
    first.start()
    first.wait_recv()
    place = out_ref.at[s]
    second = remote(place, place, pair_send.at[1], pair_recv.at[1], {"section": 1 - s})
    second.start()
    second.wait_recv()
    for copy in copies + [first, second]:
        copy.wait_send()


def spread(bits, shard):
    width, count = shard.shape[0], 2 ** len(bits)
    block = (16, max(width, 128))
    padded = jnp.pad(shard[None, :], ((0, block[0] - 1), (0, block[1] - width)))
    dma = pltpu.SemaphoreType.DMA
    out = pl.pallas_call(
        functools.partial(spread_kernel, bits),
        out_shape=jax.ShapeDtypeStruct((2, 2, count) + block, shard.dtype),
        in_specs=[pl.BlockSpec(memory_space=pltpu.VMEM)],
        out_specs=pl.BlockSpec(memory_space=pltpu.VMEM),
        scratch_shapes=[dma((count,)), dma((count,)), dma((2,)), dma((2,))],
        compiler_params=pltpu.CompilerParams(collective_id=4, has_side_effects=True),
        cost_estimate=lasting(12),
    )(padded)
    return out[:, :, :, 0, :width].reshape((2, -1))


def chips(bits):
    return tuple(reversed(bits))


def swap(value, axis):
    return lax.ppermute(value, axis, [(0, 1), (1, 0)])


def at_home():
    return lax.axis_index("q") == lax.axis_index("section")


def to_home(value):
    return lax.ppermute(value, ("section", "q"), [(1, 0), (2, 3)])


def from_home(value):
    return lax.ppermute(value, ("section", "q"), [(0, 1), (3, 2)])


def own_tokens(pair):
    low = lax.axis_index("q") == 0
    keep = jnp.where(low, pair[0], pair[1])
    return jnp.where(at_home(), keep, from_home(jnp.where(low, pair[1], pair[0])))


def own_block(piece, layer):
    other = 1 - layer
    sent = lax.ppermute(piece, ("section", "q"), [(layer * 2 + other, other * 2 + other)])
    held = jnp.where(lax.axis_index("section") == layer, piece, sent)
    return jnp.where(at_home(), held, from_home(held))


def column_blocks(bits, rows):
    depth = rows.shape[0]
    blocks = jnp.transpose(rows.reshape((depth, 2, 2, 2 ** len(bits), -1)), (2, 3, 0, 1, 4))
    return blocks.reshape((2, 2 ** len(bits), depth, -1))


def own_columns(bits, blocks, layer):
    sent = lax.ppermute(blocks[1 - layer], "section", [(layer, 1 - layer)])
    mine = jnp.where(lax.axis_index("section") == layer, blocks[layer], sent)
    mine = lax.all_to_all(mine, chips(bits), split_axis=0, concat_axis=0, tiled=True)
    other = swap(mine, "q")
    low = lax.axis_index("q") == 0
    both = jnp.stack([jnp.where(low, mine, other), jnp.where(low, other, mine)])
    return both.reshape((-1, blocks.shape[3]))


def home_rows(bits, grad, layer):
    pieces = grad.reshape((2, 2 ** len(bits), -1, grad.shape[1]))
    low = lax.axis_index("q") == 0
    give = jnp.where(low, pieces[1], pieces[0])
    total = jnp.where(low, pieces[0], pieces[1]).astype(F32) + swap(give, "q").astype(F32)
    mine = lax.all_to_all(total.astype(BF), chips(bits), split_axis=0, concat_axis=0, tiled=True)
    return mine, lax.ppermute(mine, "section", [(1 - layer, layer)])


def home_block(piece, layer):
    total = piece + to_home(piece.astype(BF)).astype(F32)
    other = 1 - layer
    sent = lax.ppermute(total.astype(BF), ("section", "q"), [(other * 2 + other, layer * 2 + other)])
    return total, sent


def home_tokens(rows, layer):
    got = to_home(rows)
    low = lax.axis_index("q") == 0
    both = jnp.stack([jnp.where(low, rows, got), jnp.where(low, got, rows)])
    other = 1 - layer
    sent = lax.ppermute(both, ("section", "q"), [(other * 2 + other, layer * 2 + other)])
    return jnp.where(at_home(), both, sent)


def silu_slope(v):
    gate = jax.nn.sigmoid(v)
    return gate, gate * (1.0 + v * (1.0 - gate))


def normalize(stream, gain):
    inverse = lax.rsqrt(jnp.mean(stream * stream, axis=-1, keepdims=True) + norm_eps)
    return inverse, (stream * inverse * gain[None, :]).astype(BF)


def layer_forward(bits, stream, inverse, normed, weights):
    gain, in_weight, conv_weight, conv_bias, xproj_weight, dt_weight, dt_bias, skip, out_weight = weights
    channels = conv_bias.shape[0]
    projected = forward_dot(normed, in_weight).astype(BF)
    inner = projected[:, :channels].astype(F32)
    gate_in = projected[:, channels:].astype(F32)
    tokens = inner.shape[0]
    extended = jnp.concatenate([jnp.zeros((KC - 1, channels), F32), inner], axis=0)
    conv = jnp.broadcast_to(conv_bias[None, :], (tokens, channels))
    for tap in range(KC):
        conv = conv + conv_weight[tap][None, :] * extended[tap : tap + tokens]
    act = jax.nn.silu(conv)
    xproj = sum_columns(bits, back_dot(xproj_weight, act.astype(BF)))
    key_t, query_t = xproj[R : R + N].astype(F32), xproj[R + N :].astype(F32)
    key_norm = jnp.sum(key_t * key_t, axis=0)[:, None]
    write = jax.nn.sigmoid(cross_dot(xproj[:R], dt_weight) + dt_bias[None, :])
    rate = write / (1.0 + write * key_norm)
    recur, before, last = recur_forward(rate, act, key_t, query_t)
    recur = recur + skip[None, :] * act
    gated = (recur * jax.nn.silu(gate_in)).astype(BF)
    out = scatter_dot(bits, gated, out_weight, False)
    saved = (stream, inverse, normed, extended, gate_in, conv, act, xproj, key_t, query_t, key_norm, write, rate, recur, gated, before, last)
    return stream + out, saved


def layer_backward(bits, grad_out, grad_low, saved, weights, homing):
    gain, in_weight, conv_weight, conv_bias, xproj_weight, dt_weight, dt_bias, skip, out_weight = weights
    stream, inverse, normed, extended, gate_in, conv, act, xproj, key_t, query_t, key_norm, write, rate, recur, gated, before, last = saved
    tokens = act.shape[0]
    d_out_weight = cross_dot(gated, grad_low)
    d_gated = back_dot(grad_low, out_weight).astype(BF).astype(F32)
    gate, slope = silu_slope(gate_in)
    d_recur = d_gated * (gate_in * gate)
    d_gate_in = d_gated * recur * slope
    d_skip = jnp.sum(d_recur * act, axis=0)
    d_rate, d_act_rec, d_key_t, d_query_t = recur_backward(rate, act, d_recur, key_t, query_t, before, last)
    share = 1.0 / (1.0 + write * key_norm)
    pulled = d_rate * share * share
    d_pre = pulled * write * (1.0 - write)
    d_key_rate = -2.0 * key_t * jnp.sum(pulled * write * write, axis=1)[None, :]
    d_dt_bias = jnp.sum(d_pre, axis=0)
    d_delta = d_pre.astype(BF)
    d_dt_weight = forward_dot(xproj[:R], d_delta)
    d_xproj = jnp.concatenate([back_dot(dt_weight, d_delta), d_key_t + d_key_rate, d_query_t], axis=0)
    d_xproj = sum_columns(bits, d_xproj)
    d_xproj_weight = forward_dot(d_xproj, act.astype(BF))
    d_act = cross_dot(d_xproj, xproj_weight) + skip[None, :] * d_recur + d_act_rec
    d_conv = d_act * silu_slope(conv)[1]
    d_conv_weight = jnp.stack([jnp.sum(d_conv * extended[tap : tap + tokens], axis=0) for tap in range(KC)])
    d_conv_bias = jnp.sum(d_conv, axis=0)
    later = jnp.concatenate([d_conv, jnp.zeros((KC - 1, d_conv.shape[1]), F32)], axis=0)
    d_inner = sum(conv_weight[tap][None, :] * later[KC - 1 - tap : KC - 1 - tap + tokens] for tap in range(KC))
    d_projected = jnp.concatenate([d_inner, d_gate_in], axis=1).astype(BF)
    d_in_weight = cross_dot(normed, d_projected).astype(BF)
    if homing:
        pieces = d_in_weight.reshape((2, 2 ** len(bits), -1, d_in_weight.shape[1]))
        d_normed, *d_in_weight = scatter_dot(bits, d_projected, in_weight, True, pieces)
    else:
        d_normed = scatter_dot(bits, d_projected, in_weight, True)
    scaled = gain[None, :] * d_normed
    mean = jnp.mean(stream * scaled, axis=-1, keepdims=True)
    d_stream = grad_out + inverse * scaled - stream * inverse**3 * mean
    small = jnp.concatenate(
        [d_conv_weight, d_conv_bias[None], d_dt_bias[None], d_skip[None], d_dt_weight, d_xproj_weight],
        axis=0,
    )
    return d_stream, (d_in_weight, small, d_out_weight)


def on_device(
    bits, hidden_in, cotangent, norm_gain, in_weight, conv_weight, conv_bias, xproj_weight, dt_weight, dt_bias, skip_gain, out_weight
):
    small = jnp.concatenate(
        [conv_weight[0], conv_bias, dt_bias, skip_gain, dt_weight[0], jnp.swapaxes(xproj_weight[0], 0, 1)], axis=0
    )
    small = jnp.pad(small, ((0, -small.shape[0] % 16), (0, 0)))
    blocks = column_blocks(bits, in_weight[0])
    stream = own_tokens(hidden_in).astype(F32)
    grad = own_tokens(cotangent)
    gains = spread(bits, norm_gain[0]).astype(F32)
    inverse, normed = normalize(stream, gains[0])
    normed, grad_low, columns, own_small = gather_call(
        bits, [normed, grad.astype(BF)], 0, (blocks, small), us=70
    )
    own_small, blocks, small, out_block = lax.optimization_barrier((own_small, blocks, small, out_weight[0]))
    weights = []
    for layer in range(2):
        part = own_small if layer == 0 else own_block(small, layer)
        part_f = part.astype(F32)
        weights.append(
            (
                gains[layer],
                columns.reshape((-1, columns.shape[3])) if layer == 0 else own_columns(bits, blocks, layer),
                part_f[:KC],
                part_f[KC],
                part[KC + 3 + R : KC + 3 + 2 * R + 2 * N],
                part[KC + 3 : KC + 3 + R],
                part_f[KC + 1],
                part_f[KC + 2],
                own_block(out_block, layer),
            )
        )

    first, saved_first = layer_forward(bits, stream, inverse, normed, weights[0])
    first = first.astype(BF)
    stream = first.astype(F32)
    inverse, normed = normalize(stream, gains[1])
    second, saved_second = layer_forward(bits, stream, inverse, gather_tokens(bits, normed), weights[1])
    grad_second, grads_second = layer_backward(bits, grad, grad_low, saved_second, weights[1], False)
    grad_low = grad_second.astype(BF)
    grad_first, grads_first = layer_backward(
        bits, grad_low.astype(F32), gather_tokens(bits, grad_low), saved_first, weights[0], True
    )

    upper = lax.axis_index("section") == 1

    def of_layer(pair):
        return jnp.where(upper, pair[1], pair[0])

    layer_outputs = of_layer((home_tokens(first, 0), home_tokens(second.astype(BF), 1))).astype(F32)
    input_grads = of_layer((home_tokens(grad_first.astype(BF), 0), home_tokens(grad_second.astype(BF), 1))).astype(F32)
    columns = [grads_first[0], home_rows(bits, grads_second[0], 1)]
    mine, sent = of_layer([c[0] for c in columns]), of_layer([c[1] for c in columns])
    both = jnp.stack([jnp.where(upper, sent, mine), jnp.where(upper, mine, sent)])
    both = both.reshape((2, mine.shape[0], mine.shape[1], 2, -1))
    d_in = jnp.transpose(both, (2, 3, 0, 1, 4)).reshape((mine.shape[1], -1)).astype(F32)
    d_gain = jnp.sum(d_in * in_weight[0].astype(F32), axis=1) / norm_gain[0].astype(F32)

    def block_of(which):
        pieces = [home_block(grads[which], layer) for layer, grads in enumerate((grads_first, grads_second))]
        held, sent = of_layer([p[0] for p in pieces]), of_layer([p[1] for p in pieces])
        return jnp.where(at_home(), held, sent.astype(F32))

    small, d_out = block_of(1), block_of(2)
    return (
        layer_outputs[None],
        input_grads[None],
        d_gain[None],
        d_in[None],
        small[None, :KC],
        small[None, KC],
        jnp.swapaxes(small[KC + 3 + R :], 0, 1)[None],
        small[None, KC + 3 : KC + 3 + R],
        small[None, KC + 1],
        small[None, KC + 2],
        d_out[None],
    )


def solution(mesh):
    sections, chip_count = mesh.devices.shape
    n = chip_count.bit_length() - 2
    bits = tuple("c%d" % d for d in range(n))
    split = Mesh(mesh.devices.reshape((sections,) + (2,) * (n + 1)), ("section", "q") + chips(bits))
    seq = ("q",) + chips(bits)
    placed = (
        P(None, seq, None),
        P(None, seq, None),
        P("section", seq),
        P("section", seq, None),
        P("section", None, seq),
        P("section", seq),
        P("section", seq, None),
        P("section", None, seq),
        P("section", seq),
        P("section", seq),
        P("section", seq, None),
    )
    return jax.shard_map(
        functools.partial(on_device, bits),
        mesh=split,
        in_specs=placed,
        out_specs=(P("section", None, seq, None), P("section", None, seq, None)) + placed[2:],
        check_vma=False,
    )
```

time: 1100 us -> 1020 us (0.927)
  starting transfers between devices: 104 us -> 77.2 us
  local copies, waits for them, and re-layouts: 49.3 us -> 26.8 us
  other arithmetic: 108 us -> 87.3 us
  between operations: 16 us -> 3.15 us
  Pallas kernels: 601 us -> 612 us
    all_to_all x4 -> x2, waiting for transfers between devices: 41 us -> 0.01 us  [the longest x1 0.01 us: own_columns(): lax.all_to_all(mine, chips(bits), split_axis=0, concat_axis=0, tiled=True)]
    ppermute x4 -> x2, waiting for transfers between devices: 7.12 us -> 38.9 us  [swap(): return lax.ppermute(value, axis, [(0, 1), (1, 0)])]
    all_to_all x4 -> x2, starting transfers between devices: 29.9 us -> 8.94 us  [the longest x1 4.75 us: own_columns(): lax.all_to_all(mine, chips(bits), split_axis=0, concat_axis=0, tiled=True)]
    ppermute x26 -> x24, waiting for transfers between devices: 73.2 us -> 89.6 us  [the longest x8 77.3 us: to_home(): return lax.ppermute(value, ('section', 'q'), [(1, 0), (2, 3)])]
    pallas_call x11 -> x12, Pallas kernels: 503 us -> 515 us  [the longest x4 238 us: scatter_columns(): pl.pallas_call(functools.partial(scatter_kernel, bits, turned, grad is no...]
    dot_general x7 -> x6, matrix products: 23 us -> 17.4 us  [forward_dot(): return jnp.dot(operand, factor, preferred_element_type=F32)]
    ppermute x26 -> x24, starting transfers between devices: 58.1 us -> 60.7 us  [the longest x8 26.4 us: to_home(): return lax.ppermute(value, ('section', 'q'), [(1, 0), (2, 3)])]
  transfers between devices with their start and end apart: 40 -> 30, of which waited for: 10 -> 4; matrix products, arithmetic and copies ran while one was open for 15% -> 16% of each run, Pallas kernels for 50% -> 50%
where the time goes in v2:
time: 1020 us; the launch traced here: 1010 us
  Pallas kernels  612 us (60%)
  waiting for transfers between devices  129 us (13%)
  other arithmetic  87.3 us (9%)
  starting transfers between devices  77.2 us (8%)
  matrix products  76.6 us (8%)
  local copies, waits for them, and re-layouts  26.8 us (3%)
    pallas_call x4, Pallas kernels, scatter_columns(): pl.pallas_call(functools.partial(scatter_kernel, bits, turned, grad is no...  238 us
    pallas_call x3, Pallas kernels, gather_call(): pl.pallas_call(functools.partial(gather_kernel, bits, len(shards), layer)...  174 us
    pallas_call x4, Pallas kernels, sum_columns(): pl.pallas_call(functools.partial(total_kernel, bits), out_shape=jax.Shape...  81.3 us
    ppermute x8, waiting for transfers between devices, to_home(): return lax.ppermute(value, ('section', 'q'), [(1, 0), (2, 3)])  77.3 us
    pallas_call x2, Pallas kernels, recur_backward(): pl.pallas_call(recur_backward_kernel, grid=(count,), in_specs=[rows, rows...  60.8 us
    dot_general x8, matrix products, cross_dot(): lax.dot_general(operand, factor, (((0,), (0,)), ((), ())), preferred_elem...  45 us
    ppermute x2, waiting for transfers between devices, swap(): return lax.ppermute(value, axis, [(0, 1), (1, 0)])  38.9 us
    pallas_call x2, Pallas kernels, recur_forward(): pl.pallas_call(recur_forward_kernel, grid=(tokens // BLOCK,), in_specs=[r...  36.4 us
  transfers between devices with their start and end apart: 30, of which 4 were waited for; matrix products, arithmetic and copies ran while one was open for 16% of the time, Pallas kernels for 50%

profile of v2, /device:TPU:9, one launch (start us, length us, event | category | flops | bytes accessed | tf_op | source)
XLA Modules:
  0.0 1011.9 jit_solution(7771842315015569176)
XLA Ops:
  7.9 22.4 %shard_map.194 = bf16[2,2,8,16,128]{4,3,2,1,0:T(8,128)(2,1)} custom-call(bf16[16,128]{1,0:T(8,128)(2,1)} %pad.12.shard_ref), custom_call_target="tpu_custom_call" | custom-call | bytes 40800000 | tf_op jit(solution)/shard_map/pallas_call | solution.py:692
  45.0 105.4 %shard_map.195 = (bf16[2,8,128,2048]{3,2,1,0:T(8,128)(2,1)}, bf16[2,8,128,2048]{3,2,1,0:T(8,128)(2,1)}, bf16[2,8,128,512]{3,2,1,0:T(8,128)(2,1)}, bf16[304,256]{1,0:T(8,128)(2,1)}) custom-call(bf16[128,2048]{1,0:T(8,128)(2,1)} %fusion.35.refs_0_, bf16[128,2048]{1,0:T(8,128)(2,1)} %get-tuple-element.89.refs_1_, bf16[2,8,128,512]{3,2,1,0:T(8,128)(2,1)} %reshape.130.refs_2_, ...), custom_call_target="tpu_custom_call" | custom-call | bytes 238000000 | tf_op jit(solution)/shard_map/pallas_call | solution.py:389
  152.2 13.4 %collective-permute-start.8 = (bf16[256,2048]{1,0:T(8,128)(2,1)}, bf16[256,2048]{1,0:T(8,128)(2,1)}, u32[]{:S(2)}, u32[]{:S(2)}) collective-permute-start(bf16[256,2048]{1,0:T(8,128)(2,1)} %bitcast.153), channel_id=1, source_target_pairs={{16,0},{17,1},{18,2},{19,3},{20,4},{21,5},{22,6},{23,7}} | collective-permute-start | bytes 3145736 | tf_op jit(solution)/shard_map/ppermute | solution.py:732
  170.4 8.1 convolution_convert_fusion.3
  183.9 18.2 %shard_map.196 = bf16[160,2048]{1,0:T(8,128)(2,1)} custom-call(f32[160,2048]{1,0:T(8,128)} %fusion.63.x_ref), custom_call_target="tpu_custom_call" | custom-call | bytes 74800000 | tf_op jit(solution)/shard_map/pallas_call | solution.py:642
  207.2 18.3 %shard_map.197 = (f32[2048,256]{1,0:T(8,128)S(1)}, f32[2048,16,256]{2,1,0:T(8,128)}, f32[16,256]{1,0:T(8,128)S(1)}) custom-call(f32[2048,256]{1,0:T(8,128)S(1)} %get-tuple-element.147.rate_ref, f32[2048,256]{1,0:T(8,128)S(1)} %get-tuple-element.87.act_ref, f32[16,2048]{1,0:T(8,128)S(1)} %get-tuple-element.121.key_ref, ...), custom_call_target="tpu_custom_call" | custom-call | flops 83886080 | bytes 39845888 | tf_op jit(solution)/shard_map/pallas_call | solution.py:94
  239.1 12.3 %collective-permute-done.5 = bf16[304,256]{1,0:T(8,128)(2,1)S(1)} collective-permute-done((bf16[304,256]{1,0:T(8,128)(2,1)S(1)}, bf16[304,256]{1,0:T(8,128)(2,1)S(1)}, u32[]{:S(2)}, u32[]{:S(2)}) %collective-permute-start.5) | collective-permute-done | bytes 155680 | tf_op jit(solution)/shard_map/ppermute | solution.py:721
  255.1 60.7 %shard_map.198 = f32[128,2048]{1,0:T(8,128)} custom-call(bf16[2048,256]{1,0:T(8,128)(2,1)} %multiply_convert_fusion.1.a_ref, bf16[256,2048]{1,0:T(8,128)(2,1)} %broadcast_select_fusion.9.b_ref), custom_call_target="tpu_custom_call" | custom-call | bytes 136000000 | tf_op jit(solution)/shard_map/pallas_call | solution.py:557
  325.3 34.9 %shard_map.199 = bf16[2,8,128,2048]{3,2,1,0:T(8,128)(2,1)} custom-call(bf16[128,2048]{1,0:T(8,128)(2,1)} %fusion.43.refs_0_), custom_call_target="tpu_custom_call" | custom-call | bytes 119000000 | tf_op jit(solution)/shard_map/pallas_call | solution.py:389
  370.2 38.9 %collective-permute-done.7 = bf16[8,128,512]{2,1,0:T(8,128)(2,1)S(1)} collective-permute-done((bf16[8,128,512]{2,1,0:T(8,128)(2,1)}, bf16[8,128,512]{2,1,0:T(8,128)(2,1)S(1)}, u32[]{:S(2)}, u32[]{:S(2)}) %collective-permute-start.7) | collective-permute-done | bytes 1048608 | tf_op jit(solution)/shard_map/ppermute | solution.py:709
  420.0 21.9 %shard_map.200 = bf16[160,2048]{1,0:T(8,128)(2,1)} custom-call(f32[160,2048]{1,0:T(8,128)} %fusion.59.x_ref), custom_call_target="tpu_custom_call" | custom-call | bytes 74800000 | tf_op jit(solution)/shard_map/pallas_call | solution.py:642
  453.1 18.1 %shard_map.201 = (f32[2048,256]{1,0:T(8,128)S(1)}, f32[2048,16,256]{2,1,0:T(8,128)}, f32[16,256]{1,0:T(8,128)S(1)}) custom-call(f32[2048,256]{1,0:T(8,128)S(1)} %get-tuple-element.149.rate_ref, f32[2048,256]{1,0:T(8,128)S(1)} %get-tuple-element.83.act_ref, f32[16,2048]{1,0:T(8,128)S(1)} %get-tuple-element.119.key_ref, ...), custom_call_target="tpu_custom_call" | custom-call | flops 83886080 | bytes 39845888 | tf_op jit(solution)/shard_map/pallas_call | solution.py:94
  471.3 30.3 %shard_map.203 = (f32[2048,256]{1,0:T(8,128)S(1)}, f32[2048,256]{1,0:T(8,128)S(1)}, f32[16,2048]{1,0:T(8,128)S(1)}, f32[16,2048]{1,0:T(8,128)S(1)}) custom-call(f32[2048,256]{1,0:T(8,128)S(1)} %get-tuple-element.149.rate_ref, f32[2048,256]{1,0:T(8,128)S(1)} %get-tuple-element.83.act_ref, f32[2048,256]{1,0:T(8,128)S(1)} %get-tuple-element.151.grad_ref, ...), custom_call_target="tpu_custom_call" | custom-call | flops 251658240 | bytes 44040192 | tf_op jit(solution)/shard_map/pallas_call | solution.py:185
  505.9 20.8 %shard_map.204 = bf16[160,2048]{1,0:T(8,128)(2,1)} custom-call(f32[160,2048]{1,0:T(8,128)} %pad_maximum_fusion.3.x_ref), custom_call_target="tpu_custom_call" | custom-call | bytes 74800000 | tf_op jit(solution)/shard_map/pallas_call | solution.py:642
  536.8 35.3 %shard_map.202 = f32[128,2048]{1,0:T(8,128)} custom-call(bf16[2048,256]{1,0:T(8,128)(2,1)} %get-tuple-element.96.a_ref, bf16[256,2048]{1,0:T(8,128)(2,1)} %broadcast_select_fusion.8.b_ref), custom_call_target="tpu_custom_call" | custom-call | bytes 136000000 | tf_op jit(solution)/shard_map/pallas_call | solution.py:557
  572.2 7.6 fusion.87
  581.2 37.3 %shard_map.205 = f32[128,2048]{1,0:T(8,128)} custom-call(bf16[2048,512]{1,0:T(8,128)(2,1)} %pad_maximum_fusion.1.a_ref, bf16[2048,512]{1,0:T(8,128)(2,1)} %bitcast.145), custom_call_target="tpu_custom_call" | custom-call | bytes 136000000 | tf_op jit(solution)/shard_map/pallas_call | solution.py:557
  621.5 33.5 %shard_map.206 = bf16[2,8,128,2048]{3,2,1,0:T(8,128)(2,1)} custom-call(bf16[128,2048]{1,0:T(8,128)(2,1)} %get-tuple-element.122.refs_0_), custom_call_target="tpu_custom_call" | custom-call | bytes 119000000 | tf_op jit(solution)/shard_map/pallas_call | solution.py:389
  665.5 30.5 %shard_map.207 = (f32[2048,256]{1,0:T(8,128)S(1)}, f32[2048,256]{1,0:T(8,128)S(1)}, f32[16,2048]{1,0:T(8,128)S(1)}, f32[16,2048]{1,0:T(8,128)S(1)}) custom-call(f32[2048,256]{1,0:T(8,128)S(1)} %copy-done.3, f32[2048,256]{1,0:T(8,128)S(1)} %get-tuple-element.87.act_ref, f32[2048,256]{1,0:T(8,128)S(1)} %get-tuple-element.153.grad_ref, ...), custom_call_target="tpu_custom_call" | custom-call | flops 251658240 | bytes 44040192 | tf_op jit(solution)/shard_map/pallas_call | solution.py:185
  708.6 20.4 %shard_map.208 = bf16[160,2048]{1,0:T(8,128)(2,1)} custom-call(f32[160,2048]{1,0:T(8,128)} %pad_maximum_fusion.4.x_ref), custom_call_target="tpu_custom_call" | custom-call | bytes 74800000 | tf_op jit(solution)/shard_map/pallas_call | solution.py:642
  739.1 9.6 convolution_convert_fusion.1
  760.0 104.4 %shard_map.209 = (f32[128,2048]{1,0:T(8,128)}, bf16[8,128,512]{2,1,0:T(8,128)(2,1)}, bf16[8,128,512]{2,1,0:T(8,128)(2,1)}) custom-call(bf16[2048,512]{1,0:T(8,128)(2,1)} %pad_maximum_fusion.2.a_ref, bf16[2048,512]{1,0:T(8,128)(2,1)} %bitcast.147, bf16[2,8,128,512]{3,2,1,0:T(8,128)(2,1)} %bitcast.149), custom_call_target="tpu_custom_call" | custom-call | bytes 204000000 | tf_op jit(solution)/shard_map/pallas_call | solution.py:557
  879.1 67.5 %collective-permute-done.16 = bf16[128,2048]{1,0:T(8,128)(2,1)S(1)} collective-permute-done((bf16[128,2048]{1,0:T(8,128)(2,1)S(1)}, bf16[128,2048]{1,0:T(8,128)(2,1)S(1)}, u32[]{:S(2)}, u32[]{:S(2)}) %collective-permute-start.16) | collective-permute-done | bytes 524320 | tf_op jit(solution)/shard_map/ppermute | solution.py:717
  953.8 9.7 collective-permute-done.10
  (410 shorter events, 229.3 us)
Async XLA Ops:
  2.1 37.1 %collective-permute-start = (bf16[128,2048]{1,0:T(8,128)(2,1)S(1)}, bf16[128,2048]{1,0:T(8,128)(2,1)}, u32[]{:S(2)}, u32[]{:S(2)}) collective-permute-start(bf16[128,2048]{1,0:T(8,128)(2,1)S(1)} %select_bitcast_fusion.12), channel_id=1, source_target_pairs={{0,8},{24,16},{1,9},{25,17},{2,10},{26,18},{3,11},{27,19},{4,12},{... | collective-permute-start | bytes 1572872 | tf_op jit(solution)/shard_map/ppermute | solution.py:721
  6.0 36.4 %collective-permute-start.1 = (f32[128,2048]{1,0:T(8,128)}, f32[128,2048]{1,0:T(8,128)}, u32[]{:S(2)}, u32[]{:S(2)}) collective-permute-start(f32[128,2048]{1,0:T(8,128)} %select_bitcast_fusion.3), channel_id=1, source_target_pairs={{0,8},{24,16},{1,9},{25,17},{2,10},{26,18},{3,11},{27,19},{4,12},{... | collective-permute-start | bytes 3145736 | tf_op jit(solution)/shard_map/ppermute | solution.py:721
  150.4 75.1 %collective-permute-start.2 = (bf16[256,2048]{1,0:T(8,128)(2,1)}, bf16[256,2048]{1,0:T(8,128)(2,1)}, u32[]{:S(2)}, u32[]{:S(2)}) collective-permute-start(bf16[256,2048]{1,0:T(8,128)(2,1)} %bitcast.152), channel_id=1, source_target_pairs={{8,24},{9,25},{10,26},{11,27},{12,28},{13,29},{14,30},{15,31}} | collective-permute-start | bytes 3145736 | tf_op jit(solution)/shard_map/ppermute | solution.py:732
  152.2 73.2 %collective-permute-start.8 = (bf16[256,2048]{1,0:T(8,128)(2,1)}, bf16[256,2048]{1,0:T(8,128)(2,1)}, u32[]{:S(2)}, u32[]{:S(2)}) collective-permute-start(bf16[256,2048]{1,0:T(8,128)(2,1)} %bitcast.153), channel_id=1, source_target_pairs={{16,0},{17,1},{18,2},{19,3},{20,4},{21,5},{22,6},{23,7}} | collective-permute-start | bytes 3145736 | tf_op jit(solution)/shard_map/ppermute | solution.py:732
  165.6 66.4 %collective-permute-start.4 = (bf16[304,256]{1,0:T(8,128)(2,1)S(1)}, bf16[304,256]{1,0:T(8,128)(2,1)S(1)}, u32[]{:S(2)}, u32[]{:S(2)}) collective-permute-start(bf16[304,256]{1,0:T(8,128)(2,1)S(1)} %copy-done.70), channel_id=1, source_target_pairs={{16,0},{17,1},{18,2},{19,3},{20,4},{21,5},{22,6},{23,7}} | collective-permute-start | bytes 466952 | tf_op jit(solution)/shard_map/ppermute | solution.py:732
  168.0 65.3 %collective-permute-start.6 = (bf16[8,128,512]{2,1,0:T(8,128)(2,1)}, bf16[8,128,512]{2,1,0:T(8,128)(2,1)}, u32[]{:S(2)}, u32[]{:S(2)}) collective-permute-start(bf16[8,128,512]{2,1,0:T(8,128)(2,1)} %slice_bitcast_fusion), channel_id=1, source_target_pairs={{16,0},{17,1},{18,2},{19,3},{20,4},{21,5},{22,6},{23,7},{24,8},{25... | collective-permute-start | bytes 3145736 | tf_op jit(solution)/shard_map/ppermute | solution.py:744
  229.0 23.8 %collective-permute-start.3 = (bf16[256,2048]{1,0:T(8,128)(2,1)}, bf16[256,2048]{1,0:T(8,128)(2,1)}, u32[]{:S(2)}, u32[]{:S(2)}) collective-permute-start(bf16[256,2048]{1,0:T(8,128)(2,1)} %get-tuple-element.115), channel_id=1, source_target_pairs={{0,8},{24,16},{1,9},{25,17},{2,10},{26,18},{3,11},{27,19},{4,12},{... | collective-permute-start | bytes 3145736 | tf_op jit(solution)/shard_map/ppermute | solution.py:721
  232.0 19.4 %collective-permute-start.5 = (bf16[304,256]{1,0:T(8,128)(2,1)S(1)}, bf16[304,256]{1,0:T(8,128)(2,1)S(1)}, u32[]{:S(2)}, u32[]{:S(2)}) collective-permute-start(bf16[304,256]{1,0:T(8,128)(2,1)S(1)} %broadcast_select_fusion.10), channel_id=1, source_target_pairs={{0,8},{24,16},{1,9},{25,17},{2,10},{26,18},{3,11},{27,19},{4,12},{... | collective-permute-start | bytes 466952 | tf_op jit(solution)/shard_map/ppermute | solution.py:721
  234.4 125.8 %all-to-all-start = ((bf16[8,128,512]{2,1,0:T(8,128)(2,1)}), bf16[8,128,512]{2,1,0:T(8,128)(2,1)}, u32[]{:S(2)}, u32[]{:S(2)}) async-start(bf16[8,128,512]{2,1,0:T(8,128)(2,1)} %bitcast_select_fusion), calls=%async_computation | async-start | bytes 2097152 | tf_op jit(solution)/shard_map/all_to_all | solution.py:746
  251.5 112.4 %collective-permute-start.9 = (bf16[256,2048]{1,0:T(8,128)(2,1)}, bf16[256,2048]{1,0:T(8,128)(2,1)}, u32[]{:S(2)}, u32[]{:S(2)}) collective-permute-start(bf16[256,2048]{1,0:T(8,128)(2,1)} %get-tuple-element.114), channel_id=1, source_target_pairs={{0,8},{24,16},{1,9},{25,17},{2,10},{26,18},{3,11},{27,19},{4,12},{... | collective-permute-start | bytes 3145736 | tf_op jit(solution)/shard_map/ppermute | solution.py:721
  317.3 49.0 %collective-permute-start.12 = (bf16[128,2048]{1,0:T(8,128)(2,1)S(1)}, bf16[128,2048]{1,0:T(8,128)(2,1)S(1)}, u32[]{:S(2)}, u32[]{:S(2)}) collective-permute-start(bf16[128,2048]{1,0:T(8,128)(2,1)S(1)} %get-tuple-element.86), channel_id=1, source_target_pairs={{8,0},{16,24},{9,1},{17,25},{10,2},{18,26},{11,3},{19,27},{12,4},{... | collective-permute-start | bytes 1572872 | tf_op jit(solution)/shard_map/ppermute | solution.py:717
  360.2 48.9 %collective-permute-start.7 = (bf16[8,128,512]{2,1,0:T(8,128)(2,1)}, bf16[8,128,512]{2,1,0:T(8,128)(2,1)S(1)}, u32[]{:S(2)}, u32[]{:S(2)}) collective-permute-start(bf16[8,128,512]{2,1,0:T(8,128)(2,1)} %all-to-all-done), channel_id=1, source_target_pairs={{0,8},{8,0},{1,9},{9,1},{2,10},{10,2},{3,11},{11,3},{4,12},{12,4},... | collective-permute-start | bytes 3145736 | tf_op jit(solution)/shard_map/ppermute | solution.py:709
  368.3 618.0 %collective-permute-start.13 = (bf16[2,128,2048]{2,1,0:T(8,128)(2,1)}, bf16[2,128,2048]{2,1,0:T(8,128)(2,1)}, u32[]{:S(2)}, u32[]{:S(2)}) collective-permute-start(bf16[2,128,2048]{2,1,0:T(8,128)(2,1)} %pad_maximum_fusion.6), channel_id=1, source_target_pairs={{24,8},{25,9},{26,10},{27,11},{28,12},{29,13},{30,14},{31,15}} | collective-permute-start | bytes 3145736 | tf_op jit(solution)/shard_map/ppermute | solution.py:774
  750.3 127.6 %collective-permute-start.14 = (bf16[128,2048]{1,0:T(8,128)(2,1)S(1)}, bf16[128,2048]{1,0:T(8,128)(2,1)}, u32[]{:S(2)}, u32[]{:S(2)}) collective-permute-start(bf16[128,2048]{1,0:T(8,128)(2,1)S(1)} %copy-done.32), channel_id=1, source_target_pairs={{8,0},{16,24},{9,1},{17,25},{10,2},{18,26},{11,3},{19,27},{12,4},{... | collective-permute-start | bytes 1572872 | tf_op jit(solution)/shard_map/ppermute | solution.py:717
  754.6 218.5 %collective-permute-start.25 = (bf16[256,2048]{1,0:T(8,128)(2,1)}, bf16[256,2048]{1,0:T(8,128)(2,1)S(1)}, u32[]{:S(2)}, u32[]{:S(2)}) collective-permute-start(bf16[256,2048]{1,0:T(8,128)(2,1)} %get-tuple-element.157), channel_id=1, source_target_pairs={{8,0},{16,24},{9,1},{17,25},{10,2},{18,26},{11,3},{19,27},{12,4},{... | collective-permute-start | bytes 3145736 | tf_op jit(solution)/shard_map/ppermute | solution.py:717
  756.7 109.7 %collective-permute-start.21 = (bf16[295,256]{1,0:T(8,128)(2,1)S(1)}, bf16[295,256]{1,0:T(8,128)(2,1)S(1)}, u32[]{:S(2)}, u32[]{:S(2)}) collective-permute-start(bf16[295,256]{1,0:T(8,128)(2,1)S(1)} %convert_element_type.246), channel_id=1, source_target_pairs={{8,0},{16,24},{9,1},{17,25},{10,2},{18,26},{11,3},{19,27},{12,4},{... | collective-permute-start | bytes 453128 | tf_op jit(solution)/shard_map/ppermute | solution.py:717
  758.7 108.6 %collective-permute-start.20 = (bf16[295,256]{1,0:T(8,128)(2,1)S(1)}, bf16[295,256]{1,0:T(8,128)(2,1)S(1)}, u32[]{:S(2)}, u32[]{:S(2)}) collective-permute-start(bf16[295,256]{1,0:T(8,128)(2,1)S(1)} %convert_element_type.244), channel_id=1, source_target_pairs={{8,0},{16,24},{9,1},{17,25},{10,2},{18,26},{11,3},{19,27},{12,4},{... | collective-permute-start | bytes 453128 | tf_op jit(solution)/shard_map/ppermute | solution.py:717
  868.8 107.0 %collective-permute-start.24 = (bf16[256,2048]{1,0:T(8,128)(2,1)}, bf16[256,2048]{1,0:T(8,128)(2,1)}, u32[]{:S(2)}, u32[]{:S(2)}) collective-permute-start(bf16[256,2048]{1,0:T(8,128)(2,1)} %get-tuple-element.155), channel_id=1, source_target_pairs={{8,0},{16,24},{9,1},{17,25},{10,2},{18,26},{11,3},{19,27},{12,4},{... | collective-permute-start | bytes 3145736 | tf_op jit(solution)/shard_map/ppermute | solution.py:717
  874.0 72.7 %collective-permute-start.16 = (bf16[128,2048]{1,0:T(8,128)(2,1)S(1)}, bf16[128,2048]{1,0:T(8,128)(2,1)S(1)}, u32[]{:S(2)}, u32[]{:S(2)}) collective-permute-start(bf16[128,2048]{1,0:T(8,128)(2,1)S(1)} %fusion.39), channel_id=1, source_target_pairs={{8,0},{16,24},{9,1},{17,25},{10,2},{18,26},{11,3},{19,27},{12,4},{... | collective-permute-start | bytes 1572872 | tf_op jit(solution)/shard_map/ppermute | solution.py:717
  877.9 86.9 %collective-permute-start.18 = (bf16[8,128,512]{2,1,0:T(8,128)(2,1)S(1)}, bf16[8,128,512]{2,1,0:T(8,128)(2,1)S(1)}, u32[]{:S(2)}, u32[]{:S(2)}) collective-permute-start(bf16[8,128,512]{2,1,0:T(8,128)(2,1)S(1)} %bitcast.151), channel_id=1, source_target_pairs={{0,8},{8,0},{1,9},{9,1},{2,10},{10,2},{3,11},{11,3},{4,12},{12,4},... | collective-permute-start | bytes 3145736 | tf_op jit(solution)/shard_map/ppermute | solution.py:709
  946.6 16.8 %collective-permute-start.10 = (bf16[128,2048]{1,0:T(8,128)(2,1)S(1)}, bf16[128,2048]{1,0:T(8,128)(2,1)S(1)}, u32[]{:S(2)}, u32[]{:S(2)}) collective-permute-start(bf16[128,2048]{1,0:T(8,128)(2,1)S(1)} %copy-done.69), channel_id=1, source_target_pairs={{8,0},{16,24},{9,1},{17,25},{10,2},{18,26},{11,3},{19,27},{12,4},{... | collective-permute-start | bytes 1572872 | tf_op jit(solution)/shard_map/ppermute | solution.py:717
  963.5 16.6 %collective-permute-start.15 = (bf16[2,128,2048]{2,1,0:T(8,128)(2,1)}, bf16[2,128,2048]{2,1,0:T(8,128)(2,1)}, u32[]{:S(2)}, u32[]{:S(2)}) collective-permute-start(bf16[2,128,2048]{2,1,0:T(8,128)(2,1)} %pad_maximum_fusion.7), channel_id=1, source_target_pairs={{0,16},{1,17},{2,18},{3,19},{4,20},{5,21},{6,22},{7,23}} | collective-permute-start | bytes 3145736 | tf_op jit(solution)/shard_map/ppermute | solution.py:774
  964.9 16.6 %collective-permute-start.17 = (bf16[2,128,2048]{2,1,0:T(8,128)(2,1)}, bf16[2,128,2048]{2,1,0:T(8,128)(2,1)}, u32[]{:S(2)}, u32[]{:S(2)}) collective-permute-start(bf16[2,128,2048]{2,1,0:T(8,128)(2,1)} %pad_maximum_fusion.8), channel_id=1, source_target_pairs={{24,8},{25,9},{26,10},{27,11},{28,12},{29,13},{30,14},{31,15}} | collective-permute-start | bytes 3145736 | tf_op jit(solution)/shard_map/ppermute | solution.py:774
  967.9 16.8 %all-to-all-start.1 = ((bf16[8,128,512]{2,1,0:T(8,128)(2,1)}), bf16[8,128,512]{2,1,0:T(8,128)(2,1)}, u32[]{:S(2)}, u32[]{:S(2)}) async-start(bf16[8,128,512]{2,1,0:T(8,128)(2,1)} %fusion.26), calls=%async_computation.1 | async-start | bytes 2097152 | tf_op jit(solution)/shard_map/all_to_all | solution.py:758
  (129 other events, 2302.0 us)

commit v3 on v2

v3 whole, which is shorter than its diff:
```python
import functools

import jax
import jax.numpy as jnp
from jax import lax
from jax.experimental import pallas as pl
from jax.experimental.pallas import tpu as pltpu
from jax.sharding import Mesh, PartitionSpec as P


N = 16
R = 128
KC = 4
BLOCK = 128
norm_eps = 1e-05
BF = jnp.bfloat16
F32 = jnp.float32
MESH = pl.DeviceIdType.MESH


def forward_dot(operand, factor):
    return jnp.dot(operand, factor, preferred_element_type=F32)


def cross_dot(operand, factor):
    return lax.dot_general(operand, factor, (((0,), (0,)), ((), ())), preferred_element_type=F32)


def back_dot(operand, factor):
    return lax.dot_general(operand, factor, (((1,), (1,)), ((), ())), preferred_element_type=F32)


def lasting(us):
    return pl.CostEstimate(flops=0, bytes_accessed=int(us * 3.4e6), transcendentals=0)


def widths(channels):
    wide = min(channels, 128)
    return wide, channels // wide


def sum_rows(pieces):
    row = lax.broadcasted_iota(jnp.int32, pieces[0].shape, 0)
    shift = 1
    while len(pieces) > 1:
        keep = (row & shift) == 0
        pieces = [
            jnp.where(keep, a, b) + pltpu.roll(jnp.where(keep, b, a), shift, 0)
            for a, b in zip(pieces[0::2], pieces[1::2])
        ]
        shift *= 2
    return pieces[0]


def halves(v):
    return v[:8] + v[8:]


def lanes_of(p, wide):
    return slice(p * wide, (p + 1) * wide)


def recur_forward_kernel(rate_ref, act_ref, key_ref, query_ref, out_ref, before_ref, last_ref, memory_ref):
    wide, parts = widths(rate_ref.shape[1])

    @pl.when(pl.program_id(0) == 0)
    def _():
        memory_ref[...] = jnp.zeros_like(memory_ref)

    memory = [memory_ref[:, lanes_of(p, wide)] for p in range(parts)]
    for base in range(0, rate_ref.shape[0], 8):
        rates = rate_ref[base : base + 8, :]
        feeds = rates * act_ref[base : base + 8, :]
        sums = [[] for _ in range(parts)]
        for i in range(8):
            key = jnp.broadcast_to(key_ref[:, base + i : base + i + 1], (N, wide))
            query = jnp.broadcast_to(query_ref[:, base + i : base + i + 1], (N, wide))
            square = key * key
            for p in range(parts):
                lanes = lanes_of(p, wide)
                before_ref[base + i, :, lanes] = memory[p]
                memory[p] = (1.0 - rates[i : i + 1, lanes] * square) * memory[p] + key * feeds[i : i + 1, lanes]
                sums[p].append(halves(memory[p] * query))
        for p in range(parts):
            out_ref[base : base + 8, lanes_of(p, wide)] = sum_rows(sums[p])
    for p in range(parts):
        memory_ref[:, lanes_of(p, wide)] = memory[p]

    @pl.when(pl.program_id(0) == pl.num_programs(0) - 1)
    def _():
        last_ref[...] = memory_ref[...]


def recur_forward(rate, act, key_t, query_t):
    tokens, channels = rate.shape
    rows = pl.BlockSpec((BLOCK, channels), lambda i: (i, 0))
    cols = pl.BlockSpec((N, BLOCK), lambda i: (0, i))
    return pl.pallas_call(
        recur_forward_kernel,
        grid=(tokens // BLOCK,),
        in_specs=[rows, rows, cols, cols],
        out_specs=[
            rows,
            pl.BlockSpec((BLOCK, N, channels), lambda i: (i, 0, 0)),
            pl.BlockSpec((N, channels), lambda i: (0, 0)),
        ],
        out_shape=[
            jax.ShapeDtypeStruct((tokens, channels), F32),
            jax.ShapeDtypeStruct((tokens, N, channels), F32),
            jax.ShapeDtypeStruct((N, channels), F32),
        ],
        scratch_shapes=[pltpu.VMEM((N, channels), F32)],
        compiler_params=pltpu.CompilerParams(
            dimension_semantics=("arbitrary",), vmem_limit_bytes=40 * 2**20
        ),
        cost_estimate=lasting(1),
    )(rate, act, key_t, query_t)


def recur_backward_kernel(bits, kinds, rate_ref, act_ref, grad_ref, key_ref, query_ref, before_ref, last_ref, *refs):
    along = len(kinds)
    rider_in, refs = refs[:along], refs[along:]
    d_rate_ref, d_act_ref, d_key_ref, d_query_ref = refs[:4]
    rider_out, refs = refs[4 : 4 + along], refs[4 + along :]
    lam_ref, memory_ref, key_rows, query_rows = refs[:4]
    here = Place(bits)
    ride_start, ride_end = ride(here, kinds, rider_in + rider_out + refs[4:])
    wide, parts = widths(rate_ref.shape[1])
    block = rate_ref.shape[0]

    @pl.when(pl.program_id(0) == 0)
    def _():
        here.meet(rider_peers(here, kinds))
        ride_start()
        lam_ref[...] = jnp.zeros_like(lam_ref)
        memory_ref[...] = last_ref[...]

    lam = [lam_ref[:, lanes_of(p, wide)] for p in range(parts)]
    memory = [memory_ref[:, lanes_of(p, wide)] for p in range(parts)]
    for base in reversed(range(0, block, 8)):
        rates = rate_ref[base : base + 8, :]
        acts = act_ref[base : base + 8, :]
        grads = grad_ref[base : base + 8, :]
        d_rates = [[None] * 8 for _ in range(parts)]
        d_acts = [[None] * 8 for _ in range(parts)]
        for i in reversed(range(8)):
            at = base + i
            key = jnp.broadcast_to(key_ref[:, at : at + 1], (N, wide))
            query = jnp.broadcast_to(query_ref[:, at : at + 1], (N, wide))
            square = key * key
            key_sum = query_sum = None
            for p in range(parts):
                lanes = lanes_of(p, wide)
                grad = grads[i : i + 1, lanes]
                before = before_ref[at, :, lanes]
                pulled = query * grad + lam[p]
                kept = key * before
                missing = acts[i : i + 1, lanes] - kept
                keyed = pulled * key
                scaled = pulled * rates[i : i + 1, lanes]
                d_acts[p][i] = halves(keyed)
                d_rates[p][i] = halves(keyed * missing)
                to_key = scaled * (missing - kept)
                to_query = memory[p] * grad
                key_sum = to_key if key_sum is None else key_sum + to_key
                query_sum = to_query if query_sum is None else query_sum + to_query
                lam[p] = pulled - scaled * square
                memory[p] = before
            key_rows[at * N : (at + 1) * N, :] = key_sum.astype(BF)
            query_rows[at * N : (at + 1) * N, :] = query_sum.astype(BF)
        for p in range(parts):
            lanes = lanes_of(p, wide)
            d_rate_ref[base : base + 8, lanes] = sum_rows(d_rates[p])
            d_act_ref[base : base + 8, lanes] = rates[:, lanes] * sum_rows(d_acts[p])
    for p in range(parts):
        lam_ref[:, lanes_of(p, wide)] = lam[p]
        memory_ref[:, lanes_of(p, wide)] = memory[p]

    ones = jnp.ones((wide, block), BF)
    token = lax.broadcasted_iota(jnp.int32, (block, N, block), 0)
    own = token == lax.broadcasted_iota(jnp.int32, (block, N, block), 2)
    for rows, result in ((key_rows, d_key_ref), (query_rows, d_query_ref)):
        sums = forward_dot(rows[...], ones).reshape(block, N, block)
        result[...] = jnp.sum(jnp.where(own, sums, 0.0), axis=0)

    pl.when(pl.program_id(0) == pl.num_programs(0) - 1)(ride_end)


def recur_backward(bits, cid, rate, act, grad, key_t, query_t, before, last, riders):
    tokens, channels = rate.shape
    count = tokens // BLOCK
    rows = pl.BlockSpec((BLOCK, channels), lambda i: (count - 1 - i, 0))
    cols = pl.BlockSpec((N, BLOCK), lambda i: (0, count - 1 - i))
    products = pltpu.VMEM((BLOCK * N, widths(channels)[0]), BF)
    arrays, more_shapes, more_scratch = rider_shapes(bits, riders)
    outside = [pl.BlockSpec(memory_space=pl.ANY)] * len(arrays)
    return pl.pallas_call(
        functools.partial(recur_backward_kernel, bits, tuple(kind for kind, _ in riders)),
        grid=(count,),
        in_specs=[
            rows, rows, rows, cols, cols,
            pl.BlockSpec((BLOCK, N, channels), lambda i: (count - 1 - i, 0, 0)),
            pl.BlockSpec((N, channels), lambda i: (0, 0)),
        ] + outside,
        out_specs=[rows, rows, cols, cols] + outside,
        out_shape=[
            jax.ShapeDtypeStruct((tokens, channels), F32),
            jax.ShapeDtypeStruct((tokens, channels), F32),
            jax.ShapeDtypeStruct((N, tokens), F32),
            jax.ShapeDtypeStruct((N, tokens), F32),
        ] + more_shapes,
        scratch_shapes=[pltpu.VMEM((N, channels), F32), pltpu.VMEM((N, channels), F32), products, products]
        + more_scratch,
        compiler_params=pltpu.CompilerParams(
            dimension_semantics=("arbitrary",), vmem_limit_bytes=40 * 2**20, collective_id=cid, has_side_effects=True
        ),
        cost_estimate=lasting(1),
    )(rate, act, grad, key_t, query_t, before, last, *arrays)


class Place:
    def __init__(self, bits):
        self.bits = bits
        self.n = len(bits)
        self.count = 2**self.n
        self.at = [lax.axis_index(name) for name in bits]
        self.s = lax.axis_index("section")

    def other(self, e):
        return sum(2**d * (c + e // 2**d % 2 * (1 - 2 * c)) for d, c in enumerate(self.at))

    def toward(self, e):
        return {self.bits[d]: 1 - self.at[d] for d in range(self.n) if e // 2**d % 2}

    def dims(self, p, m):
        return sum(2 ** ((p + t) % self.n) for t in range(self.n) if m // 2**t % 2)

    def positions(self, p, e):
        return sum(2**t * (e // 2 ** ((p + t) % self.n) % 2) for t in range(self.n))

    def names(self, e):
        return tuple(self.bits[d] for d in range(self.n) if e // 2**d % 2)

    def meet(self, peers):
        barrier = pltpu.get_barrier_semaphore()
        peers = list(dict.fromkeys(peers))
        for axes in peers:
            where = {name: 1 - lax.axis_index(name) for name in axes}
            pl.semaphore_signal(barrier, inc=1, device_id=where, device_id_type=MESH)
        pl.semaphore_wait(barrier, len(peers))


def spans_of(width, n, shares=None):
    tiles = width // 128
    sizes = [(tiles // n + (p < tiles % n)) * 128 for p in range(n)]
    if shares is not None and len(shares) == n and sum(shares) == tiles:
        sizes = [share * 128 for share in shares]
    return [(sum(sizes[:p]), size) for p, size in enumerate(sizes)]


def remote(src, dst, send, recv, where):
    return pltpu.make_async_remote_copy(
        src_ref=src, dst_ref=dst, send_sem=send, recv_sem=recv, device_id=where, device_id_type=MESH
    )


def arrived(place, sem):
    pltpu.make_async_copy(place, place, sem).wait()


def rider_peers(here, kinds):
    peers = [here.names(e) for e in range(1, here.count)] if "cube" in kinds else []
    return peers + ([("q",)] if set(kinds) - {"cube"} else [])


def ride(here, kinds, refs):
    k = len(kinds)
    riders = list(zip(kinds, refs[:k], refs[k : 2 * k], refs[2 * k : 3 * k], refs[3 * k :]))
    q, chip = lax.axis_index("q"), here.other(0)

    def copies(kind, src, dst, send, recv):
        if kind == "cube":
            return [
                remote(src.at[here.other(e)], dst.at[chip], send.at[e], recv.at[e], here.toward(e))
                for e in range(1, here.count)
            ]
        return [remote(src, dst.at[q] if kind == "stack" else dst, send.at[0], recv.at[0], {"q": 1 - q})]

    def when(kind, sending, do):
        if kind in ("home", "leave"):
            pl.when((q != here.s) if sending == (kind == "home") else (q == here.s))(do)
        else:
            do()

    def start():
        for kind, src, dst, send, recv in riders:
            if kind == "cube":
                pltpu.make_async_copy(src.at[chip], dst.at[chip], recv.at[0]).start()
            if kind == "stack":
                pltpu.make_async_copy(src, dst.at[q], recv.at[1]).start()
            for copy in copies(kind, src, dst, send, recv):
                when(kind, True, copy.start)

    def finish():
        for kind, src, dst, send, recv in riders:
            if kind == "cube":
                for e in range(here.count):
                    arrived(dst.at[here.other(e)], recv.at[e])
            elif kind == "stack":
                arrived(dst.at[1 - q], recv.at[0])
                arrived(dst.at[q], recv.at[1])
            else:
                when(kind, False, lambda: arrived(dst, recv.at[0]))
            for copy in copies(kind, src, dst, send, recv):
                when(kind, True, copy.wait_send)

    return start, finish


def rider_shapes(bits, riders):
    sems = pltpu.SemaphoreType.DMA((2 ** len(bits),))
    shapes = [
        jax.ShapeDtypeStruct(((2,) if kind == "stack" else ()) + array.shape, array.dtype) for kind, array in riders
    ]
    return [array for _, array in riders], shapes, [sems] * (2 * len(riders))


def gather_kernel(bits, total, layer, kinds, shares, *refs):
    here = Place(bits)
    n, s, count = here.n, here.s, here.count
    q, chip = lax.axis_index("q"), here.other(0)
    along, own_count = len(kinds), total + (0 if layer is None else 3)
    inputs, refs = refs[: own_count + along], refs[own_count + along :]
    outputs, sems = refs[: own_count + along], refs[own_count + along :]
    given, made = inputs[:own_count], outputs[:own_count]
    ride_start, ride_end = ride(
        here, kinds, inputs[own_count:] + outputs[own_count:] + sems[len(sems) - 2 * along :]
    )
    local_sem, send, recv, core_send, core_recv = sems[:5]
    spans = spans_of(given[0].shape[1], n, shares)
    parts = [(k, p) for k in range(total) for p in range(n) if spans[p][1]]

    def block(k, e, p, s_of):
        return made[k].at[s_of, here.other(e), :, pl.ds(*spans[p])]

    def source(k, e, p):
        return block(k, e, p, s) if e else given[k].at[:, pl.ds(*spans[p])]

    def deliver(k, p, m):
        t = m.bit_length() - 1
        held = here.dims(p, m - 2**t)
        where = here.toward(2 ** ((p + t) % n))
        return remote(source(k, held, p), block(k, held, p, s), send.at[k, p, m], recv.at[k, p, m], where)

    def core(k, p, m):
        held = here.dims(p, m)
        sems = core_send.at[k, p, m], core_recv.at[k, p, m]
        return remote(source(k, held, p), block(k, held, p, s), *sems, {"section": 1 - s})

    if layer is None:
        here.meet([here.names(2**d) for d in range(n)] + [("section",)] + rider_peers(here, kinds))
    else:
        blocks, small = given[total : total + 2], given[total + 2]
        rows, own_small = made[total : total + 2], made[total + 2]
        lands = [rows[i].at[q, chip] for i in range(2)]
        piece_send, piece_recv, q_send, q_recv, small_send, small_recv = sems[5:]
        peers = [here.names(e) + extra for e in range(count) for extra in ((), ("section",)) if e or extra]
        here.meet(peers + [("q",), ("q", "section")])

        def piece(i, r, e):
            where = dict(here.toward(e), **({"section": 1 - s} if r else {}))
            src = blocks[i].at[1 - s if r else s, here.other(e)]
            return remote(src, lands[i], piece_send.at[i, r, e], piece_recv.at[i, e], where)

        def pass_on(i, e):
            place = rows[i].at[q, here.other(e)]
            return remote(place, place, q_send.at[i, e], q_recv.at[i, e], {"q": 1 - q})

        def hand_small(k, where):
            return remote(small, own_small, small_send.at[k], small_recv, where)

        keep_pieces = [pltpu.make_async_copy(blocks[i].at[s, chip], lands[i], piece_recv.at[i, 0]) for i in range(2)]
        keep_small = pltpu.make_async_copy(small, own_small, small_recv)
        at_layer = s == layer
        stays, leaves = jnp.logical_and(at_layer, q == s), jnp.logical_and(at_layer, q != s)

        @pl.when(at_layer)
        def _():
            for i in range(2):
                keep_pieces[i].start()
                for e in range(count):
                    for r in range(2):
                        if e or r:
                            piece(i, r, e).start()

        @pl.when(stays)
        def _():
            keep_small.start()
            hand_small(0, {"q": 1 - q}).start()

        @pl.when(leaves)
        def _():
            hand_small(0, {"section": 1 - s}).start()
            hand_small(1, {"section": 1 - s, "q": 1 - q}).start()

    own = [pltpu.make_async_copy(given[k], made[k].at[s, chip], local_sem.at[k]) for k in range(total)]
    for k in range(total):
        for t in range(n):
            for p in range(n):
                if spans[p][1]:
                    deliver(k, p, 2**t).start()
        own[k].start()
    ride_start()
    for k, p in parts:
        core(k, p, 0).start()
    for m in range(1, count):
        if layer is not None and m < 3:
            for e in range(count):
                arrived(rows[m - 1].at[q, here.other(e)], piece_recv.at[m - 1, e])
                pass_on(m - 1, e).start()
        for k, p in parts:
            arrived(block(k, here.dims(p, m), p, s), recv.at[k, p, m])
            for t in range(m.bit_length(), n):
                deliver(k, p, m + 2**t).start()
            core(k, p, m).start()
    for copy in own:
        copy.wait()
    for m in range(count):
        for k, p in parts:
            arrived(block(k, here.dims(p, m), p, 1 - s), core_recv.at[k, p, m])
    for m in range(count):
        for k, p in parts:
            core(k, p, m).wait_send()
            if m:
                deliver(k, p, m).wait_send()
    ride_end()
    if layer is not None:
        arrived(own_small, small_recv)
        for i in range(2):
            for e in range(count):
                arrived(rows[i].at[1 - q, here.other(e)], q_recv.at[i, e])
                pass_on(i, e).wait_send()

        @pl.when(at_layer)
        def _():
            for i in range(2):
                for e in range(count):
                    for r in range(2):
                        if e or r:
                            piece(i, r, e).wait_send()

        pl.when(stays)(lambda: hand_small(0, {"q": 1 - q}).wait_send())

        @pl.when(leaves)
        def _():
            hand_small(0, {"section": 1 - s}).wait_send()
            hand_small(1, {"section": 1 - s, "q": 1 - q}).wait_send()


def gather_call(bits, cid, shards, layer=None, extras=(), riders=(), shares=None, us=35):
    rows, width = shards[0].shape
    n = len(bits)
    count = 2**n
    dma = pltpu.SemaphoreType.DMA
    sems = dma((len(shards), n, count))
    shapes = [jax.ShapeDtypeStruct((2, count, rows, width), shard.dtype) for shard in shards]
    scratch = [dma((len(shards),)), sems, sems, sems, sems]
    if layer is not None:
        shapes += [jax.ShapeDtypeStruct(extra.shape, extra.dtype) for extra in extras]
        scratch += [dma((2, 2, count)), dma((2, count)), dma((2, count)), dma((2, count)), dma((2,)), dma]
    arrays, more_shapes, more_scratch = rider_shapes(bits, riders)
    shapes += more_shapes
    out = pl.pallas_call(
        functools.partial(gather_kernel, bits, len(shards), layer, tuple(kind for kind, _ in riders), shares),
        out_shape=shapes,
        in_specs=[pl.BlockSpec(memory_space=pl.ANY)] * len(shapes),
        out_specs=[pl.BlockSpec(memory_space=pl.ANY)] * len(shapes),
        scratch_shapes=scratch + more_scratch,
        compiler_params=pltpu.CompilerParams(collective_id=cid, has_side_effects=True),
        cost_estimate=lasting(us),
    )(*shards, *extras, *arrays)
    return [o.reshape((-1, width)) for o in out[: len(shards)]] + list(out[len(shards) :])


def add_rows(place, terms, out=None):
    step = 32
    out = place if out is None else out

    @pl.loop(0, place.shape[0] // step)
    def _(r):
        lines = pl.ds(pl.multiple_of(r * step, step), step)
        total = place[lines, :].astype(F32)
        for term in terms:
            total = total + term[lines, :].astype(F32)
        out[lines, :] = total.astype(out.dtype)


def scatter_kernel(bits, turned, homing, kinds, shares, terms, *refs):
    here = Place(bits)
    along = len(kinds)
    a_refs, b_refs, refs = refs[:terms], refs[terms : 2 * terms], refs[2 * terms :]
    if homing:
        grad, refs = refs[0], refs[1:]
    rider_in, refs = refs[:along], refs[along:]
    out_ref, refs = refs[0], refs[1:]
    if homing:
        home, other_home = refs[:2]
        refs = refs[2:]
    rider_out, refs = refs[:along], refs[along:]
    mine, give, core_in, landed, core_send, core_recv, send, recv = refs[:8]
    if homing:
        q_in, ready, q_send, q_recv, home_send, home_recv, over_send, over_recv = refs[8:16]
    ride_start, ride_end = ride(here, kinds, rider_in + rider_out + refs[len(refs) - 2 * along :])
    n, s, count = here.n, here.s, here.count
    rows, width = out_ref.shape
    tile = min(width, 512)
    spans = spans_of(width, n, shares)
    parts = [p for p in range(n) if spans[p][1]]

    def core(chip):
        return remote(give.at[chip], core_in.at[chip], core_send.at[chip], core_recv.at[chip], {"section": 1 - s})

    def hand(p, m, t):
        e = here.dims(p, m) if isinstance(m, int) else sum(
            2 ** ((p + u) % n) * (m // 2**u % 2) for u in range(n)
        )
        cols = pl.ds(*spans[p])
        return remote(
            mine.at[here.other(e), :, cols], landed.at[m, :, cols], send.at[p, m], recv.at[p, m],
            here.toward(2 ** ((p + t) % n)),
        )

    def to_q(e):
        q, chip = lax.axis_index("q"), here.other(e)
        return remote(grad.at[1 - q, chip], q_in.at[chip], q_send.at[e], q_recv.at[e], {"q": 1 - q})

    def to_chip(e):
        return remote(ready.at[here.other(e)], home.at[here.other(0)], home_send.at[e], home_recv.at[e], here.toward(e))

    def to_core(e):
        chip = here.other(e)
        return remote(home.at[chip], other_home.at[chip], over_send.at[e], over_recv.at[e], {"section": 1 - s})

    def home_step(e):
        chip = here.other(e)
        arrived(q_in.at[chip], q_recv.at[e])
        place = ready.at[chip] if e else home.at[chip]
        add_rows(q_in.at[chip], [grad.at[lax.axis_index("q"), chip]], place)
        (to_chip(e) if e else to_core(0)).start()

    def home_end(e):
        if e:
            arrived(home.at[here.other(e)], home_recv.at[e])
            to_core(e).start()

    peers = [here.names(2**d) for d in range(n)] + [("section",)]
    if homing:
        peers = [here.names(e) for e in range(1, count)] + [("section",), ("q",)]
    here.meet(peers + rider_peers(here, kinds))
    if homing:
        for e in range(count):
            to_q(e).start()
    ride_start()

    @pl.loop(0, count + 1)
    def _(i):
        @pl.when(i < count)
        def _():
            chip = here.other(count - 1 - i)

            def lines(s_of):
                return pl.ds(pl.multiple_of((s_of * count + chip) * rows, rows), rows)

            lefts = [jnp.concatenate([a_ref[lines(1 - s), :], a_ref[lines(s), :]], axis=0) for a_ref in a_refs]
            for c in range(0, width, tile):
                if turned:
                    value = sum(back_dot(left, b_ref[c : c + tile, :]) for left, b_ref in zip(lefts, b_refs))
                else:
                    value = sum(forward_dot(left, b_ref[:, c : c + tile]) for left, b_ref in zip(lefts, b_refs))
                value = value.astype(BF)
                give[chip, :, c : c + tile] = value[:rows]
                mine[chip, :, c : c + tile] = value[rows:]
            core(chip).start()

        @pl.when(i > 0)
        def _():
            e = count - i
            chip = here.other(e)
            arrived(core_in.at[chip], core_recv.at[chip])
            add_rows(mine.at[chip], [core_in.at[chip]])
            for p in parts:
                pl.when(e // 2 ** ((p + n - 1) % n) % 2 == 1)(
                    lambda p=p: hand(p, here.positions(p, e), n - 1).start()
                )

    def waiting(p, m):
        cols = pl.ds(*spans[p])
        terms = [m + 2**t for t in range(m.bit_length(), n)]
        for term in terms:
            arrived(landed.at[term, :, cols], recv.at[p, term])
        return mine.at[here.other(here.dims(p, m)), :, cols], [landed.at[term, :, cols] for term in terms]

    steps = count // 2
    for m in range(steps - 1, 0, -1):
        if homing:
            home_step(steps - 1 - m)
        for p in parts:
            add_rows(*waiting(p, m))
            hand(p, m, m.bit_length() - 1).start()
    for p in parts:
        place, terms = waiting(p, 0)
        add_rows(place, terms, out_ref.at[:, pl.ds(*spans[p])])
    if homing:
        for e in range(steps - 1, count):
            home_step(e)
        for e in range(count):
            home_end(e)
        for e in range(count):
            arrived(other_home.at[here.other(e)], over_recv.at[e])
            to_core(e).wait_send()
            to_q(e).wait_send()
            if e:
                to_chip(e).wait_send()
    ride_end()
    for chip in range(count):
        core(chip).wait_send()
    for m in range(1, count):
        for p in parts:
            hand(p, m, m.bit_length() - 1).wait_send()


def scatter_columns(bits, cid, a, b, turned, grad=None, riders=(), shares=None):
    tokens, width = a[0].shape[0], b[0].shape[0 if turned else 1]
    n = len(bits)
    count = 2**n
    block = (tokens // (2 * count), width)
    dma = pltpu.SemaphoreType.DMA
    blocks = pltpu.VMEM((count,) + block, BF)
    operands = list(a) + list(b)
    shapes = [jax.ShapeDtypeStruct(block, F32)]
    scratch = [blocks] * 4 + [dma((count,))] * 2 + [dma((n, count))] * 2
    if grad is not None:
        operands += [grad]
        shapes += [jax.ShapeDtypeStruct(grad.shape[1:], BF)] * 2
        scratch += [pltpu.VMEM(grad.shape[1:], BF)] * 2 + [dma((count,))] * 6
    arrays, more_shapes, more_scratch = rider_shapes(bits, riders)
    inside, outside = pl.BlockSpec(memory_space=pltpu.VMEM), pl.BlockSpec(memory_space=pl.ANY)
    return pl.pallas_call(
        functools.partial(
            scatter_kernel, bits, turned, grad is not None, tuple(kind for kind, _ in riders), shares, len(a)
        ),
        out_shape=shapes + more_shapes,
        in_specs=[inside] * len(operands) + [outside] * len(arrays),
        out_specs=[inside] * len(shapes) + [outside] * len(arrays),
        scratch_shapes=scratch + more_scratch,
        compiler_params=pltpu.CompilerParams(
            collective_id=cid, has_side_effects=True, vmem_limit_bytes=56 * 2**20
        ),
        cost_estimate=lasting(40 if grad is None else 60),
    )(*operands, *arrays)


def scatter_dot(bits, cid, a, b, turned, grad=None, riders=(), shares=None):
    tokens, width = a[0].shape[0], b[0].shape[0 if turned else 1]
    pieces = max(1, tokens * width // 2**22)
    size = width // pieces
    cuts = [
        [f[i * size : (i + 1) * size] if turned else f[:, i * size : (i + 1) * size] for f in b] for i in range(pieces)
    ]
    first = scatter_columns(bits, cid, a, cuts[0], turned, grad, riders, shares)
    rest = [scatter_columns(bits, 14 + turned, a, cut, turned)[0] for cut in cuts[1:]]
    return [jnp.concatenate([first[0]] + rest, axis=1)] + list(first[1:])


def total_kernel(bits, kinds, x_ref, *refs):
    here = Place(bits)
    s, count = here.s, here.count
    along = len(kinds)
    rider_in, out_ref, rider_out, refs = refs[:along], refs[along], refs[along + 1 : 2 * along + 1], refs[2 * along + 1 :]
    part, core_in, ready, landed, done, pair_send, pair_recv, send, recv, back_send, back_recv = refs[:11]
    ride_start, ride_end = ride(here, kinds, rider_in + rider_out + refs[11:])
    lanes = part.shape[3]

    def span(s_of, chip):
        at = (s_of * count + chip) * lanes
        return slice(at, at + lanes)

    for s_of in range(2):
        for chip in range(count):
            part[s_of, chip] = x_ref[:, span(s_of, chip)]
    here.meet([here.names(e) for e in range(1, count)] + [("section",)] + rider_peers(here, kinds))
    first = remote(part.at[1 - s], core_in, pair_send.at[0], pair_recv.at[0], {"section": 1 - s})
    first.start()
    first.wait_recv()
    for chip in range(count):
        total = part[s, chip] + core_in[chip]
        part[s, chip] = total
        ready[chip] = total.astype(BF)

    def out(e):
        return remote(ready.at[here.other(e)], landed.at[e], send.at[e], recv.at[e], here.toward(e))

    def back(e):
        place = done.at[s, here.other(0)]
        return remote(place, place, back_send.at[e], back_recv.at[e], here.toward(e))

    others = range(1, count)
    for e in others:
        out(e).start()
    ride_start()
    total = part[s, here.other(0)]
    for e in others:
        out(e).wait_recv()
        total = total + landed[e].astype(F32)
    done[s, here.other(0)] = total.astype(BF)
    for e in others:
        back(e).start()
    for e in others:
        place = done.at[s, here.other(e)]
        arrived(place, back_recv.at[e])
    last = remote(done.at[s], done.at[s], pair_send.at[1], pair_recv.at[1], {"section": 1 - s})
    last.start()
    last.wait_recv()
    for s_of in range(2):
        for chip in range(count):
            out_ref[:, span(s_of, chip)] = done[s_of, chip]
    ride_end()
    first.wait_send()
    last.wait_send()
    for e in others:
        out(e).wait_send()
        back(e).wait_send()


def sum_columns(bits, cid, x, riders=()):
    rows, tokens = x.shape
    count = 2 ** len(bits)
    block = (rows, tokens // (2 * count))
    dma, vmem = pltpu.SemaphoreType.DMA, pltpu.VMEM
    arrays, more_shapes, more_scratch = rider_shapes(bits, riders)
    inside, outside = pl.BlockSpec(memory_space=pltpu.VMEM), pl.BlockSpec(memory_space=pl.ANY)
    return pl.pallas_call(
        functools.partial(total_kernel, bits, tuple(kind for kind, _ in riders)),
        out_shape=[jax.ShapeDtypeStruct((rows, tokens), BF)] + more_shapes,
        in_specs=[inside] + [outside] * len(arrays),
        out_specs=[inside] + [outside] * len(arrays),
        scratch_shapes=[
            vmem((2, count) + block, F32),
            vmem((count,) + block, F32),
            vmem((count,) + block, BF),
            vmem((count,) + block, BF),
            vmem((2, count) + block, BF),
        ]
        + [dma((2,))] * 2
        + [dma((count,))] * 4
        + more_scratch,
        compiler_params=pltpu.CompilerParams(
            collective_id=cid, has_side_effects=True, vmem_limit_bytes=56 * 2**20
        ),
        cost_estimate=lasting(22),
    )(x, *arrays)


def spread_kernel(bits, shard_ref, out_ref, send, recv, pair_send, pair_recv):
    here = Place(bits)
    s, q, chip = here.s, lax.axis_index("q"), here.other(0)
    others = range(1, here.count)
    here.meet([here.names(e) for e in others] + [("section",), ("q",)])
    out_ref[s, q, chip] = shard_ref[...]
    own = out_ref.at[s, q, chip]
    copies = [remote(own, own, send.at[e], recv.at[e], here.toward(e)) for e in others]
    for copy in copies:
        copy.start()
    for e in others:
        arrived(out_ref.at[s, q, here.other(e)], recv.at[e])
    place = out_ref.at[s, q]
    first = remote(place, place, pair_send.at[0], pair_recv.at[0], {"q": 1 - q})
    first.start()
    first.wait_recv()
    place = out_ref.at[s]
    second = remote(place, place, pair_send.at[1], pair_recv.at[1], {"section": 1 - s})
    second.start()
    second.wait_recv()
    for copy in copies + [first, second]:
        copy.wait_send()


def spread(bits, shard):
    width, count = shard.shape[0], 2 ** len(bits)
    block = (16, max(width, 128))
    padded = jnp.pad(shard[None, :], ((0, block[0] - 1), (0, block[1] - width)))
    dma = pltpu.SemaphoreType.DMA
    out = pl.pallas_call(
        functools.partial(spread_kernel, bits),
        out_shape=jax.ShapeDtypeStruct((2, 2, count) + block, shard.dtype),
        in_specs=[pl.BlockSpec(memory_space=pltpu.VMEM)],
        out_specs=pl.BlockSpec(memory_space=pltpu.VMEM),
        scratch_shapes=[dma((count,)), dma((count,)), dma((2,)), dma((2,))],
        compiler_params=pltpu.CompilerParams(collective_id=0, has_side_effects=True),
        cost_estimate=lasting(12),
    )(padded)
    return out[:, :, :, 0, :width].reshape((2, -1))


def chips(bits):
    return tuple(reversed(bits))


def at_home():
    return lax.axis_index("q") == lax.axis_index("section")


def low_first(mine, other):
    low = lax.axis_index("q") == 0
    return jnp.stack([jnp.where(low, mine, other), jnp.where(low, other, mine)])


def by_q(pair):
    low = lax.axis_index("q") == 0
    return jnp.where(low, pair[0], pair[1]), jnp.where(low, pair[1], pair[0])


def leave(value):
    return lax.ppermute(value, ("section", "q"), [(0, 1), (3, 2)])


def home(value):
    return lax.ppermute(value, ("section", "q"), [(1, 0), (2, 3)])


def swap(value):
    return lax.ppermute(value, "q", [(0, 1), (1, 0)])


def after(value, *earlier):
    return lax.optimization_barrier((value,) + earlier)[0]


def over_core(piece, layer):
    other = 1 - layer
    sent = lax.ppermute(piece, ("section", "q"), [(layer * 2 + other, other * 2 + other)])
    return jnp.where(lax.axis_index("section") == layer, piece, sent)


def back_over_core(piece, layer):
    other = 1 - layer
    return lax.ppermute(piece, ("section", "q"), [(other * 2 + other, layer * 2 + other)])


def column_blocks(bits, rows):
    parts = rows.reshape((rows.shape[0], 2, 2, 2 ** len(bits), -1))
    return [jnp.transpose(parts[:, i], (1, 2, 0, 3)) for i in range(2)]


def silu_slope(v):
    gate = jax.nn.sigmoid(v)
    return gate, gate * (1.0 + v * (1.0 - gate))


def normalize(stream, gain):
    inverse = lax.rsqrt(jnp.mean(stream * stream, axis=-1, keepdims=True) + norm_eps)
    return inverse, (stream * inverse * gain[None, :]).astype(BF)


class Small:
    def __init__(self, packed):
        self.taps = packed[:KC].astype(F32)
        self.conv_bias = packed[KC].astype(F32)
        self.dt_bias = packed[KC + 1].astype(F32)
        self.skip = packed[KC + 2].astype(F32)
        self.dt = packed[KC + 3 : KC + 3 + R]
        self.xproj = packed[KC + 3 + R : KC + 3 + 2 * R + 2 * N]


def mixer_inputs(normed, in_inner, small):
    inner = forward_dot(normed, in_inner).astype(BF).astype(F32)
    tokens, channels = inner.shape
    extended = jnp.concatenate([jnp.zeros((KC - 1, channels), F32), inner], axis=0)
    conv = jnp.broadcast_to(small.conv_bias[None, :], (tokens, channels))
    for tap in range(KC):
        conv = conv + small.taps[tap][None, :] * extended[tap : tap + tokens]
    act = jax.nn.silu(conv)
    return extended, conv, act, back_dot(small.xproj, act.astype(BF))


def mixer(xproj, act, normed, in_gate, small):
    gate_in = forward_dot(normed, in_gate).astype(BF).astype(F32)
    key_t, query_t = xproj[R : R + N].astype(F32), xproj[R + N :].astype(F32)
    key_norm = jnp.sum(key_t * key_t, axis=0)[:, None]
    write = jax.nn.sigmoid(cross_dot(xproj[:R], small.dt) + small.dt_bias[None, :])
    rate = write / (1.0 + write * key_norm)
    recur, before, last = recur_forward(rate, act, key_t, query_t)
    recur = recur + small.skip[None, :] * act
    gated = (recur * jax.nn.silu(gate_in)).astype(BF)
    return gate_in, key_t, query_t, key_norm, write, rate, recur, gated, before, last


def gate_back(grad_low, out_weight, kept):
    gate_in, recur = kept[0], kept[6]
    d_gated = back_dot(grad_low, out_weight).astype(BF).astype(F32)
    gate, slope = silu_slope(gate_in)
    return d_gated * (gate_in * gate), (d_gated * recur * slope).astype(BF)


def mixer_back(bits, cid, d_recur, act, xproj, kept, small, riders):
    key_t, query_t, key_norm, write, rate, recur, gated, before, last = kept[1:]
    d_skip = jnp.sum(d_recur * act, axis=0)
    d_rate, d_act_rec, d_key_t, d_query_t, *gots = recur_backward(
        bits, cid, rate, act, d_recur, key_t, query_t, before, last, riders
    )
    share = 1.0 / (1.0 + write * key_norm)
    pulled = d_rate * share * share
    d_pre = pulled * write * (1.0 - write)
    d_key_rate = -2.0 * key_t * jnp.sum(pulled * write * write, axis=1)[None, :]
    d_dt_bias = jnp.sum(d_pre, axis=0)
    d_delta = d_pre.astype(BF)
    d_dt = forward_dot(xproj[:R], d_delta)
    d_xproj = jnp.concatenate([back_dot(small.dt, d_delta), d_key_t + d_key_rate, d_query_t], axis=0)
    return d_act_rec, d_xproj, (d_dt_bias[None], d_skip[None], d_dt), gots


def inputs_back(d_xproj, d_recur, d_act_rec, extended, conv, act, small):
    tokens = act.shape[0]
    d_act = cross_dot(d_xproj, small.xproj) + small.skip[None, :] * d_recur + d_act_rec
    d_conv = d_act * silu_slope(conv)[1]
    d_taps = jnp.stack([jnp.sum(d_conv * extended[tap : tap + tokens], axis=0) for tap in range(KC)])
    d_bias = jnp.sum(d_conv, axis=0)
    later = jnp.concatenate([d_conv, jnp.zeros((KC - 1, d_conv.shape[1]), F32)], axis=0)
    d_inner = sum(small.taps[tap][None, :] * later[KC - 1 - tap : KC - 1 - tap + tokens] for tap in range(KC))
    return d_inner.astype(BF), (d_taps, d_bias[None]), forward_dot(d_xproj, act.astype(BF))


def norm_back(grad_out, d_normed, stream, inverse, gain):
    scaled = gain[None, :] * d_normed
    mean = jnp.mean(stream * scaled, axis=-1, keepdims=True)
    return grad_out + inverse * scaled - stream * inverse**3 * mean


def pack(first, second, third):
    packed = jnp.concatenate(first + second + (third,), axis=0)
    return jnp.pad(packed, ((0, -packed.shape[0] % 16), (0, 0)))


def on_device(
    bits, hidden_in, cotangent, norm_gain, in_weight, conv_weight, conv_bias, xproj_weight, dt_weight, dt_bias, skip_gain, out_weight
):
    packed = pack(
        (conv_weight[0], conv_bias),
        (dt_bias, skip_gain, dt_weight[0]),
        jnp.swapaxes(xproj_weight[0], 0, 1),
    )
    blocks = column_blocks(bits, in_weight[0])
    tight = (2, 5, 9)

    def weight(pair):
        return pair.reshape((-1, pair.shape[-1]))

    def weight_grad(normed, d_out):
        return cross_dot(normed, d_out).astype(BF).reshape((2,) + blocks[0].shape[1:])

    gains = spread(bits, norm_gain[0]).astype(F32)
    mine, others = by_q(hidden_in)
    stream0 = jnp.where(at_home(), mine, leave(others)).astype(F32)

    inverse0, normed = normalize(stream0, gains[0])
    normed0, inner, gate, packed0 = gather_call(bits, 1, [normed], 0, (*blocks, packed), shares=tight, us=60)
    out_weight, packed, blocks, cotangent = lax.optimization_barrier((out_weight, packed, blocks, cotangent, packed0))[:4]
    inner0, small0 = weight(inner), Small(packed0)
    extended0, conv0, act0, part = mixer_inputs(normed0, inner0, small0)
    out_held = over_core(out_weight[0], 0)
    part = after(part, out_held)
    upper = lax.axis_index("section") == 1
    columns = [jnp.where(upper, b[1], lax.ppermute(b[0], "section", [(1, 0)])) for b in blocks]
    xproj0, inner, late_gate = sum_columns(bits, 4, part, [("cube", columns[0]), ("cube", columns[1])])
    gate0 = weight(gate)
    out0 = jnp.where(at_home(), out_held, leave(after(out_held, xproj0)))
    kept0 = mixer(xproj0, act0, normed0, gate0, small0)
    packed_held = over_core(packed, 1)
    grad_mine, grad_others = by_q(cotangent)
    added, got, grad_got = scatter_dot(
        bits, 8, [kept0[7]], [out0], False, riders=[("leave", packed_held), ("leave", grad_others.astype(BF))]
    )
    grad1 = jnp.where(at_home(), grad_mine, grad_got.astype(F32))
    small1 = Small(jnp.where(at_home(), packed_held, got))
    output0 = (stream0 + added).astype(BF)

    stream1 = output0.astype(F32)
    inverse1, normed = normalize(stream1, gains[1])
    normed1, grad_low1, inner, output0_home = gather_call(
        bits, 2, [normed, grad1.astype(BF)], riders=[("stack", inner), ("home", output0)], shares=(3, 5, 8), us=65
    )
    inner1 = weight(inner)
    extended1, conv1, act1, part = mixer_inputs(normed1, inner1, small1)
    out_held = over_core(out_weight[0], 1)
    xproj1, gate = sum_columns(bits, 5, after(part, out_held), [("stack", late_gate)])
    gate1 = weight(gate)
    out1 = jnp.where(at_home(), out_held, leave(after(out_held, xproj1)))
    kept1 = mixer(xproj1, act1, normed1, gate1, small1)

    d_out1 = cross_dot(kept1[7], grad_low1)
    d_recur, d_gate1 = gate_back(grad_low1, out1, kept1)
    keep, give = by_q(weight_grad(normed1, d_gate1))
    d_act_rec, part, d_small, (got,) = mixer_back(bits, 16, d_recur, act1, xproj1, kept1, small1, [("swap", give)])
    (d_xproj,) = sum_columns(bits, 6, part)
    d_gate_in1 = (keep.astype(F32) + got.astype(F32)).astype(BF)
    d_inner, d_conv, d_xproj_weight = inputs_back(d_xproj, d_recur, d_act_rec, extended1, conv1, act1, small1)
    d_packed1 = pack(d_conv, d_small, d_xproj_weight)
    d_normed, d_gate_in1, d_packed1_home, d_out1_home = scatter_dot(
        bits, 11, [d_inner, d_gate1], [inner1, gate1], True,
        riders=[("cube", d_gate_in1), ("home", d_packed1.astype(BF)), ("home", d_out1.astype(BF))], shares=(4, 5, 7),
    )
    keep, give = by_q(weight_grad(normed1, d_inner))
    input_grad1 = norm_back(grad1, d_normed, stream1, inverse1, gains[1])
    grad0 = input_grad1.astype(BF)
    grad_low0, got, grad1_home = gather_call(
        bits, 3, [grad0], riders=[("swap", give), ("home", grad0)], shares=(3, 5, 8), us=45
    )
    d_inner1 = (keep.astype(F32) + got.astype(F32)).astype(BF)

    d_out0 = cross_dot(kept0[7], grad_low0)
    d_recur, d_gate0 = gate_back(grad_low0, out0, kept0)
    added, d_inner1, d_out0_home = scatter_dot(
        bits, 10, [kept1[7]], [out1], False, riders=[("cube", d_inner1), ("home", d_out0.astype(BF))], shares=(4, 5, 7)
    )
    output1 = (stream1 + added).astype(BF)
    keep, give = by_q(weight_grad(normed0, d_gate0))
    d_act_rec, part, d_small, (got, output1_home) = mixer_back(
        bits, 17, d_recur, act0, xproj0, kept0, small0, [("swap", give), ("home", output1)]
    )
    d_gate_in0 = (keep.astype(F32) + got.astype(F32)).astype(BF)
    d_xproj, d_gate_in0 = sum_columns(bits, 7, part, [("cube", d_gate_in0)])
    d_inner, d_conv, d_xproj_weight = inputs_back(d_xproj, d_recur, d_act_rec, extended0, conv0, act0, small0)
    d_packed0 = pack(d_conv, d_small, d_xproj_weight)
    d_normed, d_inner0, d_inner0_other, d_packed0_home = scatter_dot(
        bits, 13, [d_inner, d_gate0], [inner0, gate0], True,
        weight_grad(normed0, d_inner), [("home", d_packed0.astype(BF))], shares=(3, 5, 8),
    )
    input_grad0 = norm_back(grad0.astype(F32), d_normed, stream0, inverse0, gains[0]).astype(BF)

    def settled(pairs):
        sent = [back_over_core(pair, layer) for layer, pair in enumerate(pairs)]
        return jnp.where(at_home(), jnp.where(upper, pairs[1], pairs[0]), jnp.where(upper, sent[1], sent[0]))

    layer_outputs = settled((low_first(output0, output0_home), low_first(output1, output1_home))).astype(F32)
    grads1 = low_first(grad0, grad1_home)
    grads1 = jnp.where(at_home(), grads1, back_over_core(grads1, 1))
    of_first = lax.ppermute(input_grad0, ("section", "q"), [(2, 1)])
    of_second = lax.ppermute(input_grad0, ("section", "q"), [(1, 0), (3, 1)])
    grads0 = jnp.stack([jnp.where(lax.axis_index("q") == 0, input_grad0, of_first), of_second])
    input_grads = jnp.where(upper, grads1, grads0).astype(F32)
    d_packed = settled(
        tuple(
            (mine + other.astype(F32)).astype(BF)
            for mine, other in ((d_packed0, d_packed0_home), (d_packed1, d_packed1_home))
        )
    ).astype(F32)
    d_out = settled(
        tuple(
            (mine + other.astype(F32)).astype(BF) for mine, other in ((d_out0, d_out0_home), (d_out1, d_out1_home))
        )
    ).astype(F32)
    own, others = [], []
    for lower_part, upper_part in ((d_inner0, d_inner1), (d_gate_in0, d_gate_in1)):
        own.append(jnp.where(upper, upper_part, lower_part))
        others.append(jnp.where(upper, lower_part, upper_part))
    others = [d_inner0_other, lax.ppermute(others[1], "section", [(0, 1), (1, 0)])]
    others[0] = jnp.where(upper, lax.ppermute(d_inner1, "section", [(0, 1)]), others[0])
    parts = [part for m, o in zip(own, others) for part in (jnp.where(upper, o, m), jnp.where(upper, m, o))]
    d_in = jnp.concatenate([jnp.swapaxes(part, 0, 1).reshape((part.shape[1], -1)) for part in parts], axis=1).astype(F32)
    d_gain = jnp.sum(d_in * in_weight[0].astype(F32), axis=1) / norm_gain[0].astype(F32)
    return (
        layer_outputs[None],
        input_grads[None],
        d_gain[None],
        d_in[None],
        d_packed[None, :KC],
        d_packed[None, KC],
        jnp.swapaxes(d_packed[KC + 3 + R : KC + 3 + 2 * R + 2 * N], 0, 1)[None],
        d_packed[None, KC + 3 : KC + 3 + R],
        d_packed[None, KC + 1],
        d_packed[None, KC + 2],
        d_out[None],
    )


def solution(mesh):
    sections, chip_count = mesh.devices.shape
    n = chip_count.bit_length() - 2
    bits = tuple("c%d" % d for d in range(n))
    split = Mesh(mesh.devices.reshape((sections,) + (2,) * (n + 1)), ("section", "q") + chips(bits))
    seq = ("q",) + chips(bits)
    placed = (
        P(None, seq, None),
        P(None, seq, None),
        P("section", seq),
        P("section", seq, None),
        P("section", None, seq),
        P("section", seq),
        P("section", seq, None),
        P("section", None, seq),
        P("section", seq),
        P("section", seq),
        P("section", seq, None),
    )
    return jax.shard_map(
        functools.partial(on_device, bits),
        mesh=split,
        in_specs=placed,
        out_specs=(P("section", None, seq, None), P("section", None, seq, None)) + placed[2:],
        check_vma=False,
    )
```

time: 1020 us -> 863 us (0.85)
  waiting for transfers between devices: 129 us -> 0.05 us
  starting transfers between devices: 77.2 us -> 35.4 us
    ppermute x28 -> x19, waiting for transfers between devices: 129 us -> 0.05 us  [the longest x7 0.02 us: back_over_core(): lax.ppermute(piece, ('section', 'q'), [(other * 2 + other, layer * 2 + ot...]
    pallas_call x9, Pallas kernels: 316 us -> 362 us  [the longest x3 179 us: gather_call(): pl.pallas_call(functools.partial(gather_kernel, bits, len(shards), layer,...]
    pallas_call x4, Pallas kernels: 238 us -> 199 us  [scatter_columns(): pl.pallas_call(functools.partial(scatter_kernel, bits, turned, grad is no...]
    ppermute x28 -> x19, starting transfers between devices: 68.2 us -> 35.4 us  [the longest x3 13.2 us: leave(): return lax.ppermute(value, ('section', 'q'), [(0, 1), (3, 2)])]
    unnamed x247 -> x270, local copies, waits for them, and re-layouts: 5.56 us -> 20 us
    dot_general x6 -> x8, matrix products: 17.4 us -> 30.2 us  [forward_dot(): return jnp.dot(operand, factor, preferred_element_type=F32)]
    dot_general x8 -> x10, matrix products: 45 us -> 43 us  [cross_dot(): lax.dot_general(operand, factor, (((0,), (0,)), ((), ())), preferred_elem...]
  transfers between devices with their start and end apart: 30 -> 19, of which waited for: 4 -> 0; matrix products, arithmetic and copies ran while one was open for 16% -> 19% of each run, Pallas kernels for 50% -> 44%
where the time goes in v3:
time: 863 us; the launch traced here: 851 us
  Pallas kernels  618 us (72%)
  matrix products  85.1 us (10%)
  other arithmetic  79.3 us (9%)
  starting transfers between devices  35.4 us (4%)
  local copies, waits for them, and re-layouts  30.2 us (3%)
    pallas_call x4, Pallas kernels, scatter_columns(): pl.pallas_call(functools.partial(scatter_kernel, bits, turned, grad is no...  199 us
    pallas_call x3, Pallas kernels, gather_call(): pl.pallas_call(functools.partial(gather_kernel, bits, len(shards), layer,...  179 us
    pallas_call x4, Pallas kernels, sum_columns(): pl.pallas_call(functools.partial(total_kernel, bits, tuple((kind for kind...  111 us
    pallas_call x2, Pallas kernels, recur_backward(): pl.pallas_call(functools.partial(recur_backward_kernel, bits, tuple((kind...  72.6 us
    dot_general x10, matrix products, cross_dot(): lax.dot_general(operand, factor, (((0,), (0,)), ((), ())), preferred_elem...  43 us
    pallas_call x2, Pallas kernels, recur_forward(): pl.pallas_call(recur_forward_kernel, grid=(tokens // BLOCK,), in_specs=[r...  36.7 us
    dot_general x8, matrix products, forward_dot(): return jnp.dot(operand, factor, preferred_element_type=F32)  30.2 us
    unnamed x270, local copies, waits for them, and re-layouts  20 us
  transfers between devices with their start and end apart: 19, of which 0 were waited for; matrix products, arithmetic and copies ran while one was open for 19% of the time, Pallas kernels for 44%

profile of v3, /device:TPU:9, one launch (start us, length us, event | category | flops | bytes accessed | tf_op | source)
XLA Modules:
  0.0 851.0 jit_solution(16543666538063781582)
XLA Ops:
  9.5 20.0 %shard_map.194 = bf16[2,2,8,16,128]{4,3,2,1,0:T(8,128)(2,1)} custom-call(bf16[16,128]{1,0:T(8,128)(2,1)} %pad.19.shard_ref), custom_call_target="tpu_custom_call" | custom-call | bytes 40800000 | tf_op jit(solution)/shard_map/pallas_call | solution.py:793
  38.4 63.6 %shard_map.195 = (bf16[2,8,128,2048]{3,2,1,0:T(8,128)(2,1)}, bf16[2,8,128,256]{3,2,1,0:T(8,128)(2,1)}, bf16[2,8,128,256]{3,2,1,0:T(8,128)(2,1)}, bf16[304,256]{1,0:T(8,128)(2,1)}) custom-call(bf16[128,2048]{1,0:T(8,128)(2,1)} %fusion.35.refs_0_, bf16[2,8,128,256]{3,2,1,0:T(8,128)(2,1)} %bitcast.180, bf16[2,8,128,256]{3,2,1,0:T(8,128)(2,1)} %bitcast.183, ...), custom_call_target="tpu_custom_call" | custom-call | bytes 204000000 | tf_op jit(solution)/shard_map/pallas_call | solution.py:473
  125.3 33.6 %shard_map.196 = (bf16[160,2048]{1,0:T(8,128)(2,1)}, bf16[8,128,256]{2,1,0:T(8,128)(2,1)}, bf16[8,128,256]{2,1,0:T(8,128)(2,1)}) custom-call(f32[160,2048]{1,0:T(8,128)} %fusion.69.x_ref, bf16[8,128,256]{2,1,0:T(8,128)(2,1)} %bitcast_select_fusion.2.refs_0_, bf16[8,128,256]{2,1,0:T(8,128)(2,1)} %bitcast_select_fusion.1.refs_1_), custom_call_target="tpu_custom_call" | custom-call | bytes 74800000 | tf_op jit(solution)/shard_map/pallas_call | solution.py:742
  165.3 18.5 %shard_map.197 = (f32[2048,256]{1,0:T(8,128)S(1)}, f32[2048,16,256]{2,1,0:T(8,128)}, f32[16,256]{1,0:T(8,128)S(1)}) custom-call(f32[2048,256]{1,0:T(8,128)S(1)} %get-tuple-element.218.rate_ref, f32[2048,256]{1,0:T(8,128)S(1)} %get-tuple-element.156.act_ref, f32[16,2048]{1,0:T(8,128)S(1)} %get-tuple-element.194.key_ref, ...), custom_call_target="tpu_custom_call" | custom-call | bytes 3400000 | tf_op jit(solution)/shard_map/pallas_call | solution.py:98
  183.8 8.3 multiply_convert_fusion.1
  193.2 42.6 %shard_map.198 = (f32[128,2048]{1,0:T(8,128)}, bf16[304,256]{1,0:T(8,128)(2,1)}, bf16[128,2048]{1,0:T(8,128)(2,1)}) custom-call(bf16[2048,256]{1,0:T(8,128)(2,1)} %get-tuple-element.220.refs_0_, bf16[256,2048]{1,0:T(8,128)(2,1)} %broadcast_select_fusion.2.refs_1_, bf16[304,256]{1,0:T(8,128)(2,1)} %broadcast_select_fusion.15.refs_2_, ...), custom_call_target="tpu_custom_call" | custom-call | bytes 136000000 | tf_op jit(solution)/shard_map/pallas_call | solution.py:648
  240.8 68.7 %shard_map.199 = (bf16[2,8,128,2048]{3,2,1,0:T(8,128)(2,1)}, bf16[2,8,128,2048]{3,2,1,0:T(8,128)(2,1)}, bf16[2,8,128,256]{3,2,1,0:T(8,128)(2,1)}, bf16[128,2048]{1,0:T(8,128)(2,1)}) custom-call(bf16[128,2048]{1,0:T(8,128)(2,1)} %fusion.43.refs_0_, bf16[128,2048]{1,0:T(8,128)(2,1)} %fusion.83.refs_1_, bf16[8,128,256]{2,1,0:T(8,128)(2,1)} %get-tuple-element.85.refs_2_, ...), custom_call_target="tpu_custom_call" | custom-call | bytes 221000000 | tf_op jit(solution)/shard_map/pallas_call | solution.py:473
  309.5 6.1 fusion.11
  319.8 32.1 %shard_map.200 = (bf16[160,2048]{1,0:T(8,128)(2,1)}, bf16[2,8,128,256]{3,2,1,0:T(8,128)(2,1)}) custom-call(f32[160,2048]{1,0:T(8,128)} %fusion.65.x_ref, bf16[8,128,256]{2,1,0:T(8,128)(2,1)} %get-tuple-element.89.refs_0_), custom_call_target="tpu_custom_call" | custom-call | bytes 74800000 | tf_op jit(solution)/shard_map/pallas_call | solution.py:742
  352.8 10.6 %collective-permute-start.7 = (bf16[256,2048]{1,0:T(8,128)(2,1)}, bf16[256,2048]{1,0:T(8,128)(2,1)S(1)}, u32[]{:S(2)}, u32[]{:S(2)}) collective-permute-start(bf16[256,2048]{1,0:T(8,128)(2,1)} %get-tuple-element.93), channel_id=1, source_target_pairs={{0,8},{24,16},{1,9},{25,17},{2,10},{26,18},{3,11},{27,19},{4,12},{... | collective-permute-start | bytes 3145736 | tf_op jit(solution)/shard_map/ppermute | solution.py:824
  368.8 18.2 %shard_map.201 = (f32[2048,256]{1,0:T(8,128)S(1)}, f32[2048,16,256]{2,1,0:T(8,128)}, f32[16,256]{1,0:T(8,128)S(1)}) custom-call(f32[2048,256]{1,0:T(8,128)S(1)} %get-tuple-element.222.rate_ref, f32[2048,256]{1,0:T(8,128)S(1)} %get-tuple-element.152.act_ref, f32[16,2048]{1,0:T(8,128)S(1)} %get-tuple-element.192.key_ref, ...), custom_call_target="tpu_custom_call" | custom-call | bytes 3400000 | tf_op jit(solution)/shard_map/pallas_call | solution.py:98
  391.5 6.2 multiply_convert_fusion
  401.3 36.3 %shard_map.202 = (f32[2048,256]{1,0:T(8,128)S(1)}, f32[2048,256]{1,0:T(8,128)S(1)}, f32[16,2048]{1,0:T(8,128)S(1)}, f32[16,2048]{1,0:T(8,128)S(1)}, bf16[8,128,256]{2,1,0:T(8,128)(2,1)S(1)}) custom-call(f32[2048,256]{1,0:T(8,128)S(1)} %get-tuple-element.222.rate_ref, f32[2048,256]{1,0:T(8,128)S(1)} %get-tuple-element.152.act_ref, ...), custom_call_target="tpu_custom_call" | custom-call | bytes 3400000 | tf_op jit(solution)/shard_map/pallas_call | solution.py:197
  446.8 20.4 %shard_map.203 = bf16[160,2048]{1,0:T(8,128)(2,1)} custom-call(f32[160,2048]{1,0:T(8,128)} %pad_maximum_fusion.x_ref), custom_call_target="tpu_custom_call" | custom-call | bytes 74800000 | tf_op jit(solution)/shard_map/pallas_call | solution.py:742
  477.0 6.2 convolution_convert_fusion.3
  484.1 50.8 %shard_map.204 = (f32[128,2048]{1,0:T(8,128)}, bf16[8,128,256]{2,1,0:T(8,128)(2,1)}, bf16[304,256]{1,0:T(8,128)(2,1)}, bf16[256,2048]{1,0:T(8,128)(2,1)}) custom-call(bf16[2048,256]{1,0:T(8,128)(2,1)} %get-tuple-element.172.refs_0_, bf16[2048,256]{1,0:T(8,128)(2,1)} %copy-done.70, bf16[2048,256]{1,0:T(8,128)(2,1)} %bitcast.203, bf16[2048,256]{1,0:T(8,128)(2,1)} %bitcast.204, ...), custom_call_target="tpu_custom_call" | custom-call | bytes 136000000 | tf_op jit(solution)/shard_map/pallas_call | solution.py:648
  538.8 46.3 %shard_map.205 = (bf16[2,8,128,2048]{3,2,1,0:T(8,128)(2,1)}, bf16[8,128,256]{2,1,0:T(8,128)(2,1)}, bf16[128,2048]{1,0:T(8,128)(2,1)}) custom-call(bf16[128,2048]{1,0:T(8,128)(2,1)} %fusion.46.refs_0_.refs_2_, bf16[8,128,256]{2,1,0:T(8,128)(2,1)} %bitcast.195, bf16[128,2048]{1,0:T(8,128)(2,1)} %fusion.46.refs_0_.refs_2_), custom_call_target="tpu_custom_call" | custom-call | bytes 153000000 | tf_op jit(solution)/shard_map/pallas_call | solution.py:473
  585.2 7.9 fusion.93
  602.4 48.8 %shard_map.206 = (f32[128,2048]{1,0:T(8,128)}, bf16[8,128,256]{2,1,0:T(8,128)(2,1)}, bf16[256,2048]{1,0:T(8,128)(2,1)}) custom-call(bf16[2048,256]{1,0:T(8,128)(2,1)} %get-tuple-element.160.refs_0_, bf16[256,2048]{1,0:T(8,128)(2,1)} %copy-done.41, bf16[8,128,256]{2,1,0:T(8,128)(2,1)} %fusion.53.refs_2_, bf16[256,2048]{1,0:T(8,128)(2,1)} %get-tuple-element.227.refs_3_), custom_call_target="tpu_custom_call" | custom-call | bytes 136000000 | tf_op jit(solution)/shard_map/pallas_call | solution.py:648
  652.6 36.3 %shard_map.207 = (f32[2048,256]{1,0:T(8,128)S(1)}, f32[2048,256]{1,0:T(8,128)S(1)}, f32[16,2048]{1,0:T(8,128)S(1)}, f32[16,2048]{1,0:T(8,128)S(1)}, bf16[8,128,2...) custom-call(f32[2048,256]{1,0:T(8,128)S(1)} %copy-done.1, f32[2048,256]{1,0:T(8,128)S(1)} %get-tuple-element.156.act_ref, ...), custom_call_target="tpu_custom_call" | custom-call | bytes 3400000 | tf_op jit(solution)/shard_map/pallas_call | solution.py:197
  693.9 24.8 %shard_map.208 = (bf16[160,2048]{1,0:T(8,128)(2,1)}, bf16[8,128,256]{2,1,0:T(8,128)(2,1)}) custom-call(f32[160,2048]{1,0:T(8,128)} %pad_maximum_fusion.1.x_ref, bf16[8,128,256]{2,1,0:T(8,128)(2,1)} %fusion.51.refs_0_), custom_call_target="tpu_custom_call" | custom-call | bytes 74800000 | tf_op jit(solution)/shard_map/pallas_call | solution.py:742
  727.6 6.9 convolution_convert_fusion
  734.5 57.0 %shard_map.209 = (f32[128,2048]{1,0:T(8,128)}, bf16[8,128,256]{2,1,0:T(8,128)(2,1)}, bf16[8,128,256]{2,1,0:T(8,128)(2,1)}, bf16[304,256]{1,0:T(8,128)(2,1)}) custom-call(bf16[2048,256]{1,0:T(8,128)(2,1)} %copy-done.46, bf16[2048,256]{1,0:T(8,128)(2,1)} %copy-done.69, bf16[2048,256]{1,0:T(8,128)(2,1)} %bitcast.198, bf16[2048,256]{1,0:T(8,128)(2,1)} %bitcast.200, ...), custom_call_target="tpu_custom_call" | custom-call | bytes 204000000 | tf_op jit(solution)/shard_map/pallas_call | solution.py:648
  829.6 9.3 %fusion = f32[128]{0:T(128)S(1)} fusion(bf16[128,2048]{0,1:T(8,128)(2,1)} %bitcast.82, bf16[128,2048]{0,1:T(8,128)(2,1)} %bitcast.191, bf16[128,2048]{0,1:T(8,128)(2,1)S(1)} %bitcast.189, bf16[128,2048]{0,1:T(8,128)(2,1)S(1)} %bitcast.187, bf16[1,128,8192]{1,2,0:T(8,128)(2,1)S(1)} %copy-done.11), kind=kLoop, calls=%fused_computation.1 | loop fusion | flops 11534208 | bytes 4194816 | tf_op jit(solution)/shard_map/reduce_sum | solution.py:1070
  (419 shorter events, 168.7 us)
Async XLA Ops:
  2.7 32.8 %collective-permute-start = (bf16[128,2048]{1,0:T(8,128)(2,1)}, bf16[128,2048]{1,0:T(8,128)(2,1)}, u32[]{:S(2)}, u32[]{:S(2)}) collective-permute-start(bf16[128,2048]{1,0:T(8,128)(2,1)} %select_bitcast_fusion.11), channel_id=1, source_target_pairs={{0,8},{24,16},{1,9},{25,17},{2,10},{26,18},{3,11},{27,19},{4,12},{... | collective-permute-start | bytes 1572872 | tf_op jit(solution)/shard_map/ppermute | solution.py:824
  35.5 204.3 %copy-start.88 = (f32[1,2,8,1,128]{4,3,2,1,0:T(1,128)}, f32[1,2,8,1,128]{4,3,2,1,0:T(1,128)S(1)}, u32[]{:S(2)}) copy-start(f32[1,2,8,1,128]{4,3,2,1,0:T(1,128)S(1)} %get-tuple-element.204) | copy-start | bytes 24580
  36.9 202.1 %copy-start.13 = (bf16[128,2048]{1,0:T(8,128)(2,1)}, bf16[128,2048]{1,0:T(8,128)(2,1)S(1)}, u32[]{:S(2)}) copy-start(bf16[128,2048]{1,0:T(8,128)(2,1)S(1)} %get-tuple-element.159) | copy-start | bytes 1572868
  103.7 80.1 %copy-start.118 = (f32[1,256]{1,0:T(1,128)}, f32[1,256]{1,0:T(1,128)S(1)}, u32[]{:S(2)}) copy-start(f32[1,256]{1,0:T(1,128)S(1)} %get-tuple-element.201) | copy-start | bytes 3076
  103.7 20.4 %collective-permute-start.1 = (bf16[256,2048]{1,0:T(8,128)(2,1)}, bf16[256,2048]{1,0:T(8,128)(2,1)S(1)}, u32[]{:S(2)}, u32[]{:S(2)}) collective-permute-start(bf16[256,2048]{1,0:T(8,128)(2,1)} %bitcast.196), channel_id=1, source_target_pairs={{8,24},{9,25},{10,26},{11,27},{12,28},{13,29},{14,30},{15,31}} | collective-permute-start | bytes 3145736 | tf_op jit(solution)/shard_map/ppermute | solution.py:841
  104.4 19.6 %collective-permute-start.6 = (bf16[256,2048]{1,0:T(8,128)(2,1)}, bf16[256,2048]{1,0:T(8,128)(2,1)S(1)}, u32[]{:S(2)}, u32[]{:S(2)}) collective-permute-start(bf16[256,2048]{1,0:T(8,128)(2,1)} %bitcast.197), channel_id=1, source_target_pairs={{16,0},{17,1},{18,2},{19,3},{20,4},{21,5},{22,6},{23,7}} | collective-permute-start | bytes 3145736 | tf_op jit(solution)/shard_map/ppermute | solution.py:841
  106.6 15.7 %collective-permute-start.3 = (bf16[8,128,256]{2,1,0:T(8,128)(2,1)S(1)}, bf16[8,128,256]{2,1,0:T(8,128)(2,1)S(1)}, u32[]{:S(2)}, u32[]{:S(2)}) collective-permute-start(bf16[8,128,256]{2,1,0:T(8,128)(2,1)S(1)} %slice_bitcast_fusion), channel_id=1, source_target_pairs={{16,0},{17,1},{18,2},{19,3},{20,4},{21,5},{22,6},{23,7},{24,8},{25... | collective-permute-start | bytes 1572872 | tf_op jit(solution)/shard_map/ppermute | solution.py:973
  108.0 15.2 %collective-permute-start.2 = (bf16[8,128,256]{2,1,0:T(8,128)(2,1)S(1)}, bf16[8,128,256]{2,1,0:T(8,128)(2,1)S(1)}, u32[]{:S(2)}, u32[]{:S(2)}) collective-permute-start(bf16[8,128,256]{2,1,0:T(8,128)(2,1)S(1)} %slice_bitcast_fusion.1), channel_id=1, source_target_pairs={{16,0},{17,1},{18,2},{19,3},{20,4},{21,5},{22,6},{23,7},{24,8},{25... | collective-permute-start | bytes 1572872 | tf_op jit(solution)/shard_map/ppermute | solution.py:973
  109.4 12.3 %collective-permute-start.5 = (bf16[304,256]{1,0:T(8,128)(2,1)S(1)}, bf16[304,256]{1,0:T(8,128)(2,1)S(1)}, u32[]{:S(2)}, u32[]{:S(2)}) collective-permute-start(bf16[304,256]{1,0:T(8,128)(2,1)S(1)} %copy-done.58), channel_id=1, source_target_pairs={{16,0},{17,1},{18,2},{19,3},{20,4},{21,5},{22,6},{23,7}} | collective-permute-start | bytes 466952 | tf_op jit(solution)/shard_map/ppermute | solution.py:841
  160.7 31.4 %collective-permute-start.4 = (bf16[256,2048]{1,0:T(8,128)(2,1)S(1)}, bf16[256,2048]{1,0:T(8,128)(2,1)S(1)}, u32[]{:S(2)}, u32[]{:S(2)}) collective-permute-start(bf16[256,2048]{1,0:T(8,128)(2,1)S(1)} %get-tuple-element.79), channel_id=1, source_target_pairs={{0,8},{24,16},{1,9},{25,17},{2,10},{26,18},{3,11},{27,19},{4,12},{... | collective-permute-start | bytes 3145736 | tf_op jit(solution)/shard_map/ppermute | solution.py:824
  236.9 153.7 %copy-start.120 = (f32[1,256]{1,0:T(1,128)}, f32[1,256]{1,0:T(1,128)S(1)}, u32[]{:S(2)}) copy-start(f32[1,256]{1,0:T(1,128)S(1)} %get-tuple-element.198) | copy-start | bytes 3076
  236.9 78.6 %copy-start.102 = (f32[1,256]{1,0:T(1,128)}, f32[1,256]{1,0:T(1,128)S(1)}, u32[]{:S(2)}) copy-start(f32[1,256]{1,0:T(1,128)S(1)} %get-tuple-element.206) | copy-start | bytes 3076
  352.8 34.2 %collective-permute-start.7 = (bf16[256,2048]{1,0:T(8,128)(2,1)}, bf16[256,2048]{1,0:T(8,128)(2,1)S(1)}, u32[]{:S(2)}, u32[]{:S(2)}) collective-permute-start(bf16[256,2048]{1,0:T(8,128)(2,1)} %get-tuple-element.93), channel_id=1, source_target_pairs={{0,8},{24,16},{1,9},{25,17},{2,10},{26,18},{3,11},{27,19},{4,12},{... | collective-permute-start | bytes 3145736 | tf_op jit(solution)/shard_map/ppermute | solution.py:824
  364.6 481.8 %collective-permute-start.9 = (bf16[2,128,2048]{2,1,0:T(8,128)(2,1)}, bf16[2,128,2048]{2,1,0:T(8,128)(2,1)}, u32[]{:S(2)}, u32[]{:S(2)}) collective-permute-start(bf16[2,128,2048]{2,1,0:T(8,128)(2,1)} %pad_maximum_fusion.3), channel_id=1, source_target_pairs={{24,8},{25,9},{26,10},{27,11},{28,12},{29,13},{30,14},{31,15}} | collective-permute-start | bytes 3145736 | tf_op jit(solution)/shard_map/ppermute | solution.py:847
  794.4 45.1 %collective-permute-start.11 = (bf16[128,2048]{1,0:T(8,128)(2,1)}, bf16[128,2048]{1,0:T(8,128)(2,1)}, u32[]{:S(2)}, u32[]{:S(2)}) collective-permute-start(bf16[128,2048]{1,0:T(8,128)(2,1)} %fusion.39), channel_id=1, source_target_pairs={{16,8},{17,9},{18,10},{19,11},{20,12},{21,13},{22,14},{23,15}} | collective-permute-start | bytes 1572872 | tf_op jit(solution)/shard_map/ppermute | solution.py:1047
  796.5 51.6 %collective-permute-start.12 = (bf16[128,2048]{1,0:T(8,128)(2,1)}, bf16[128,2048]{1,0:T(8,128)(2,1)}, u32[]{:S(2)}, u32[]{:S(2)}) collective-permute-start(bf16[128,2048]{1,0:T(8,128)(2,1)} %fusion.39), channel_id=1, source_target_pairs={{8,0},{24,8},{9,1},{25,9},{10,2},{26,10},{11,3},{27,11},{12,4},{28... | collective-permute-start | bytes 1572872 | tf_op jit(solution)/shard_map/ppermute | solution.py:1048
  798.0 11.2 %collective-permute-start.16 = (bf16[304,256]{1,0:T(8,128)(2,1)S(1)}, bf16[304,256]{1,0:T(8,128)(2,1)S(1)}, u32[]{:S(2)}, u32[]{:S(2)}) collective-permute-start(bf16[304,256]{1,0:T(8,128)(2,1)S(1)} %add_convert_fusion.4), channel_id=1, source_target_pairs={{24,8},{25,9},{26,10},{27,11},{28,12},{29,13},{30,14},{31,15}} | collective-permute-start | bytes 466952 | tf_op jit(solution)/shard_map/ppermute | solution.py:847
  798.8 11.7 %collective-permute-start.15 = (bf16[304,256]{1,0:T(8,128)(2,1)S(1)}, bf16[304,256]{1,0:T(8,128)(2,1)S(1)}, u32[]{:S(2)}, u32[]{:S(2)}) collective-permute-start(bf16[304,256]{1,0:T(8,128)(2,1)S(1)} %add_convert_fusion.5), channel_id=1, source_target_pairs={{0,16},{1,17},{2,18},{3,19},{4,20},{5,21},{6,22},{7,23}} | collective-permute-start | bytes 466952 | tf_op jit(solution)/shard_map/ppermute | solution.py:847
  809.2 5.1 collective-permute-start.13
  810.5 6.2 collective-permute-start.14
  814.3 27.6 %collective-permute-start.18 = (bf16[256,2048]{1,0:T(8,128)(2,1)}, bf16[256,2048]{1,0:T(8,128)(2,1)}, u32[]{:S(2)}, u32[]{:S(2)}) collective-permute-start(bf16[256,2048]{1,0:T(8,128)(2,1)} %add_convert_fusion), channel_id=1, source_target_pairs={{24,8},{25,9},{26,10},{27,11},{28,12},{29,13},{30,14},{31,15}} | collective-permute-start | bytes 3145736 | tf_op jit(solution)/shard_map/ppermute | solution.py:847
  816.7 26.6 %collective-permute-start.17 = (bf16[256,2048]{1,0:T(8,128)(2,1)}, bf16[256,2048]{1,0:T(8,128)(2,1)}, u32[]{:S(2)}, u32[]{:S(2)}) collective-permute-start(bf16[256,2048]{1,0:T(8,128)(2,1)} %add_convert_fusion.1), channel_id=1, source_target_pairs={{0,16},{1,17},{2,18},{3,19},{4,20},{5,21},{6,22},{7,23}} | collective-permute-start | bytes 3145736 | tf_op jit(solution)/shard_map/ppermute | solution.py:847
  839.5 7.0 collective-permute-start.8
  841.9 6.2 collective-permute-start.10
  (128 other events, 1823.0 us)

commit v4 on v3

--- a/solution.py
+++ b/solution.py
@@ -117,24 +117,38 @@
     )(rate, act, key_t, query_t)
 
 
-def recur_backward_kernel(bits, kinds, rate_ref, act_ref, grad_ref, key_ref, query_ref, before_ref, last_ref, *refs):
-    along = len(kinds)
+def recur_backward_kernel(bits, kinds, shares, steps, rate_ref, act_ref, grad_ref, key_ref, query_ref, before_ref, last_ref, *refs):
+    along, beside = len(kinds), 1 if steps else 0
+    product, refs = refs[: 2 * beside], refs[2 * beside :]
     rider_in, refs = refs[:along], refs[along:]
     d_rate_ref, d_act_ref, d_key_ref, d_query_ref = refs[:4]
-    rider_out, refs = refs[4 : 4 + along], refs[4 + along :]
+    scattered, refs = refs[4 : 4 + beside], refs[4 + beside :]
+    rider_out, refs = refs[:along], refs[along:]
     lam_ref, memory_ref, key_rows, query_rows = refs[:4]
     here = Place(bits)
-    ride_start, ride_end = ride(here, kinds, rider_in + rider_out + refs[4:])
+    ride_start, ride_end = ride(here, kinds, rider_in + rider_out + refs[len(refs) - 2 * along :])
+    stages = {}
+    peers = rider_peers(here, kinds)
+    if beside:
+        work = Scatter(here, False, shares, product[:1], product[1:], scattered[0], refs[4:12])
+        peers = peers + work.peers
+        half = here.count // 2
+        for k in range(half + 1):
+            stages[k] = functools.partial(work.produce, 2 * k, min(2 * k + 2, here.count + 1))
+        for k, m in enumerate(range(half - 1, 0, -1)):
+            stages[steps - 1 - 2 * (half - 1 - k)] = functools.partial(work.pass_on, m)
     wide, parts = widths(rate_ref.shape[1])
     block = rate_ref.shape[0]
 
     @pl.when(pl.program_id(0) == 0)
     def _():
-        here.meet(rider_peers(here, kinds))
+        here.meet(peers)
         ride_start()
         lam_ref[...] = jnp.zeros_like(lam_ref)
         memory_ref[...] = last_ref[...]
 
+    for at, stage in stages.items():
+        pl.when(pl.program_id(0) == at)(stage)
     lam = [lam_ref[:, lanes_of(p, wide)] for p in range(parts)]
     memory = [memory_ref[:, lanes_of(p, wide)] for p in range(parts)]
     for base in reversed(range(0, block, 8)):
@@ -183,10 +197,15 @@
         sums = forward_dot(rows[...], ones).reshape(block, N, block)
         result[...] = jnp.sum(jnp.where(own, sums, 0.0), axis=0)
 
-    pl.when(pl.program_id(0) == pl.num_programs(0) - 1)(ride_end)
-
-
-def recur_backward(bits, cid, rate, act, grad, key_t, query_t, before, last, riders):
+    @pl.when(pl.program_id(0) == pl.num_programs(0) - 1)
+    def _():
+        if beside:
+            work.settle()
+            work.drain()
+        ride_end()
+
+
+def recur_backward(bits, cid, rate, act, grad, key_t, query_t, before, last, riders, product=(), shares=None):
     tokens, channels = rate.shape
     count = tokens // BLOCK
     rows = pl.BlockSpec((BLOCK, channels), lambda i: (count - 1 - i, 0))
@@ -194,15 +213,22 @@
     products = pltpu.VMEM((BLOCK * N, widths(channels)[0]), BF)
     arrays, more_shapes, more_scratch = rider_shapes(bits, riders)
     outside = [pl.BlockSpec(memory_space=pl.ANY)] * len(arrays)
+    inside = [pl.BlockSpec(memory_space=pltpu.VMEM)] * len(product)
+    if product:
+        block = (tokens // 2 ** (len(bits) + 1), product[1].shape[1])
+        more_shapes = [jax.ShapeDtypeStruct(block, F32)] + more_shapes
+        more_scratch = scatter_scratch(bits, block) + more_scratch
     return pl.pallas_call(
-        functools.partial(recur_backward_kernel, bits, tuple(kind for kind, _ in riders)),
+        functools.partial(
+            recur_backward_kernel, bits, tuple(kind for kind, _ in riders), shares, count if product else 0
+        ),
         grid=(count,),
         in_specs=[
             rows, rows, rows, cols, cols,
             pl.BlockSpec((BLOCK, N, channels), lambda i: (count - 1 - i, 0, 0)),
             pl.BlockSpec((N, channels), lambda i: (0, 0)),
-        ] + outside,
-        out_specs=[rows, rows, cols, cols] + outside,
+        ] + inside + outside,
+        out_specs=[rows, rows, cols, cols] + inside[:1] + outside,
         out_shape=[
             jax.ShapeDtypeStruct((tokens, channels), F32),
             jax.ShapeDtypeStruct((tokens, channels), F32),
@@ -212,10 +238,10 @@
         scratch_shapes=[pltpu.VMEM((N, channels), F32), pltpu.VMEM((N, channels), F32), products, products]
         + more_scratch,
         compiler_params=pltpu.CompilerParams(
-            dimension_semantics=("arbitrary",), vmem_limit_bytes=40 * 2**20, collective_id=cid, has_side_effects=True
+            dimension_semantics=("arbitrary",), vmem_limit_bytes=56 * 2**20, collective_id=cid, has_side_effects=True
         ),
         cost_estimate=lasting(1),
-    )(rate, act, grad, key_t, query_t, before, last, *arrays)
+    )(rate, act, grad, key_t, query_t, before, last, *product, *arrays)
 
 
 class Place:
@@ -270,7 +296,11 @@
 
 def rider_peers(here, kinds):
     peers = [here.names(e) for e in range(1, here.count)] if "cube" in kinds else []
-    return peers + ([("q",)] if set(kinds) - {"cube"} else [])
+    if set(kinds) & {"swap", "stack", "home", "leave"}:
+        peers.append(("q",))
+    if set(kinds) & {"over", "over_at", "out0", "out1", "back0", "back1"}:
+        peers.append(("section",))
+    return peers
 
 
 def ride(here, kinds, refs):
@@ -284,11 +314,18 @@
                 remote(src.at[here.other(e)], dst.at[chip], send.at[e], recv.at[e], here.toward(e))
                 for e in range(1, here.count)
             ]
+        if kind in ("over", "over_at") or kind[:-1] in ("out", "back"):
+            src = src.at[1 - here.s] if kind == "over_at" else src
+            return [remote(src, dst, send.at[0], recv.at[0], {"section": 1 - here.s})]
         return [remote(src, dst.at[q] if kind == "stack" else dst, send.at[0], recv.at[0], {"q": 1 - q})]
 
     def when(kind, sending, do):
         if kind in ("home", "leave"):
             pl.when((q != here.s) if sending == (kind == "home") else (q == here.s))(do)
+        elif kind[:-1] in ("out", "back"):
+            at_layer = (here.s == int(kind[-1])) if sending == (kind[:-1] == "out") else (here.s != int(kind[-1]))
+            away = (q != here.s) if sending == (kind[:-1] == "out") else (q == here.s)
+            pl.when(jnp.logical_and(at_layer, away))(do)
         else:
             do()
 
@@ -320,7 +357,10 @@
 def rider_shapes(bits, riders):
     sems = pltpu.SemaphoreType.DMA((2 ** len(bits),))
     shapes = [
-        jax.ShapeDtypeStruct(((2,) if kind == "stack" else ()) + array.shape, array.dtype) for kind, array in riders
+        jax.ShapeDtypeStruct(
+            array.shape[1:] if kind == "over_at" else ((2,) if kind == "stack" else ()) + array.shape, array.dtype
+        )
+        for kind, array in riders
     ]
     return [array for _, array in riders], shapes, [sems] * (2 * len(riders))
 
@@ -363,7 +403,7 @@
         blocks, small = given[total : total + 2], given[total + 2]
         rows, own_small = made[total : total + 2], made[total + 2]
         lands = [rows[i].at[q, chip] for i in range(2)]
-        piece_send, piece_recv, q_send, q_recv, small_send, small_recv = sems[5:]
+        piece_send, piece_recv, q_send, q_recv, small_send, small_recv = sems[5:11]
         peers = [here.names(e) + extra for e in range(count) for extra in ((), ("section",)) if e or extra]
         here.meet(peers + [("q",), ("q", "section")])
 
@@ -495,8 +535,99 @@
         out[lines, :] = total.astype(out.dtype)
 
 
+class Scatter:
+    def __init__(self, here, turned, shares, a_refs, b_refs, out_ref, scratch):
+        self.here, self.turned, self.a_refs, self.b_refs, self.out_ref = here, turned, a_refs, b_refs, out_ref
+        self.mine, self.give, self.core_in, self.landed, self.core_send, self.core_recv, self.send, self.recv = scratch
+        self.rows, self.width = out_ref.shape
+        self.spans = spans_of(self.width, here.n, shares)
+        self.parts = [p for p in range(here.n) if self.spans[p][1]]
+        self.peers = [here.names(2**d) for d in range(here.n)] + [("section",)]
+
+    def core(self, chip):
+        sems = self.core_send.at[chip], self.core_recv.at[chip]
+        return remote(self.give.at[chip], self.core_in.at[chip], *sems, {"section": 1 - self.here.s})
+
+    def hand(self, p, m, t):
+        n = self.here.n
+        e = sum(2 ** ((p + u) % n) * (m // 2**u % 2) for u in range(n))
+        cols = pl.ds(*self.spans[p])
+        return remote(
+            self.mine.at[self.here.other(e), :, cols], self.landed.at[m, :, cols], self.send.at[p, m], self.recv.at[p, m],
+            self.here.toward(2 ** ((p + t) % n)),
+        )
+
+    def produce(self, low, high):
+        here, rows, width = self.here, self.rows, self.width
+        s, n, count = here.s, here.n, here.count
+        tile = min(width, 512)
+
+        @pl.loop(low, high)
+        def _(i):
+            @pl.when(i < count)
+            def _():
+                chip = here.other(count - 1 - i)
+
+                def lines(s_of):
+                    return pl.ds(pl.multiple_of((s_of * count + chip) * rows, rows), rows)
+
+                lefts = [jnp.concatenate([a[lines(1 - s), :], a[lines(s), :]], axis=0) for a in self.a_refs]
+                for c in range(0, width, tile):
+                    if self.turned:
+                        values = [back_dot(left, b[c : c + tile, :]) for left, b in zip(lefts, self.b_refs)]
+                    else:
+                        values = [forward_dot(left, b[:, c : c + tile]) for left, b in zip(lefts, self.b_refs)]
+                    value = functools.reduce(jnp.add, values).astype(BF)
+                    self.give[chip, :, c : c + tile] = value[:rows]
+                    self.mine[chip, :, c : c + tile] = value[rows:]
+                self.core(chip).start()
+
+            @pl.when(i > 0)
+            def _():
+                e = count - i
+                chip = here.other(e)
+                arrived(self.core_in.at[chip], self.core_recv.at[chip])
+                add_rows(self.mine.at[chip], [self.core_in.at[chip]])
+                for p in self.parts:
+                    pl.when(e // 2 ** ((p + n - 1) % n) % 2 == 1)(
+                        lambda p=p: self.hand(p, here.positions(p, e), n - 1).start()
+                    )
+
+    def waiting(self, p, m):
+        cols = pl.ds(*self.spans[p])
+        terms = [m + 2**t for t in range(m.bit_length(), self.here.n)]
+        for term in terms:
+            arrived(self.landed.at[term, :, cols], self.recv.at[p, term])
+        place = self.mine.at[self.here.other(self.here.dims(p, m)), :, cols]
+        return place, [self.landed.at[term, :, cols] for term in terms]
+
+    def pass_on(self, m):
+        for p in self.parts:
+            add_rows(*self.waiting(p, m))
+            self.hand(p, m, m.bit_length() - 1).start()
+
+    def settle(self):
+        for p in self.parts:
+            place, terms = self.waiting(p, 0)
+            add_rows(place, terms, self.out_ref.at[:, pl.ds(*self.spans[p])])
+
+    def drain(self):
+        for chip in range(self.here.count):
+            self.core(chip).wait_send()
+        for m in range(1, self.here.count):
+            for p in self.parts:
+                self.hand(p, m, m.bit_length() - 1).wait_send()
+
+
+def scatter_scratch(bits, block):
+    n, count = len(bits), 2 ** len(bits)
+    dma = pltpu.SemaphoreType.DMA
+    return [pltpu.VMEM((count,) + block, BF)] * 4 + [dma((count,))] * 2 + [dma((n, count))] * 2
+
+
 def scatter_kernel(bits, turned, homing, kinds, shares, terms, *refs):
     here = Place(bits)
+    s, count = here.s, here.count
     along = len(kinds)
     a_refs, b_refs, refs = refs[:terms], refs[terms : 2 * terms], refs[2 * terms :]
     if homing:
@@ -507,28 +638,10 @@
         home, other_home = refs[:2]
         refs = refs[2:]
     rider_out, refs = refs[:along], refs[along:]
-    mine, give, core_in, landed, core_send, core_recv, send, recv = refs[:8]
+    work = Scatter(here, turned, shares, a_refs, b_refs, out_ref, refs[:8])
     if homing:
         q_in, ready, q_send, q_recv, home_send, home_recv, over_send, over_recv = refs[8:16]
     ride_start, ride_end = ride(here, kinds, rider_in + rider_out + refs[len(refs) - 2 * along :])
-    n, s, count = here.n, here.s, here.count
-    rows, width = out_ref.shape
-    tile = min(width, 512)
-    spans = spans_of(width, n, shares)
-    parts = [p for p in range(n) if spans[p][1]]
-
-    def core(chip):
-        return remote(give.at[chip], core_in.at[chip], core_send.at[chip], core_recv.at[chip], {"section": 1 - s})
-
-    def hand(p, m, t):
-        e = here.dims(p, m) if isinstance(m, int) else sum(
-            2 ** ((p + u) % n) * (m // 2**u % 2) for u in range(n)
-        )
-        cols = pl.ds(*spans[p])
-        return remote(
-            mine.at[here.other(e), :, cols], landed.at[m, :, cols], send.at[p, m], recv.at[p, m],
-            here.toward(2 ** ((p + t) % n)),
-        )
 
     def to_q(e):
         q, chip = lax.axis_index("q"), here.other(e)
@@ -553,7 +666,7 @@
             arrived(home.at[here.other(e)], home_recv.at[e])
             to_core(e).start()
 
-    peers = [here.names(2**d) for d in range(n)] + [("section",)]
+    peers = work.peers
     if homing:
         peers = [here.names(e) for e in range(1, count)] + [("section",), ("q",)]
     here.meet(peers + rider_peers(here, kinds))
@@ -561,55 +674,13 @@
         for e in range(count):
             to_q(e).start()
     ride_start()
-
-    @pl.loop(0, count + 1)
-    def _(i):
-        @pl.when(i < count)
-        def _():
-            chip = here.other(count - 1 - i)
-
-            def lines(s_of):
-                return pl.ds(pl.multiple_of((s_of * count + chip) * rows, rows), rows)
-
-            lefts = [jnp.concatenate([a_ref[lines(1 - s), :], a_ref[lines(s), :]], axis=0) for a_ref in a_refs]
-            for c in range(0, width, tile):
-                if turned:
-                    value = sum(back_dot(left, b_ref[c : c + tile, :]) for left, b_ref in zip(lefts, b_refs))
-                else:
-                    value = sum(forward_dot(left, b_ref[:, c : c + tile]) for left, b_ref in zip(lefts, b_refs))
-                value = value.astype(BF)
-                give[chip, :, c : c + tile] = value[:rows]
-                mine[chip, :, c : c + tile] = value[rows:]
-            core(chip).start()
-
-        @pl.when(i > 0)
-        def _():
-            e = count - i
-            chip = here.other(e)
-            arrived(core_in.at[chip], core_recv.at[chip])
-            add_rows(mine.at[chip], [core_in.at[chip]])
-            for p in parts:
-                pl.when(e // 2 ** ((p + n - 1) % n) % 2 == 1)(
-                    lambda p=p: hand(p, here.positions(p, e), n - 1).start()
-                )
-
-    def waiting(p, m):
-        cols = pl.ds(*spans[p])
-        terms = [m + 2**t for t in range(m.bit_length(), n)]
-        for term in terms:
-            arrived(landed.at[term, :, cols], recv.at[p, term])
-        return mine.at[here.other(here.dims(p, m)), :, cols], [landed.at[term, :, cols] for term in terms]
-
+    work.produce(0, count + 1)
     steps = count // 2
     for m in range(steps - 1, 0, -1):
         if homing:
             home_step(steps - 1 - m)
-        for p in parts:
-            add_rows(*waiting(p, m))
-            hand(p, m, m.bit_length() - 1).start()
-    for p in parts:
-        place, terms = waiting(p, 0)
-        add_rows(place, terms, out_ref.at[:, pl.ds(*spans[p])])
+        work.pass_on(m)
+    work.settle()
     if homing:
         for e in range(steps - 1, count):
             home_step(e)
@@ -622,23 +693,17 @@
             if e:
                 to_chip(e).wait_send()
     ride_end()
-    for chip in range(count):
-        core(chip).wait_send()
-    for m in range(1, count):
-        for p in parts:
-            hand(p, m, m.bit_length() - 1).wait_send()
+    work.drain()
 
 
 def scatter_columns(bits, cid, a, b, turned, grad=None, riders=(), shares=None):
     tokens, width = a[0].shape[0], b[0].shape[0 if turned else 1]
-    n = len(bits)
-    count = 2**n
+    count = 2 ** len(bits)
     block = (tokens // (2 * count), width)
     dma = pltpu.SemaphoreType.DMA
-    blocks = pltpu.VMEM((count,) + block, BF)
     operands = list(a) + list(b)
     shapes = [jax.ShapeDtypeStruct(block, F32)]
-    scratch = [blocks] * 4 + [dma((count,))] * 2 + [dma((n, count))] * 2
+    scratch = scatter_scratch(bits, block)
     if grad is not None:
         operands += [grad]
         shapes += [jax.ShapeDtypeStruct(grad.shape[1:], BF)] * 2
@@ -761,8 +826,12 @@
     )(x, *arrays)
 
 
-def spread_kernel(bits, shard_ref, out_ref, send, recv, pair_send, pair_recv):
+def spread_kernel(bits, kinds, shard_ref, *refs):
     here = Place(bits)
+    along = len(kinds)
+    rider_in, out_ref, rider_out, refs = refs[:along], refs[along], refs[along + 1 : 2 * along + 1], refs[2 * along + 1 :]
+    send, recv, pair_send, pair_recv = refs[:4]
+    ride_start, ride_end = ride(here, kinds, rider_in + rider_out + refs[4:])
     s, q, chip = here.s, lax.axis_index("q"), here.other(0)
     others = range(1, here.count)
     here.meet([here.names(e) for e in others] + [("section",), ("q",)])
@@ -771,6 +840,7 @@
     copies = [remote(own, own, send.at[e], recv.at[e], here.toward(e)) for e in others]
     for copy in copies:
         copy.start()
+    ride_start()
     for e in others:
         arrived(out_ref.at[s, q, here.other(e)], recv.at[e])
     place = out_ref.at[s, q]
@@ -781,25 +851,28 @@
     second = remote(place, place, pair_send.at[1], pair_recv.at[1], {"section": 1 - s})
     second.start()
     second.wait_recv()
+    ride_end()
     for copy in copies + [first, second]:
         copy.wait_send()
 
 
-def spread(bits, shard):
+def spread(bits, shard, riders):
+    arrays, more_shapes, more_scratch = rider_shapes(bits, riders)
+    outside = [pl.BlockSpec(memory_space=pl.ANY)] * len(arrays)
     width, count = shard.shape[0], 2 ** len(bits)
     block = (16, max(width, 128))
     padded = jnp.pad(shard[None, :], ((0, block[0] - 1), (0, block[1] - width)))
     dma = pltpu.SemaphoreType.DMA
-    out = pl.pallas_call(
-        functools.partial(spread_kernel, bits),
-        out_shape=jax.ShapeDtypeStruct((2, 2, count) + block, shard.dtype),
-        in_specs=[pl.BlockSpec(memory_space=pltpu.VMEM)],
-        out_specs=pl.BlockSpec(memory_space=pltpu.VMEM),
-        scratch_shapes=[dma((count,)), dma((count,)), dma((2,)), dma((2,))],
+    out, *gots = pl.pallas_call(
+        functools.partial(spread_kernel, bits, tuple(kind for kind, _ in riders)),
+        out_shape=[jax.ShapeDtypeStruct((2, 2, count) + block, shard.dtype)] + more_shapes,
+        in_specs=[pl.BlockSpec(memory_space=pltpu.VMEM)] + outside,
+        out_specs=[pl.BlockSpec(memory_space=pltpu.VMEM)] + outside,
+        scratch_shapes=[dma((count,)), dma((count,)), dma((2,)), dma((2,))] + more_scratch,
         compiler_params=pltpu.CompilerParams(collective_id=0, has_side_effects=True),
         cost_estimate=lasting(12),
-    )(padded)
-    return out[:, :, :, 0, :width].reshape((2, -1))
+    )(padded, *arrays)
+    return [out[:, :, :, 0, :width].reshape((2, -1))] + gots
 
 
 def chips(bits):
@@ -836,20 +909,44 @@
     return lax.optimization_barrier((value,) + earlier)[0]
 
 
-def over_core(piece, layer):
-    other = 1 - layer
-    sent = lax.ppermute(piece, ("section", "q"), [(layer * 2 + other, other * 2 + other)])
-    return jnp.where(lax.axis_index("section") == layer, piece, sent)
-
-
-def back_over_core(piece, layer):
-    other = 1 - layer
-    return lax.ppermute(piece, ("section", "q"), [(other * 2 + other, layer * 2 + other)])
-
-
 def column_blocks(bits, rows):
     parts = rows.reshape((rows.shape[0], 2, 2, 2 ** len(bits), -1))
     return [jnp.transpose(parts[:, i], (1, 2, 0, 3)) for i in range(2)]
+
+
+def assemble_kernel(lower_refs, upper_refs, weight_ref, out_ref, gain_ref):
+    depth = weight_ref.shape[0]
+    step = min(depth, 32)
+
+    def fill(parts):
+        chips, _, wide = parts[0].shape
+
+        @pl.loop(0, depth // step)
+        def _(r):
+            lines = pl.ds(pl.multiple_of(r * step, step), step)
+            total = jnp.zeros((step, wide), F32)
+            for i, part in enumerate(parts):
+                for chip in range(chips):
+                    at = (i * chips + chip) * wide
+                    value = part[chip, lines, :].astype(F32)
+                    out_ref[lines, at : at + wide] = value
+                    total = total + value * weight_ref[lines, at : at + wide].astype(F32)
+            gain_ref[lines, :] = jnp.sum(total, axis=1, keepdims=True)
+
+    upper = lax.axis_index("section") == 1
+    pl.when(jnp.logical_not(upper))(lambda: fill(lower_refs))
+    pl.when(upper)(lambda: fill(upper_refs))
+
+
+def assemble(lower, upper, weight):
+    inside = pl.BlockSpec(memory_space=pltpu.VMEM)
+    return pl.pallas_call(
+        assemble_kernel,
+        out_shape=[jax.ShapeDtypeStruct(weight.shape, F32), jax.ShapeDtypeStruct((weight.shape[0], 1), F32)],
+        in_specs=[[inside] * 4, [inside] * 4, inside],
+        out_specs=[inside, inside],
+        compiler_params=pltpu.CompilerParams(vmem_limit_bytes=40 * 2**20),
+    )(lower, upper, weight)
 
 
 def silu_slope(v):
@@ -902,11 +999,11 @@
     return d_gated * (gate_in * gate), (d_gated * recur * slope).astype(BF)
 
 
-def mixer_back(bits, cid, d_recur, act, xproj, kept, small, riders):
+def mixer_back(bits, cid, d_recur, act, xproj, kept, small, riders, product=(), shares=None):
     key_t, query_t, key_norm, write, rate, recur, gated, before, last = kept[1:]
     d_skip = jnp.sum(d_recur * act, axis=0)
     d_rate, d_act_rec, d_key_t, d_query_t, *gots = recur_backward(
-        bits, cid, rate, act, d_recur, key_t, query_t, before, last, riders
+        bits, cid, rate, act, d_recur, key_t, query_t, before, last, riders, product, shares
     )
     share = 1.0 / (1.0 + write * key_norm)
     pulled = d_rate * share * share
@@ -958,24 +1055,27 @@
     def weight_grad(normed, d_out):
         return cross_dot(normed, d_out).astype(BF).reshape((2,) + blocks[0].shape[1:])
 
-    gains = spread(bits, norm_gain[0]).astype(F32)
     mine, others = by_q(hidden_in)
-    stream0 = jnp.where(at_home(), mine, leave(others)).astype(F32)
+    gains, got = spread(bits, norm_gain[0], [("leave", others)])
+    gains = gains.astype(F32)
+    stream0 = jnp.where(at_home(), mine, got).astype(F32)
 
     inverse0, normed = normalize(stream0, gains[0])
-    normed0, inner, gate, packed0 = gather_call(bits, 1, [normed], 0, (*blocks, packed), shares=tight, us=60)
-    out_weight, packed, blocks, cotangent = lax.optimization_barrier((out_weight, packed, blocks, cotangent, packed0))[:4]
+    normed0, inner, gate, packed0, *sent = gather_call(
+        bits, 1, [normed], 0, (*blocks, packed), shares=tight, us=60,
+        riders=[("over_at", b) for b in blocks] + [("out1", packed)] + [("out%d" % l, out_weight[0]) for l in range(2)],
+    )
+    upper = lax.axis_index("section") == 1
+    columns = [jnp.where(upper, b[1], got) for b, got in zip(blocks, sent)]
+    packed_held = jnp.where(upper, packed, sent[2])
+    out_held = jnp.where(upper, sent[3], out_weight[0]), jnp.where(upper, out_weight[0], sent[4])
     inner0, small0 = weight(inner), Small(packed0)
     extended0, conv0, act0, part = mixer_inputs(normed0, inner0, small0)
-    out_held = over_core(out_weight[0], 0)
-    part = after(part, out_held)
-    upper = lax.axis_index("section") == 1
-    columns = [jnp.where(upper, b[1], lax.ppermute(b[0], "section", [(1, 0)])) for b in blocks]
+    part = after(part, out_held[0])
     xproj0, inner, late_gate = sum_columns(bits, 4, part, [("cube", columns[0]), ("cube", columns[1])])
     gate0 = weight(gate)
-    out0 = jnp.where(at_home(), out_held, leave(after(out_held, xproj0)))
+    out0 = jnp.where(at_home(), out_held[0], leave(after(out_held[0], xproj0)))
     kept0 = mixer(xproj0, act0, normed0, gate0, small0)
-    packed_held = over_core(packed, 1)
     grad_mine, grad_others = by_q(cotangent)
     added, got, grad_got = scatter_dot(
         bits, 8, [kept0[7]], [out0], False, riders=[("leave", packed_held), ("leave", grad_others.astype(BF))]
@@ -991,17 +1091,24 @@
     )
     inner1 = weight(inner)
     extended1, conv1, act1, part = mixer_inputs(normed1, inner1, small1)
-    out_held = over_core(out_weight[0], 1)
-    xproj1, gate = sum_columns(bits, 5, after(part, out_held), [("stack", late_gate)])
+    xproj1, gate = sum_columns(bits, 5, after(part, out_held[1]), [("stack", late_gate)])
     gate1 = weight(gate)
-    out1 = jnp.where(at_home(), out_held, leave(after(out_held, xproj1)))
+    out1 = jnp.where(at_home(), out_held[1], leave(after(out_held[1], xproj1)))
     kept1 = mixer(xproj1, act1, normed1, gate1, small1)
 
     d_out1 = cross_dot(kept1[7], grad_low1)
     d_recur, d_gate1 = gate_back(grad_low1, out1, kept1)
     keep, give = by_q(weight_grad(normed1, d_gate1))
-    d_act_rec, part, d_small, (got,) = mixer_back(bits, 16, d_recur, act1, xproj1, kept1, small1, [("swap", give)])
-    (d_xproj,) = sum_columns(bits, 6, part)
+    beside = kept1[7].shape[0] * out1.shape[1] <= 2**22 and kept1[7].shape[0] >= 16 * BLOCK
+    if beside:
+        d_act_rec, part, d_small, (added, got) = mixer_back(
+            bits, 16, d_recur, act1, xproj1, kept1, small1, [("swap", give)], (kept1[7], out1), (4, 5, 7)
+        )
+    else:
+        (added,) = scatter_dot(bits, 10, [kept1[7]], [out1], False)
+        d_act_rec, part, d_small, (got,) = mixer_back(bits, 16, d_recur, act1, xproj1, kept1, small1, [("swap", give)])
+    output1 = (stream1 + added).astype(BF)
+    d_xproj, output1_home = sum_columns(bits, 6, part, [("home", output1)])
     d_gate_in1 = (keep.astype(F32) + got.astype(F32)).astype(BF)
     d_inner, d_conv, d_xproj_weight = inputs_back(d_xproj, d_recur, d_act_rec, extended1, conv1, act1, small1)
     d_packed1 = pack(d_conv, d_small, d_xproj_weight)
@@ -1019,55 +1126,48 @@
 
     d_out0 = cross_dot(kept0[7], grad_low0)
     d_recur, d_gate0 = gate_back(grad_low0, out0, kept0)
-    added, d_inner1, d_out0_home = scatter_dot(
-        bits, 10, [kept1[7]], [out1], False, riders=[("cube", d_inner1), ("home", d_out0.astype(BF))], shares=(4, 5, 7)
-    )
-    output1 = (stream1 + added).astype(BF)
     keep, give = by_q(weight_grad(normed0, d_gate0))
-    d_act_rec, part, d_small, (got, output1_home) = mixer_back(
-        bits, 17, d_recur, act0, xproj0, kept0, small0, [("swap", give), ("home", output1)]
-    )
+    d_act_rec, part, d_small, (got,) = mixer_back(bits, 17, d_recur, act0, xproj0, kept0, small0, [("swap", give)])
     d_gate_in0 = (keep.astype(F32) + got.astype(F32)).astype(BF)
-    d_xproj, d_gate_in0 = sum_columns(bits, 7, part, [("cube", d_gate_in0)])
+    d_xproj, d_gate_in0, d_inner1, d_out0_home = sum_columns(
+        bits, 7, part, [("cube", d_gate_in0), ("cube", d_inner1), ("home", d_out0.astype(BF))]
+    )
     d_inner, d_conv, d_xproj_weight = inputs_back(d_xproj, d_recur, d_act_rec, extended0, conv0, act0, small0)
     d_packed0 = pack(d_conv, d_small, d_xproj_weight)
-    d_normed, d_inner0, d_inner0_other, d_packed0_home = scatter_dot(
-        bits, 13, [d_inner, d_gate0], [inner0, gate0], True,
-        weight_grad(normed0, d_inner), [("home", d_packed0.astype(BF))], shares=(3, 5, 8),
+    d_out = [
+        (mine + other.astype(F32)).astype(BF) for mine, other in ((d_out0, d_out0_home), (d_out1, d_out1_home))
+    ]
+    d_packed1 = (d_packed1 + d_packed1_home.astype(F32)).astype(BF)
+    gate_over = jnp.where(upper, d_gate_in0, d_gate_in1)
+    d_normed, d_inner0, d_inner0_other, d_packed0_home, inner_other, gate_other, *backs = scatter_dot(
+        bits, 13, [d_inner, d_gate0], [inner0, gate0], True, weight_grad(normed0, d_inner), shares=(3, 5, 8),
+        riders=[
+            ("home", d_packed0.astype(BF)), ("over", d_inner1), ("over", gate_over), ("back0", d_out[0]), ("back1", d_out[1]),
+            ("back1", d_packed1), ("back0", output0), ("back0", output0_home), ("back1", output1), ("back1", output1_home),
+            ("back1", grad0), ("back1", grad1_home),
+        ],
     )
     input_grad0 = norm_back(grad0.astype(F32), d_normed, stream0, inverse0, gains[0]).astype(BF)
 
-    def settled(pairs):
-        sent = [back_over_core(pair, layer) for layer, pair in enumerate(pairs)]
-        return jnp.where(at_home(), jnp.where(upper, pairs[1], pairs[0]), jnp.where(upper, sent[1], sent[0]))
-
-    layer_outputs = settled((low_first(output0, output0_home), low_first(output1, output1_home))).astype(F32)
-    grads1 = low_first(grad0, grad1_home)
-    grads1 = jnp.where(at_home(), grads1, back_over_core(grads1, 1))
+    def settled(lower, upper_one, lower_back, upper_back):
+        return jnp.where(at_home(), jnp.where(upper, upper_one, lower), jnp.where(upper, upper_back, lower_back))
+
+    d_out = settled(*d_out, *backs[:2]).astype(F32)
+    d_packed0 = (d_packed0 + d_packed0_home.astype(F32)).astype(BF)
+    d_packed = settled(d_packed0, d_packed1, lax.ppermute(d_packed0, ("section", "q"), [(3, 1)]), backs[2]).astype(F32)
+    low = lax.axis_index("q") == 0
+    mine, other = settled(output0, output1, backs[3], backs[5]), settled(output0_home, output1_home, backs[4], backs[6])
+    layer_outputs = low_first(mine, other).astype(F32)
+    mine, other = jnp.where(at_home(), grad0, backs[7]), jnp.where(at_home(), grad1_home, backs[8])
+    grads1 = low_first(mine, other)
     of_first = lax.ppermute(input_grad0, ("section", "q"), [(2, 1)])
     of_second = lax.ppermute(input_grad0, ("section", "q"), [(1, 0), (3, 1)])
-    grads0 = jnp.stack([jnp.where(lax.axis_index("q") == 0, input_grad0, of_first), of_second])
+    grads0 = jnp.stack([jnp.where(low, input_grad0, of_first), of_second])
     input_grads = jnp.where(upper, grads1, grads0).astype(F32)
-    d_packed = settled(
-        tuple(
-            (mine + other.astype(F32)).astype(BF)
-            for mine, other in ((d_packed0, d_packed0_home), (d_packed1, d_packed1_home))
-        )
-    ).astype(F32)
-    d_out = settled(
-        tuple(
-            (mine + other.astype(F32)).astype(BF) for mine, other in ((d_out0, d_out0_home), (d_out1, d_out1_home))
-        )
-    ).astype(F32)
-    own, others = [], []
-    for lower_part, upper_part in ((d_inner0, d_inner1), (d_gate_in0, d_gate_in1)):
-        own.append(jnp.where(upper, upper_part, lower_part))
-        others.append(jnp.where(upper, lower_part, upper_part))
-    others = [d_inner0_other, lax.ppermute(others[1], "section", [(0, 1), (1, 0)])]
-    others[0] = jnp.where(upper, lax.ppermute(d_inner1, "section", [(0, 1)]), others[0])
-    parts = [part for m, o in zip(own, others) for part in (jnp.where(upper, o, m), jnp.where(upper, m, o))]
-    d_in = jnp.concatenate([jnp.swapaxes(part, 0, 1).reshape((part.shape[1], -1)) for part in parts], axis=1).astype(F32)
-    d_gain = jnp.sum(d_in * in_weight[0].astype(F32), axis=1) / norm_gain[0].astype(F32)
+    d_in, d_gain = assemble(
+        [d_inner0, d_inner0_other, d_gate_in0, gate_other], [inner_other, d_inner1, gate_other, d_gate_in1], in_weight[0]
+    )
+    d_gain = d_gain[:, 0] / norm_gain[0].astype(F32)
     return (
         layer_outputs[None],
         input_grads[None],

time: 863 us -> 811 us (0.940)
  starting transfers between devices: 35.4 us -> 11 us
  other arithmetic: 79.3 us -> 64.6 us
    pallas_call x4 -> x3, Pallas kernels: 199 us -> 153 us  [scatter_columns(): pl.pallas_call(functools.partial(scatter_kernel, bits, turned, grad is no...]
    pallas_call x4, Pallas kernels: 111 us -> 136 us  [sum_columns(): pl.pallas_call(functools.partial(total_kernel, bits, tuple((kind for kind...]
    ppermute x14 -> x1, starting transfers between devices: 18.7 us -> 1.35 us  [on_device(): lax.ppermute(d_packed0, ('section', 'q'), [(3, 1)])]
    pallas_call x2, Pallas kernels: 72.6 us -> 85.4 us  [recur_backward(): pl.pallas_call(functools.partial(recur_backward_kernel, bits, tuple((kind...]
    pallas_call x3, Pallas kernels: 179 us -> 189 us  [gather_call(): pl.pallas_call(functools.partial(gather_kernel, bits, len(shards), layer,...]
    ppermute x3 -> x2, starting transfers between devices: 13.2 us -> 3.12 us  [leave(): return lax.ppermute(value, ('section', 'q'), [(0, 1), (3, 2)])]
    reduce_sum x1 -> x0, other arithmetic: 9.33 us -> none  [on_device(): jnp.sum(d_in * in_weight[0].astype(F32), axis=1) / norm_gain[0].astype(F32)]
    unnamed x270 -> x237, local copies, waits for them, and re-layouts: 20 us -> 11.4 us
  transfers between devices with their start and end apart: 19 -> 5, of which waited for: 0 -> 0; matrix products, arithmetic and copies ran while one was open for 19% -> 4% of each run, Pallas kernels for 44% -> 5%
where the time goes in v4:
time: 811 us; the launch traced here: 800 us
  Pallas kernels  618 us (76%)
  matrix products  80.6 us (10%)
  other arithmetic  64.6 us (8%)
  local copies, waits for them, and re-layouts  24.1 us (3%)
  starting transfers between devices  11 us (1%)
    pallas_call x3, Pallas kernels, gather_call(): pl.pallas_call(functools.partial(gather_kernel, bits, len(shards), layer,...  189 us
    pallas_call x3, Pallas kernels, scatter_columns(): pl.pallas_call(functools.partial(scatter_kernel, bits, turned, grad is no...  153 us
    pallas_call x4, Pallas kernels, sum_columns(): pl.pallas_call(functools.partial(total_kernel, bits, tuple((kind for kind...  136 us
    pallas_call x2, Pallas kernels, recur_backward(): pl.pallas_call(functools.partial(recur_backward_kernel, bits, tuple((kind...  85.4 us
    dot_general x10, matrix products, cross_dot(): lax.dot_general(operand, factor, (((0,), (0,)), ((), ())), preferred_elem...  38 us
    pallas_call x2, Pallas kernels, recur_forward(): pl.pallas_call(recur_forward_kernel, grid=(tokens // BLOCK,), in_specs=[r...  36.7 us
    dot_general x8, matrix products, forward_dot(): return jnp.dot(operand, factor, preferred_element_type=F32)  27.8 us
  transfers between devices with their start and end apart: 5, of which 0 were waited for; matrix products, arithmetic and copies ran while one was open for 4% of the time, Pallas kernels for 5%

profile of v4, /device:TPU:9, one launch (start us, length us, event | category | flops | bytes accessed | tf_op | source)
XLA Modules:
  0.0 800.4 jit_solution(8508120372786179805)
XLA Ops:
  7.4 14.7 %shard_map.194 = (bf16[2,2,8,16,128]{4,3,2,1,0:T(8,128)(2,1)}, bf16[128,2048]{1,0:T(8,128)(2,1)}) custom-call(bf16[16,128]{1,0:T(8,128)(2,1)} %pad.19.shard_ref, bf16[128,2048]{1,0:T(8,128)(2,1)} %select_bitcast_fusion.5.refs_0_), custom_call_target="tpu_custom_call" | custom-call | bytes 40800000 | tf_op jit(solution)/shard_map/pallas_call | solution.py:866
  33.0 73.0 %shard_map.195 = (bf16[2,8,128,2048]{3,2,1,0:T(8,128)(2,1)}, bf16[2,8,128,256]{3,2,1,0:T(8,128)(2,1)}, bf16[2,8,128,256]{3,2,1,0:T(8,128)(2,1)}, bf16[304,256]{1...) custom-call(bf16[128,2048]{1,0:T(8,128)(2,1)} %fusion.32.refs_0_, ...), custom_call_target="tpu_custom_call" | custom-call | bytes 204000000 | tf_op jit(solution)/shard_map/pallas_call | solution.py:513
  107.4 6.1 fusion.9
  123.0 34.6 %shard_map.196 = (bf16[160,2048]{1,0:T(8,128)(2,1)}, bf16[8,128,256]{2,1,0:T(8,128)(2,1)}, bf16[8,128,256]{2,1,0:T(8,128)(2,1)}) custom-call(f32[160,2048]{1,0:T(8,128)} %fusion.67.x_ref, bf16[8,128,256]{2,1,0:T(8,128)(2,1)} %get-tuple-element.247.refs_0_, bf16[8,128,256]{2,1,0:T(8,128)(2,1)} %get-tuple-element.246.refs_1_), custom_call_target="tpu_custom_call" | custom-call | bytes 74800000 | tf_op jit(solution)/shard_map/pallas_call | solution.py:807
  164.8 18.5 %shard_map.197 = (f32[2048,256]{1,0:T(8,128)S(1)}, f32[2048,16,256]{2,1,0:T(8,128)}, f32[16,256]{1,0:T(8,128)S(1)}) custom-call(f32[2048,256]{1,0:T(8,128)S(1)} %get-tuple-element.234.rate_ref, f32[2048,256]{1,0:T(8,128)S(1)} %get-tuple-element.180.act_ref, f32[16,2048]{1,0:T(8,128)S(1)} %get-tuple-element.210.key_ref, ...), custom_call_target="tpu_custom_call" | custom-call | bytes 3400000 | tf_op jit(solution)/shard_map/pallas_call | solution.py:98
  183.4 4.1 multiply_convert_fusion.1
  188.6 44.3 %shard_map.198 = (f32[128,2048]{1,0:T(8,128)}, bf16[304,256]{1,0:T(8,128)(2,1)}, bf16[128,2048]{1,0:T(8,128)(2,1)}) custom-call(bf16[2048,256]{1,0:T(8,128)(2,1)} %get-tuple-element.236.refs_0_, bf16[256,2048]{1,0:T(8,128)(2,1)} %broadcast_select_fusion.1.refs_1_, bf16[304,256]{1,0:T(8,128)(2,1)} %broadcast_select_fusion.14.refs_2_, ...), custom_call_target="tpu_custom_call" | custom-call | bytes 136000000 | tf_op jit(solution)/shard_map/pallas_call | solution.py:713
  237.5 69.7 %shard_map.199 = (bf16[2,8,128,2048]{3,2,1,0:T(8,128)(2,1)}, bf16[2,8,128,2048]{3,2,1,0:T(8,128)(2,1)}, bf16[2,8,128,256]{3,2,1,0:T(8,128)(2,1)}, bf16[128,2048]{1,0:T(8,128)(2,1)}) custom-call(bf16[128,2048]{1,0:T(8,128)(2,1)} %fusion.40.refs_0_, bf16[128,2048]{1,0:T(8,128)(2,1)} %fusion.83.refs_1_, bf16[8,128,256]{2,1,0:T(8,128)(2,1)} %get-tuple-element.102.refs_2_, ...), custom_call_target="tpu_custom_call" | custom-call | bytes 221000000 | tf_op jit(solution)/shard_map/pallas_call | solution.py:513
  307.2 6.0 fusion.8
  317.5 32.8 %shard_map.200 = (bf16[160,2048]{1,0:T(8,128)(2,1)}, bf16[2,8,128,256]{3,2,1,0:T(8,128)(2,1)}) custom-call(f32[160,2048]{1,0:T(8,128)} %fusion.63.x_ref, bf16[8,128,256]{2,1,0:T(8,128)(2,1)} %get-tuple-element.107.refs_0_), custom_call_target="tpu_custom_call" | custom-call | bytes 74800000 | tf_op jit(solution)/shard_map/pallas_call | solution.py:807
  357.4 18.2 %shard_map.201 = (f32[2048,256]{1,0:T(8,128)S(1)}, f32[2048,16,256]{2,1,0:T(8,128)}, f32[16,256]{1,0:T(8,128)S(1)}) custom-call(f32[2048,256]{1,0:T(8,128)S(1)} %get-tuple-element.238.rate_ref, f32[2048,256]{1,0:T(8,128)S(1)} %get-tuple-element.176.act_ref, f32[16,2048]{1,0:T(8,128)S(1)} %get-tuple-element.208.key_ref, ...), custom_call_target="tpu_custom_call" | custom-call | bytes 3400000 | tf_op jit(solution)/shard_map/pallas_call | solution.py:98
  375.6 5.9 convolution_convert_fusion.5
  381.7 5.2 fusion.11
  394.6 52.9 %shard_map.202 = (f32[2048,256]{1,0:T(8,128)}, f32[2048,256]{1,0:T(8,128)}, f32[16,2048]{1,0:T(8,128)}, f32[16,2048]{1,0:T(8,128)}, f32[128,2048]{1,0:T(8,128)}, /*index=5*/bf16[8,128,256]{2,1,0:T(8,128)(2,1)}) custom-call(f32[2048,256]{1,0:T(8,128)} %copy-done.7, f32[2048,256]{1,0:T(8,128)} %copy-done.2, f32[2048,256]{1,0:T(8,128)} %get-tuple-element.196.grad_ref, ...), custom_call_target="tpu_custom_call" | custom-call | bytes 3400000 | tf_op jit(solution)/shard_map/pallas_call | solution.py:221
  453.6 25.1 %shard_map.203 = (bf16[160,2048]{1,0:T(8,128)(2,1)}, bf16[128,2048]{1,0:T(8,128)(2,1)}) custom-call(f32[160,2048]{1,0:T(8,128)} %pad_maximum_fusion.x_ref, bf16[128,2048]{1,0:T(8,128)(2,1)} %fusion.41.refs_0_.refs_13_), custom_call_target="tpu_custom_call" | custom-call | bytes 74800000 | tf_op jit(solution)/shard_map/pallas_call | solution.py:807
  495.5 49.8 %shard_map.204 = (f32[128,2048]{1,0:T(8,128)}, bf16[8,128,256]{2,1,0:T(8,128)(2,1)}, bf16[304,256]{1,0:T(8,128)(2,1)}, bf16[256,2048]{1,0:T(8,128)(2,1)}) custom-call(bf16[2048,256]{1,0:T(8,128)(2,1)} %copy-done.48, bf16[2048,256]{1,0:T(8,128)(2,1)} %copy-done.65, bf16[2048,256]{1,0:T(8,128)(2,1)} %bitcast.170, bf16[2048,256]{1,0:T(8,128)(2,1)} %bitcast.171, ...), custom_call_target="tpu_custom_call" | custom-call | bytes 136000000 | tf_op jit(solution)/shard_map/pallas_call | solution.py:713
  548.2 46.5 %shard_map.205 = (bf16[2,8,128,2048]{3,2,1,0:T(8,128)(2,1)}, bf16[8,128,256]{2,1,0:T(8,128)(2,1)}, bf16[128,2048]{1,0:T(8,128)(2,1)}) custom-call(bf16[128,2048]{1,0:T(8,128)(2,1)} %fusion.44.refs_0_.refs_2_.refs_15_, bf16[8,128,256]{2,1,0:T(8,128)(2,1)} %bitcast.162, bf16[128,2048]{1,0:T(8,128)(2,1)} %fusion.44.refs_0_.refs_2_.refs_15_), custom_call_target="tpu_custom_call" | custom-call | bytes 153000000 | tf_op jit(solution)/shard_map/pallas_call | solution.py:513
  594.7 7.9 fusion.93
  602.7 5.3 multiply_reduce_fusion
  611.5 32.5 %shard_map.206 = (f32[2048,256]{1,0:T(8,128)}, f32[2048,256]{1,0:T(8,128)}, f32[16,2048]{1,0:T(8,128)}, f32[16,2048]{1,0:T(8,128)}, bf16[8,128,256]{2,1,0:T(8,128)(2,1)}) custom-call(f32[2048,256]{1,0:T(8,128)} %copy-done.6, f32[2048,256]{1,0:T(8,128)} %copy-done, f32[2048,256]{1,0:T(8,128)} %get-tuple-element.193.grad_ref, f32[16,2048]{1,0:T(8,128)} %copy-done.13, ...), custom_call_target="tpu_custom_call" | custom-call | bytes 3400000 | tf_op jit(solution)/shard_map/pallas_call | solution.py:221
  652.0 43.9 %shard_map.207 = (bf16[160,2048]{1,0:T(8,128)(2,1)}, bf16[8,128,256]{2,1,0:T(8,128)(2,1)}, bf16[8,128,256]{2,1,0:T(8,128)(2,1)}, bf16[256,2048]{1,0:T(8,128)(2,1)}) custom-call(f32[160,2048]{1,0:T(8,128)} %pad_maximum_fusion.1.x_ref, bf16[8,128,256]{2,1,0:T(8,128)(2,1)} %fusion.48.refs_0_, bf16[8,128,256]{2,1,0:T(8,128)(2,1)} %fusion.47.refs_1_, ...), custom_call_target="tpu_custom_call" | custom-call | bytes 74800000 | tf_op jit(solution)/shard_map/pallas_call | solution.py:807
  701.8 7.3 convolution_convert_fusion
  715.2 58.4 %shard_map.208 = (f32[128,2048]{1,0:T(8,128)}, bf16[8,128,256]{2,1,0:T(8,128)(2,1)}, bf16[8,128,256]{2,1,0:T(8,128)(2,1)}, bf16[304,256]{1,0:T(8,128)(2,1)}, bf1...) custom-call(bf16[2048,256]{1,0:T(8,128)(2,1)} %copy-done.45, ...), custom_call_target="tpu_custom_call" | custom-call | bytes 204000000 | tf_op jit(solution)/shard_map/pallas_call | solution.py:713
  776.4 5.8 collective-permute-start.2
  (347 shorter events, 129.4 us)
Async XLA Ops:
  116.2 486.5 %copy-start = (f32[2048,256]{1,0:T(8,128)}, f32[2048,256]{1,0:T(8,128)S(1)}, u32[]{:S(2)}) copy-start(f32[2048,256]{1,0:T(8,128)S(1)} %get-tuple-element.180.act_ref) | copy-start | bytes 6291460
  123.0 37.8 %copy-start.40 = (f32[2,128,2048]{2,1,0:T(8,128)S(1)}, f32[2,128,2048]{2,1,0:T(8,128)}, u32[]{:S(2)}) copy-start(f32[2,128,2048]{2,1,0:T(8,128)} %param.12) | copy-start | bytes 6291460
  123.0 38.8 %copy-start.87 = (bf16[304,256]{1,0:T(8,128)(2,1)S(1)}, bf16[304,256]{1,0:T(8,128)(2,1)}, u32[]{:S(2)}) copy-start(bf16[304,256]{1,0:T(8,128)(2,1)} %get-tuple-element.98) | copy-start | bytes 466948
  157.6 29.9 %collective-permute-start = (bf16[256,2048]{1,0:T(8,128)(2,1)}, bf16[256,2048]{1,0:T(8,128)(2,1)S(1)}, u32[]{:S(2)}, u32[]{:S(2)}) collective-permute-start(bf16[256,2048]{1,0:T(8,128)(2,1)} %get-tuple-element.97), channel_id=1, source_target_pairs={{0,8},{24,16},{1,9},{25,17},{2,10},{26,18},{3,11},{27,19},{4,12},{... | collective-permute-start | bytes 3145736 | tf_op jit(solution)/shard_map/ppermute | solution.py:897
  188.6 44.3 %copy-start.59 = (bf16[304,256]{1,0:T(8,128)(2,1)S(1)}, bf16[304,256]{1,0:T(8,128)(2,1)}, u32[]{:S(2)}) copy-start(bf16[304,256]{1,0:T(8,128)(2,1)} %broadcast_select_fusion.14.refs_2_) | copy-start | bytes 466948
  315.8 65.9 %copy-start.2 = (f32[2048,256]{1,0:T(8,128)}, f32[2048,256]{1,0:T(8,128)S(1)}, u32[]{:S(2)}) copy-start(f32[2048,256]{1,0:T(8,128)S(1)} %get-tuple-element.176.act_ref) | copy-start | bytes 6291460
  351.2 30.3 %collective-permute-start.1 = (bf16[256,2048]{1,0:T(8,128)(2,1)}, bf16[256,2048]{1,0:T(8,128)(2,1)S(1)}, u32[]{:S(2)}, u32[]{:S(2)}) collective-permute-start(bf16[256,2048]{1,0:T(8,128)(2,1)} %get-tuple-element.110), channel_id=1, source_target_pairs={{0,8},{24,16},{1,9},{25,17},{2,10},{26,18},{3,11},{27,19},{4,12},{... | collective-permute-start | bytes 3145736 | tf_op jit(solution)/shard_map/ppermute | solution.py:897
  394.6 52.9 %copy-start.55 = (f32[2048,256]{1,0:T(8,128)S(1)}, f32[2048,256]{1,0:T(8,128)}, u32[]{:S(2)}) copy-start(f32[2048,256]{1,0:T(8,128)} %get-tuple-element.239) | copy-start | bytes 6291460
  452.4 26.4 %copy-start.3 = (f32[2048,256]{1,0:T(8,128)S(1)}, f32[2048,256]{1,0:T(8,128)}, u32[]{:S(2)}) copy-start(f32[2048,256]{1,0:T(8,128)} %copy-done.2) | copy-start | bytes 6291460
  453.6 27.5 %copy-start.50 = (f32[2048,256]{1,0:T(8,128)S(1)}, f32[2048,256]{1,0:T(8,128)}, u32[]{:S(2)}) copy-start(f32[2048,256]{1,0:T(8,128)} %get-tuple-element.177) | copy-start | bytes 6291460
  495.5 51.4 %copy-start.41 = (f32[2,128,2048]{2,1,0:T(8,128)S(1)}, f32[2,128,2048]{2,1,0:T(8,128)}, u32[]{:S(2)}) copy-start(f32[2,128,2048]{2,1,0:T(8,128)} %param.12) | copy-start | bytes 6291460
  495.5 51.4 %copy-start.57 = (bf16[128,2048]{1,0:T(8,128)(2,1)S(1)}, bf16[128,2048]{1,0:T(8,128)(2,1)}, u32[]{:S(2)}) copy-start(bf16[128,2048]{1,0:T(8,128)(2,1)} %get-tuple-element.101) | copy-start | bytes 1572868
  611.5 32.6 %copy-start.54 = (f32[2048,256]{1,0:T(8,128)S(1)}, f32[2048,256]{1,0:T(8,128)}, u32[]{:S(2)}) copy-start(f32[2048,256]{1,0:T(8,128)} %get-tuple-element.235) | copy-start | bytes 6291460
  649.9 47.7 %copy-start.106 = (bf16[2048,256]{1,0:T(8,128)(2,1)S(1)}, bf16[2048,256]{1,0:T(8,128)(2,1)}, u32[]{:S(2)}) copy-start(bf16[2048,256]{1,0:T(8,128)(2,1)} %get-tuple-element.243) | copy-start | bytes 3145732
  650.8 46.7 %copy-start.101 = (f32[2048,256]{1,0:T(8,128)S(1)}, f32[2048,256]{1,0:T(8,128)}, u32[]{:S(2)}) copy-start(f32[2048,256]{1,0:T(8,128)} %get-tuple-element.132) | copy-start | bytes 6291460
  652.0 43.9 %copy-start.1 = (f32[2048,256]{1,0:T(8,128)S(1)}, f32[2048,256]{1,0:T(8,128)}, u32[]{:S(2)}) copy-start(f32[2048,256]{1,0:T(8,128)} %copy-done) | copy-start | bytes 6291460
  652.0 45.5 %copy-start.105 = (bf16[2048,256]{1,0:T(8,128)(2,1)S(1)}, bf16[2048,256]{1,0:T(8,128)(2,1)}, u32[]{:S(2)}) copy-start(bf16[2048,256]{1,0:T(8,128)(2,1)} %get-tuple-element.237) | copy-start | bytes 3145732
  715.2 58.5 %copy-start.92 = (f32[1,2,8,1,128]{4,3,2,1,0:T(1,128)S(1)}, f32[1,2,8,1,128]{4,3,2,1,0:T(1,128)}, u32[]{:S(2)}) copy-start(f32[1,2,8,1,128]{4,3,2,1,0:T(1,128)} %copy-done.91) | copy-start | bytes 24580
  715.2 60.1 %copy-start.27 = (bf16[128,2048]{1,0:T(8,128)(2,1)S(1)}, bf16[128,2048]{1,0:T(8,128)(2,1)}, u32[]{:S(2)}) copy-start(bf16[128,2048]{1,0:T(8,128)(2,1)} %fusion.44.refs_0_.refs_2_.refs_15_) | copy-start | bytes 1572868
  715.2 60.1 %copy-start.98 = (f32[128]{0:T(128)S(1)}, f32[128]{0:T(128)}, u32[]{:S(2)}) copy-start(f32[128]{0:T(128)} %copy-done.97) | copy-start | bytes 1540
  715.2 60.1 %copy-start.100 = (f32[128]{0:T(128)S(1)}, f32[128]{0:T(128)}, u32[]{:S(2)}) copy-start(f32[128]{0:T(128)} %get-tuple-element.230) | copy-start | bytes 1540
  775.7 23.0 %collective-permute-start.3 = (bf16[128,2048]{1,0:T(8,128)(2,1)S(1)}, bf16[128,2048]{1,0:T(8,128)(2,1)S(1)}, u32[]{:S(2)}, u32[]{:S(2)}) collective-permute-start(bf16[128,2048]{1,0:T(8,128)(2,1)S(1)} %fusion.36), channel_id=1, source_target_pairs={{8,0},{24,8},{9,1},{25,9},{10,2},{26,10},{11,3},{27,11},{12,4},{28... | collective-permute-start | bytes 1572872 | tf_op jit(solution)/shard_map/ppermute | solution.py:1164
  776.4 22.2 %collective-permute-start.2 = (bf16[128,2048]{1,0:T(8,128)(2,1)S(1)}, bf16[128,2048]{1,0:T(8,128)(2,1)S(1)}, u32[]{:S(2)}, u32[]{:S(2)}) collective-permute-start(bf16[128,2048]{1,0:T(8,128)(2,1)S(1)} %fusion.36), channel_id=1, source_target_pairs={{16,8},{17,9},{18,10},{19,11},{20,12},{21,13},{22,14},{23,15}} | collective-permute-start | bytes 1572872 | tf_op jit(solution)/shard_map/ppermute | solution.py:1163
  782.3 12.8 %collective-permute-start.4 = (bf16[304,256]{1,0:T(8,128)(2,1)S(1)}, bf16[304,256]{1,0:T(8,128)(2,1)}, u32[]{:S(2)}, u32[]{:S(2)}) collective-permute-start(bf16[304,256]{1,0:T(8,128)(2,1)S(1)} %add_convert_fusion.4), channel_id=1, source_target_pairs={{24,8},{25,9},{26,10},{27,11},{28,12},{29,13},{30,14},{31,15}} | collective-permute-start | bytes 466952 | tf_op jit(solution)/shard_map/ppermute | solution.py:1157
  (98 other events, 545.2 us)

commit v5 on v4

--- a/solution.py
+++ b/solution.py
@@ -365,17 +365,14 @@
     return [array for _, array in riders], shapes, [sems] * (2 * len(riders))
 
 
-def gather_kernel(bits, total, layer, kinds, shares, *refs):
+def gather_kernel(bits, total, kinds, shares, *refs):
     here = Place(bits)
     n, s, count = here.n, here.s, here.count
-    q, chip = lax.axis_index("q"), here.other(0)
-    along, own_count = len(kinds), total + (0 if layer is None else 3)
-    inputs, refs = refs[: own_count + along], refs[own_count + along :]
-    outputs, sems = refs[: own_count + along], refs[own_count + along :]
-    given, made = inputs[:own_count], outputs[:own_count]
-    ride_start, ride_end = ride(
-        here, kinds, inputs[own_count:] + outputs[own_count:] + sems[len(sems) - 2 * along :]
-    )
+    chip, along = here.other(0), len(kinds)
+    inputs, refs = refs[: total + along], refs[total + along :]
+    outputs, sems = refs[: total + along], refs[total + along :]
+    given, made = inputs[:total], outputs[:total]
+    ride_start, ride_end = ride(here, kinds, inputs[total:] + outputs[total:] + sems[len(sems) - 2 * along :])
     local_sem, send, recv, core_send, core_recv = sems[:5]
     spans = spans_of(given[0].shape[1], n, shares)
     parts = [(k, p) for k in range(total) for p in range(n) if spans[p][1]]
@@ -397,52 +394,7 @@
         sems = core_send.at[k, p, m], core_recv.at[k, p, m]
         return remote(source(k, held, p), block(k, held, p, s), *sems, {"section": 1 - s})
 
-    if layer is None:
-        here.meet([here.names(2**d) for d in range(n)] + [("section",)] + rider_peers(here, kinds))
-    else:
-        blocks, small = given[total : total + 2], given[total + 2]
-        rows, own_small = made[total : total + 2], made[total + 2]
-        lands = [rows[i].at[q, chip] for i in range(2)]
-        piece_send, piece_recv, q_send, q_recv, small_send, small_recv = sems[5:11]
-        peers = [here.names(e) + extra for e in range(count) for extra in ((), ("section",)) if e or extra]
-        here.meet(peers + [("q",), ("q", "section")])
-
-        def piece(i, r, e):
-            where = dict(here.toward(e), **({"section": 1 - s} if r else {}))
-            src = blocks[i].at[1 - s if r else s, here.other(e)]
-            return remote(src, lands[i], piece_send.at[i, r, e], piece_recv.at[i, e], where)
-
-        def pass_on(i, e):
-            place = rows[i].at[q, here.other(e)]
-            return remote(place, place, q_send.at[i, e], q_recv.at[i, e], {"q": 1 - q})
-
-        def hand_small(k, where):
-            return remote(small, own_small, small_send.at[k], small_recv, where)
-
-        keep_pieces = [pltpu.make_async_copy(blocks[i].at[s, chip], lands[i], piece_recv.at[i, 0]) for i in range(2)]
-        keep_small = pltpu.make_async_copy(small, own_small, small_recv)
-        at_layer = s == layer
-        stays, leaves = jnp.logical_and(at_layer, q == s), jnp.logical_and(at_layer, q != s)
-
-        @pl.when(at_layer)
-        def _():
-            for i in range(2):
-                keep_pieces[i].start()
-                for e in range(count):
-                    for r in range(2):
-                        if e or r:
-                            piece(i, r, e).start()
-
-        @pl.when(stays)
-        def _():
-            keep_small.start()
-            hand_small(0, {"q": 1 - q}).start()
-
-        @pl.when(leaves)
-        def _():
-            hand_small(0, {"section": 1 - s}).start()
-            hand_small(1, {"section": 1 - s, "q": 1 - q}).start()
-
+    here.meet([here.names(2**d) for d in range(n)] + [("section",)] + rider_peers(here, kinds))
     own = [pltpu.make_async_copy(given[k], made[k].at[s, chip], local_sem.at[k]) for k in range(total)]
     for k in range(total):
         for t in range(n):
@@ -454,10 +406,6 @@
     for k, p in parts:
         core(k, p, 0).start()
     for m in range(1, count):
-        if layer is not None and m < 3:
-            for e in range(count):
-                arrived(rows[m - 1].at[q, here.other(e)], piece_recv.at[m - 1, e])
-                pass_on(m - 1, e).start()
         for k, p in parts:
             arrived(block(k, here.dims(p, m), p, s), recv.at[k, p, m])
             for t in range(m.bit_length(), n):
@@ -474,30 +422,9 @@
             if m:
                 deliver(k, p, m).wait_send()
     ride_end()
-    if layer is not None:
-        arrived(own_small, small_recv)
-        for i in range(2):
-            for e in range(count):
-                arrived(rows[i].at[1 - q, here.other(e)], q_recv.at[i, e])
-                pass_on(i, e).wait_send()
-
-        @pl.when(at_layer)
-        def _():
-            for i in range(2):
-                for e in range(count):
-                    for r in range(2):
-                        if e or r:
-                            piece(i, r, e).wait_send()
-
-        pl.when(stays)(lambda: hand_small(0, {"q": 1 - q}).wait_send())
-
-        @pl.when(leaves)
-        def _():
-            hand_small(0, {"section": 1 - s}).wait_send()
-            hand_small(1, {"section": 1 - s, "q": 1 - q}).wait_send()
-
-
-def gather_call(bits, cid, shards, layer=None, extras=(), riders=(), shares=None, us=35):
+
+
+def gather_call(bits, cid, shards, riders=(), shares=None, us=35):
     rows, width = shards[0].shape
     n = len(bits)
     count = 2**n
@@ -505,20 +432,17 @@
     sems = dma((len(shards), n, count))
     shapes = [jax.ShapeDtypeStruct((2, count, rows, width), shard.dtype) for shard in shards]
     scratch = [dma((len(shards),)), sems, sems, sems, sems]
-    if layer is not None:
-        shapes += [jax.ShapeDtypeStruct(extra.shape, extra.dtype) for extra in extras]
-        scratch += [dma((2, 2, count)), dma((2, count)), dma((2, count)), dma((2, count)), dma((2,)), dma]
     arrays, more_shapes, more_scratch = rider_shapes(bits, riders)
     shapes += more_shapes
     out = pl.pallas_call(
-        functools.partial(gather_kernel, bits, len(shards), layer, tuple(kind for kind, _ in riders), shares),
+        functools.partial(gather_kernel, bits, len(shards), tuple(kind for kind, _ in riders), shares),
         out_shape=shapes,
         in_specs=[pl.BlockSpec(memory_space=pl.ANY)] * len(shapes),
         out_specs=[pl.BlockSpec(memory_space=pl.ANY)] * len(shapes),
         scratch_shapes=scratch + more_scratch,
         compiler_params=pltpu.CompilerParams(collective_id=cid, has_side_effects=True),
         cost_estimate=lasting(us),
-    )(*shards, *extras, *arrays)
+    )(*shards, *arrays)
     return [o.reshape((-1, width)) for o in out[: len(shards)]] + list(out[len(shards) :])
 
 
@@ -640,7 +564,8 @@
     rider_out, refs = refs[:along], refs[along:]
     work = Scatter(here, turned, shares, a_refs, b_refs, out_ref, refs[:8])
     if homing:
-        q_in, ready, q_send, q_recv, home_send, home_recv, over_send, over_recv = refs[8:16]
+        q_in, ready, kept, kept_sem, q_send, q_recv, home_send, home_recv, over_send, over_recv = refs[8:18]
+        keep = pltpu.make_async_copy(grad.at[lax.axis_index("q")], kept, kept_sem)
     ride_start, ride_end = ride(here, kinds, rider_in + rider_out + refs[len(refs) - 2 * along :])
 
     def to_q(e):
@@ -658,7 +583,7 @@
         chip = here.other(e)
         arrived(q_in.at[chip], q_recv.at[e])
         place = ready.at[chip] if e else home.at[chip]
-        add_rows(q_in.at[chip], [grad.at[lax.axis_index("q"), chip]], place)
+        add_rows(q_in.at[chip], [kept.at[chip]], place)
         (to_chip(e) if e else to_core(0)).start()
 
     def home_end(e):
@@ -673,8 +598,11 @@
     if homing:
         for e in range(count):
             to_q(e).start()
+        keep.start()
     ride_start()
     work.produce(0, count + 1)
+    if homing:
+        keep.wait()
     steps = count // 2
     for m in range(steps - 1, 0, -1):
         if homing:
@@ -707,7 +635,7 @@
     if grad is not None:
         operands += [grad]
         shapes += [jax.ShapeDtypeStruct(grad.shape[1:], BF)] * 2
-        scratch += [pltpu.VMEM(grad.shape[1:], BF)] * 2 + [dma((count,))] * 6
+        scratch += [pltpu.VMEM(grad.shape[1:], BF)] * 3 + [dma] + [dma((count,))] * 6
     arrays, more_shapes, more_scratch = rider_shapes(bits, riders)
     inside, outside = pl.BlockSpec(memory_space=pltpu.VMEM), pl.BlockSpec(memory_space=pl.ANY)
     return pl.pallas_call(
@@ -715,7 +643,7 @@
             scatter_kernel, bits, turned, grad is not None, tuple(kind for kind, _ in riders), shares, len(a)
         ),
         out_shape=shapes + more_shapes,
-        in_specs=[inside] * len(operands) + [outside] * len(arrays),
+        in_specs=[inside] * (2 * len(a)) + [outside] * (len(operands) - 2 * len(a) + len(arrays)),
         out_specs=[inside] * len(shapes) + [outside] * len(arrays),
         scratch_shapes=scratch + more_scratch,
         compiler_params=pltpu.CompilerParams(
@@ -826,21 +754,59 @@
     )(x, *arrays)
 
 
-def spread_kernel(bits, kinds, shard_ref, *refs):
+def spread_kernel(bits, kinds, shard_ref, inner_ref, gate_ref, small, *refs):
     here = Place(bits)
     along = len(kinds)
-    rider_in, out_ref, rider_out, refs = refs[:along], refs[along], refs[along + 1 : 2 * along + 1], refs[2 * along + 1 :]
-    send, recv, pair_send, pair_recv = refs[:4]
-    ride_start, ride_end = ride(here, kinds, rider_in + rider_out + refs[4:])
-    s, q, chip = here.s, lax.axis_index("q"), here.other(0)
-    others = range(1, here.count)
-    here.meet([here.names(e) for e in others] + [("section",), ("q",)])
+    blocks = inner_ref, gate_ref
+    rider_in, refs = refs[:along], refs[along:]
+    out_ref, rows, own_small, refs = refs[0], refs[1:3], refs[3], refs[4:]
+    rider_out, refs = refs[:along], refs[along:]
+    send, recv, pair_send, pair_recv, piece_send, piece_recv, small_send, small_recv = refs[:8]
+    ride_start, ride_end = ride(here, kinds, rider_in + rider_out + refs[8:])
+    s, q, chip, count = here.s, lax.axis_index("q"), here.other(0), here.count
+    others = range(1, count)
+    peers = [here.names(e) + extra for e in range(count) for extra in ((), ("section",)) if e or extra]
+    here.meet(peers + [("q",), ("q", "section")])
+
+    def piece(i, r, e):
+        where = dict(here.toward(e), **({"section": 1 - s} if r else {}))
+        src = blocks[i].at[1 - s if r else s, here.other(e)]
+        return remote(src, rows[i].at[chip], piece_send.at[i, r, e], piece_recv.at[i, e], where)
+
+    def hand_small(k, where):
+        return remote(small, own_small, small_send.at[k], small_recv, where)
+
+    keep_pieces = [pltpu.make_async_copy(blocks[i].at[s, chip], rows[i].at[chip], piece_recv.at[i, 0]) for i in range(2)]
+    keep_small = pltpu.make_async_copy(small, own_small, small_recv)
+    at_layer = s == 0
+    stays, leaves = jnp.logical_and(at_layer, q == s), jnp.logical_and(at_layer, q != s)
+
     out_ref[s, q, chip] = shard_ref[...]
     own = out_ref.at[s, q, chip]
     copies = [remote(own, own, send.at[e], recv.at[e], here.toward(e)) for e in others]
     for copy in copies:
         copy.start()
     ride_start()
+
+    @pl.when(at_layer)
+    def _():
+        for i in range(2):
+            keep_pieces[i].start()
+            for e in range(count):
+                for r in range(2):
+                    if e or r:
+                        piece(i, r, e).start()
+
+    @pl.when(stays)
+    def _():
+        keep_small.start()
+        hand_small(0, {"q": 1 - q}).start()
+
+    @pl.when(leaves)
+    def _():
+        hand_small(0, {"section": 1 - s}).start()
+        hand_small(1, {"section": 1 - s, "q": 1 - q}).start()
+
     for e in others:
         arrived(out_ref.at[s, q, here.other(e)], recv.at[e])
     place = out_ref.at[s, q]
@@ -852,26 +818,49 @@
     second.start()
     second.wait_recv()
     ride_end()
+    arrived(own_small, small_recv)
+    for i in range(2):
+        for e in range(count):
+            arrived(rows[i].at[here.other(e)], piece_recv.at[i, e])
     for copy in copies + [first, second]:
         copy.wait_send()
 
-
-def spread(bits, shard, riders):
+    @pl.when(at_layer)
+    def _():
+        for i in range(2):
+            for e in range(count):
+                for r in range(2):
+                    if e or r:
+                        piece(i, r, e).wait_send()
+
+    pl.when(stays)(lambda: hand_small(0, {"q": 1 - q}).wait_send())
+
+    @pl.when(leaves)
+    def _():
+        hand_small(0, {"section": 1 - s}).wait_send()
+        hand_small(1, {"section": 1 - s, "q": 1 - q}).wait_send()
+
+
+def spread(bits, shard, blocks, small, riders):
     arrays, more_shapes, more_scratch = rider_shapes(bits, riders)
-    outside = [pl.BlockSpec(memory_space=pl.ANY)] * len(arrays)
     width, count = shard.shape[0], 2 ** len(bits)
     block = (16, max(width, 128))
     padded = jnp.pad(shard[None, :], ((0, block[0] - 1), (0, block[1] - width)))
     dma = pltpu.SemaphoreType.DMA
+    shapes = [jax.ShapeDtypeStruct((2, 2, count) + block, shard.dtype)]
+    shapes += [jax.ShapeDtypeStruct(b.shape[1:], b.dtype) for b in blocks] + [jax.ShapeDtypeStruct(small.shape, small.dtype)]
+    inside, outside = pl.BlockSpec(memory_space=pltpu.VMEM), pl.BlockSpec(memory_space=pl.ANY)
     out, *gots = pl.pallas_call(
         functools.partial(spread_kernel, bits, tuple(kind for kind, _ in riders)),
-        out_shape=[jax.ShapeDtypeStruct((2, 2, count) + block, shard.dtype)] + more_shapes,
-        in_specs=[pl.BlockSpec(memory_space=pltpu.VMEM)] + outside,
-        out_specs=[pl.BlockSpec(memory_space=pltpu.VMEM)] + outside,
-        scratch_shapes=[dma((count,)), dma((count,)), dma((2,)), dma((2,))] + more_scratch,
+        out_shape=shapes + more_shapes,
+        in_specs=[inside] + [outside] * (3 + len(arrays)),
+        out_specs=[inside] + [outside] * (3 + len(arrays)),
+        scratch_shapes=[dma((count,)), dma((count,)), dma((2,)), dma((2,))]
+        + [dma((2, 2, count)), dma((2, count)), dma((2,)), dma]
+        + more_scratch,
         compiler_params=pltpu.CompilerParams(collective_id=0, has_side_effects=True),
         cost_estimate=lasting(12),
-    )(padded, *arrays)
+    )(padded, *blocks, small, *arrays)
     return [out[:, :, :, 0, :width].reshape((2, -1))] + gots
 
 
@@ -1056,14 +1045,14 @@
         return cross_dot(normed, d_out).astype(BF).reshape((2,) + blocks[0].shape[1:])
 
     mine, others = by_q(hidden_in)
-    gains, got = spread(bits, norm_gain[0], [("leave", others)])
+    gains, inner, gate, packed0, got = spread(bits, norm_gain[0], blocks, packed, [("leave", others)])
     gains = gains.astype(F32)
     stream0 = jnp.where(at_home(), mine, got).astype(F32)
 
     inverse0, normed = normalize(stream0, gains[0])
-    normed0, inner, gate, packed0, *sent = gather_call(
-        bits, 1, [normed], 0, (*blocks, packed), shares=tight, us=60,
-        riders=[("over_at", b) for b in blocks] + [("out1", packed)] + [("out%d" % l, out_weight[0]) for l in range(2)],
+    normed0, inner, gate, *sent = gather_call(
+        bits, 1, [normed], shares=tight, us=60,
+        riders=[("stack", inner), ("stack", gate)] + [("over_at", b) for b in blocks] + [("out1", packed)] + [("out%d" % l, out_weight[0]) for l in range(2)],
     )
     upper = lax.axis_index("section") == 1
     columns = [jnp.where(upper, b[1], got) for b, got in zip(blocks, sent)]
@@ -1077,9 +1066,11 @@
     out0 = jnp.where(at_home(), out_held[0], leave(after(out_held[0], xproj0)))
     kept0 = mixer(xproj0, act0, normed0, gate0, small0)
     grad_mine, grad_others = by_q(cotangent)
-    added, got, grad_got = scatter_dot(
-        bits, 8, [kept0[7]], [out0], False, riders=[("leave", packed_held), ("leave", grad_others.astype(BF))]
-    )
+    added, got, grad_got, gate = scatter_dot(
+        bits, 8, [kept0[7]], [out0], False, shares=(3, 5, 8),
+        riders=[("leave", packed_held), ("leave", grad_others.astype(BF)), ("stack", late_gate)],
+    )
+    gate1 = weight(gate)
     grad1 = jnp.where(at_home(), grad_mine, grad_got.astype(F32))
     small1 = Small(jnp.where(at_home(), packed_held, got))
     output0 = (stream0 + added).astype(BF)
@@ -1091,12 +1082,11 @@
     )
     inner1 = weight(inner)
     extended1, conv1, act1, part = mixer_inputs(normed1, inner1, small1)
-    xproj1, gate = sum_columns(bits, 5, after(part, out_held[1]), [("stack", late_gate)])
-    gate1 = weight(gate)
+    (xproj1,) = sum_columns(bits, 5, after(part, out_held[1]))
     out1 = jnp.where(at_home(), out_held[1], leave(after(out_held[1], xproj1)))
     kept1 = mixer(xproj1, act1, normed1, gate1, small1)
 
-    d_out1 = cross_dot(kept1[7], grad_low1)
+    d_out1 = cross_dot(kept1[7], grad_low1).astype(BF)
     d_recur, d_gate1 = gate_back(grad_low1, out1, kept1)
     keep, give = by_q(weight_grad(normed1, d_gate1))
     beside = kept1[7].shape[0] * out1.shape[1] <= 2**22 and kept1[7].shape[0] >= 16 * BLOCK
@@ -1114,7 +1104,7 @@
     d_packed1 = pack(d_conv, d_small, d_xproj_weight)
     d_normed, d_gate_in1, d_packed1_home, d_out1_home = scatter_dot(
         bits, 11, [d_inner, d_gate1], [inner1, gate1], True,
-        riders=[("cube", d_gate_in1), ("home", d_packed1.astype(BF)), ("home", d_out1.astype(BF))], shares=(4, 5, 7),
+        riders=[("cube", d_gate_in1), ("home", d_packed1.astype(BF)), ("home", d_out1)], shares=(4, 5, 7),
     )
     keep, give = by_q(weight_grad(normed1, d_inner))
     input_grad1 = norm_back(grad1, d_normed, stream1, inverse1, gains[1])
@@ -1124,18 +1114,20 @@
     )
     d_inner1 = (keep.astype(F32) + got.astype(F32)).astype(BF)
 
-    d_out0 = cross_dot(kept0[7], grad_low0)
+    d_out0 = cross_dot(kept0[7], grad_low0).astype(BF)
     d_recur, d_gate0 = gate_back(grad_low0, out0, kept0)
     keep, give = by_q(weight_grad(normed0, d_gate0))
-    d_act_rec, part, d_small, (got,) = mixer_back(bits, 17, d_recur, act0, xproj0, kept0, small0, [("swap", give)])
+    d_act_rec, part, d_small, (got, d_inner1) = mixer_back(
+        bits, 17, d_recur, act0, xproj0, kept0, small0, [("swap", give), ("cube", d_inner1)]
+    )
     d_gate_in0 = (keep.astype(F32) + got.astype(F32)).astype(BF)
-    d_xproj, d_gate_in0, d_inner1, d_out0_home = sum_columns(
-        bits, 7, part, [("cube", d_gate_in0), ("cube", d_inner1), ("home", d_out0.astype(BF))]
+    d_xproj, d_gate_in0, d_out0_home = sum_columns(
+        bits, 7, part, [("cube", d_gate_in0), ("home", d_out0)]
     )
     d_inner, d_conv, d_xproj_weight = inputs_back(d_xproj, d_recur, d_act_rec, extended0, conv0, act0, small0)
     d_packed0 = pack(d_conv, d_small, d_xproj_weight)
     d_out = [
-        (mine + other.astype(F32)).astype(BF) for mine, other in ((d_out0, d_out0_home), (d_out1, d_out1_home))
+        (mine.astype(F32) + other.astype(F32)).astype(BF) for mine, other in ((d_out0, d_out0_home), (d_out1, d_out1_home))
     ]
     d_packed1 = (d_packed1 + d_packed1_home.astype(F32)).astype(BF)
     gate_over = jnp.where(upper, d_gate_in0, d_gate_in1)

time: 811 us -> 793 us (0.978)
  Pallas kernels: 618 us -> 599 us
    pallas_call x4, Pallas kernels: 136 us -> 115 us  [sum_columns(): pl.pallas_call(functools.partial(total_kernel, bits, tuple((kind for kind...]
    pallas_call x3, Pallas kernels: 189 us -> 170 us  [gather_call(): pl.pallas_call(functools.partial(gather_kernel, bits, len(shards), tuple(...]
    pallas_call x1, Pallas kernels: 14.7 us -> 29.2 us  [spread(): pl.pallas_call(functools.partial(spread_kernel, bits, tuple((kind for kin...]
where the time goes in v5:
time: 793 us; the launch traced here: 783 us
  Pallas kernels  599 us (76%)
  matrix products  79.6 us (10%)
  other arithmetic  65.4 us (8%)
  local copies, waits for them, and re-layouts  25.7 us (3%)
  starting transfers between devices  11.7 us (1%)
    pallas_call x3, Pallas kernels, gather_call(): pl.pallas_call(functools.partial(gather_kernel, bits, len(shards), tuple(...  170 us
    pallas_call x3, Pallas kernels, scatter_columns(): pl.pallas_call(functools.partial(scatter_kernel, bits, turned, grad is no...  160 us
    pallas_call x4, Pallas kernels, sum_columns(): pl.pallas_call(functools.partial(total_kernel, bits, tuple((kind for kind...  115 us
    pallas_call x2, Pallas kernels, recur_backward(): pl.pallas_call(functools.partial(recur_backward_kernel, bits, tuple((kind...  84.7 us
    dot_general x10, matrix products, cross_dot(): lax.dot_general(operand, factor, (((0,), (0,)), ((), ())), preferred_elem...  36.7 us
    pallas_call x2, Pallas kernels, recur_forward(): pl.pallas_call(recur_forward_kernel, grid=(tokens // BLOCK,), in_specs=[r...  36.5 us
    pallas_call x1, Pallas kernels, spread(): pl.pallas_call(functools.partial(spread_kernel, bits, tuple((kind for kin...  29.2 us
    dot_general x8, matrix products, forward_dot(): return jnp.dot(operand, factor, preferred_element_type=F32)  27.2 us
  transfers between devices with their start and end apart: 5, of which 0 were waited for; matrix products, arithmetic and copies ran while one was open for 4% of the time, Pallas kernels for 5%

profile of v5, /device:TPU:9, one launch (start us, length us, event | category | flops | bytes accessed | tf_op | source)
XLA Modules:
  0.0 783.3 jit_solution(11147470957994960632)
XLA Ops:
  14.5 29.2 %shard_map.194 = (bf16[2,2,8,16,128]{4,3,2,1,0:T(8,128)(2,1)}, bf16[8,128,256]{2,1,0:T(8,128)(2,1)}, bf16[8,128,256]{2,1,0:T(8,128)(2,1)}, bf16[304,256]{1,0:T(8,128)(2,1)}, bf16[128,2048]{1,0:T(8,128)(2,1)}) custom-call(bf16[16,128]{1,0:T(8,128)(2,1)} %pad.19.shard_ref, bf16[2,8,128,256]{3,2,1,0:T(8,128)(2,1)} %bitcast.152, ...), custom_call_target="tpu_custom_call" | custom-call | bytes 40800000 | tf_op jit(solution)/shard_map/pallas_call | solution.py:853
  49.0 52.8 %shard_map.195 = (bf16[2,8,128,2048]{3,2,1,0:T(8,128)(2,1)}, bf16[2,8,128,256]{3,2,1,0:T(8,128)(2,1)}, bf16[2,8,128,256]{3,2,1,0:T(8,128)(2,1)}, bf16[8,128,256]...) custom-call(bf16[128,2048]{1,0:T(8,128)(2,1)} %fusion.32.refs_0_, ...), custom_call_target="tpu_custom_call" | custom-call | bytes 204000000 | tf_op jit(solution)/shard_map/pallas_call | solution.py:437
  101.8 6.1 fusion.9
  117.0 29.7 %shard_map.196 = (bf16[160,2048]{1,0:T(8,128)(2,1)}, bf16[8,128,256]{2,1,0:T(8,128)(2,1)}, bf16[8,128,256]{2,1,0:T(8,128)(2,1)}) custom-call(f32[160,2048]{1,0:T(8,128)} %fusion.67.x_ref, bf16[8,128,256]{2,1,0:T(8,128)(2,1)} %get-tuple-element.245.refs_0_, bf16[8,128,256]{2,1,0:T(8,128)(2,1)} %get-tuple-element.244.refs_1_), custom_call_target="tpu_custom_call" | custom-call | bytes 74800000 | tf_op jit(solution)/shard_map/pallas_call | solution.py:735
  153.8 18.4 %shard_map.197 = (f32[2048,256]{1,0:T(8,128)S(1)}, f32[2048,16,256]{2,1,0:T(8,128)}, f32[16,256]{1,0:T(8,128)S(1)}) custom-call(f32[2048,256]{1,0:T(8,128)S(1)} %get-tuple-element.236.rate_ref, f32[2048,256]{1,0:T(8,128)S(1)} %get-tuple-element.182.act_ref, f32[16,2048]{1,0:T(8,128)S(1)} %get-tuple-element.212.key_ref, ...), custom_call_target="tpu_custom_call" | custom-call | bytes 3400000 | tf_op jit(solution)/shard_map/pallas_call | solution.py:98
  172.3 4.1 multiply_convert_fusion.1
  177.6 50.3 %shard_map.198 = (f32[128,2048]{1,0:T(8,128)}, bf16[304,256]{1,0:T(8,128)(2,1)}, bf16[128,2048]{1,0:T(8,128)(2,1)}, bf16[2,8,128,256]{3,2,1,0:T(8,128)(2,1)}) custom-call(bf16[2048,256]{1,0:T(8,128)(2,1)} %get-tuple-element.238.refs_0_, bf16[256,2048]{1,0:T(8,128)(2,1)} %broadcast_select_fusion.1.refs_1_, bf16[304,256]{1,0:T(8,128)(2,1)} %broadcast_select_fusion.14.refs_2_, ...), custom_call_target="tpu_custom_call" | custom-call | bytes 136000000 | tf_op jit(solution)/shard_map/pallas_call | solution.py:641
  232.4 71.4 %shard_map.199 = (bf16[2,8,128,2048]{3,2,1,0:T(8,128)(2,1)}, bf16[2,8,128,2048]{3,2,1,0:T(8,128)(2,1)}, bf16[2,8,128,256]{3,2,1,0:T(8,128)(2,1)}, bf16[128,2048]{1,0:T(8,128)(2,1)}) custom-call(bf16[128,2048]{1,0:T(8,128)(2,1)} %fusion.40.refs_0_, bf16[128,2048]{1,0:T(8,128)(2,1)} %fusion.83.refs_1_, bf16[8,128,256]{2,1,0:T(8,128)(2,1)} %get-tuple-element.106.refs_2_, ...), custom_call_target="tpu_custom_call" | custom-call | bytes 221000000 | tf_op jit(solution)/shard_map/pallas_call | solution.py:437
  303.8 6.0 fusion.8
  313.9 25.1 %shard_map.200 = bf16[160,2048]{1,0:T(8,128)(2,1)} custom-call(f32[160,2048]{1,0:T(8,128)} %fusion.63.x_ref), custom_call_target="tpu_custom_call" | custom-call | bytes 74800000 | tf_op jit(solution)/shard_map/pallas_call | solution.py:735
  346.2 18.1 %shard_map.201 = (f32[2048,256]{1,0:T(8,128)S(1)}, f32[2048,16,256]{2,1,0:T(8,128)}, f32[16,256]{1,0:T(8,128)S(1)}) custom-call(f32[2048,256]{1,0:T(8,128)S(1)} %get-tuple-element.240.rate_ref, f32[2048,256]{1,0:T(8,128)S(1)} %get-tuple-element.178.act_ref, f32[16,2048]{1,0:T(8,128)S(1)} %get-tuple-element.210.key_ref, ...), custom_call_target="tpu_custom_call" | custom-call | bytes 3400000 | tf_op jit(solution)/shard_map/pallas_call | solution.py:98
  364.3 5.9 convolution_convert_fusion.7
  370.4 5.2 fusion.11
  382.5 48.9 %shard_map.202 = (f32[2048,256]{1,0:T(8,128)}, f32[2048,256]{1,0:T(8,128)}, f32[16,2048]{1,0:T(8,128)}, f32[16,2048]{1,0:T(8,128)}, f32[128,2048]{1,0:T(8,128)}, /*index=5*/bf16[8,128,256]{2,1,0:T(8,128)(2,1)}) custom-call(f32[2048,256]{1,0:T(8,128)} %copy-done.6, f32[2048,256]{1,0:T(8,128)} %copy-done.2, f32[2048,256]{1,0:T(8,128)} %get-tuple-element.198.grad_ref, ...), custom_call_target="tpu_custom_call" | custom-call | bytes 3400000 | tf_op jit(solution)/shard_map/pallas_call | solution.py:221
  437.9 25.3 %shard_map.203 = (bf16[160,2048]{1,0:T(8,128)(2,1)}, bf16[128,2048]{1,0:T(8,128)(2,1)}) custom-call(f32[160,2048]{1,0:T(8,128)} %pad_maximum_fusion.x_ref, bf16[128,2048]{1,0:T(8,128)(2,1)} %fusion.41.refs_0_.refs_13_), custom_call_target="tpu_custom_call" | custom-call | bytes 74800000 | tf_op jit(solution)/shard_map/pallas_call | solution.py:735
  480.2 49.9 %shard_map.204 = (f32[128,2048]{1,0:T(8,128)}, bf16[8,128,256]{2,1,0:T(8,128)(2,1)}, bf16[304,256]{1,0:T(8,128)(2,1)}, bf16[256,2048]{1,0:T(8,128)(2,1)}) custom-call(bf16[2048,256]{1,0:T(8,128)(2,1)} %copy-done.48, bf16[2048,256]{1,0:T(8,128)(2,1)} %copy-done.68, bf16[2048,256]{1,0:T(8,128)(2,1)} %bitcast.172, bf16[2048,256]{1,0:T(8,128)(2,1)} %bitcast.169, ...), custom_call_target="tpu_custom_call" | custom-call | bytes 136000000 | tf_op jit(solution)/shard_map/pallas_call | solution.py:641
  533.0 46.2 %shard_map.205 = (bf16[2,8,128,2048]{3,2,1,0:T(8,128)(2,1)}, bf16[8,128,256]{2,1,0:T(8,128)(2,1)}, bf16[128,2048]{1,0:T(8,128)(2,1)}) custom-call(bf16[128,2048]{1,0:T(8,128)(2,1)} %fusion.44.refs_0_.refs_2_.refs_15_, bf16[8,128,256]{2,1,0:T(8,128)(2,1)} %bitcast.162, bf16[128,2048]{1,0:T(8,128)(2,1)} %fusion.44.refs_0_.refs_2_.refs_15_), custom_call_target="tpu_custom_call" | custom-call | bytes 153000000 | tf_op jit(solution)/shard_map/pallas_call | solution.py:437
  579.2 7.2 convolution_convert_fusion.1.refs_1_
  586.4 6.5 multiply_reduce_fusion
  597.9 35.8 %shard_map.206 = (f32[2048,256]{1,0:T(8,128)}, f32[2048,256]{1,0:T(8,128)}, f32[16,2048]{1,0:T(8,128)}, f32[16,2048]{1,0:T(8,128)}, bf16[8,128,256]{2,1,0:T(8,128)(2,1)}, /*index=5*/bf16[8,128,256]{2,1,0:T(8,128)(2,1)}) custom-call(f32[2048,256]{1,0:T(8,128)} %copy-done.5, f32[2048,256]{1,0:T(8,128)} %copy-done, f32[2048,256]{1,0:T(8,128)} %get-tuple-element.195.grad_ref, ...), custom_call_target="tpu_custom_call" | custom-call | bytes 3400000 | tf_op jit(solution)/shard_map/pallas_call | solution.py:221
  641.6 35.2 %shard_map.207 = (bf16[160,2048]{1,0:T(8,128)(2,1)}, bf16[8,128,256]{2,1,0:T(8,128)(2,1)}, bf16[256,2048]{1,0:T(8,128)(2,1)}) custom-call(f32[160,2048]{1,0:T(8,128)} %pad_maximum_fusion.1.x_ref, bf16[8,128,256]{2,1,0:T(8,128)(2,1)} %fusion.47.refs_0_, bf16[256,2048]{1,0:T(8,128)(2,1)} %convolution_convert_fusion.1.refs_1_), custom_call_target="tpu_custom_call" | custom-call | bytes 74800000 | tf_op jit(solution)/shard_map/pallas_call | solution.py:735
  684.0 6.9 convolution_convert_fusion
  693.1 59.6 %shard_map.208 = (f32[128,2048]{1,0:T(8,128)}, bf16[8,128,256]{2,1,0:T(8,128)(2,1)}, bf16[8,128,256]{2,1,0:T(8,128)(2,1)}, bf16[304,256]{1,0:T(8,128)(2,1)}, bf1...) custom-call(bf16[2048,256]{1,0:T(8,128)(2,1)} %copy-done.43, ...), custom_call_target="tpu_custom_call" | custom-call | bytes 204000000 | tf_op jit(solution)/shard_map/pallas_call | solution.py:641
  757.1 5.8 collective-permute-start.2
  (341 shorter events, 131.3 us)
Async XLA Ops:
  47.2 54.6 %copy-start.97 = (f32[128]{0:T(128)}, f32[128]{0:T(128)S(1)}, u32[]{:S(2)}) copy-start(f32[128]{0:T(128)S(1)} %get-tuple-element.233) | copy-start | bytes 1540
  48.0 53.8 %copy-start.91 = (f32[1,2,8,1,128]{4,3,2,1,0:T(1,128)}, f32[1,2,8,1,128]{4,3,2,1,0:T(1,128)S(1)}, u32[]{:S(2)}) copy-start(f32[1,2,8,1,128]{4,3,2,1,0:T(1,128)S(1)} %get-tuple-element.223) | copy-start | bytes 24580
  110.6 475.8 %copy-start = (f32[2048,256]{1,0:T(8,128)}, f32[2048,256]{1,0:T(8,128)S(1)}, u32[]{:S(2)}) copy-start(f32[2048,256]{1,0:T(8,128)S(1)} %get-tuple-element.182.act_ref) | copy-start | bytes 6291460
  117.0 32.9 %copy-start.37 = (f32[2,128,2048]{2,1,0:T(8,128)S(1)}, f32[2,128,2048]{2,1,0:T(8,128)}, u32[]{:S(2)}) copy-start(f32[2,128,2048]{2,1,0:T(8,128)} %param.12) | copy-start | bytes 6291460
  117.0 33.8 %copy-start.87 = (bf16[304,256]{1,0:T(8,128)(2,1)S(1)}, bf16[304,256]{1,0:T(8,128)(2,1)}, u32[]{:S(2)}) copy-start(bf16[304,256]{1,0:T(8,128)(2,1)} %get-tuple-element.101) | copy-start | bytes 466948
  146.6 29.8 %collective-permute-start = (bf16[256,2048]{1,0:T(8,128)(2,1)S(1)}, bf16[256,2048]{1,0:T(8,128)(2,1)S(1)}, u32[]{:S(2)}, u32[]{:S(2)}) collective-permute-start(bf16[256,2048]{1,0:T(8,128)(2,1)S(1)} %get-tuple-element.100), channel_id=1, source_target_pairs={{0,8},{24,16},{1,9},{25,17},{2,10},{26,18},{3,11},{27,19},{4,12},{... | collective-permute-start | bytes 3145736 | tf_op jit(solution)/shard_map/ppermute | solution.py:886
  177.6 50.3 %copy-start.60 = (bf16[304,256]{1,0:T(8,128)(2,1)S(1)}, bf16[304,256]{1,0:T(8,128)(2,1)}, u32[]{:S(2)}) copy-start(bf16[304,256]{1,0:T(8,128)(2,1)} %broadcast_select_fusion.14.refs_2_) | copy-start | bytes 466948
  312.4 57.9 %copy-start.2 = (f32[2048,256]{1,0:T(8,128)}, f32[2048,256]{1,0:T(8,128)S(1)}, u32[]{:S(2)}) copy-start(f32[2048,256]{1,0:T(8,128)S(1)} %get-tuple-element.178.act_ref) | copy-start | bytes 6291460
  312.4 27.6 %copy-start.45 = (bf16[256,2048]{1,0:T(8,128)(2,1)S(1)}, bf16[256,2048]{1,0:T(8,128)(2,1)}, u32[]{:S(2)}) copy-start(bf16[256,2048]{1,0:T(8,128)(2,1)} %get-tuple-element.112) | copy-start | bytes 3145732
  340.0 30.2 %collective-permute-start.1 = (bf16[256,2048]{1,0:T(8,128)(2,1)S(1)}, bf16[256,2048]{1,0:T(8,128)(2,1)S(1)}, u32[]{:S(2)}, u32[]{:S(2)}) collective-permute-start(bf16[256,2048]{1,0:T(8,128)(2,1)S(1)} %copy-done.45), channel_id=1, source_target_pairs={{0,8},{24,16},{1,9},{25,17},{2,10},{26,18},{3,11},{27,19},{4,12},{... | collective-permute-start | bytes 3145736 | tf_op jit(solution)/shard_map/ppermute | solution.py:886
  436.8 26.5 %copy-start.3 = (f32[2048,256]{1,0:T(8,128)S(1)}, f32[2048,256]{1,0:T(8,128)}, u32[]{:S(2)}) copy-start(f32[2048,256]{1,0:T(8,128)} %copy-done.2) | copy-start | bytes 6291460
  480.2 51.5 %copy-start.38 = (f32[2,128,2048]{2,1,0:T(8,128)S(1)}, f32[2,128,2048]{2,1,0:T(8,128)}, u32[]{:S(2)}) copy-start(f32[2,128,2048]{2,1,0:T(8,128)} %param.12) | copy-start | bytes 6291460
  480.2 51.5 %copy-start.57 = (bf16[128,2048]{1,0:T(8,128)(2,1)S(1)}, bf16[128,2048]{1,0:T(8,128)(2,1)}, u32[]{:S(2)}) copy-start(bf16[128,2048]{1,0:T(8,128)(2,1)} %get-tuple-element.105) | copy-start | bytes 1572868
  597.9 35.8 %copy-start.55 = (f32[2048,256]{1,0:T(8,128)S(1)}, f32[2048,256]{1,0:T(8,128)}, u32[]{:S(2)}) copy-start(f32[2048,256]{1,0:T(8,128)} %get-tuple-element.237) | copy-start | bytes 6291460
  640.4 38.0 %copy-start.101 = (f32[2048,256]{1,0:T(8,128)S(1)}, f32[2048,256]{1,0:T(8,128)}, u32[]{:S(2)}) copy-start(f32[2048,256]{1,0:T(8,128)} %get-tuple-element.134) | copy-start | bytes 6291460
  640.4 38.0 %copy-start.103 = (bf16[2048,256]{1,0:T(8,128)(2,1)S(1)}, bf16[2048,256]{1,0:T(8,128)(2,1)}, u32[]{:S(2)}) copy-start(bf16[2048,256]{1,0:T(8,128)(2,1)} %get-tuple-element.239) | copy-start | bytes 3145732
  641.6 35.2 %copy-start.1 = (f32[2048,256]{1,0:T(8,128)S(1)}, f32[2048,256]{1,0:T(8,128)}, u32[]{:S(2)}) copy-start(f32[2048,256]{1,0:T(8,128)} %copy-done) | copy-start | bytes 6291460
  693.1 59.6 %copy-start.92 = (f32[1,2,8,1,128]{4,3,2,1,0:T(1,128)S(1)}, f32[1,2,8,1,128]{4,3,2,1,0:T(1,128)}, u32[]{:S(2)}) copy-start(f32[1,2,8,1,128]{4,3,2,1,0:T(1,128)} %copy-done.91) | copy-start | bytes 24580
  693.1 61.2 %copy-start.26 = (bf16[128,2048]{1,0:T(8,128)(2,1)S(1)}, bf16[128,2048]{1,0:T(8,128)(2,1)}, u32[]{:S(2)}) copy-start(bf16[128,2048]{1,0:T(8,128)(2,1)} %fusion.44.refs_0_.refs_2_.refs_15_) | copy-start | bytes 1572868
  693.1 61.2 %copy-start.98 = (f32[128]{0:T(128)S(1)}, f32[128]{0:T(128)}, u32[]{:S(2)}) copy-start(f32[128]{0:T(128)} %copy-done.97) | copy-start | bytes 1540
  693.1 61.3 %copy-start.100 = (f32[128]{0:T(128)S(1)}, f32[128]{0:T(128)}, u32[]{:S(2)}) copy-start(f32[128]{0:T(128)} %get-tuple-element.232) | copy-start | bytes 1540
  755.6 24.9 %collective-permute-start.3 = (bf16[128,2048]{1,0:T(8,128)(2,1)}, bf16[128,2048]{1,0:T(8,128)(2,1)}, u32[]{:S(2)}, u32[]{:S(2)}) collective-permute-start(bf16[128,2048]{1,0:T(8,128)(2,1)} %fusion.36), channel_id=1, source_target_pairs={{8,0},{24,8},{9,1},{25,9},{10,2},{26,10},{11,3},{27,11},{12,4},{28... | collective-permute-start | bytes 1572872 | tf_op jit(solution)/shard_map/ppermute | solution.py:1156
  757.1 22.3 %collective-permute-start.2 = (bf16[128,2048]{1,0:T(8,128)(2,1)}, bf16[128,2048]{1,0:T(8,128)(2,1)}, u32[]{:S(2)}, u32[]{:S(2)}) collective-permute-start(bf16[128,2048]{1,0:T(8,128)(2,1)} %fusion.36), channel_id=1, source_target_pairs={{16,8},{17,9},{18,10},{19,11},{20,12},{21,13},{22,14},{23,15}} | collective-permute-start | bytes 1572872 | tf_op jit(solution)/shard_map/ppermute | solution.py:1155
  763.0 13.0 %collective-permute-start.4 = (bf16[304,256]{1,0:T(8,128)(2,1)S(1)}, bf16[304,256]{1,0:T(8,128)(2,1)}, u32[]{:S(2)}, u32[]{:S(2)}) collective-permute-start(bf16[304,256]{1,0:T(8,128)(2,1)S(1)} %add_convert_fusion.4), channel_id=1, source_target_pairs={{24,8},{25,9},{26,10},{27,11},{28,12},{29,13},{30,14},{31,15}} | collective-permute-start | bytes 466952 | tf_op jit(solution)/shard_map/ppermute | solution.py:1149
  (95 other events, 509.1 us)

commit v6 on v5

--- a/solution.py
+++ b/solution.py
@@ -295,10 +295,10 @@
 
 
 def rider_peers(here, kinds):
-    peers = [here.names(e) for e in range(1, here.count)] if "cube" in kinds else []
+    peers = [here.names(e) for e in range(1, here.count)] if set(kinds) & {"cube", "cube_cols"} else []
     if set(kinds) & {"swap", "stack", "home", "leave"}:
         peers.append(("q",))
-    if set(kinds) & {"over", "over_at", "out0", "out1", "back0", "back1"}:
+    if set(kinds) & {"over", "over_at", "over_cols0", "over_cols1", "out0", "out1", "back0", "back1"}:
         peers.append(("section",))
     return peers
 
@@ -308,14 +308,23 @@
     riders = list(zip(kinds, refs[:k], refs[k : 2 * k], refs[2 * k : 3 * k], refs[3 * k :]))
     q, chip = lax.axis_index("q"), here.other(0)
 
+    def row(kind, src, at):
+        if kind == "cube":
+            return src.at[at]
+        wide = src.shape[1] // here.count
+        return src.at[:, pl.ds(pl.multiple_of(at * wide, 128), wide)]
+
     def copies(kind, src, dst, send, recv):
-        if kind == "cube":
+        if kind in ("cube", "cube_cols"):
             return [
-                remote(src.at[here.other(e)], dst.at[chip], send.at[e], recv.at[e], here.toward(e))
+                remote(row(kind, src, here.other(e)), dst.at[chip], send.at[e], recv.at[e], here.toward(e))
                 for e in range(1, here.count)
             ]
-        if kind in ("over", "over_at") or kind[:-1] in ("out", "back"):
+        if kind in ("over", "over_at") or kind[:-1] in ("out", "back", "over_cols"):
             src = src.at[1 - here.s] if kind == "over_at" else src
+            if kind[:-1] == "over_cols":
+                wide = src.shape[1] // 4
+                src = src.at[:, pl.ds(pl.multiple_of((int(kind[-1]) * 2 + 1 - here.s) * wide, 128), wide)]
             return [remote(src, dst, send.at[0], recv.at[0], {"section": 1 - here.s})]
         return [remote(src, dst.at[q] if kind == "stack" else dst, send.at[0], recv.at[0], {"q": 1 - q})]
 
@@ -331,8 +340,8 @@
 
     def start():
         for kind, src, dst, send, recv in riders:
-            if kind == "cube":
-                pltpu.make_async_copy(src.at[chip], dst.at[chip], recv.at[0]).start()
+            if kind in ("cube", "cube_cols"):
+                pltpu.make_async_copy(row(kind, src, chip), dst.at[chip], recv.at[0]).start()
             if kind == "stack":
                 pltpu.make_async_copy(src, dst.at[q], recv.at[1]).start()
             for copy in copies(kind, src, dst, send, recv):
@@ -340,7 +349,7 @@
 
     def finish():
         for kind, src, dst, send, recv in riders:
-            if kind == "cube":
+            if kind in ("cube", "cube_cols"):
                 for e in range(here.count):
                     arrived(dst.at[here.other(e)], recv.at[e])
             elif kind == "stack":
@@ -356,12 +365,16 @@
 
 def rider_shapes(bits, riders):
     sems = pltpu.SemaphoreType.DMA((2 ** len(bits),))
-    shapes = [
-        jax.ShapeDtypeStruct(
-            array.shape[1:] if kind == "over_at" else ((2,) if kind == "stack" else ()) + array.shape, array.dtype
-        )
-        for kind, array in riders
-    ]
+    def made(kind, shape):
+        if kind == "over_at":
+            return shape[1:]
+        if kind[:-1] == "over_cols":
+            return (shape[0], shape[1] // 4)
+        if kind == "cube_cols":
+            return (2 ** len(bits), shape[0], shape[1] // 2 ** len(bits))
+        return ((2,) if kind == "stack" else ()) + shape
+
+    shapes = [jax.ShapeDtypeStruct(made(kind, array.shape), array.dtype) for kind, array in riders]
     return [array for _, array in riders], shapes, [sems] * (2 * len(riders))
 
 
@@ -754,10 +767,10 @@
     )(x, *arrays)
 
 
-def spread_kernel(bits, kinds, shard_ref, inner_ref, gate_ref, small, *refs):
+def spread_kernel(bits, kinds, count_blocks, shard_ref, *refs):
     here = Place(bits)
     along = len(kinds)
-    blocks = inner_ref, gate_ref
+    blocks, small, refs = refs[:count_blocks], refs[count_blocks], refs[count_blocks + 1 :]
     rider_in, refs = refs[:along], refs[along:]
     out_ref, rows, own_small, refs = refs[0], refs[1:3], refs[3], refs[4:]
     rider_out, refs = refs[:along], refs[along:]
@@ -768,15 +781,21 @@
     peers = [here.names(e) + extra for e in range(count) for extra in ((), ("section",)) if e or extra]
     here.meet(peers + [("q",), ("q", "section")])
 
+    def block(i, s_of, chip_of):
+        if count_blocks == 2:
+            return blocks[i].at[s_of, chip_of]
+        wide = blocks[0].shape[1] // (4 * count)
+        return blocks[0].at[:, pl.ds(pl.multiple_of(((i * 2 + s_of) * count + chip_of) * wide, 128), wide)]
+
     def piece(i, r, e):
         where = dict(here.toward(e), **({"section": 1 - s} if r else {}))
-        src = blocks[i].at[1 - s if r else s, here.other(e)]
+        src = block(i, 1 - s if r else s, here.other(e))
         return remote(src, rows[i].at[chip], piece_send.at[i, r, e], piece_recv.at[i, e], where)
 
     def hand_small(k, where):
         return remote(small, own_small, small_send.at[k], small_recv, where)
 
-    keep_pieces = [pltpu.make_async_copy(blocks[i].at[s, chip], rows[i].at[chip], piece_recv.at[i, 0]) for i in range(2)]
+    keep_pieces = [pltpu.make_async_copy(block(i, s, chip), rows[i].at[chip], piece_recv.at[i, 0]) for i in range(2)]
     keep_small = pltpu.make_async_copy(small, own_small, small_recv)
     at_layer = s == 0
     stays, leaves = jnp.logical_and(at_layer, q == s), jnp.logical_and(at_layer, q != s)
@@ -848,12 +867,16 @@
     padded = jnp.pad(shard[None, :], ((0, block[0] - 1), (0, block[1] - width)))
     dma = pltpu.SemaphoreType.DMA
     shapes = [jax.ShapeDtypeStruct((2, 2, count) + block, shard.dtype)]
-    shapes += [jax.ShapeDtypeStruct(b.shape[1:], b.dtype) for b in blocks] + [jax.ShapeDtypeStruct(small.shape, small.dtype)]
+    if len(blocks) == 2:
+        piece = blocks[0].shape[1:]
+    else:
+        piece = (count, blocks[0].shape[0], blocks[0].shape[1] // (4 * count))
+    shapes += [jax.ShapeDtypeStruct(piece, b.dtype) for b in (blocks[0], blocks[0])] + [jax.ShapeDtypeStruct(small.shape, small.dtype)]
     inside, outside = pl.BlockSpec(memory_space=pltpu.VMEM), pl.BlockSpec(memory_space=pl.ANY)
     out, *gots = pl.pallas_call(
-        functools.partial(spread_kernel, bits, tuple(kind for kind, _ in riders)),
+        functools.partial(spread_kernel, bits, tuple(kind for kind, _ in riders), len(blocks)),
         out_shape=shapes + more_shapes,
-        in_specs=[inside] + [outside] * (3 + len(arrays)),
+        in_specs=[inside] + [outside] * (len(blocks) + 1 + len(arrays)),
         out_specs=[inside] + [outside] * (3 + len(arrays)),
         scratch_shapes=[dma((count,)), dma((count,)), dma((2,)), dma((2,))]
         + [dma((2, 2, count)), dma((2, count)), dma((2,)), dma]
@@ -1035,14 +1058,17 @@
         (dt_bias, skip_gain, dt_weight[0]),
         jnp.swapaxes(xproj_weight[0], 0, 1),
     )
-    blocks = column_blocks(bits, in_weight[0])
+    rows = in_weight[0]
+    channels = conv_bias.shape[1]
+    aligned = channels % 128 == 0
+    blocks = [rows] if aligned else column_blocks(bits, rows)
     tight = (2, 5, 9)
 
     def weight(pair):
         return pair.reshape((-1, pair.shape[-1]))
 
     def weight_grad(normed, d_out):
-        return cross_dot(normed, d_out).astype(BF).reshape((2,) + blocks[0].shape[1:])
+        return cross_dot(normed, d_out).astype(BF).reshape((2, 2 ** len(bits), rows.shape[0], channels))
 
     mine, others = by_q(hidden_in)
     gains, inner, gate, packed0, got = spread(bits, norm_gain[0], blocks, packed, [("leave", others)])
@@ -1052,16 +1078,22 @@
     inverse0, normed = normalize(stream0, gains[0])
     normed0, inner, gate, *sent = gather_call(
         bits, 1, [normed], shares=tight, us=60,
-        riders=[("stack", inner), ("stack", gate)] + [("over_at", b) for b in blocks] + [("out1", packed)] + [("out%d" % l, out_weight[0]) for l in range(2)],
+        riders=[("stack", inner), ("stack", gate)] + ([("over_cols0", rows), ("over_cols1", rows)] if aligned else [("over_at", b) for b in blocks])
+        + [("out1", packed)] + [("out%d" % l, out_weight[0]) for l in range(2)],
     )
     upper = lax.axis_index("section") == 1
-    columns = [jnp.where(upper, b[1], got) for b, got in zip(blocks, sent)]
+    if aligned:
+        slab = rows.shape[1] // 4
+        columns = [("cube_cols", jnp.where(upper, rows[:, slab : 2 * slab], sent[0]))]
+        columns += [("cube_cols", jnp.where(upper, rows[:, 3 * slab :], sent[1]))]
+    else:
+        columns = [("cube", jnp.where(upper, b[1], got)) for b, got in zip(blocks, sent)]
     packed_held = jnp.where(upper, packed, sent[2])
     out_held = jnp.where(upper, sent[3], out_weight[0]), jnp.where(upper, out_weight[0], sent[4])
     inner0, small0 = weight(inner), Small(packed0)
     extended0, conv0, act0, part = mixer_inputs(normed0, inner0, small0)
     part = after(part, out_held[0])
-    xproj0, inner, late_gate = sum_columns(bits, 4, part, [("cube", columns[0]), ("cube", columns[1])])
+    xproj0, inner, late_gate = sum_columns(bits, 4, part, columns)
     gate0 = weight(gate)
     out0 = jnp.where(at_home(), out_held[0], leave(after(out_held[0], xproj0)))
     kept0 = mixer(xproj0, act0, normed0, gate0, small0)
@@ -1077,12 +1109,12 @@
 
     stream1 = output0.astype(F32)
     inverse1, normed = normalize(stream1, gains[1])
-    normed1, grad_low1, inner, output0_home = gather_call(
-        bits, 2, [normed, grad1.astype(BF)], riders=[("stack", inner), ("home", output0)], shares=(3, 5, 8), us=65
+    normed1, grad_low1, inner = gather_call(
+        bits, 2, [normed, grad1.astype(BF)], riders=[("stack", inner)], shares=(4, 5, 7), us=65
     )
     inner1 = weight(inner)
     extended1, conv1, act1, part = mixer_inputs(normed1, inner1, small1)
-    (xproj1,) = sum_columns(bits, 5, after(part, out_held[1]))
+    xproj1, output0_home = sum_columns(bits, 5, after(part, out_held[1]), [("home", output0)])
     out1 = jnp.where(at_home(), out_held[1], leave(after(out_held[1], xproj1)))
     kept1 = mixer(xproj1, act1, normed1, gate1, small1)
 

time: 793 us -> 784 us (0.989)
  no operation moved by 1% of the time
where the time goes in v6:
time: 784 us; the launch traced here: 775 us
  Pallas kernels  600 us (77%)
  matrix products  81.6 us (10%)
  other arithmetic  62.7 us (8%)
  local copies, waits for them, and re-layouts  18.6 us (2%)
  starting transfers between devices  10.3 us (1%)
    pallas_call x3, Pallas kernels, gather_call(): pl.pallas_call(functools.partial(gather_kernel, bits, len(shards), tuple(...  168 us
    pallas_call x3, Pallas kernels, scatter_columns(): pl.pallas_call(functools.partial(scatter_kernel, bits, turned, grad is no...  162 us
    pallas_call x4, Pallas kernels, sum_columns(): pl.pallas_call(functools.partial(total_kernel, bits, tuple((kind for kind...  115 us
    pallas_call x2, Pallas kernels, recur_backward(): pl.pallas_call(functools.partial(recur_backward_kernel, bits, tuple((kind...  86.9 us
    dot_general x10, matrix products, cross_dot(): lax.dot_general(operand, factor, (((0,), (0,)), ((), ())), preferred_elem...  38.2 us
    pallas_call x2, Pallas kernels, recur_forward(): pl.pallas_call(recur_forward_kernel, grid=(tokens // BLOCK,), in_specs=[r...  36.5 us
    pallas_call x1, Pallas kernels, spread(): pl.pallas_call(functools.partial(spread_kernel, bits, tuple((kind for kin...  29.3 us
    dot_general x8, matrix products, forward_dot(): return jnp.dot(operand, factor, preferred_element_type=F32)  27.2 us
  transfers between devices with their start and end apart: 5, of which 0 were waited for; matrix products, arithmetic and copies ran while one was open for 4% of the time, Pallas kernels for 5%

profile of v6, /device:TPU:9, one launch (start us, length us, event | category | flops | bytes accessed | tf_op | source)
XLA Modules:
  0.0 775.3 jit_solution(9432352262470093484)
XLA Ops:
  7.3 29.3 %shard_map.194 = (bf16[2,2,8,16,128]{4,3,2,1,0:T(8,128)(2,1)}, bf16[8,128,256]{2,1,0:T(8,128)(2,1)}, bf16[8,128,256]{2,1,0:T(8,128)(2,1)}, bf16[304,256]{1,0:T(8,128)(2,1)}, bf16[128,2048]{1,0:T(8,128)(2,1)}) custom-call(bf16[16,128]{1,0:T(8,128)(2,1)} %pad.19.shard_ref, bf16[128,8192]{1,0:T(8,128)(2,1)} %bitcast.127, bf16[304,256]{1,0:T(8,128)(2,1)} %pad.20.refs_1_.refs_5_, ...), custom_call_target="tpu_custom_call" | custom-call | bytes 40800000 | tf_op jit(solution)/shard_map/pallas_call | solution.py:876
  42.4 52.8 %shard_map.195 = (bf16[2,8,128,2048]{3,2,1,0:T(8,128)(2,1)}, bf16[2,8,128,256]{3,2,1,0:T(8,128)(2,1)}, bf16[2,8,128,256]{3,2,1,0:T(8,128)(2,1)}, bf16[128,2048]{...) custom-call(bf16[128,2048]{1,0:T(8,128)(2,1)} %fusion.32.refs_0_, ...), custom_call_target="tpu_custom_call" | custom-call | bytes 204000000 | tf_op jit(solution)/shard_map/pallas_call | solution.py:450
  95.2 6.1 fusion.9
  110.7 29.7 %shard_map.196 = (bf16[160,2048]{1,0:T(8,128)(2,1)}, bf16[8,128,256]{2,1,0:T(8,128)(2,1)}, bf16[8,128,256]{2,1,0:T(8,128)(2,1)}) custom-call(f32[160,2048]{1,0:T(8,128)} %fusion.65.x_ref, bf16[128,2048]{1,0:T(8,128)(2,1)} %get-tuple-element.202.refs_0_, bf16[128,2048]{1,0:T(8,128)(2,1)} %get-tuple-element.201.refs_1_), custom_call_target="tpu_custom_call" | custom-call | bytes 74800000 | tf_op jit(solution)/shard_map/pallas_call | solution.py:748
  147.6 18.4 %shard_map.197 = (f32[2048,256]{1,0:T(8,128)S(1)}, f32[2048,16,256]{2,1,0:T(8,128)}, f32[16,256]{1,0:T(8,128)S(1)}) custom-call(f32[2048,256]{1,0:T(8,128)S(1)} %get-tuple-element.238.rate_ref, f32[2048,256]{1,0:T(8,128)S(1)} %get-tuple-element.184.act_ref, f32[16,2048]{1,0:T(8,128)S(1)} %get-tuple-element.214.key_ref, ...), custom_call_target="tpu_custom_call" | custom-call | bytes 3400000 | tf_op jit(solution)/shard_map/pallas_call | solution.py:98
  166.1 4.1 multiply_convert_fusion.1
  171.4 51.6 %shard_map.198 = (f32[128,2048]{1,0:T(8,128)}, bf16[304,256]{1,0:T(8,128)(2,1)}, bf16[128,2048]{1,0:T(8,128)(2,1)}, bf16[2,8,128,256]{3,2,1,0:T(8,128)(2,1)}) custom-call(bf16[2048,256]{1,0:T(8,128)(2,1)} %get-tuple-element.240.refs_0_, bf16[256,2048]{1,0:T(8,128)(2,1)} %broadcast_select_fusion.1.refs_1_, bf16[304,256]{1,0:T(8,128)(2,1)} %broadcast_select_fusion.14.refs_2_, ...), custom_call_target="tpu_custom_call" | custom-call | bytes 136000000 | tf_op jit(solution)/shard_map/pallas_call | solution.py:654
  227.4 69.3 %shard_map.199 = (bf16[2,8,128,2048]{3,2,1,0:T(8,128)(2,1)}, bf16[2,8,128,2048]{3,2,1,0:T(8,128)(2,1)}, bf16[2,8,128,256]{3,2,1,0:T(8,128)(2,1)}) custom-call(bf16[128,2048]{1,0:T(8,128)(2,1)} %fusion.40.refs_0_, bf16[128,2048]{1,0:T(8,128)(2,1)} %fusion.81.refs_1_, bf16[8,128,256]{2,1,0:T(8,128)(2,1)} %get-tuple-element.107.refs_2_), custom_call_target="tpu_custom_call" | custom-call | bytes 221000000 | tf_op jit(solution)/shard_map/pallas_call | solution.py:450
  296.8 6.0 fusion.8
  307.0 24.6 %shard_map.200 = (bf16[160,2048]{1,0:T(8,128)(2,1)}, bf16[128,2048]{1,0:T(8,128)(2,1)}) custom-call(f32[160,2048]{1,0:T(8,128)} %fusion.61.x_ref, bf16[128,2048]{1,0:T(8,128)(2,1)} %copy-done.23), custom_call_target="tpu_custom_call" | custom-call | bytes 74800000 | tf_op jit(solution)/shard_map/pallas_call | solution.py:748
  338.6 18.1 %shard_map.201 = (f32[2048,256]{1,0:T(8,128)S(1)}, f32[2048,16,256]{2,1,0:T(8,128)}, f32[16,256]{1,0:T(8,128)S(1)}) custom-call(f32[2048,256]{1,0:T(8,128)S(1)} %get-tuple-element.242.rate_ref, f32[2048,256]{1,0:T(8,128)S(1)} %get-tuple-element.180.act_ref, f32[16,2048]{1,0:T(8,128)S(1)} %get-tuple-element.212.key_ref, ...), custom_call_target="tpu_custom_call" | custom-call | bytes 3400000 | tf_op jit(solution)/shard_map/pallas_call | solution.py:98
  356.8 5.9 convolution_convert_fusion.7
  362.9 5.2 fusion.11
  375.1 50.7 %shard_map.202 = (f32[2048,256]{1,0:T(8,128)}, f32[2048,256]{1,0:T(8,128)}, f32[16,2048]{1,0:T(8,128)}, f32[16,2048]{1,0:T(8,128)}, f32[128,2048]{1,0:T(8,128)}, /*index=5*/bf16[8,128,256]{2,1,0:T(8,128)(2,1)}) custom-call(f32[2048,256]{1,0:T(8,128)} %copy-done.7, f32[2048,256]{1,0:T(8,128)} %copy-done.2, f32[2048,256]{1,0:T(8,128)} %get-tuple-element.200.grad_ref, ...), custom_call_target="tpu_custom_call" | custom-call | bytes 3400000 | tf_op jit(solution)/shard_map/pallas_call | solution.py:221
  431.9 25.4 %shard_map.203 = (bf16[160,2048]{1,0:T(8,128)(2,1)}, bf16[128,2048]{1,0:T(8,128)(2,1)}) custom-call(f32[160,2048]{1,0:T(8,128)} %pad_maximum_fusion.x_ref, bf16[128,2048]{1,0:T(8,128)(2,1)} %fusion.41.refs_0_.refs_13_), custom_call_target="tpu_custom_call" | custom-call | bytes 74800000 | tf_op jit(solution)/shard_map/pallas_call | solution.py:748
  474.0 51.0 %shard_map.204 = (f32[128,2048]{1,0:T(8,128)}, bf16[8,128,256]{2,1,0:T(8,128)(2,1)}, bf16[304,256]{1,0:T(8,128)(2,1)}, bf16[256,2048]{1,0:T(8,128)(2,1)}) custom-call(bf16[2048,256]{1,0:T(8,128)(2,1)} %copy-done.47, bf16[2048,256]{1,0:T(8,128)(2,1)} %copy-done.64, bf16[2048,256]{1,0:T(8,128)(2,1)} %bitcast.154, bf16[2048,256]{1,0:T(8,128)(2,1)} %bitcast.151, ...), custom_call_target="tpu_custom_call" | custom-call | bytes 136000000 | tf_op jit(solution)/shard_map/pallas_call | solution.py:654
  527.8 45.6 %shard_map.205 = (bf16[2,8,128,2048]{3,2,1,0:T(8,128)(2,1)}, bf16[8,128,256]{2,1,0:T(8,128)(2,1)}, bf16[128,2048]{1,0:T(8,128)(2,1)}) custom-call(bf16[128,2048]{1,0:T(8,128)(2,1)} %fusion.44.refs_0_.refs_2_.refs_15_, bf16[8,128,256]{2,1,0:T(8,128)(2,1)} %bitcast.144, bf16[128,2048]{1,0:T(8,128)(2,1)} %fusion.44.refs_0_.refs_2_.refs_15_), custom_call_target="tpu_custom_call" | custom-call | bytes 153000000 | tf_op jit(solution)/shard_map/pallas_call | solution.py:450
  573.5 7.2 convolution_convert_fusion.1.refs_1_
  580.7 6.8 multiply_reduce_fusion
  592.6 36.1 %shard_map.206 = (f32[2048,256]{1,0:T(8,128)}, f32[2048,256]{1,0:T(8,128)}, f32[16,2048]{1,0:T(8,128)}, f32[16,2048]{1,0:T(8,128)}, bf16[8,128,256]{2,1,0:T(8,128)(2,1)}, /*index=5*/bf16[8,128,256]{2,1,0:T(8,128)(2,1)}) custom-call(f32[2048,256]{1,0:T(8,128)} %copy-done.6, f32[2048,256]{1,0:T(8,128)} %copy-done, f32[2048,256]{1,0:T(8,128)} %get-tuple-element.197.grad_ref, ...), custom_call_target="tpu_custom_call" | custom-call | bytes 3400000 | tf_op jit(solution)/shard_map/pallas_call | solution.py:221
  635.1 35.3 %shard_map.207 = (bf16[160,2048]{1,0:T(8,128)(2,1)}, bf16[8,128,256]{2,1,0:T(8,128)(2,1)}, bf16[256,2048]{1,0:T(8,128)(2,1)}) custom-call(f32[160,2048]{1,0:T(8,128)} %pad_maximum_fusion.1.x_ref, bf16[8,128,256]{2,1,0:T(8,128)(2,1)} %fusion.47.refs_0_, bf16[256,2048]{1,0:T(8,128)(2,1)} %convolution_convert_fusion.1.refs_1_), custom_call_target="tpu_custom_call" | custom-call | bytes 74800000 | tf_op jit(solution)/shard_map/pallas_call | solution.py:748
  677.7 7.3 convolution_convert_fusion
  690.8 59.3 %shard_map.208 = (f32[128,2048]{1,0:T(8,128)}, bf16[8,128,256]{2,1,0:T(8,128)(2,1)}, bf16[8,128,256]{2,1,0:T(8,128)(2,1)}, bf16[304,256]{1,0:T(8,128)(2,1)}, bf1...) custom-call(bf16[2048,256]{1,0:T(8,128)(2,1)} %copy-done.44, ...), custom_call_target="tpu_custom_call" | custom-call | bytes 204000000 | tf_op jit(solution)/shard_map/pallas_call | solution.py:654
  753.0 5.8 collective-permute-start.2
  (334 shorter events, 121.4 us)
Async XLA Ops:
  5.2 32.9 %copy-start.43 = (bf16[2,128,2048]{2,1,0:T(8,128)(2,1)S(1)}, bf16[2,128,2048]{2,1,0:T(8,128)(2,1)}, u32[]{:S(2)}) copy-start(bf16[2,128,2048]{2,1,0:T(8,128)(2,1)} %param.11) | copy-start | bytes 3145732
  40.0 55.2 %copy-start.95 = (f32[128]{0:T(128)}, f32[128]{0:T(128)S(1)}, u32[]{:S(2)}) copy-start(f32[128]{0:T(128)S(1)} %get-tuple-element.235) | copy-start | bytes 1540
  103.9 476.8 %copy-start = (f32[2048,256]{1,0:T(8,128)}, f32[2048,256]{1,0:T(8,128)S(1)}, u32[]{:S(2)}) copy-start(f32[2048,256]{1,0:T(8,128)S(1)} %get-tuple-element.184.act_ref) | copy-start | bytes 6291460
  110.7 32.9 %copy-start.38 = (f32[2,128,2048]{2,1,0:T(8,128)S(1)}, f32[2,128,2048]{2,1,0:T(8,128)}, u32[]{:S(2)}) copy-start(f32[2,128,2048]{2,1,0:T(8,128)} %param.12) | copy-start | bytes 6291460
  110.7 33.9 %copy-start.85 = (bf16[304,256]{1,0:T(8,128)(2,1)S(1)}, bf16[304,256]{1,0:T(8,128)(2,1)}, u32[]{:S(2)}) copy-start(bf16[304,256]{1,0:T(8,128)(2,1)} %get-tuple-element.102) | copy-start | bytes 466948
  140.4 29.8 %collective-permute-start = (bf16[256,2048]{1,0:T(8,128)(2,1)}, bf16[256,2048]{1,0:T(8,128)(2,1)S(1)}, u32[]{:S(2)}, u32[]{:S(2)}) collective-permute-start(bf16[256,2048]{1,0:T(8,128)(2,1)} %get-tuple-element.101), channel_id=1, source_target_pairs={{0,8},{24,16},{1,9},{25,17},{2,10},{26,18},{3,11},{27,19},{4,12},{... | collective-permute-start | bytes 3145736 | tf_op jit(solution)/shard_map/ppermute | solution.py:909
  171.4 51.6 %copy-start.58 = (bf16[304,256]{1,0:T(8,128)(2,1)S(1)}, bf16[304,256]{1,0:T(8,128)(2,1)}, u32[]{:S(2)}) copy-start(bf16[304,256]{1,0:T(8,128)(2,1)} %broadcast_select_fusion.14.refs_2_) | copy-start | bytes 466948
  225.5 71.3 %copy-start.23 = (bf16[128,2048]{1,0:T(8,128)(2,1)}, bf16[128,2048]{1,0:T(8,128)(2,1)S(1)}, u32[]{:S(2)}) copy-start(bf16[128,2048]{1,0:T(8,128)(2,1)S(1)} %get-tuple-element.183.refs_0_.refs_11_) | copy-start | bytes 1572868
  305.3 57.5 %copy-start.2 = (f32[2048,256]{1,0:T(8,128)}, f32[2048,256]{1,0:T(8,128)S(1)}, u32[]{:S(2)}) copy-start(f32[2048,256]{1,0:T(8,128)S(1)} %get-tuple-element.180.act_ref) | copy-start | bytes 6291460
  332.5 30.2 %collective-permute-start.1 = (bf16[256,2048]{1,0:T(8,128)(2,1)}, bf16[256,2048]{1,0:T(8,128)(2,1)S(1)}, u32[]{:S(2)}, u32[]{:S(2)}) collective-permute-start(bf16[256,2048]{1,0:T(8,128)(2,1)} %get-tuple-element.114), channel_id=1, source_target_pairs={{0,8},{24,16},{1,9},{25,17},{2,10},{26,18},{3,11},{27,19},{4,12},{... | collective-permute-start | bytes 3145736 | tf_op jit(solution)/shard_map/ppermute | solution.py:909
  375.1 50.7 %copy-start.54 = (f32[2048,256]{1,0:T(8,128)S(1)}, f32[2048,256]{1,0:T(8,128)}, u32[]{:S(2)}) copy-start(f32[2048,256]{1,0:T(8,128)} %get-tuple-element.243) | copy-start | bytes 6291460
  474.0 52.5 %copy-start.39 = (f32[2,128,2048]{2,1,0:T(8,128)S(1)}, f32[2,128,2048]{2,1,0:T(8,128)}, u32[]{:S(2)}) copy-start(f32[2,128,2048]{2,1,0:T(8,128)} %param.12) | copy-start | bytes 6291460
  474.0 52.5 %copy-start.56 = (bf16[128,2048]{1,0:T(8,128)(2,1)S(1)}, bf16[128,2048]{1,0:T(8,128)(2,1)}, u32[]{:S(2)}) copy-start(bf16[128,2048]{1,0:T(8,128)(2,1)} %get-tuple-element.106) | copy-start | bytes 1572868
  592.6 36.2 %copy-start.53 = (f32[2048,256]{1,0:T(8,128)S(1)}, f32[2048,256]{1,0:T(8,128)}, u32[]{:S(2)}) copy-start(f32[2048,256]{1,0:T(8,128)} %get-tuple-element.239) | copy-start | bytes 6291460
  633.9 38.1 %copy-start.99 = (f32[2048,256]{1,0:T(8,128)S(1)}, f32[2048,256]{1,0:T(8,128)}, u32[]{:S(2)}) copy-start(f32[2048,256]{1,0:T(8,128)} %get-tuple-element.136) | copy-start | bytes 6291460
  633.9 38.1 %copy-start.102 = (bf16[2048,256]{1,0:T(8,128)(2,1)S(1)}, bf16[2048,256]{1,0:T(8,128)(2,1)}, u32[]{:S(2)}) copy-start(bf16[2048,256]{1,0:T(8,128)(2,1)} %get-tuple-element.241) | copy-start | bytes 3145732
  635.1 35.3 %copy-start.1 = (f32[2048,256]{1,0:T(8,128)S(1)}, f32[2048,256]{1,0:T(8,128)}, u32[]{:S(2)}) copy-start(f32[2048,256]{1,0:T(8,128)} %copy-done) | copy-start | bytes 6291460
  690.8 59.3 %copy-start.90 = (f32[1,2,8,1,128]{4,3,2,1,0:T(1,128)S(1)}, f32[1,2,8,1,128]{4,3,2,1,0:T(1,128)}, u32[]{:S(2)}) copy-start(f32[1,2,8,1,128]{4,3,2,1,0:T(1,128)} %copy-done.89) | copy-start | bytes 24580
  690.8 61.0 %copy-start.27 = (bf16[128,2048]{1,0:T(8,128)(2,1)S(1)}, bf16[128,2048]{1,0:T(8,128)(2,1)}, u32[]{:S(2)}) copy-start(bf16[128,2048]{1,0:T(8,128)(2,1)} %fusion.44.refs_0_.refs_2_.refs_15_) | copy-start | bytes 1572868
  690.8 61.0 %copy-start.96 = (f32[128]{0:T(128)S(1)}, f32[128]{0:T(128)}, u32[]{:S(2)}) copy-start(f32[128]{0:T(128)} %copy-done.95) | copy-start | bytes 1540
  690.8 61.0 %copy-start.98 = (f32[128]{0:T(128)S(1)}, f32[128]{0:T(128)}, u32[]{:S(2)}) copy-start(f32[128]{0:T(128)} %get-tuple-element.234) | copy-start | bytes 1540
  752.3 21.4 %collective-permute-start.3 = (bf16[128,2048]{1,0:T(8,128)(2,1)S(1)}, bf16[128,2048]{1,0:T(8,128)(2,1)S(1)}, u32[]{:S(2)}, u32[]{:S(2)}) collective-permute-start(bf16[128,2048]{1,0:T(8,128)(2,1)S(1)} %fusion.36), channel_id=1, source_target_pairs={{8,0},{24,8},{9,1},{25,9},{10,2},{26,10},{11,3},{27,11},{12,4},{28... | collective-permute-start | bytes 1572872 | tf_op jit(solution)/shard_map/ppermute | solution.py:1188
  753.0 20.6 %collective-permute-start.2 = (bf16[128,2048]{1,0:T(8,128)(2,1)S(1)}, bf16[128,2048]{1,0:T(8,128)(2,1)S(1)}, u32[]{:S(2)}, u32[]{:S(2)}) collective-permute-start(bf16[128,2048]{1,0:T(8,128)(2,1)S(1)} %fusion.36), channel_id=1, source_target_pairs={{16,8},{17,9},{18,10},{19,11},{20,12},{21,13},{22,14},{23,15}} | collective-permute-start | bytes 1572872 | tf_op jit(solution)/shard_map/ppermute | solution.py:1187
  758.9 12.1 %collective-permute-start.4 = (bf16[304,256]{1,0:T(8,128)(2,1)S(1)}, bf16[304,256]{1,0:T(8,128)(2,1)S(1)}, u32[]{:S(2)}, u32[]{:S(2)}) collective-permute-start(bf16[304,256]{1,0:T(8,128)(2,1)S(1)} %add_convert_fusion.4), channel_id=1, source_target_pairs={{24,8},{25,9},{26,10},{27,11},{28,12},{29,13},{30,14},{31,15}} | collective-permute-start | bytes 466952 | tf_op jit(solution)/shard_map/ppermute | solution.py:1181
  (94 other events, 552.9 us)

commit v7 on v6

--- a/solution.py
+++ b/solution.py
@@ -619,11 +619,12 @@
     steps = count // 2
     for m in range(steps - 1, 0, -1):
         if homing:
-            home_step(steps - 1 - m)
+            home_step(2 * (steps - 1 - m))
+            home_step(2 * (steps - 1 - m) + 1)
         work.pass_on(m)
     work.settle()
     if homing:
-        for e in range(steps - 1, count):
+        for e in range(count - 2, count):
             home_step(e)
         for e in range(count):
             home_end(e)

time: 784 us -> 784 us (level)
  no operation moved by 1% of the time
where the time goes in v7:
time: 784 us; the launch traced here: 775 us
  Pallas kernels  600 us (77%)
  matrix products  81.6 us (10%)
  other arithmetic  62.7 us (8%)
  local copies, waits for them, and re-layouts  18.6 us (2%)
  starting transfers between devices  10.3 us (1%)
    pallas_call x3, Pallas kernels, gather_call(): pl.pallas_call(functools.partial(gather_kernel, bits, len(shards), tuple(...  168 us
    pallas_call x3, Pallas kernels, scatter_columns(): pl.pallas_call(functools.partial(scatter_kernel, bits, turned, grad is no...  162 us
    pallas_call x4, Pallas kernels, sum_columns(): pl.pallas_call(functools.partial(total_kernel, bits, tuple((kind for kind...  115 us
    pallas_call x2, Pallas kernels, recur_backward(): pl.pallas_call(functools.partial(recur_backward_kernel, bits, tuple((kind...  86.9 us
    dot_general x10, matrix products, cross_dot(): lax.dot_general(operand, factor, (((0,), (0,)), ((), ())), preferred_elem...  38.2 us
    pallas_call x2, Pallas kernels, recur_forward(): pl.pallas_call(recur_forward_kernel, grid=(tokens // BLOCK,), in_specs=[r...  36.5 us
    pallas_call x1, Pallas kernels, spread(): pl.pallas_call(functools.partial(spread_kernel, bits, tuple((kind for kin...  29.3 us
    dot_general x8, matrix products, forward_dot(): return jnp.dot(operand, factor, preferred_element_type=F32)  27.2 us
  transfers between devices with their start and end apart: 5, of which 0 were waited for; matrix products, arithmetic and copies ran while one was open for 4% of the time, Pallas kernels for 5%

profile of v7, /device:TPU:9, one launch (start us, length us, event | category | flops | bytes accessed | tf_op | source)
XLA Modules:
  0.0 775.5 jit_solution(6947165893034690182)
XLA Ops:
  7.3 29.3 %shard_map.194 = (bf16[2,2,8,16,128]{4,3,2,1,0:T(8,128)(2,1)}, bf16[8,128,256]{2,1,0:T(8,128)(2,1)}, bf16[8,128,256]{2,1,0:T(8,128)(2,1)}, bf16[304,256]{1,0:T(8,128)(2,1)}, bf16[128,2048]{1,0:T(8,128)(2,1)}) custom-call(bf16[16,128]{1,0:T(8,128)(2,1)} %pad.19.shard_ref, bf16[128,8192]{1,0:T(8,128)(2,1)} %bitcast.127, bf16[304,256]{1,0:T(8,128)(2,1)} %pad.20.refs_1_.refs_5_, ...), custom_call_target="tpu_custom_call" | custom-call | bytes 40800000 | tf_op jit(solution)/shard_map/pallas_call | solution.py:877
  42.4 52.8 %shard_map.195 = (bf16[2,8,128,2048]{3,2,1,0:T(8,128)(2,1)}, bf16[2,8,128,256]{3,2,1,0:T(8,128)(2,1)}, bf16[2,8,128,256]{3,2,1,0:T(8,128)(2,1)}, bf16[128,2048]{...) custom-call(bf16[128,2048]{1,0:T(8,128)(2,1)} %fusion.32.refs_0_, ...), custom_call_target="tpu_custom_call" | custom-call | bytes 204000000 | tf_op jit(solution)/shard_map/pallas_call | solution.py:450
  95.2 6.1 fusion.9
  110.7 29.7 %shard_map.196 = (bf16[160,2048]{1,0:T(8,128)(2,1)}, bf16[8,128,256]{2,1,0:T(8,128)(2,1)}, bf16[8,128,256]{2,1,0:T(8,128)(2,1)}) custom-call(f32[160,2048]{1,0:T(8,128)} %fusion.65.x_ref, bf16[128,2048]{1,0:T(8,128)(2,1)} %get-tuple-element.202.refs_0_, bf16[128,2048]{1,0:T(8,128)(2,1)} %get-tuple-element.201.refs_1_), custom_call_target="tpu_custom_call" | custom-call | bytes 74800000 | tf_op jit(solution)/shard_map/pallas_call | solution.py:749
  147.6 18.4 %shard_map.197 = (f32[2048,256]{1,0:T(8,128)S(1)}, f32[2048,16,256]{2,1,0:T(8,128)}, f32[16,256]{1,0:T(8,128)S(1)}) custom-call(f32[2048,256]{1,0:T(8,128)S(1)} %get-tuple-element.238.rate_ref, f32[2048,256]{1,0:T(8,128)S(1)} %get-tuple-element.184.act_ref, f32[16,2048]{1,0:T(8,128)S(1)} %get-tuple-element.214.key_ref, ...), custom_call_target="tpu_custom_call" | custom-call | bytes 3400000 | tf_op jit(solution)/shard_map/pallas_call | solution.py:98
  166.1 4.1 multiply_convert_fusion.1
  171.4 51.6 %shard_map.198 = (f32[128,2048]{1,0:T(8,128)}, bf16[304,256]{1,0:T(8,128)(2,1)}, bf16[128,2048]{1,0:T(8,128)(2,1)}, bf16[2,8,128,256]{3,2,1,0:T(8,128)(2,1)}) custom-call(bf16[2048,256]{1,0:T(8,128)(2,1)} %get-tuple-element.240.refs_0_, bf16[256,2048]{1,0:T(8,128)(2,1)} %broadcast_select_fusion.1.refs_1_, bf16[304,256]{1,0:T(8,128)(2,1)} %broadcast_select_fusion.14.refs_2_, ...), custom_call_target="tpu_custom_call" | custom-call | bytes 136000000 | tf_op jit(solution)/shard_map/pallas_call | solution.py:655
  227.4 69.3 %shard_map.199 = (bf16[2,8,128,2048]{3,2,1,0:T(8,128)(2,1)}, bf16[2,8,128,2048]{3,2,1,0:T(8,128)(2,1)}, bf16[2,8,128,256]{3,2,1,0:T(8,128)(2,1)}) custom-call(bf16[128,2048]{1,0:T(8,128)(2,1)} %fusion.40.refs_0_, bf16[128,2048]{1,0:T(8,128)(2,1)} %fusion.81.refs_1_, bf16[8,128,256]{2,1,0:T(8,128)(2,1)} %get-tuple-element.107.refs_2_), custom_call_target="tpu_custom_call" | custom-call | bytes 221000000 | tf_op jit(solution)/shard_map/pallas_call | solution.py:450
  296.8 6.0 fusion.8
  307.0 24.6 %shard_map.200 = (bf16[160,2048]{1,0:T(8,128)(2,1)}, bf16[128,2048]{1,0:T(8,128)(2,1)}) custom-call(f32[160,2048]{1,0:T(8,128)} %fusion.61.x_ref, bf16[128,2048]{1,0:T(8,128)(2,1)} %copy-done.23), custom_call_target="tpu_custom_call" | custom-call | bytes 74800000 | tf_op jit(solution)/shard_map/pallas_call | solution.py:749
  338.6 18.1 %shard_map.201 = (f32[2048,256]{1,0:T(8,128)S(1)}, f32[2048,16,256]{2,1,0:T(8,128)}, f32[16,256]{1,0:T(8,128)S(1)}) custom-call(f32[2048,256]{1,0:T(8,128)S(1)} %get-tuple-element.242.rate_ref, f32[2048,256]{1,0:T(8,128)S(1)} %get-tuple-element.180.act_ref, f32[16,2048]{1,0:T(8,128)S(1)} %get-tuple-element.212.key_ref, ...), custom_call_target="tpu_custom_call" | custom-call | bytes 3400000 | tf_op jit(solution)/shard_map/pallas_call | solution.py:98
  356.8 5.9 convolution_convert_fusion.7
  362.9 5.2 fusion.11
  375.1 50.7 %shard_map.202 = (f32[2048,256]{1,0:T(8,128)}, f32[2048,256]{1,0:T(8,128)}, f32[16,2048]{1,0:T(8,128)}, f32[16,2048]{1,0:T(8,128)}, f32[128,2048]{1,0:T(8,128)}, /*index=5*/bf16[8,128,256]{2,1,0:T(8,128)(2,1)}) custom-call(f32[2048,256]{1,0:T(8,128)} %copy-done.7, f32[2048,256]{1,0:T(8,128)} %copy-done.2, f32[2048,256]{1,0:T(8,128)} %get-tuple-element.200.grad_ref, ...), custom_call_target="tpu_custom_call" | custom-call | bytes 3400000 | tf_op jit(solution)/shard_map/pallas_call | solution.py:221
  431.9 25.4 %shard_map.203 = (bf16[160,2048]{1,0:T(8,128)(2,1)}, bf16[128,2048]{1,0:T(8,128)(2,1)}) custom-call(f32[160,2048]{1,0:T(8,128)} %pad_maximum_fusion.x_ref, bf16[128,2048]{1,0:T(8,128)(2,1)} %fusion.41.refs_0_.refs_13_), custom_call_target="tpu_custom_call" | custom-call | bytes 74800000 | tf_op jit(solution)/shard_map/pallas_call | solution.py:749
  474.0 51.0 %shard_map.204 = (f32[128,2048]{1,0:T(8,128)}, bf16[8,128,256]{2,1,0:T(8,128)(2,1)}, bf16[304,256]{1,0:T(8,128)(2,1)}, bf16[256,2048]{1,0:T(8,128)(2,1)}) custom-call(bf16[2048,256]{1,0:T(8,128)(2,1)} %copy-done.47, bf16[2048,256]{1,0:T(8,128)(2,1)} %copy-done.64, bf16[2048,256]{1,0:T(8,128)(2,1)} %bitcast.154, bf16[2048,256]{1,0:T(8,128)(2,1)} %bitcast.151, ...), custom_call_target="tpu_custom_call" | custom-call | bytes 136000000 | tf_op jit(solution)/shard_map/pallas_call | solution.py:655
  527.8 45.6 %shard_map.205 = (bf16[2,8,128,2048]{3,2,1,0:T(8,128)(2,1)}, bf16[8,128,256]{2,1,0:T(8,128)(2,1)}, bf16[128,2048]{1,0:T(8,128)(2,1)}) custom-call(bf16[128,2048]{1,0:T(8,128)(2,1)} %fusion.44.refs_0_.refs_2_.refs_15_, bf16[8,128,256]{2,1,0:T(8,128)(2,1)} %bitcast.144, bf16[128,2048]{1,0:T(8,128)(2,1)} %fusion.44.refs_0_.refs_2_.refs_15_), custom_call_target="tpu_custom_call" | custom-call | bytes 153000000 | tf_op jit(solution)/shard_map/pallas_call | solution.py:450
  573.5 7.2 convolution_convert_fusion.1.refs_1_
  580.7 6.8 multiply_reduce_fusion
  592.6 36.1 %shard_map.206 = (f32[2048,256]{1,0:T(8,128)}, f32[2048,256]{1,0:T(8,128)}, f32[16,2048]{1,0:T(8,128)}, f32[16,2048]{1,0:T(8,128)}, bf16[8,128,256]{2,1,0:T(8,128)(2,1)}, /*index=5*/bf16[8,128,256]{2,1,0:T(8,128)(2,1)}) custom-call(f32[2048,256]{1,0:T(8,128)} %copy-done.6, f32[2048,256]{1,0:T(8,128)} %copy-done, f32[2048,256]{1,0:T(8,128)} %get-tuple-element.197.grad_ref, ...), custom_call_target="tpu_custom_call" | custom-call | bytes 3400000 | tf_op jit(solution)/shard_map/pallas_call | solution.py:221
  635.1 35.3 %shard_map.207 = (bf16[160,2048]{1,0:T(8,128)(2,1)}, bf16[8,128,256]{2,1,0:T(8,128)(2,1)}, bf16[256,2048]{1,0:T(8,128)(2,1)}) custom-call(f32[160,2048]{1,0:T(8,128)} %pad_maximum_fusion.1.x_ref, bf16[8,128,256]{2,1,0:T(8,128)(2,1)} %fusion.47.refs_0_, bf16[256,2048]{1,0:T(8,128)(2,1)} %convolution_convert_fusion.1.refs_1_), custom_call_target="tpu_custom_call" | custom-call | bytes 74800000 | tf_op jit(solution)/shard_map/pallas_call | solution.py:749
  677.7 7.3 convolution_convert_fusion
  690.8 59.4 %shard_map.208 = (f32[128,2048]{1,0:T(8,128)}, bf16[8,128,256]{2,1,0:T(8,128)(2,1)}, bf16[8,128,256]{2,1,0:T(8,128)(2,1)}, bf16[304,256]{1,0:T(8,128)(2,1)}, bf1...) custom-call(bf16[2048,256]{1,0:T(8,128)(2,1)} %copy-done.44, ...), custom_call_target="tpu_custom_call" | custom-call | bytes 204000000 | tf_op jit(solution)/shard_map/pallas_call | solution.py:655
  753.1 5.8 collective-permute-start.2
  (334 shorter events, 121.4 us)
Async XLA Ops:
  5.2 32.9 %copy-start.43 = (bf16[2,128,2048]{2,1,0:T(8,128)(2,1)S(1)}, bf16[2,128,2048]{2,1,0:T(8,128)(2,1)}, u32[]{:S(2)}) copy-start(bf16[2,128,2048]{2,1,0:T(8,128)(2,1)} %param.11) | copy-start | bytes 3145732
  40.0 55.2 %copy-start.95 = (f32[128]{0:T(128)}, f32[128]{0:T(128)S(1)}, u32[]{:S(2)}) copy-start(f32[128]{0:T(128)S(1)} %get-tuple-element.235) | copy-start | bytes 1540
  103.9 476.8 %copy-start = (f32[2048,256]{1,0:T(8,128)}, f32[2048,256]{1,0:T(8,128)S(1)}, u32[]{:S(2)}) copy-start(f32[2048,256]{1,0:T(8,128)S(1)} %get-tuple-element.184.act_ref) | copy-start | bytes 6291460
  110.7 32.9 %copy-start.38 = (f32[2,128,2048]{2,1,0:T(8,128)S(1)}, f32[2,128,2048]{2,1,0:T(8,128)}, u32[]{:S(2)}) copy-start(f32[2,128,2048]{2,1,0:T(8,128)} %param.12) | copy-start | bytes 6291460
  110.7 33.9 %copy-start.85 = (bf16[304,256]{1,0:T(8,128)(2,1)S(1)}, bf16[304,256]{1,0:T(8,128)(2,1)}, u32[]{:S(2)}) copy-start(bf16[304,256]{1,0:T(8,128)(2,1)} %get-tuple-element.102) | copy-start | bytes 466948
  140.4 29.8 %collective-permute-start = (bf16[256,2048]{1,0:T(8,128)(2,1)}, bf16[256,2048]{1,0:T(8,128)(2,1)S(1)}, u32[]{:S(2)}, u32[]{:S(2)}) collective-permute-start(bf16[256,2048]{1,0:T(8,128)(2,1)} %get-tuple-element.101), channel_id=1, source_target_pairs={{0,8},{24,16},{1,9},{25,17},{2,10},{26,18},{3,11},{27,19},{4,12},{... | collective-permute-start | bytes 3145736 | tf_op jit(solution)/shard_map/ppermute | solution.py:910
  171.4 51.6 %copy-start.58 = (bf16[304,256]{1,0:T(8,128)(2,1)S(1)}, bf16[304,256]{1,0:T(8,128)(2,1)}, u32[]{:S(2)}) copy-start(bf16[304,256]{1,0:T(8,128)(2,1)} %broadcast_select_fusion.14.refs_2_) | copy-start | bytes 466948
  225.5 71.3 %copy-start.23 = (bf16[128,2048]{1,0:T(8,128)(2,1)}, bf16[128,2048]{1,0:T(8,128)(2,1)S(1)}, u32[]{:S(2)}) copy-start(bf16[128,2048]{1,0:T(8,128)(2,1)S(1)} %get-tuple-element.183.refs_0_.refs_11_) | copy-start | bytes 1572868
  305.3 57.5 %copy-start.2 = (f32[2048,256]{1,0:T(8,128)}, f32[2048,256]{1,0:T(8,128)S(1)}, u32[]{:S(2)}) copy-start(f32[2048,256]{1,0:T(8,128)S(1)} %get-tuple-element.180.act_ref) | copy-start | bytes 6291460
  332.5 30.2 %collective-permute-start.1 = (bf16[256,2048]{1,0:T(8,128)(2,1)}, bf16[256,2048]{1,0:T(8,128)(2,1)S(1)}, u32[]{:S(2)}, u32[]{:S(2)}) collective-permute-start(bf16[256,2048]{1,0:T(8,128)(2,1)} %get-tuple-element.114), channel_id=1, source_target_pairs={{0,8},{24,16},{1,9},{25,17},{2,10},{26,18},{3,11},{27,19},{4,12},{... | collective-permute-start | bytes 3145736 | tf_op jit(solution)/shard_map/ppermute | solution.py:910
  375.1 50.7 %copy-start.54 = (f32[2048,256]{1,0:T(8,128)S(1)}, f32[2048,256]{1,0:T(8,128)}, u32[]{:S(2)}) copy-start(f32[2048,256]{1,0:T(8,128)} %get-tuple-element.243) | copy-start | bytes 6291460
  474.0 52.5 %copy-start.39 = (f32[2,128,2048]{2,1,0:T(8,128)S(1)}, f32[2,128,2048]{2,1,0:T(8,128)}, u32[]{:S(2)}) copy-start(f32[2,128,2048]{2,1,0:T(8,128)} %param.12) | copy-start | bytes 6291460
  474.0 52.5 %copy-start.56 = (bf16[128,2048]{1,0:T(8,128)(2,1)S(1)}, bf16[128,2048]{1,0:T(8,128)(2,1)}, u32[]{:S(2)}) copy-start(bf16[128,2048]{1,0:T(8,128)(2,1)} %get-tuple-element.106) | copy-start | bytes 1572868
  592.6 36.2 %copy-start.53 = (f32[2048,256]{1,0:T(8,128)S(1)}, f32[2048,256]{1,0:T(8,128)}, u32[]{:S(2)}) copy-start(f32[2048,256]{1,0:T(8,128)} %get-tuple-element.239) | copy-start | bytes 6291460
  633.9 38.1 %copy-start.99 = (f32[2048,256]{1,0:T(8,128)S(1)}, f32[2048,256]{1,0:T(8,128)}, u32[]{:S(2)}) copy-start(f32[2048,256]{1,0:T(8,128)} %get-tuple-element.136) | copy-start | bytes 6291460
  633.9 38.1 %copy-start.102 = (bf16[2048,256]{1,0:T(8,128)(2,1)S(1)}, bf16[2048,256]{1,0:T(8,128)(2,1)}, u32[]{:S(2)}) copy-start(bf16[2048,256]{1,0:T(8,128)(2,1)} %get-tuple-element.241) | copy-start | bytes 3145732
  635.1 35.3 %copy-start.1 = (f32[2048,256]{1,0:T(8,128)S(1)}, f32[2048,256]{1,0:T(8,128)}, u32[]{:S(2)}) copy-start(f32[2048,256]{1,0:T(8,128)} %copy-done) | copy-start | bytes 6291460
  690.8 59.5 %copy-start.90 = (f32[1,2,8,1,128]{4,3,2,1,0:T(1,128)S(1)}, f32[1,2,8,1,128]{4,3,2,1,0:T(1,128)}, u32[]{:S(2)}) copy-start(f32[1,2,8,1,128]{4,3,2,1,0:T(1,128)} %copy-done.89) | copy-start | bytes 24580
  690.8 61.1 %copy-start.27 = (bf16[128,2048]{1,0:T(8,128)(2,1)S(1)}, bf16[128,2048]{1,0:T(8,128)(2,1)}, u32[]{:S(2)}) copy-start(bf16[128,2048]{1,0:T(8,128)(2,1)} %fusion.44.refs_0_.refs_2_.refs_15_) | copy-start | bytes 1572868
  690.8 61.1 %copy-start.96 = (f32[128]{0:T(128)S(1)}, f32[128]{0:T(128)}, u32[]{:S(2)}) copy-start(f32[128]{0:T(128)} %copy-done.95) | copy-start | bytes 1540
  690.8 61.1 %copy-start.98 = (f32[128]{0:T(128)S(1)}, f32[128]{0:T(128)}, u32[]{:S(2)}) copy-start(f32[128]{0:T(128)} %get-tuple-element.234) | copy-start | bytes 1540
  752.4 21.4 %collective-permute-start.3 = (bf16[128,2048]{1,0:T(8,128)(2,1)S(1)}, bf16[128,2048]{1,0:T(8,128)(2,1)S(1)}, u32[]{:S(2)}, u32[]{:S(2)}) collective-permute-start(bf16[128,2048]{1,0:T(8,128)(2,1)S(1)} %fusion.36), channel_id=1, source_target_pairs={{8,0},{24,8},{9,1},{25,9},{10,2},{26,10},{11,3},{27,11},{12,4},{28... | collective-permute-start | bytes 1572872 | tf_op jit(solution)/shard_map/ppermute | solution.py:1189
  753.1 20.6 %collective-permute-start.2 = (bf16[128,2048]{1,0:T(8,128)(2,1)S(1)}, bf16[128,2048]{1,0:T(8,128)(2,1)S(1)}, u32[]{:S(2)}, u32[]{:S(2)}) collective-permute-start(bf16[128,2048]{1,0:T(8,128)(2,1)S(1)} %fusion.36), channel_id=1, source_target_pairs={{16,8},{17,9},{18,10},{19,11},{20,12},{21,13},{22,14},{23,15}} | collective-permute-start | bytes 1572872 | tf_op jit(solution)/shard_map/ppermute | solution.py:1188
  759.0 12.1 %collective-permute-start.4 = (bf16[304,256]{1,0:T(8,128)(2,1)S(1)}, bf16[304,256]{1,0:T(8,128)(2,1)S(1)}, u32[]{:S(2)}, u32[]{:S(2)}) collective-permute-start(bf16[304,256]{1,0:T(8,128)(2,1)S(1)} %add_convert_fusion.4), channel_id=1, source_target_pairs={{24,8},{25,9},{26,10},{27,11},{28,12},{29,13},{30,14},{31,15}} | collective-permute-start | bytes 466952 | tf_op jit(solution)/shard_map/ppermute | solution.py:1182
  (94 other events, 552.9 us)
